TPU v7x, 32 devices: a whole 2x2x4 slice. The times are simulated.
32 devices in a mesh: wide: 16 (over z, x, core), narrow: 2 (over y).
Axes of the slice: x: 2, y: 2, z: 4, core: 2. Of those that a mesh axis runs over, the one named last changes fastest.
Arguments:
- images: bfloat16 [64, 16, 14, 1024], P('wide', 'narrow')
- crop: int32 [64], replicated, may hold values from 96 to 224, as said below
- micro: int32 [64], replicated, may hold values from 0 to 1, as said below
- first_reduce: bfloat16 [1024, 512], replicated, may hold values from -0.1875 to 0.1875
- first_reduce_gain: bfloat16 [512], replicated, may hold values from 0.099609375 to 1.8984375
- first_reduce_bias: bfloat16 [512], replicated, may hold values from -2.5 to 2.5
- first_spatial: bfloat16 [3, 3, 512, 512], replicated, may hold values from -0.09375 to 0.09375
- first_spatial_gain: bfloat16 [512], replicated, may hold values from 0.099609375 to 1.8984375
- first_spatial_bias: bfloat16 [512], replicated, may hold values from -2.5 to 2.5
- first_expand: bfloat16 [512, 2048], replicated, may hold values from -0.25 to 0.25
- first_expand_gain: bfloat16 [2048], replicated, may hold values from 0.099609375 to 1.8984375
- first_expand_bias: bfloat16 [2048], replicated, may hold values from -2.5 to 2.5
- first_project: bfloat16 [1024, 2048], replicated, may hold values from -0.1875 to 0.1875
- first_project_gain: bfloat16 [2048], replicated, may hold values from 0.099609375 to 1.8984375
- first_project_bias: bfloat16 [2048], replicated, may hold values from -2.5 to 2.5
- first_squeeze: bfloat16 [2048, 128], replicated, may hold values from -0.25 to 0.25
- first_squeeze_bias: bfloat16 [128], replicated, may hold values from -2.5 to 2.5
- first_excite: bfloat16 [128, 2048], replicated, may hold values from -0.5 to 0.5
- first_excite_bias: bfloat16 [2048], replicated, may hold values from -2.5 to 2.5
- second_reduce: bfloat16 [2048, 512], P('narrow'), may hold values from -0.125 to 0.125
- second_reduce_gain: bfloat16 [512], replicated, may hold values from 0.099609375 to 1.8984375
- second_reduce_bias: bfloat16 [512], replicated, may hold values from -2.5 to 2.5
- second_spatial: bfloat16 [3, 3, 512, 512], P(None, None, None, 'narrow'), may hold values from -0.09375 to 0.09375
- second_spatial_gain: bfloat16 [512], P('narrow'), may hold values from 0.099609375 to 1.8984375
- second_spatial_bias: bfloat16 [512], P('narrow'), may hold values from -2.5 to 2.5
- second_expand: bfloat16 [512, 2048], P('narrow'), may hold values from -0.25 to 0.25
- second_expand_gain: bfloat16 [2048], P('narrow'), may hold values from 0.099609375 to 1.8984375
- second_expand_bias: bfloat16 [2048], P('narrow'), may hold values from -2.5 to 2.5
- second_squeeze: bfloat16 [2048, 128], P('narrow'), may hold values from -0.25 to 0.25
- second_squeeze_bias: bfloat16 [128], replicated, may hold values from -2.5 to 2.5
- second_excite: bfloat16 [128, 2048], P(None, 'narrow'), may hold values from -0.5 to 0.5
- second_excite_bias: bfloat16 [2048], P('narrow'), may hold values from -2.5 to 2.5
- out_grad: bfloat16 [64, 8, 7, 2048], P('wide', None, None, 'narrow'), may hold values from -6 to 6
Outputs:
- result: bfloat16 [64, 8, 7, 2048], P('wide', None, None, 'narrow')
- grad_images: float32 [64, 16, 14, 1024], P('wide', 'narrow')
- grad_first_reduce: float32 [1024, 512], P('wide', 'narrow')
- grad_first_reduce_gain: float32 [512], replicated
- grad_first_reduce_bias: float32 [512], replicated
- grad_first_spatial: float32 [3, 3, 512, 512], P(None, None, 'wide', 'narrow')
- grad_first_spatial_gain: float32 [512], replicated
- grad_first_spatial_bias: float32 [512], replicated
- grad_first_expand: float32 [512, 2048], P('wide', 'narrow')
- grad_first_expand_gain: float32 [2048], replicated
- grad_first_expand_bias: float32 [2048], replicated
- grad_first_project: float32 [1024, 2048], P('wide', 'narrow')
- grad_first_project_gain: float32 [2048], replicated
- grad_first_project_bias: float32 [2048], replicated
- grad_first_squeeze: float32 [2048, 128], P('narrow', 'wide')
- grad_first_squeeze_bias: float32 [128], replicated
- grad_first_excite: float32 [128, 2048], P('wide', 'narrow')
- grad_first_excite_bias: float32 [2048], replicated
- grad_second_reduce: float32 [2048, 512], P('narrow', 'wide')
- grad_second_reduce_gain: float32 [512], replicated
- grad_second_reduce_bias: float32 [512], replicated
- grad_second_spatial: float32 [3, 3, 512, 512], P(None, None, 'wide', 'narrow')
- grad_second_spatial_gain: float32 [512], P('narrow')
- grad_second_spatial_bias: float32 [512], P('narrow')
- grad_second_expand: float32 [512, 2048], P('narrow', 'wide')
- grad_second_expand_gain: float32 [2048], P('narrow')
- grad_second_expand_bias: float32 [2048], P('narrow')
- grad_second_squeeze: float32 [2048, 128], P('narrow', 'wide')
- grad_second_squeeze_bias: float32 [128], replicated
- grad_second_excite: float32 [128, 2048], P('wide', 'narrow')
- grad_second_excite_bias: float32 [2048], P('narrow')
- norms: float32 [5], replicated
Inputs may be any that keep to these rules, and one draw needn't show every extreme that they name: Each image's crop is 96 or 224 pixels; at least one image of the batch is 224. Each micro-batch holds exactly 32 images.
All inputs are finite; a program needn't handle non-finite values.
Results may differ from a plain program's by a relative error of at most 0.025.
Values may be sent and summed in bfloat16 or wider, within the bound.
No kernel may reach another device: no remote copies, remote signals or barrier semaphores. Data moves between devices by JAX's collectives and lax.ppermute only.
A program may use at most 192 MiB of HBM per device.

v0:
```python
import jax
import jax.numpy as jnp
from jax import lax
from jax.sharding import PartitionSpec as P

C_OUT = 2048
MICRO = 2


EPSILON = 1e-05
HIGHEST = lax.Precision.HIGHEST


def passed_along(value, axis, steps):
    count = lax.axis_size(axis)
    leading, last = (max(0, -steps), min(count, count - steps))
    return lax.ppermute(value, axis, [(source, source + steps) for source in range(leading, last)])


def as_sent(array):

    def short(part):
        return part.astype(jnp.bfloat16) if part.dtype == jnp.float32 else part

    return jax.tree.map(short, array)


def silu_slope(values):
    logistic = jax.nn.sigmoid(values)
    return logistic * (1.0 + values * (1.0 - logistic))


def cell_mask(side_len, first_row, row_count, col_count):
    row_ids = first_row + jnp.arange(row_count, dtype=jnp.int32)
    col_ids = jnp.arange(col_count, dtype=jnp.int32)
    inside = (row_ids[None, :, None] < side_len[:, None, None]) & (
        col_ids[None, None, :] < side_len[:, None, None]
    )
    return inside.astype(jnp.float32)[..., None]


def as_float(values):
    return values.astype(jnp.float32)


def pointwise(values, weights):
    return jnp.einsum("brci,io->brco", values, weights, preferred_element_type=jnp.float32)


def transposed(gradient, weights):
    return jnp.einsum("brco,io->brci", gradient, weights, preferred_element_type=jnp.float32)


def weight_grad(values, gradient):
    return jnp.einsum("brci,brco->io", values, gradient, preferred_element_type=jnp.float32)


def tap_window(padded, offset_row, offset_col, stride, row_count, col_count):
    return padded[
        :,
        offset_row : offset_row + stride * (row_count - 1) + 1 : stride,
        offset_col : offset_col + stride * (col_count - 1) + 1 : stride,
        :,
    ]


def taps_forward(padded, weights, stride, row_count, col_count):
    running = None
    for offset_row in range(3):
        for offset_col in range(3):
            product_term = pointwise(
                tap_window(padded, offset_row, offset_col, stride, row_count, col_count),
                weights[offset_row, offset_col],
            )
            running = product_term if running is None else running + product_term
    return running


def taps_weight(padded, gradient, stride):
    row_count, col_count = (gradient.shape[1], gradient.shape[2])
    stacked_rows = []
    for offset_row in range(3):
        row_terms = []
        for offset_col in range(3):
            row_terms.append(
                weight_grad(
                    tap_window(padded, offset_row, offset_col, stride, row_count, col_count),
                    gradient,
                )
            )
        stacked_rows.append(jnp.stack(row_terms))
    return jnp.stack(stacked_rows)


def taps_input(gradient, weights, stride, padded_rows, padded_cols):
    row_count, col_count = (gradient.shape[1], gradient.shape[2])
    zero_value = jnp.zeros((), jnp.float32)
    running = None
    for offset_row in range(3):
        for offset_col in range(3):
            product_term = transposed(gradient, weights[offset_row, offset_col])
            placed = lax.pad(
                product_term,
                zero_value,
                (
                    (0, 0, 0),
                    (
                        offset_row,
                        padded_rows - offset_row - stride * (row_count - 1) - 1,
                        stride - 1,
                    ),
                    (
                        offset_col,
                        padded_cols - offset_col - stride * (col_count - 1) - 1,
                        stride - 1,
                    ),
                    (0, 0, 0),
                ),
            )
            running = placed if running is None else running + placed
    return running


def total_all(flattened):
    return lax.psum(flattened, ("wide", "narrow"))


def total_wide(flattened):
    return lax.psum(flattened, "wide")


def total_pair(values):
    return lax.psum(values.astype(jnp.bfloat16), "narrow").astype(jnp.float32)


def joined_sum(members, reducer):
    flattened = jnp.concatenate([segment.reshape(-1) for segment in members])
    summed = reducer(flattened)
    results = []
    offset = 0
    for segment in members:
        results.append(summed[offset : offset + segment.size].reshape(segment.shape))
        offset = offset + segment.size
    return results


def image_groups(onehot, per_image):
    return jnp.dot(onehot.T, per_image, precision=HIGHEST)


def forward_stats(values, keep_mask, onehot):
    masked = values * keep_mask
    return [
        image_groups(onehot, jnp.sum(masked, axis=(1, 2))),
        image_groups(onehot, jnp.sum(masked * values, axis=(1, 2))),
    ]


def backward_stats(grad_out, normed, onehot):
    return [
        image_groups(onehot, jnp.sum(grad_out, axis=(1, 2))),
        image_groups(onehot, jnp.sum(grad_out * normed, axis=(1, 2))),
    ]


def normalize(values, sums, onehot, counts):
    mean_value = sums[0] / counts[:, None]
    square_value = sums[1] / counts[:, None]
    scale_value = lax.rsqrt(square_value - mean_value * mean_value + EPSILON)
    mean_rows = jnp.dot(onehot, mean_value, precision=HIGHEST)[:, None, None, :]
    scale_rows = jnp.dot(onehot, scale_value, precision=HIGHEST)[:, None, None, :]
    return ((values - mean_rows) * scale_rows, scale_rows)


def normalize_back(grad_out, normed, scale_rows, gain_vector, keep_mask, sums, onehot, counts):
    mean_grad = jnp.dot(onehot, sums[0] / counts[:, None], precision=HIGHEST)[:, None, None, :]
    mean_cross = jnp.dot(onehot, sums[1] / counts[:, None], precision=HIGHEST)[:, None, None, :]
    grad_values = (
        (grad_out - mean_grad - normed * mean_cross) * (scale_rows * gain_vector) * keep_mask
    )
    return (grad_values, jnp.sum(sums[1], axis=0), jnp.sum(sums[0], axis=0))


def pair_totals(reduce_grad, spatial_grad, expand_grad, project_grad, squeeze_grad, excite_grad):
    return (
        lax.psum_scatter(
            reduce_grad.astype(jnp.bfloat16), "narrow", scatter_dimension=1, tiled=True
        ).astype(jnp.float32),
        lax.psum_scatter(
            spatial_grad.astype(jnp.bfloat16), "narrow", scatter_dimension=3, tiled=True
        ).astype(jnp.float32),
        lax.psum_scatter(
            expand_grad.astype(jnp.bfloat16), "narrow", scatter_dimension=1, tiled=True
        ).astype(jnp.float32),
        lax.psum_scatter(
            project_grad.astype(jnp.bfloat16), "narrow", scatter_dimension=1, tiled=True
        ).astype(jnp.float32),
        lax.psum_scatter(
            squeeze_grad.astype(jnp.bfloat16), "narrow", scatter_dimension=0, tiled=True
        ).astype(jnp.float32),
        lax.psum_scatter(
            excite_grad.astype(jnp.bfloat16), "narrow", scatter_dimension=1, tiled=True
        ).astype(jnp.float32),
    )


def wide_totals(reduce_grad, spatial_grad, expand_grad, project_grad, squeeze_grad, excite_grad):
    return (
        lax.psum_scatter(reduce_grad, "wide", scatter_dimension=0, tiled=True),
        lax.psum_scatter(spatial_grad, "wide", scatter_dimension=2, tiled=True),
        lax.psum_scatter(expand_grad, "wide", scatter_dimension=0, tiled=True),
        lax.psum_scatter(project_grad, "wide", scatter_dimension=0, tiled=True),
        lax.psum_scatter(squeeze_grad, "wide", scatter_dimension=1, tiled=True),
        lax.psum_scatter(excite_grad, "wide", scatter_dimension=0, tiled=True),
    )


def local(
    images,
    crop,
    micro,
    first_reduce,
    first_reduce_gain,
    first_reduce_bias,
    first_spatial,
    first_spatial_gain,
    first_spatial_bias,
    first_expand,
    first_expand_gain,
    first_expand_bias,
    first_project,
    first_project_gain,
    first_project_bias,
    first_squeeze,
    first_squeeze_bias,
    first_excite,
    first_excite_bias,
    second_reduce,
    second_reduce_gain,
    second_reduce_bias,
    second_spatial,
    second_spatial_gain,
    second_spatial_bias,
    second_expand,
    second_expand_gain,
    second_expand_bias,
    second_squeeze,
    second_squeeze_bias,
    second_excite,
    second_excite_bias,
    out_grad,
):
    pair_total = lax.axis_size("narrow")
    wide_at = lax.axis_index("wide")
    pair_at = lax.axis_index("narrow")
    local_count = images.shape[0]
    rows_in = images.shape[1]
    cols_in = images.shape[2]
    rows_half = rows_in // 2
    rows_out = out_grad.shape[1]
    cols_out = out_grad.shape[2]
    my_crop = lax.dynamic_slice_in_dim(crop, wide_at * local_count, local_count)
    my_micro = lax.dynamic_slice_in_dim(micro, wide_at * local_count, local_count)
    labels = jnp.arange(MICRO, dtype=jnp.int32)
    onehot = (my_micro[:, None] == labels[None, :]).astype(jnp.float32)
    onehot_all = (micro[:, None] == labels[None, :]).astype(jnp.float32)
    side_in_all = crop // 16
    side_out_all = crop // 32
    count_in = jnp.sum(
        onehot_all * (side_in_all * side_in_all).astype(jnp.float32)[:, None], axis=0
    )
    count_out = jnp.sum(
        onehot_all * (side_out_all * side_out_all).astype(jnp.float32)[:, None], axis=0
    )
    side_in = my_crop // 16
    side_out = my_crop // 32
    cell_counts = (side_out * side_out).astype(jnp.float32)[:, None]
    keep_in = cell_mask(side_in, pair_at * rows_in, rows_in, cols_in)
    keep_half = cell_mask(side_out, pair_at * rows_half, rows_half, cols_out)
    keep_out = cell_mask(side_out, 0, rows_out, cols_out)
    pixels = (as_float(images) * keep_in).astype(jnp.bfloat16)
    pre_one = pointwise(pixels, first_reduce)
    norm_one, scale_one = normalize(
        pre_one, joined_sum(forward_stats(pre_one, keep_in, onehot), total_all), onehot, count_in
    )
    out_one = norm_one * as_float(first_reduce_gain) + as_float(first_reduce_bias)
    hidden_one = (jax.nn.silu(out_one) * keep_in).astype(jnp.bfloat16)
    rim_row = passed_along(hidden_one[:, rows_in - 1 :], "narrow", 1)
    padded_one = jnp.pad(
        jnp.concatenate([rim_row, hidden_one], axis=1), ((0, 0), (0, 0), (1, 0), (0, 0))
    )
    pre_two = taps_forward(padded_one, first_spatial, 2, rows_half, cols_out)
    norm_two, scale_two = normalize(
        pre_two, joined_sum(forward_stats(pre_two, keep_half, onehot), total_all), onehot, count_out
    )
    out_two = norm_two * as_float(first_spatial_gain) + as_float(first_spatial_bias)
    hidden_two = (jax.nn.silu(out_two) * keep_half).astype(jnp.bfloat16)
    pre_three = pointwise(hidden_two, first_expand)
    strided = pixels[:, ::2, ::2, :]
    pre_proj = pointwise(strided, first_project)
    joint = joined_sum(
        forward_stats(pre_three, keep_half, onehot) + forward_stats(pre_proj, keep_half, onehot),
        total_all,
    )
    norm_three, scale_three = normalize(pre_three, joint[0:2], onehot, count_out)
    norm_proj, scale_proj = normalize(pre_proj, joint[2:4], onehot, count_out)
    unit_one = (norm_three * as_float(first_expand_gain) + as_float(first_expand_bias)) * keep_half
    short_one = (
        norm_proj * as_float(first_project_gain) + as_float(first_project_bias)
    ) * keep_half
    pooled_one = total_pair(jnp.sum(unit_one, axis=(1, 2))) / cell_counts
    squeeze_pre_one = jnp.dot(pooled_one, as_float(first_squeeze), precision=HIGHEST) + as_float(
        first_squeeze_bias
    )
    squeezed_one = jax.nn.silu(squeeze_pre_one)
    gate_one = jax.nn.sigmoid(
        jnp.dot(squeezed_one, as_float(first_excite), precision=HIGHEST)
        + as_float(first_excite_bias)
    )
    branch_one = unit_one * gate_one[:, None, None, :]
    join_one = branch_one + short_one
    stream_one = jax.nn.silu(join_one) * keep_half
    regrouped = lax.all_to_all(
        stream_one.astype(jnp.bfloat16), "narrow", split_axis=3, concat_axis=1, tiled=True
    )
    pre_four = lax.psum(pointwise(regrouped, second_reduce).astype(jnp.bfloat16), "narrow").astype(
        jnp.float32
    )
    norm_four, scale_four = normalize(
        pre_four,
        joined_sum(forward_stats(pre_four, keep_out, onehot), total_wide),
        onehot,
        count_out,
    )
    out_four = norm_four * as_float(second_reduce_gain) + as_float(second_reduce_bias)
    hidden_four = (jax.nn.silu(out_four) * keep_out).astype(jnp.bfloat16)
    padded_four = jnp.pad(hidden_four, ((0, 0), (1, 1), (1, 1), (0, 0)))
    pre_five = taps_forward(padded_four, second_spatial, 1, rows_out, cols_out)
    norm_five, scale_five = normalize(
        pre_five,
        joined_sum(forward_stats(pre_five, keep_out, onehot), total_wide),
        onehot,
        count_out,
    )
    out_five = norm_five * as_float(second_spatial_gain) + as_float(second_spatial_bias)
    hidden_five = (jax.nn.silu(out_five) * keep_out).astype(jnp.bfloat16)
    pre_six = lax.psum_scatter(
        pointwise(hidden_five, second_expand).astype(jnp.bfloat16),
        "narrow",
        scatter_dimension=3,
        tiled=True,
    ).astype(jnp.float32)
    norm_six, scale_six = normalize(
        pre_six, joined_sum(forward_stats(pre_six, keep_out, onehot), total_wide), onehot, count_out
    )
    unit_two = (norm_six * as_float(second_expand_gain) + as_float(second_expand_bias)) * keep_out
    pooled_two = jnp.sum(unit_two, axis=(1, 2)) / cell_counts
    squeeze_pre_two = total_pair(
        jnp.dot(pooled_two, as_float(second_squeeze), precision=HIGHEST)
    ) + as_float(second_squeeze_bias)
    squeezed_two = jax.nn.silu(squeeze_pre_two)
    gate_two = jax.nn.sigmoid(
        jnp.dot(squeezed_two, as_float(second_excite), precision=HIGHEST)
        + as_float(second_excite_bias)
    )
    branch_two = unit_two * gate_two[:, None, None, :]
    join_two = branch_two + as_float(regrouped)
    stream_two = jax.nn.silu(join_two) * keep_out
    result = stream_two.astype(jnp.bfloat16)
    squares = joined_sum(
        [
            jnp.stack(
                [
                    jnp.sum(stream_one * stream_one),
                    jnp.sum(branch_one * branch_one),
                    jnp.sum(short_one * short_one),
                    jnp.sum(branch_two * branch_two),
                    jnp.sum(stream_two * stream_two),
                ]
            )
        ],
        total_all,
    )[0]
    norms = jnp.sqrt(squares / (jnp.sum(count_out) * C_OUT))
    grad_join_two = as_float(out_grad) * keep_out * silu_slope(join_two)
    grad_gate_two = jnp.sum(grad_join_two * unit_two, axis=(1, 2))
    grad_excite_two = grad_gate_two * gate_two * (1.0 - gate_two)
    grad_second_excite = jnp.dot(squeezed_two.T, grad_excite_two, precision=HIGHEST)
    grad_squeeze_two = total_pair(
        jnp.dot(grad_excite_two, as_float(second_excite).T, precision=HIGHEST)
    ) * silu_slope(squeeze_pre_two)
    grad_second_squeeze = jnp.dot(pooled_two.T, grad_squeeze_two, precision=HIGHEST)
    grad_pooled_two = (
        jnp.dot(grad_squeeze_two, as_float(second_squeeze).T, precision=HIGHEST) / cell_counts
    )
    grad_unit_two = (
        grad_join_two * gate_two[:, None, None, :] + grad_pooled_two[:, None, None, :]
    ) * keep_out
    sums_six = joined_sum(
        backward_stats(grad_unit_two, norm_six, onehot)
        + [jnp.sum(grad_excite_two, axis=0), jnp.sum(grad_squeeze_two, axis=0)],
        total_wide,
    )
    grad_pre_six, grad_second_expand_gain, grad_second_expand_bias = normalize_back(
        grad_unit_two,
        norm_six,
        scale_six,
        as_float(second_expand_gain),
        keep_out,
        sums_six[0:2],
        onehot,
        count_out,
    )
    grad_second_excite_bias = sums_six[2]
    grad_second_squeeze_bias = sums_six[3]
    grad_six_low = grad_pre_six.astype(jnp.bfloat16)
    grad_six_full = lax.all_gather(grad_six_low, "narrow", axis=3, tiled=True)
    grad_second_expand = weight_grad(hidden_five, grad_six_full)
    grad_hidden_five = transposed(grad_six_full, second_expand)
    grad_out_five = grad_hidden_five * keep_out * silu_slope(out_five)
    sums_five = joined_sum(backward_stats(grad_out_five, norm_five, onehot), total_wide)
    grad_pre_five, grad_second_spatial_gain, grad_second_spatial_bias = normalize_back(
        grad_out_five,
        norm_five,
        scale_five,
        as_float(second_spatial_gain),
        keep_out,
        sums_five,
        onehot,
        count_out,
    )
    grad_five_low = grad_pre_five.astype(jnp.bfloat16)
    grad_second_spatial = taps_weight(padded_four, grad_five_low, 1)
    grad_padded_four = taps_input(grad_five_low, second_spatial, 1, rows_out + 2, cols_out + 2)
    grad_hidden_four = jax.tree.map(
        lambda part: part.astype(jnp.float32),
        lax.psum(as_sent(grad_padded_four[:, 1 : rows_out + 1, 1 : cols_out + 1, :]), "narrow"),
    )
    grad_out_four = grad_hidden_four * keep_out * silu_slope(out_four)
    sums_four = joined_sum(backward_stats(grad_out_four, norm_four, onehot), total_wide)
    grad_pre_four, grad_second_reduce_gain, grad_second_reduce_bias = normalize_back(
        grad_out_four,
        norm_four,
        scale_four,
        as_float(second_reduce_gain),
        keep_out,
        sums_four,
        onehot,
        count_out,
    )
    grad_four_low = grad_pre_four.astype(jnp.bfloat16)
    grad_second_reduce = weight_grad(regrouped, grad_four_low)
    grad_regrouped = (grad_join_two + transposed(grad_four_low, second_reduce)).astype(jnp.bfloat16)
    second_grads = (
        lax.psum_scatter(grad_second_reduce, "wide", scatter_dimension=1, tiled=True),
        lax.psum_scatter(grad_second_spatial, "wide", scatter_dimension=2, tiled=True),
        lax.psum_scatter(grad_second_expand, "wide", scatter_dimension=1, tiled=True),
        lax.psum_scatter(grad_second_squeeze, "wide", scatter_dimension=1, tiled=True),
        lax.psum_scatter(grad_second_excite, "wide", scatter_dimension=0, tiled=True),
    )
    grad_stream_one = lax.all_to_all(
        grad_regrouped, "narrow", split_axis=1, concat_axis=3, tiled=True
    )
    share = 1.0 / pair_total
    grad_join_one = as_float(grad_stream_one) * keep_half * silu_slope(join_one)
    grad_gate_one = total_pair(jnp.sum(grad_join_one * unit_one, axis=(1, 2)))
    grad_excite_one = grad_gate_one * gate_one * (1.0 - gate_one)
    grad_first_excite = jnp.dot(squeezed_one.T, grad_excite_one, precision=HIGHEST) * share
    grad_squeeze_one = jnp.dot(
        grad_excite_one, as_float(first_excite).T, precision=HIGHEST
    ) * silu_slope(squeeze_pre_one)
    grad_first_squeeze = jnp.dot(pooled_one.T, grad_squeeze_one, precision=HIGHEST) * share
    grad_pooled_one = (
        jnp.dot(grad_squeeze_one, as_float(first_squeeze).T, precision=HIGHEST) / cell_counts
    )
    grad_unit_one = (
        grad_join_one * gate_one[:, None, None, :] + grad_pooled_one[:, None, None, :]
    ) * keep_half
    sums_three = joined_sum(
        backward_stats(grad_unit_one, norm_three, onehot)
        + backward_stats(grad_join_one, norm_proj, onehot)
        + [jnp.sum(grad_excite_one, axis=0) * share, jnp.sum(grad_squeeze_one, axis=0) * share],
        total_all,
    )
    grad_pre_three, grad_first_expand_gain, grad_first_expand_bias = normalize_back(
        grad_unit_one,
        norm_three,
        scale_three,
        as_float(first_expand_gain),
        keep_half,
        sums_three[0:2],
        onehot,
        count_out,
    )
    grad_pre_proj, grad_first_project_gain, grad_first_project_bias = normalize_back(
        grad_join_one,
        norm_proj,
        scale_proj,
        as_float(first_project_gain),
        keep_half,
        sums_three[2:4],
        onehot,
        count_out,
    )
    grad_first_excite_bias = sums_three[4]
    grad_first_squeeze_bias = sums_three[5]
    grad_three_low = grad_pre_three.astype(jnp.bfloat16)
    grad_proj_low = grad_pre_proj.astype(jnp.bfloat16)
    grad_first_expand = weight_grad(hidden_two, grad_three_low)
    grad_first_project = weight_grad(strided, grad_proj_low)
    grad_strided = transposed(grad_proj_low, first_project)
    grad_out_two = transposed(grad_three_low, first_expand) * keep_half * silu_slope(out_two)
    sums_two = joined_sum(backward_stats(grad_out_two, norm_two, onehot), total_all)
    grad_pre_two, grad_first_spatial_gain, grad_first_spatial_bias = normalize_back(
        grad_out_two,
        norm_two,
        scale_two,
        as_float(first_spatial_gain),
        keep_half,
        sums_two,
        onehot,
        count_out,
    )
    grad_two_low = grad_pre_two.astype(jnp.bfloat16)
    grad_first_spatial = taps_weight(padded_one, grad_two_low, 2)
    grad_padded_one = taps_input(grad_two_low, first_spatial, 2, rows_in + 1, cols_in + 1)
    returned_rim = passed_along(
        grad_padded_one[:, :1, 1:, :].astype(jnp.bfloat16), "narrow", -1
    ).astype(jnp.float32)
    grad_hidden_one = jnp.concatenate(
        [grad_padded_one[:, 1:rows_in, 1:, :], grad_padded_one[:, rows_in:, 1:, :] + returned_rim],
        axis=1,
    )
    grad_out_one = grad_hidden_one * keep_in * silu_slope(out_one)
    sums_one = joined_sum(backward_stats(grad_out_one, norm_one, onehot), total_all)
    grad_pre_one, grad_first_reduce_gain, grad_first_reduce_bias = normalize_back(
        grad_out_one,
        norm_one,
        scale_one,
        as_float(first_reduce_gain),
        keep_in,
        sums_one,
        onehot,
        count_in,
    )
    grad_one_low = grad_pre_one.astype(jnp.bfloat16)
    grad_first_reduce = weight_grad(pixels, grad_one_low)
    zero_value = jnp.zeros((), jnp.float32)
    grad_spread = lax.pad(
        grad_strided,
        zero_value,
        (
            (0, 0, 0),
            (0, rows_in - 2 * rows_half + 1, 1),
            (0, cols_in - 2 * cols_out + 1, 1),
            (0, 0, 0),
        ),
    )
    grad_images = (transposed(grad_one_low, first_reduce) + grad_spread) * keep_in
    first_grads = (
        grad_first_reduce,
        grad_first_spatial,
        grad_first_expand,
        grad_first_project,
        grad_first_squeeze,
        grad_first_excite,
    )
    first_grads = wide_totals(
        first_grads[0],
        first_grads[1],
        first_grads[2],
        first_grads[3],
        first_grads[4],
        first_grads[5],
    )
    first_grads = pair_totals(
        first_grads[0],
        first_grads[1],
        first_grads[2],
        first_grads[3],
        first_grads[4],
        first_grads[5],
    )
    return (
        result,
        grad_images,
        first_grads[0],
        grad_first_reduce_gain,
        grad_first_reduce_bias,
        first_grads[1],
        grad_first_spatial_gain,
        grad_first_spatial_bias,
        first_grads[2],
        grad_first_expand_gain,
        grad_first_expand_bias,
        first_grads[3],
        grad_first_project_gain,
        grad_first_project_bias,
        first_grads[4],
        grad_first_squeeze_bias,
        first_grads[5],
        grad_first_excite_bias,
        second_grads[0],
        grad_second_reduce_gain,
        grad_second_reduce_bias,
        second_grads[1],
        grad_second_spatial_gain,
        grad_second_spatial_bias,
        second_grads[2],
        grad_second_expand_gain,
        grad_second_expand_bias,
        second_grads[3],
        grad_second_squeeze_bias,
        second_grads[4],
        grad_second_excite_bias,
        norms,
    )


def solution(mesh):
    return jax.shard_map(
        local,
        mesh=mesh,
        in_specs=(
            P("wide", "narrow", None, None),
            P(),
            P(),
            P(),
            P(),
            P(),
            P(),
            P(),
            P(),
            P(),
            P(),
            P(),
            P(),
            P(),
            P(),
            P(),
            P(),
            P(),
            P(),
            P("narrow", None),
            P(),
            P(),
            P(None, None, None, "narrow"),
            P("narrow"),
            P("narrow"),
            P("narrow", None),
            P("narrow"),
            P("narrow"),
            P("narrow", None),
            P(),
            P(None, "narrow"),
            P("narrow"),
            P("wide", None, None, "narrow"),
        ),
        out_specs=(
            P("wide", None, None, "narrow"),
            P("wide", "narrow", None, None),
            P("wide", "narrow"),
            P(),
            P(),
            P(None, None, "wide", "narrow"),
            P(),
            P(),
            P("wide", "narrow"),
            P(),
            P(),
            P("wide", "narrow"),
            P(),
            P(),
            P("narrow", "wide"),
            P(),
            P("wide", "narrow"),
            P(),
            P("narrow", "wide"),
            P(),
            P(),
            P(None, None, "wide", "narrow"),
            P("narrow"),
            P("narrow"),
            P("narrow", "wide"),
            P("narrow"),
            P("narrow"),
            P("narrow", "wide"),
            P(),
            P("wide", "narrow"),
            P("narrow"),
            P(),
        ),
        check_vma=False,
    )
```

profile of v0, /device:TPU:0, one launch (start us, length us, event | category | flops | bytes accessed | tf_op | source)
XLA Modules:
  0.0 1913.5 jit_solution(4675365603472591872)
XLA Ops:
  14.6 42.1 %psum.133 = f32[2048]{0:T(1024)S(1)} all-reduce(f32[2048]{0:T(1024)S(1)} %pad_maximum_fusion.5), channel_id=1, replica_groups=mesh['wide'=16,'narrow'=2] {'wide','narrow'}, use_global_device_ids=true, to_apply=%region_2.3 | all-reduce | flops 2048 | bytes 16384 | tf_op jit(solution)/shard_map/psum | solution.py:125
  61.0 4.2 collective-permute-start
  67.0 8.8 slice.505
  75.8 4.4 fusion.2
  80.7 5.0 slice.485
  85.6 5.0 slice.483
  90.6 5.0 slice.487
  96.5 5.0 slice.493
  118.2 39.3 %psum.134 = f32[2048]{0:T(1024)S(1)} all-reduce(f32[2048]{0:T(1024)S(1)} %pad_maximum_fusion.6), channel_id=1, replica_groups=mesh['wide'=16,'narrow'=2] {'wide','narrow'}, use_global_device_ids=true, to_apply=%region_6.7 | all-reduce | flops 2048 | bytes 16384 | tf_op jit(solution)/shard_map/psum | solution.py:125
  167.4 117.3 %all-reduce.27.cloned.1.call-done = f32[16384]{0:T(1024)} async-done(((f32[16384]{0:T(1024)}), f32[16384]{0:T(1024)}) %all-reduce.27.cloned.1.call-update) | async-done | bytes 65552 | tf_op jit(solution)/shard_map/psum | solution.py:125
  288.4 8.3 psum.136
  302.0 3.0 fusion.173
  305.1 11.9 copy.92
  317.0 18.3 reshape.672
  335.3 11.8 all_to_all.27
  347.1 23.0 %reshape.673 = bf16[2048,4,4,7]{3,2,1,0:T(4,128)(2,1)} reshape(bf16[2,2,57344]{2,1,0:T(2,128)(2,1)} %all_to_all.27) | data formatting | bytes 917504
  370.0 12.9 copy.145
  389.7 21.6 %all-reduce.29.cloned.1.call-done = bf16[4,8,7,512]{3,1,2,0:T(8,128)(2,1)} async-done(((bf16[4,8,7,512]{3,1,2,0:T(8,128)(2,1)}), bf16[4,8,7,512]{3,1,2,0:T(8,128)(2,1)}) %all-reduce.29.cloned.1.call-update) | async-done | bytes 229392 | tf_op jit(solution)/shard_map/psum | solution.py:326
  414.4 33.2 %psum.138 = f32[2048]{0:T(1024)S(1)} all-reduce(f32[2048]{0:T(1024)S(1)} %pad_maximum_fusion.7), channel_id=1, replica_groups=mesh['wide'=16,'narrow'=2] {'wide'}, use_global_device_ids=true, to_apply=%region_18.19 | all-reduce | flops 2048 | bytes 16384 | tf_op jit(solution)/shard_map/psum | solution.py:129
  458.9 29.5 %psum.139 = f32[1024]{0:T(1024)S(1)} all-reduce(f32[1024]{0:T(1024)S(1)} %pad_maximum_fusion.11), channel_id=1, replica_groups=mesh['wide'=16,'narrow'=2] {'wide'}, use_global_device_ids=true, to_apply=%region_21.22 | all-reduce | flops 1024 | bytes 8192 | tf_op jit(solution)/shard_map/psum | solution.py:129
  493.6 15.2 reduce-scatter.19.cloned.1.call-done
  512.1 61.2 %psum.140 = f32[4096]{0:T(1024)S(1)} all-reduce(f32[4096]{0:T(1024)S(1)} %pad_maximum_fusion.4), channel_id=1, replica_groups=mesh['wide'=16,'narrow'=2] {'wide'}, use_global_device_ids=true, to_apply=%region_25.26 | all-reduce | flops 4096 | bytes 32768 | tf_op jit(solution)/shard_map/psum | solution.py:129
  578.3 5.3 psum.141
  585.0 3.8 multiply_reduce_fusion.12
  589.7 4.9 psum.142
  601.0 57.6 %psum.143 = f32[5248]{0:T(1024)S(1)} all-reduce(f32[5248]{0:T(1024)S(1)} %pad_maximum_fusion.3), channel_id=1, replica_groups=mesh['wide'=16,'narrow'=2] {'wide'}, use_global_device_ids=true, to_apply=%region_34.35 | all-reduce | flops 5248 | bytes 41984 | tf_op jit(solution)/shard_map/psum | solution.py:129
  662.9 9.2 all_gather.3
  676.1 30.9 %psum.144 = f32[1024]{0:T(1024)S(1)} all-reduce(f32[1024]{0:T(1024)S(1)} %pad_maximum_fusion.12), channel_id=1, replica_groups=mesh['wide'=16,'narrow'=2] {'wide'}, use_global_device_ids=true, to_apply=%region_37.38 | all-reduce | flops 1024 | bytes 8192 | tf_op jit(solution)/shard_map/psum | solution.py:129
  716.3 19.2 %all-reduce.31.cloned.1.call-done = bf16[4,8,7,512]{3,1,2,0:T(8,128)(2,1)} async-done(((bf16[4,8,7,512]{3,1,2,0:T(8,128)(2,1)}), bf16[4,8,7,512]{3,1,2,0:T(8,128)(2,1)}) %all-reduce.31.cloned.1.call-update) | async-done | bytes 229392 | tf_op jit(solution)/shard_map/psum | solution.py:437
  740.2 33.9 %psum.146 = f32[2048]{0:T(1024)} all-reduce(f32[2048]{0:T(1024)} %pad_maximum_fusion.8), channel_id=1, replica_groups=mesh['wide'=16,'narrow'=2] {'wide'}, use_global_device_ids=true, to_apply=%region_41.42 | all-reduce | flops 2048 | bytes 16384 | tf_op jit(solution)/shard_map/psum | solution.py:129
  784.7 8.6 all_to_all.28
  794.7 3.1 reshape.624
  797.8 5.1 multiply_reduce_fusion.3
  802.9 8.1 psum.147
  828.6 113.9 %all-reduce.33.cloned.1.call-done = f32[18560]{0:T(1024)} async-done(((f32[18560]{0:T(1024)}), f32[18560]{0:T(1024)}) %all-reduce.33.cloned.1.call-update) | async-done | bytes 74256 | tf_op jit(solution)/shard_map/psum | solution.py:125
  954.9 3.3 multiply_convert_fusion.3
  961.2 42.6 %psum.149 = f32[2048]{0:T(1024)S(1)} all-reduce(f32[2048]{0:T(1024)S(1)} %pad_maximum_fusion.9), channel_id=1, replica_groups=mesh['wide'=16,'narrow'=2] {'wide','narrow'}, use_global_device_ids=true, to_apply=%region_53.54 | all-reduce | flops 2048 | bytes 16384 | tf_op jit(solution)/shard_map/psum | solution.py:125
  1014.1 5.9 pad.77
  1020.0 5.9 pad.78
  1025.9 5.9 pad.79
  1031.8 5.9 pad.80
  1037.7 5.9 pad.81
  1045.0 5.9 pad.82
  1052.3 5.9 pad.83
  1059.5 6.0 pad.84
  1065.5 5.0 add_add_fusion
  1075.5 3.2 stack.151
  1081.6 41.8 %all-reduce.21 = (f32[2048]{0:T(1024)S(1)}, f32[5]{0:T(128)}) all-reduce(f32[2048]{0:T(1024)S(1)} %pad_maximum_fusion.10, f32[5]{0:T(128)S(1)} %stack.151), channel_id=1, replica_groups=mesh['wide'=16,'narrow'=2] {'wide','narrow'}, use_global_device_ids=true, to_apply=%region_56.57 | all-reduce | flops 2053 | bytes 16424 | tf_op jit(solution)/shard_map/psum | solution.py:125
  1125.6 3.8 convolution_bitcast_fusion.4
  1133.6 4.7 convolution_bitcast_fusion
  1147.4 4.7 pad_maximum_fusion
  1155.4 43.4 %reduce-scatter.21.cloned.1.call-done = f32[64,512]{1,0:T(8,128)} async-done(((f32[1024,512]{1,0:T(8,128)}), f32[64,512]{1,0:T(8,128)}) %reduce-scatter.21.cloned.1.call-update) | async-done | bytes 131088 | tf_op jit(solution)/shard_map/reduce_scatter | solution.py:209
  1200.4 73.6 %reduce-scatter.29.cloned.1.call-done = f32[32,2048]{1,0:T(8,128)} async-done(((f32[512,2048]{1,0:T(8,128)}), f32[32,2048]{1,0:T(8,128)}) %reduce-scatter.29.cloned.1.call-update) | async-done | bytes 262160 | tf_op jit(solution)/shard_map/reduce_scatter | solution.py:211
  1275.7 106.5 %reduce-scatter.33.cloned.1.call-done = f32[64,2048]{1,0:T(8,128)} async-done(((f32[1024,2048]{1,0:T(8,128)}), f32[64,2048]{1,0:T(8,128)}) %reduce-scatter.33.cloned.1.call-update) | async-done | bytes 524304 | tf_op jit(solution)/shard_map/reduce_scatter | solution.py:212
  1384.1 114.0 %reduce-scatter.25.cloned.1.call-done = f32[3,3,32,512]{3,2,1,0:T(8,128)} async-done(((f32[3,3,512,512]{3,2,1,0:T(8,128)}), f32[3,3,32,512]{3,2,1,0:T(8,128)}) %reduce-scatter.25.cloned.1.call-update) | async-done | bytes 589840 | tf_op jit(solution)/shard_map/reduce_scatter | solution.py:210
  1524.2 3.8 fusion
  1528.0 6.4 pad.85
  1549.9 12.8 reduce-scatter.35.cloned.1.call-done
  1564.3 13.2 reduce-scatter.27.cloned.1.call-done
  1579.2 58.5 %reduce-scatter.53.cloned.1.call-done = f32[8,1024]{1,0:T(8,128)} async-done(((f32[128,1024]{1,0:T(8,128)}), f32[8,1024]{1,0:T(8,128)}) %reduce-scatter.53.cloned.1.call-update) | async-done | bytes 32784 | tf_op jit(solution)/shard_map/reduce_scatter | solution.py:459
  1637.7 59.0 %reduce-scatter.51.cloned.1.call-done = f32[1024,8]{0,1:T(8,128)} async-done(((f32[1024,128]{0,1:T(8,128)}), f32[1024,8]{0,1:T(8,128)}) %reduce-scatter.51.cloned.1.call-update) | async-done | bytes 32784 | tf_op jit(solution)/shard_map/reduce_scatter | solution.py:458
  1696.6 65.2 %reduce-scatter.49.cloned.1.call-done = f32[256,128]{1,0:T(8,128)} async-done(((f32[256,2048]{1,0:T(8,128)}), f32[256,128]{1,0:T(8,128)}) %reduce-scatter.49.cloned.1.call-update) | async-done | bytes 131088 | tf_op jit(solution)/shard_map/reduce_scatter | solution.py:457
  1761.8 64.9 %reduce-scatter.45.cloned.1.call-done = f32[1024,32]{0,1:T(8,128)} async-done(((f32[1024,512]{0,1:T(8,128)}), f32[1024,32]{0,1:T(8,128)}) %reduce-scatter.45.cloned.1.call-update) | async-done | bytes 131088 | tf_op jit(solution)/shard_map/reduce_scatter | solution.py:455
  1826.8 79.5 %reduce-scatter.47.cloned.1.call-done = f32[3,3,32,256]{3,2,1,0:T(8,128)} async-done(((f32[3,3,512,256]{3,2,1,0:T(8,128)}), f32[3,3,32,256]{3,2,1,0:T(8,128)}) %reduce-scatter.47.cloned.1.call-update) | async-done | bytes 294928 | tf_op jit(solution)/shard_map/reduce_scatter | solution.py:456
  (716 shorter events, 248.3 us)
Async XLA Ops:
  7.2 152.8 %copy-start = (bf16[512,2048]{1,0:T(8,128)(2,1)S(1)}, bf16[512,2048]{1,0:T(8,128)(2,1)}, u32[]{:S(2)}) copy-start(bf16[512,2048]{1,0:T(8,128)(2,1)} %param.42) | copy-start | bytes 6291460
  7.2 277.5 %all-reduce.27.cloned.1.call-start = ((), (), s32[]{:S(2)}) async-start(), calls=%async_computation.20 | async-start | bytes 131072 | tf_op jit(solution)/shard_map/psum | solution.py:125
  10.1 567.0 %copy-start.120 = (f32[4]{0:T(128)}, f32[4]{0:T(128)S(1)}, u32[]{:S(2)}) copy-start(f32[4]{0:T(128)S(1)} %get-tuple-element.241) | copy-start | bytes 52
  10.3 54.9 %copy-start.27 = (f32[4,8,14]{2,1,0:T(8,128)}, f32[4,8,14]{2,1,0:T(8,128)S(1)}, u32[]{:S(2)}) copy-start(f32[4,8,14]{2,1,0:T(8,128)S(1)} %and_convert_fusion.1) | copy-start | bytes 5380
  10.3 46.4 %copy-start.148 = (bf16[512]{0:T(512)(128)(2,1)S(1)}, bf16[512]{0:T(512)(128)(2,1)}, u32[]{:S(2)}) copy-start(bf16[512]{0:T(512)(128)(2,1)} %param.37) | copy-start | bytes 3076
  10.3 46.4 %copy-start.154 = (s32[64]{0:T(128)S(1)}, s32[64]{0:T(128)}, u32[]{:S(2)}) copy-start(s32[64]{0:T(128)} %param.35) | copy-start | bytes 772
  10.3 48.0 %copy-start.149 = (bf16[512]{0:T(512)(128)(2,1)S(1)}, bf16[512]{0:T(512)(128)(2,1)}, u32[]{:S(2)}) copy-start(bf16[512]{0:T(512)(128)(2,1)} %param.38) | copy-start | bytes 3076
  12.7 67.5 %copy-start.4 = (f32[4,8,14,512]{3,2,1,0:T(8,128)}, f32[4,8,14,512]{3,2,1,0:T(8,128)S(1)}, u32[]{:S(2)}) copy-start(f32[4,8,14,512]{3,2,1,0:T(8,128)S(1)} %get-tuple-element.280) | copy-start | bytes 2752516
  57.4 516.9 %copy-start.101 = (f32[2]{0:T(128)}, f32[2]{0:T(128)S(1)}, u32[]{:S(2)}) copy-start(f32[2]{0:T(128)S(1)} %get-tuple-element.228) | copy-start | bytes 28
  61.0 19.4 %collective-permute-start = (bf16[4,1,14,512]{3,2,1,0:T(8,128)(2,1)S(1)}, bf16[4,1,14,512]{3,2,1,0:T(8,128)(2,1)S(1)}, u32[]{:S(2)}, u32[]{:S(2)}) collective-permute-start(bf16[4,1,14,512]{3,2,1,0:T(8,128)(2,1)S(1)} %slice.575), channel_id=1, source_target_pairs={{0,1},{2,3},{4,5},{6,7},{8,9},{10,11},{12,13},{14,15},{16,17},{18,... | collective-permute-start | bytes 172040 | tf_op jit(solution)/shard_map/ppermute | solution.py:17
  80.3 221.6 %copy-start.29 = (f32[4,4,7]{2,1,0:T(4,128)}, f32[4,4,7]{2,1,0:T(4,128)S(1)}, u32[]{:S(2)}) copy-start(f32[4,4,7]{2,1,0:T(4,128)S(1)} %and_convert_fusion.2) | copy-start | bytes 1348
  80.4 79.6 %copy-start.140 = (f32[512]{0:T(512)}, f32[512]{0:T(512)S(1)}, u32[]{:S(2)}) copy-start(f32[512]{0:T(512)S(1)} %convert_element_type.260) | copy-start | bytes 6148
  80.4 79.6 %copy-start.143 = (f32[512]{0:T(512)}, f32[512]{0:T(512)S(1)}, u32[]{:S(2)}) copy-start(f32[512]{0:T(512)S(1)} %convert_element_type.261) | copy-start | bytes 6148
  167.2 244.2 %all-reduce.29.cloned.1.call-start = ((), (), s32[]{:S(2)}) async-start(), calls=%async_computation.21 | async-start | bytes 458752 | tf_op jit(solution)/shard_map/psum | solution.py:326
  167.3 137.7 %copy-start.55 = (f32[2048]{0:T(1024)}, f32[2048]{0:T(1024)S(1)}, u32[]{:S(2)}) copy-start(f32[2048]{0:T(1024)S(1)} %convert_element_type.263) | copy-start | bytes 24580
  167.3 137.7 %copy-start.56 = (f32[2048]{0:T(1024)}, f32[2048]{0:T(1024)S(1)}, u32[]{:S(2)}) copy-start(f32[2048]{0:T(1024)S(1)} %convert_element_type.264) | copy-start | bytes 24580
  167.4 137.6 %copy-start.64 = (f32[2048]{0:T(1024)}, f32[2048]{0:T(1024)S(1)}, u32[]{:S(2)}) copy-start(f32[2048]{0:T(1024)S(1)} %convert_element_type.270) | copy-start | bytes 24580
  167.4 137.6 %copy-start.65 = (f32[2048]{0:T(1024)}, f32[2048]{0:T(1024)S(1)}, u32[]{:S(2)}) copy-start(f32[2048]{0:T(1024)S(1)} %convert_element_type.271) | copy-start | bytes 24580
  389.4 119.4 %reduce-scatter.19.cloned.1.call-start = ((), (), s32[]{:S(2)}) async-start(), calls=%async_computation.22 | async-start | bytes 1376256 | tf_op jit(solution)/shard_map/reduce_scatter | solution.py:347
  389.6 65.6 %copy-start.89 = (f32[512]{0:T(512)}, f32[512]{0:T(512)S(1)}, u32[]{:S(2)}) copy-start(f32[512]{0:T(512)S(1)} %convert_element_type.276) | copy-start | bytes 6148
  389.6 65.5 %copy-start.90 = (f32[512]{0:T(512)}, f32[512]{0:T(512)S(1)}, u32[]{:S(2)}) copy-start(f32[512]{0:T(512)S(1)} %convert_element_type.277) | copy-start | bytes 6148
  389.6 101.1 %copy-start.161 = (f32[256]{0:T(256)}, f32[256]{0:T(256)S(1)}, u32[]{:S(2)}) copy-start(f32[256]{0:T(256)S(1)} %convert_element_type.279) | copy-start | bytes 3076
  389.6 101.1 %copy-start.164 = (f32[256]{0:T(256)}, f32[256]{0:T(256)S(1)}, u32[]{:S(2)}) copy-start(f32[256]{0:T(256)S(1)} %convert_element_type.280) | copy-start | bytes 3076
  493.5 242.0 %all-reduce.31.cloned.1.call-start = ((), (), s32[]{:S(2)}) async-start(), calls=%async_computation.23 | async-start | bytes 458752 | tf_op jit(solution)/shard_map/psum | solution.py:437
  493.6 102.3 %copy-start.124 = (f32[128]{0:T(128)}, f32[128]{0:T(128)S(1)}, u32[]{:S(2)}) copy-start(f32[128]{0:T(128)S(1)} %convert_element_type.288) | copy-start | bytes 1540
  588.8 83.3 %copy-start.53 = (f32[4,1024]{1,0:T(4,128)}, f32[4,1024]{1,0:T(4,128)S(1)}, u32[]{:S(2)}) copy-start(f32[4,1024]{1,0:T(4,128)S(1)} %get-tuple-element.237) | copy-start | bytes 49156
  716.3 226.2 %all-reduce.33.cloned.1.call-start = ((), (), s32[]{:S(2)}) async-start(), calls=%async_computation.24 | async-start | bytes 155648 | tf_op jit(solution)/shard_map/psum | solution.py:125
  825.7 326.6 %reduce-scatter.41.cloned.1.call-start = ((), (), s32[]{:S(2)}) async-start(), calls=%async_computation.35 | async-start | bytes 1114112 | tf_op jit(solution)/shard_map/reduce_scatter | solution.py:214
  828.5 325.4 %reduce-scatter.37.cloned.1.call-start = ((), (), s32[]{:S(2)}) async-start(), calls=%async_computation.33 | async-start | bytes 1114112 | tf_op jit(solution)/shard_map/reduce_scatter | solution.py:213
  958.2 47.3 %copy-start.18 = (f32[4,4,7,512]{3,2,1,0:T(8,128)S(1)}, f32[4,4,7,512]{3,2,1,0:T(8,128)}, u32[]{:S(2)}) copy-start(f32[4,4,7,512]{3,2,1,0:T(8,128)} %get-tuple-element.281) | copy-start | bytes 688132
  958.2 47.3 %copy-start.31 = (f32[4,4,7]{2,1,0:T(4,128)S(1)}, f32[4,4,7]{2,1,0:T(4,128)}, u32[]{:S(2)}) copy-start(f32[4,4,7]{2,1,0:T(4,128)} %copy-done.29) | copy-start | bytes 1348
  958.2 47.3 %copy-start.109 = (f32[4,512]{1,0:T(4,128)S(1)}, f32[4,512]{1,0:T(4,128)}, u32[]{:S(2)}) copy-start(f32[4,512]{1,0:T(4,128)} %copy-done.107) | copy-start | bytes 24580
  958.2 47.3 %copy-start.113 = (f32[4,512]{1,0:T(4,128)S(1)}, f32[4,512]{1,0:T(4,128)}, u32[]{:S(2)}) copy-start(f32[4,512]{1,0:T(4,128)} %copy-done.111) | copy-start | bytes 24580
  958.2 47.3 %copy-start.115 = (f32[4,512]{1,0:T(4,128)S(1)}, f32[4,512]{1,0:T(4,128)}, u32[]{:S(2)}) copy-start(f32[4,512]{1,0:T(4,128)} %get-tuple-element.297) | copy-start | bytes 24580
  1071.6 7.2 collective-permute-start.1
  1075.2 123.6 %reduce-scatter.21.cloned.1.call-start = ((), (), s32[]{:S(2)}) async-start(), calls=%async_computation.25 | async-start | bytes 2228224 | tf_op jit(solution)/shard_map/reduce_scatter | solution.py:209
  1078.8 46.3 %copy-start.106 = (f32[4,512]{1,0:T(4,128)S(1)}, f32[4,512]{1,0:T(4,128)}, u32[]{:S(2)}) copy-start(f32[4,512]{1,0:T(4,128)} %get-tuple-element.300) | copy-start | bytes 24580
  1129.4 144.6 %reduce-scatter.29.cloned.1.call-start = ((), (), s32[]{:S(2)}) async-start(), calls=%async_computation.29 | async-start | bytes 4456448 | tf_op jit(solution)/shard_map/reduce_scatter | solution.py:211
  1132.5 249.8 %reduce-scatter.33.cloned.1.call-start = ((), (), s32[]{:S(2)}) async-start(), calls=%async_computation.31 | async-start | bytes 8912896 | tf_op jit(solution)/shard_map/reduce_scatter | solution.py:212
  1138.3 359.8 %reduce-scatter.25.cloned.1.call-start = ((), (), s32[]{:S(2)}) async-start(), calls=%async_computation.27 | async-start | bytes 10027008 | tf_op jit(solution)/shard_map/reduce_scatter | solution.py:210
  1152.2 347.8 %copy-start.54 = (f32[4,1024]{1,0:T(4,128)S(1)}, f32[4,1024]{1,0:T(4,128)}, u32[]{:S(2)}) copy-start(f32[4,1024]{1,0:T(4,128)} %copy-done.53) | copy-start | bytes 49156
  1152.2 347.8 %copy-start.81 = (bf16[4,128]{1,0:T(4,128)(2,1)S(1)}, bf16[4,128]{1,0:T(4,128)(2,1)}, u32[]{:S(2)}) copy-start(bf16[4,128]{1,0:T(4,128)(2,1)} %copy-done.80) | copy-start | bytes 3076
  1152.2 347.8 %copy-start.125 = (f32[128]{0:T(128)S(1)}, f32[128]{0:T(128)}, u32[]{:S(2)}) copy-start(f32[128]{0:T(128)} %copy-done.124) | copy-start | bytes 1540
  1152.2 349.6 %copy-start.69 = (f32[4,1024]{1,0:T(4,128)S(1)}, f32[4,1024]{1,0:T(4,128)}, u32[]{:S(2)}) copy-start(f32[4,1024]{1,0:T(4,128)} %copy-done.68) | copy-start | bytes 49156
  1152.2 349.6 %copy-start.105 = (bf16[4,128]{1,0:T(4,128)(2,1)S(1)}, bf16[4,128]{1,0:T(4,128)(2,1)}, u32[]{:S(2)}) copy-start(bf16[4,128]{1,0:T(4,128)(2,1)} %copy-done.104) | copy-start | bytes 3076
  1152.2 349.6 %copy-start.123 = (f32[4]{0:T(128)S(1)}, f32[4]{0:T(128)}, u32[]{:S(2)}) copy-start(f32[4]{0:T(128)} %copy-done.120) | copy-start | bytes 52
  1152.2 391.5 %reduce-scatter.43.cloned.1.call-start = ((), (), s32[]{:S(2)}) async-start(), calls=%async_computation.36 | async-start | bytes 49152 | tf_op jit(solution)/shard_map/reduce_scatter | solution.py:201
  1153.8 391.3 %reduce-scatter.39.cloned.1.call-start = ((), (), s32[]{:S(2)}) async-start(), calls=%async_computation.34 | async-start | bytes 49152 | tf_op jit(solution)/shard_map/reduce_scatter | solution.py:198
  1155.4 391.1 %reduce-scatter.23.cloned.1.call-start = ((), (), s32[]{:S(2)}) async-start(), calls=%async_computation.26 | async-start | bytes 98304 | tf_op jit(solution)/shard_map/reduce_scatter | solution.py:186
  1200.4 348.0 %reduce-scatter.31.cloned.1.call-start = ((), (), s32[]{:S(2)}) async-start(), calls=%async_computation.30 | async-start | bytes 196608 | tf_op jit(solution)/shard_map/reduce_scatter | solution.py:192
  1275.6 227.7 %copy-start.22 = (bf16[4,8,7,2048]{3,1,2,0:T(8,128)(2,1)S(1)}, bf16[4,8,7,2048]{3,1,2,0:T(8,128)(2,1)}, u32[]{:S(2)}) copy-start(bf16[4,8,7,2048]{3,1,2,0:T(8,128)(2,1)} %copy-done.21) | copy-start | bytes 2752516
  1275.6 227.7 %copy-start.24 = (f32[4,8,7,256]{3,1,2,0:T(8,128)S(1)}, f32[4,8,7,256]{3,1,2,0:T(8,128)}, u32[]{:S(2)}) copy-start(f32[4,8,7,256]{3,1,2,0:T(8,128)} %get-tuple-element.283) | copy-start | bytes 688132
  1275.6 227.7 %copy-start.128 = (f32[4,256]{1,0:T(4,128)S(1)}, f32[4,256]{1,0:T(4,128)}, u32[]{:S(2)}) copy-start(f32[4,256]{1,0:T(4,128)} %copy-done.126) | copy-start | bytes 12292
  1275.6 227.7 %copy-start.131 = (f32[4,256]{1,0:T(4,128)S(1)}, f32[4,256]{1,0:T(4,128)}, u32[]{:S(2)}) copy-start(f32[4,256]{1,0:T(4,128)} %copy-done.129) | copy-start | bytes 12292
  1275.7 227.7 %copy-start.163 = (f32[256]{0:T(256)S(1)}, f32[256]{0:T(256)}, u32[]{:S(2)}) copy-start(f32[256]{0:T(256)} %copy-done.161) | copy-start | bytes 3076
  1275.7 227.7 %copy-start.166 = (f32[256]{0:T(256)S(1)}, f32[256]{0:T(256)}, u32[]{:S(2)}) copy-start(f32[256]{0:T(256)} %copy-done.164) | copy-start | bytes 3076
  1275.7 287.0 %reduce-scatter.35.cloned.1.call-start = ((), (), s32[]{:S(2)}) async-start(), calls=%async_computation.32 | async-start | bytes 393216 | tf_op jit(solution)/shard_map/reduce_scatter | solution.py:195
  1384.1 193.4 %reduce-scatter.27.cloned.1.call-start = ((), (), s32[]{:S(2)}) async-start(), calls=%async_computation.28 | async-start | bytes 442368 | tf_op jit(solution)/shard_map/reduce_scatter | solution.py:189
  1499.9 137.7 %reduce-scatter.53.cloned.1.call-start = ((), (), s32[]{:S(2)}) async-start(), calls=%async_computation.41 | async-start | bytes 557056 | tf_op jit(solution)/shard_map/reduce_scatter | solution.py:459
  1501.5 195.1 %reduce-scatter.51.cloned.1.call-start = ((), (), s32[]{:S(2)}) async-start(), calls=%async_computation.40 | async-start | bytes 557056 | tf_op jit(solution)/shard_map/reduce_scatter | solution.py:458
  1503.3 258.5 %reduce-scatter.49.cloned.1.call-start = ((), (), s32[]{:S(2)}) async-start(), calls=%async_computation.39 | async-start | bytes 2228224 | tf_op jit(solution)/shard_map/reduce_scatter | solution.py:457
  1505.4 321.4 %reduce-scatter.45.cloned.1.call-start = ((), (), s32[]{:S(2)}) async-start(), calls=%async_computation.37 | async-start | bytes 2228224 | tf_op jit(solution)/shard_map/reduce_scatter | solution.py:455
  1508.3 398.0 %reduce-scatter.47.cloned.1.call-start = ((), (), s32[]{:S(2)}) async-start(), calls=%async_computation.38 | async-start | bytes 5013504 | tf_op jit(solution)/shard_map/reduce_scatter | solution.py:456
  1538.1 368.1 %copy-start.1 = (bf16[512,2048]{1,0:T(8,128)(2,1)S(1)}, bf16[512,2048]{1,0:T(8,128)(2,1)}, u32[]{:S(2)}) copy-start(bf16[512,2048]{1,0:T(8,128)(2,1)} %param.42) | copy-start | bytes 6291460
  (127 other events, 1086.2 us)
Sparse Core Ops, SparseCore 0:
  167.3 117.3 all-reduce.26
  389.5 21.7 all-reduce.28
  493.6 15.1 reduce-scatter.18
  716.4 19.0 all-reduce.30
  825.8 116.6 all-reduce.32
  946.4 59.5 reduce-scatter.40
  1075.3 58.5 reduce-scatter.36
  1138.1 60.6 reduce-scatter.20
  1202.7 71.3 reduce-scatter.28
  1278.5 103.7 reduce-scatter.32
  1387.0 111.0 reduce-scatter.24
  1500.7 9.5 reduce-scatter.42
  1513.0 9.8 reduce-scatter.38
  1525.5 9.8 reduce-scatter.22
  1538.1 10.2 reduce-scatter.30
  1551.0 11.6 reduce-scatter.34
  1565.4 12.0 reduce-scatter.26
  1581.9 55.7 reduce-scatter.52
  1641.8 54.7 reduce-scatter.50
  1701.2 60.5 reduce-scatter.48
  1766.2 60.5 reduce-scatter.44
  1831.7 74.5 reduce-scatter.46
where the time goes:
time: 1930 us; the launch traced here: 1910 us
  waiting for transfers between devices  979 us (51%)
  blocking collectives  468 us (24%)
  local copies, waits for them, and re-layouts  198 us (10%)
  matrix products  158 us (8%)
  other arithmetic  85.6 us (4%)
    psum x6, blocking collectives, total_wide(): return lax.psum(flattened, 'wide')  246 us
    psum x2, waiting for transfers between devices, total_all(): return lax.psum(flattened, ('wide', 'narrow'))  231 us
    psum x4, blocking collectives, total_all(): return lax.psum(flattened, ('wide', 'narrow'))  166 us
    reduce_scatter x1, waiting for transfers between devices, wide_totals(): lax.psum_scatter(spatial_grad, 'wide', scatter_dimension=2, tiled=True)  114 us
    reduce_scatter x1, waiting for transfers between devices, wide_totals(): lax.psum_scatter(project_grad, 'wide', scatter_dimension=0, tiled=True)  107 us
    reduce_scatter x1, waiting for transfers between devices, local(): lax.psum_scatter(grad_second_spatial, 'wide', scatter_dimension=2, tiled=...  79.5 us
    reduce_scatter x1, waiting for transfers between devices, wide_totals(): lax.psum_scatter(expand_grad, 'wide', scatter_dimension=0, tiled=True)  73.6 us
    reduce_scatter x1, waiting for transfers between devices, local(): lax.psum_scatter(grad_second_expand, 'wide', scatter_dimension=1, tiled=T...  65.2 us
  transfers between devices with their start and end apart: 24, of which 17 were waited for; matrix products, arithmetic and copies ran while one was open for 10% of the time, Pallas kernels for 0%

commit v1 on v0

v1 whole, which is shorter than its diff:
```python
import functools

import numpy as np
import jax
import jax.numpy as jnp
from jax import lax
from jax.experimental import pallas as pl
from jax.experimental.pallas import tpu as pltpu
from jax.sharding import PartitionSpec as P

EPSILON = 1e-05
BF = jnp.bfloat16
F32 = jnp.float32
B = 4
POS = 56
LIMIT = 24
M = B * POS
HALF = 112
HROWS = B * HALF
VMEM = pl.BlockSpec(memory_space=pltpu.VMEM)
SMEM = pl.BlockSpec(memory_space=pltpu.SMEM)
ANY = pl.BlockSpec(memory_space=pl.ANY)
INV_IN, INV_OUT, CELLS, MICRO, INV_ALL = 0, 2, 4, 8, 12
NARROW, CORE, DEST = 0, 1, 2
W6_AT, EX_AT, SQ_AT, VEC_AT, PACK_ROWS = 2304, 3328, 3584, 3840, 3856


def mm(a, b):
    return lax.dot_general(a, b, (((1,), (0,)), ((), ())), preferred_element_type=F32)


def mm_nt(a, b):
    return lax.dot_general(a, b, (((1,), (1,)), ((), ())), preferred_element_type=F32)


def mm_tn(a, b):
    return lax.dot_general(a, b, (((0,), (0,)), ((), ())), preferred_element_type=F32)


def f32(v):
    return v.astype(F32)


def low(v):
    return v.astype(BF)


def split2(v):
    a = low(v)
    return a, low(v - f32(a))


def split3(v):
    a = low(v)
    r = v - f32(a)
    b = low(r)
    return a, b, low(r - f32(b))


def dot3(v, w):
    return sum(mm(p, w) for p in split3(v))


def dot3_nt(v, w):
    return sum(mm_nt(p, w) for p in split3(v))


def outer(a, b):
    a1, a2 = split2(a)
    b1, b2 = split2(b)
    return mm_tn(a1, b1) + mm_tn(a1, b2) + mm_tn(a2, b1)


def sigmoid(v):
    return 1.0 / (1.0 + jnp.exp(-v))


def slope(v):
    s = sigmoid(v)
    return s * (1.0 + v * (1.0 - s))


def cols(c, size=256):
    return pl.ds(pl.multiple_of(c * size, size), size)


def expand(rows):
    return jnp.concatenate([jnp.broadcast_to(r, (POS, r.shape[1])) for r in rows], axis=0)


def pick(r0, r1, fs):
    return expand([r0 * (1.0 - fs[MICRO + b]) + r1 * fs[MICRO + b] for b in range(B)])


def image_sums(v):
    return [jnp.sum(v[b * POS : (b + 1) * POS], axis=0, keepdims=True) for b in range(B)]


def grouped(sums, fs, reps=1):
    zero = one = 0.0
    for b in range(B):
        zero = zero + sums[b] * (1.0 - fs[MICRO + b])
        one = one + sums[b] * fs[MICRO + b]
    return [zero, one]


def group_sums(v, fs):
    return grouped(image_sums(v), fs)


def put(ref, at, rows, sl):
    for k, r in enumerate(rows):
        ref[at + k : at + k + 1, sl] = r


def add_parts(parts, tot):
    t = parts[0]
    for k in range(1, parts.shape[0]):
        t = t + parts[k]
    tot[...] = t


def coefs(tot, at, sl, fs, inv):
    i0, i1 = fs[inv], fs[inv + 1]
    m0, m1 = tot[at : at + 1, sl] * i0, tot[at + 1 : at + 2, sl] * i1
    q0 = lax.rsqrt(tot[at + 2 : at + 3, sl] * i0 - m0 * m0 + EPSILON)
    q1 = lax.rsqrt(tot[at + 3 : at + 4, sl] * i1 - m1 * m1 + EPSILON)
    return pick(m0, m1, fs), pick(q0, q1, fs)


def means(tot, at, sl, fs, inv):
    i0, i1 = fs[inv], fs[inv + 1]
    a = pick(tot[at : at + 1, sl] * i0, tot[at + 1 : at + 2, sl] * i1, fs)
    b = pick(tot[at + 2 : at + 3, sl] * i0, tot[at + 3 : at + 4, sl] * i1, fs)
    return a, b


def stat_rows(v, keep, fs):
    kept = v * keep
    return group_sums(kept, fs) + group_sums(kept * v, fs)


def back_rows(d, x, fs):
    return group_sums(d, fs) + group_sums(d * x, fs)


def loop(count, body):
    lax.fori_loop(0, count, lambda c, _: (body(c), 0)[1], 0)


def copy_all(pairs, sems):
    copies = [pltpu.make_async_copy(s, d, sems.at[k]) for k, (s, d) in enumerate(pairs)]
    for c in copies:
        c.start()
    return copies


def wait_all(copies):
    for c in copies:
        c.wait()


def at_rows(start, size):
    return pl.ds(pl.multiple_of(start, 16), size)


def flip(p):
    return (p & 1) * 8 + (p & 2) * 2 + (p & 4) // 2 + (p & 8) // 8


def setup_kernel(exact, crop, micro, fs, isc, keep, keep1, keep_half):
    n = lax.axis_index("narrow").astype(jnp.int32)
    w = lax.axis_index("wide").astype(jnp.int32)
    isc[NARROW] = n
    isc[CORE] = w & 1
    for p in range(16):
        isc[DEST + p] = (w ^ flip(p)) if exact else jnp.int32(p)

    def count(k, sums):
        c, one = crop[k], micro[k]
        a, b = (c >> 4) * (c >> 4), (c >> 5) * (c >> 5)
        return (
            sums[0] + a * (1 - one), sums[1] + a * one, sums[2] + b * (1 - one), sums[3] + b * one,
        )

    zero = jnp.int32(0)
    sums = lax.fori_loop(0, crop.shape[0], count, (zero, zero, zero, zero))
    for k in range(4):
        fs[k] = 1.0 / sums[k].astype(F32)
    fs[INV_ALL] = 1.0 / ((sums[2] + sums[3]).astype(F32) * 2048.0)
    at = lax.broadcasted_iota(jnp.int32, (POS, 1), 0)
    i8, j7 = at & 7, at >> 3
    at = lax.broadcasted_iota(jnp.int32, (HALF, 1), 0)
    r8, c14 = n * 8 + (at & 7), at >> 3

    def inside(r, c, side):
        return jnp.where((r < side) & (c < side), 1.0, 0.0).astype(F32)

    for b in range(B):
        c = crop[w * B + b]
        side_in, side_out = c >> 4, c >> 5
        fs[CELLS + b] = 1.0 / (side_out * side_out).astype(F32)
        fs[MICRO + b] = micro[w * B + b].astype(F32)
        keep[b * POS : (b + 1) * POS, :] = inside(i8, j7, side_out)
        for k in range(4):
            keep1[k, b * POS : (b + 1) * POS, :] = inside(2 * i8 + k // 2, 2 * j7 + k % 2, side_in)
        keep_half[b * HALF : (b + 1) * HALF, :] = inside(r8, c14, side_in)


def one_half_kernel(fs, x, keep, w1, st):
    def body(c):
        sl = cols(c)
        v = mm(x[...], w1[:, sl]) * keep[...]
        sums = [jnp.sum(v[b * HALF : (b + 1) * HALF], axis=0, keepdims=True) for b in range(B)]
        v2 = v * v
        sq = [jnp.sum(v2[b * HALF : (b + 1) * HALF], axis=0, keepdims=True) for b in range(B)]
        put(st, 0, grouped(sums, fs) + grouped(sq, fs), sl)

    loop(2, body)


TAPS = [(p, q) for p in range(3) for q in range(3)]


def stage_two_kernel(
    fs, isc, own, other, part, part_other, perm, keep1, keep, w1, ws, gb, sh,
    xp, strided, x1, col, pre2, st, tot1, xs, tmp, hid, tot, sems,
):
    n = isc[NARROW]
    copies = copy_all([(own, xs.at[n]), (other, xs.at[1 - n])], sems)
    tot[...] = part[...] + part_other[...]
    tot1[...] = tot[...]
    wait_all(copies)

    def permute(c):
        sl = cols(c)
        for b in range(B):
            r = mm(perm[0], xs[0, b, :, sl]) + mm(perm[1], xs[1, b, :, sl])
            for k in range(4):
                tmp[k, b * POS : (b + 1) * POS, :] = r[k * POS : (k + 1) * POS]
        for k in range(4):
            xp[k, :, sl] = low(tmp[k] * keep1[k])
        strided[:, sl] = xp[0, :, sl]

    loop(4, permute)

    def first(c):
        k, sl = c // 2, cols(c % 2)
        v = mm(xp[k], w1[:, sl])
        mean, scale = coefs(tot, 0, sl, fs, INV_IN)
        x = (v - mean) * scale
        x1[k, :, sl] = x
        o = x * gb[0:1, sl] + gb[1:2, sl]
        hid[k, :, sl] = low(o * sigmoid(o) * keep1[k])

    loop(8, first)
    for t, (p, q) in enumerate(TAPS):
        h = hid[2 * (p != 1) + (q != 1)]
        if p == 0 or q == 0:
            h = low(mm(sh[3 * (0 if p == 0 else 1) + (0 if q == 0 else 1)], h))
        col[t] = h

    def second(c):
        sl = cols(c)
        v = mm(col[0], ws[0, :, sl])
        for t in range(1, 9):
            v = v + mm(col[t], ws[t, :, sl])
        pre2[:, sl] = v
        put(st, 0, stat_rows(v, keep[...], fs), sl)

    loop(2, second)


def project_kernel(fs, x, keep, wp, prep, st):
    def body(c):
        sl = cols(c)
        v = mm(x[...], wp[:, sl])
        prep[:, sl] = v
        put(st, 0, stat_rows(v, keep[...], fs), sl)

    loop(8, body)


def stage_three_kernel(fs, parts, pre2, stp, keep, w3, gb, h2, pre3, st, tot2, tot):
    add_parts(parts, tot)
    tot2[...] = tot[...]
    sl = slice(0, 512)
    mean, scale = coefs(tot, 0, sl, fs, INV_OUT)
    o = (pre2[...] - mean) * scale * gb[2:3, :] + gb[3:4, :]
    h2[...] = low(o * sigmoid(o) * keep[...])
    st[4:8, :] = stp[...]

    def body(c):
        sl = cols(c)
        v = mm(h2[...], w3[:, sl])
        pre3[:, sl] = v
        put(st, 0, stat_rows(v, keep[...], fs), sl)

    loop(8, body)


def stage_four_kernel(
    fs, isc, parts, pre3, prep, keep, vec, sqb, sq, ex, w4own, r1, r2,
    lows, pre4, st, tot3, gate, sp, pooled, squares, unit, short, w4, acc, tot, sems,
):
    n, core = isc[NARROW], isc[CORE]
    away = (1 - n) * 1024
    copies = copy_all(
        [
            (w4own, w4.at[at_rows(n * 1024, 1024)]),
            (r1, w4.at[at_rows(away + core * 512, 512)]),
            (r2, w4.at[at_rows(away + (1 - core) * 512, 512)]),
        ],
        sems,
    )
    add_parts(parts, tot)
    tot3[...] = tot[...]
    pooled[...] = jnp.zeros((8, 2048), F32)

    def units(c):
        sl = cols(c)
        mean, scale = coefs(tot, 0, sl, fs, INV_OUT)
        u = ((pre3[:, sl] - mean) * scale * vec[0:1, sl] + vec[1:2, sl]) * keep[...]
        unit[:, sl] = u
        for b, r in enumerate(image_sums(u)):
            pooled[b : b + 1, sl] = r * fs[CELLS + b]
        mean, scale = coefs(tot, 4, sl, fs, INV_OUT)
        s = ((prep[:, sl] - mean) * scale * vec[2:3, sl] + vec[3:4, sl]) * keep[...]
        short[:, sl] = s

    loop(8, units)
    sp[...] = dot3(pooled[...], sq[...]) + sqb[0:1, :]
    squeezed = sp[...] * sigmoid(sp[...])
    gate[...] = sigmoid(dot3(squeezed, ex[...]) + vec[4:5, :])
    squares[...] = jnp.zeros((8, 256), F32)
    acc[...] = jnp.zeros((M, 512), F32)
    wait_all(copies)

    def streams(c):
        sl = cols(c)
        branch = unit[:, sl] * expand([gate[b : b + 1, sl] for b in range(B)])
        s = short[:, sl]
        join = branch + s
        stream = join * sigmoid(join) * keep[...]
        for k, v in enumerate((stream, branch, s)):
            squares[k : k + 1, :] += jnp.sum(v * v, axis=0, keepdims=True)
        lo = low(stream)
        lows[:, sl] = lo
        acc[...] += mm(lo, w4[cols(c), :])

    loop(8, streams)
    pre4[...] = acc[...]
    put(st, 0, stat_rows(acc[...], keep[...], fs), slice(0, 512))


def w5_copies(isc, own, r1, r2, w5):
    n, core = isc[NARROW], isc[CORE]
    return [
        (own, w5.at[n]),
        (r1.at[0:2304], w5.at[1 - n, at_rows(core * 2304, 2304)]),
        (r2.at[0:2304], w5.at[1 - n, at_rows((1 - core) * 2304, 2304)]),
    ]


def stage_five_kernel(
    fs, isc, parts, pre4, keep, gb, sh, vown, w5own, r1, r2,
    col, pre5, st, tot4, gain5, vec2, w5, tot, vaway, sems,
):
    n = isc[NARROW]
    pairs = w5_copies(isc, w5own, r1, r2, w5) + [(r1.at[VEC_AT:PACK_ROWS], vaway)]
    copies = copy_all(pairs, sems)
    add_parts(parts, tot)
    tot4[...] = tot[...]
    mean, scale = coefs(tot, 0, slice(0, 512), fs, INV_OUT)
    o = (pre4[...] - mean) * scale * gb[4:5, :] + gb[5:6, :]
    h = low(o * sigmoid(o) * keep[...])
    for t in range(9):
        col[t] = h if t == 4 else low(mm(sh[t], h))
    wait_all(copies)
    for side, v in ((n, f32(vown[...])), (1 - n, f32(vaway[...]))):
        for k in range(2):
            gain5[k : k + 1, cols(side)] = v[k : k + 1]
        for k in range(3):
            for c in range(4):
                at = 2 + 4 * k + c
                vec2[k : k + 1, cols(side * 4 + c)] = v[at : at + 1]

    def body(c):
        v = 0.0
        for t in range(9):
            v = v + mm(col[t], w5[c, t * 512 : (t + 1) * 512, :])
        pre5[:, cols(c)] = v
        put(st, 0, stat_rows(v, keep[...], fs), cols(c))

    loop(2, body)


def w6_copies(isc, own, r1, r2, w6):
    n, core = isc[NARROW], isc[CORE]
    pairs = [(own, w6.at[at_rows(n * 256, 256)])]
    for r, h in ((r1, core), (r2, 1 - core)):
        for c in range(8):
            pairs.append(
                (
                    r.at[W6_AT + c * 128 : W6_AT + (c + 1) * 128],
                    w6.at[at_rows((1 - n) * 256 + h * 128, 128), c * 256 : (c + 1) * 256],
                )
            )
    return pairs


def stage_six_kernel(
    fs, isc, parts, pre5, keep, gain5, w6own, r1, r2, h5, pre6, st, tot5, w6, tot, sems
):
    copies = copy_all(w6_copies(isc, w6own, r1, r2, w6), sems)
    add_parts(parts, tot)
    tot5[...] = tot[...]
    mean, scale = coefs(tot, 0, slice(0, 512), fs, INV_OUT)
    o = (pre5[...] - mean) * scale * gain5[0:1, :] + gain5[1:2, :]
    h5[...] = low(o * sigmoid(o) * keep[...])
    wait_all(copies)

    def body(c):
        sl = cols(c)
        v = mm(h5[...], w6[:, sl])
        pre6[:, sl] = v
        put(st, 0, stat_rows(v, keep[...], fs), sl)

    loop(8, body)


def turn_kernel(
    fs, isc, parts, pre6, keep, lows, vec, sqb, sq1s, sqown, exown, r1, r2, ogown, ogother,
    result, dj2, pay, extra, tot6, gate, dp, pooled, de, ds, squeezed,
    unit, og, res, sq, ex, tot, sp, sems,
):
    n, core = isc[NARROW], isc[CORE]
    pairs = [
        (sqown, sq.at[at_rows(n * 1024, 1024)]),
        (exown, ex.at[n]),
        (ogown, og.at[n]),
        (ogother, og.at[1 - n]),
    ]
    for r, h in ((r1, core), (r2, 1 - core)):
        for k in range(2):
            pairs.append(
                (
                    r.at[SQ_AT : SQ_AT + 256, k * 128 : (k + 1) * 128],
                    sq.at[at_rows((1 - n) * 1024 + h * 512 + k * 256, 256)],
                )
            )
        for c in range(4):
            pairs.append(
                (
                    r.at[EX_AT + c * 64 : EX_AT + (c + 1) * 64],
                    ex.at[1 - n, at_rows(h * 64, 64), c * 256 : (c + 1) * 256],
                )
            )
    copies = copy_all(pairs, sems)
    add_parts(parts, tot)
    tot6[...] = tot[...]
    pooled[...] = jnp.zeros((8, 2048), F32)
    de[...] = jnp.zeros((8, 2048), F32)

    def units(c):
        sl = cols(c)
        mean, scale = coefs(tot, 0, sl, fs, INV_OUT)
        u = ((pre6[:, sl] - mean) * scale * vec[0:1, sl] + vec[1:2, sl]) * keep[...]
        unit[:, sl] = u
        for b, r in enumerate(image_sums(u)):
            pooled[b : b + 1, sl] = r * fs[CELLS + b]

    loop(8, units)
    wait_all(copies)
    sp[...] = dot3(pooled[...], sq[...]) + sqb[1:2, :]
    squeezed[...] = sp[...] * sigmoid(sp[...])
    for h in range(2):
        sl = slice(h * 1024, (h + 1) * 1024)
        gate[:, sl] = sigmoid(dot3(squeezed[...], ex[h]) + vec[2:3, sl])
    extra[...] = jnp.zeros((8, 512), F32)
    for k in range(3):
        extra[5 + k // 2 : 6 + k // 2, (k % 2) * 256 : (k % 2) * 256 + 256] = sq1s[k : k + 1, :]

    def streams(c):
        sl = cols(c)
        h, part = c // 4, cols(c % 4)
        u = unit[:, sl]
        branch = u * expand([gate[b : b + 1, sl] for b in range(B)])
        join = branch + f32(lows[:, sl])
        s = sigmoid(join)
        stream = join * s * keep[...]
        res[h, :, part] = low(stream)
        d = f32(og[h, :, part]) * keep[...] * (s * (1.0 + join * (1.0 - s)))
        dj2[:, sl] = d
        for b, r in enumerate(image_sums(d * u)):
            de[b : b + 1, sl] = r
        extra[6:7, 256:512] += jnp.sum(branch * branch, axis=0, keepdims=True)
        extra[7:8, 0:256] += jnp.sum(stream * stream, axis=0, keepdims=True)

    loop(8, streams)
    result[...] = res[n]
    de[...] = de[...] * gate[...] * (1.0 - gate[...])
    back = 0.0
    for h in range(2):
        back = back + dot3_nt(de[:, h * 1024 : (h + 1) * 1024], ex[h])
    ds[...] = back * slope(sp[...])
    dp[...] = dot3_nt(ds[...], sq[...])
    for b in range(B):
        dp[b : b + 1, :] = dp[b : b + 1, :] * fs[CELLS + b]
    total = jnp.sum(de[...], axis=0, keepdims=True)
    for k in range(4):
        extra[k : k + 1, :] = total[:, k * 512 : (k + 1) * 512]
    extra[4:5, 0:128] = jnp.sum(ds[...], axis=0, keepdims=True)

    def tops(c):
        sl = cols(c)
        mean, scale = coefs(tot, 0, sl, fs, INV_OUT)
        x = (pre6[:, sl] - mean) * scale
        du = (
            dj2[:, sl] * expand([gate[b : b + 1, sl] for b in range(B)])
            + expand([dp[b : b + 1, sl] for b in range(B)])
        ) * keep[...]
        put(pay, 0, back_rows(du, x, fs), sl)

    loop(8, tops)


def whole_gain(tot, at, gain, bias):
    gain[...] = (tot[at + 2 : at + 3, :] + tot[at + 3 : at + 4, :]).reshape(gain.shape)
    bias[...] = (tot[at : at + 1, :] + tot[at + 1 : at + 2, :]).reshape(bias.shape)


def half_gain(tot, n, gain, bias):
    sl = cols(n, gain.shape[0])
    gain[...] = (tot[2:3, sl] + tot[3:4, sl]).reshape(gain.shape)
    bias[...] = (tot[0:1, sl] + tot[1:2, sl]).reshape(bias.shape)


def back_six_kernel(
    fs, isc, parts, tot6, pre6, dj2, gate, dp, pre5, tot5, extra, keep, vec, gain5, w6own, r1, r2,
    d6, do5, st, dgain, dbias, w6, tot, acc, sems,
):
    copies = copy_all(w6_copies(isc, w6own, r1, r2, w6), sems)
    add_parts(parts, tot)
    half_gain(tot, isc[NARROW], dgain, dbias)
    acc[...] = jnp.zeros((M, 512), F32)
    wait_all(copies)

    def body(c):
        sl = cols(c)
        mean, scale = coefs(tot6, 0, sl, fs, INV_OUT)
        x = (pre6[:, sl] - mean) * scale
        du = (
            dj2[:, sl] * expand([gate[b : b + 1, sl] for b in range(B)])
            + expand([dp[b : b + 1, sl] for b in range(B)])
        ) * keep[...]
        a, bb = means(tot, 0, sl, fs, INV_OUT)
        d = low((du - a - x * bb) * (scale * vec[0:1, sl]) * keep[...])
        d6[:, sl] = d
        acc[...] += mm_nt(d, w6[:, sl])

    loop(8, body)
    mean, scale = coefs(tot5, 0, slice(0, 512), fs, INV_OUT)
    x = (pre5[...] - mean) * scale
    o = x * gain5[0:1, :] + gain5[1:2, :]
    d = acc[...] * keep[...] * slope(o)
    do5[...] = d
    put(st, 0, back_rows(d, x, fs), slice(0, 512))
    st[4:12, :] = extra[...]


def back_five_kernel(
    fs, isc, parts, tot5, pre5, do5, pre4, tot4, keep, gb, gain5, sh, w5own, r1, r2,
    d5, do4, st, dgain, dbias, debias, dsbias, norms, w5, tot, sems,
):
    n = isc[NARROW]
    copies = copy_all(w5_copies(isc, w5own, r1, r2, w5), sems)
    add_parts(parts, tot)
    half_gain(tot, n, dgain, dbias)
    excite = jnp.concatenate([tot[pl.ds(4 + 2 * n, 1), :], tot[pl.ds(5 + 2 * n, 1), :]], axis=1)
    debias[...] = excite.reshape(1024)
    dsbias[...] = tot[8:9, 0:128].reshape(128)
    for k in range(5):
        v = tot[9 + k // 2 : 10 + k // 2, (k % 2) * 256 : (k % 2) * 256 + 256]
        norms[k] = jnp.sqrt(jnp.sum(v, axis=1, keepdims=True) * fs[INV_ALL])[0, 0]
    sl = slice(0, 512)
    mean, scale = coefs(tot5, 0, sl, fs, INV_OUT)
    x = (pre5[...] - mean) * scale
    a, bb = means(tot, 0, sl, fs, INV_OUT)
    d = low((do5[...] - a - x * bb) * (scale * gain5[0:1, :]) * keep[...])
    d5[...] = d
    wait_all(copies)
    acc = 0.0
    for t in range(9):
        dc = d if t == 4 else low(mm(sh[8 - t], d))
        for h in range(2):
            acc = acc + mm_nt(dc[:, h * 256 : (h + 1) * 256], w5[h, t * 512 : (t + 1) * 512, :])
    mean, scale = coefs(tot4, 0, sl, fs, INV_OUT)
    x = (pre4[...] - mean) * scale
    o = x * gb[4:5, :] + gb[5:6, :]
    d = acc * keep[...] * slope(o)
    do4[...] = d
    put(st, 0, back_rows(d, x, fs), sl)


def back_four_kernel(
    fs, isc, parts, tot4, pre4, do4, dj2, tot3, pre3, prep, gate, sp, keep, gb, vec, sq, ex,
    w4own, r1, r2,
    d4, dj1, st, dgain, dbias, dp, de, ds, bias, w4, tot, sems,
):
    n, core = isc[NARROW], isc[CORE]
    away = (1 - n) * 1024
    copies = copy_all(
        [
            (w4own, w4.at[at_rows(n * 1024, 1024)]),
            (r1, w4.at[at_rows(away + core * 512, 512)]),
            (r2, w4.at[at_rows(away + (1 - core) * 512, 512)]),
        ],
        sems,
    )
    add_parts(parts, tot)
    whole_gain(tot, 0, dgain, dbias)
    de[...] = jnp.zeros((8, 2048), F32)
    mean, scale = coefs(tot4, 0, slice(0, 512), fs, INV_OUT)
    x = (pre4[...] - mean) * scale
    a, bb = means(tot, 0, slice(0, 512), fs, INV_OUT)
    d4[...] = low((do4[...] - a - x * bb) * (scale * gb[4:5, :]) * keep[...])
    wait_all(copies)

    def joins(c):
        sl = cols(c)
        back = dj2[:, sl] + mm_nt(d4[...], w4[cols(c), :])
        mean, scale = coefs(tot3, 0, sl, fs, INV_OUT)
        u = ((pre3[:, sl] - mean) * scale * vec[0:1, sl] + vec[1:2, sl]) * keep[...]
        mean, scale = coefs(tot3, 4, sl, fs, INV_OUT)
        s = ((prep[:, sl] - mean) * scale * vec[2:3, sl] + vec[3:4, sl]) * keep[...]
        join = u * expand([gate[b : b + 1, sl] for b in range(B)]) + s
        d = f32(low(back)) * keep[...] * slope(join)
        dj1[:, sl] = d
        for b, r in enumerate(image_sums(d * u)):
            de[b : b + 1, sl] = r

    loop(8, joins)
    de[...] = de[...] * gate[...] * (1.0 - gate[...])
    ds[...] = dot3_nt(de[...], ex[...]) * slope(sp[...])
    dp[...] = dot3_nt(ds[...], sq[...])
    for b in range(B):
        dp[b : b + 1, :] = dp[b : b + 1, :] * fs[CELLS + b]
    total = jnp.sum(de[...], axis=0, keepdims=True)
    bias[...] = jnp.zeros((8, 512), F32)
    for k in range(4):
        bias[k : k + 1, :] = total[:, k * 512 : (k + 1) * 512]
    bias[4:5, 0:128] = jnp.sum(ds[...], axis=0, keepdims=True)

    def tops(c):
        sl = cols(c)
        d = dj1[:, sl]
        mean, scale = coefs(tot3, 0, sl, fs, INV_OUT)
        x = (pre3[:, sl] - mean) * scale
        du = (
            d * expand([gate[b : b + 1, sl] for b in range(B)])
            + expand([dp[b : b + 1, sl] for b in range(B)])
        ) * keep[...]
        put(st, 0, back_rows(du, x, fs), sl)
        mean, scale = coefs(tot3, 4, sl, fs, INV_OUT)
        put(st, 4, back_rows(d, (prep[:, sl] - mean) * scale, fs), sl)

    loop(8, tops)


def back_three_kernel(
    fs, parts, tot3, pre3, prep, dj1, gate, dp, bias, pre2, tot2, keep, vec, gb, w3,
    d3, dproj, do2, st, dgain, dbias, dgainp, dbiasp, tot, acc,
):
    add_parts(parts, tot)
    whole_gain(tot, 0, dgain, dbias)
    whole_gain(tot, 4, dgainp, dbiasp)
    acc[...] = jnp.zeros((M, 512), F32)

    def body(c):
        sl = cols(c)
        mean, scale = coefs(tot3, 0, sl, fs, INV_OUT)
        x = (pre3[:, sl] - mean) * scale
        dj = dj1[:, sl]
        du = (
            dj * expand([gate[b : b + 1, sl] for b in range(B)])
            + expand([dp[b : b + 1, sl] for b in range(B)])
        ) * keep[...]
        a, bb = means(tot, 0, sl, fs, INV_OUT)
        d = low((du - a - x * bb) * (scale * vec[0:1, sl]) * keep[...])
        d3[:, sl] = d
        acc[...] += mm_nt(d, w3[:, sl])
        mean, scale = coefs(tot3, 4, sl, fs, INV_OUT)
        x = (prep[:, sl] - mean) * scale
        a, bb = means(tot, 4, sl, fs, INV_OUT)
        dproj[:, sl] = low((dj - a - x * bb) * (scale * vec[2:3, sl]) * keep[...])

    loop(8, body)
    sl = slice(0, 512)
    mean, scale = coefs(tot2, 0, sl, fs, INV_OUT)
    x = (pre2[...] - mean) * scale
    o = x * gb[2:3, :] + gb[3:4, :]
    d = acc[...] * keep[...] * slope(o)
    do2[...] = d
    put(st, 0, back_rows(d, x, fs), sl)
    st[4:12, :] = bias[...]


def back_two_kernel(
    fs, parts, tot2, pre2, do2, x1, keep1, keep, gb, sh, ws,
    d2, do1, st, dgain, dbias, debias, dsbias, tot, dcol,
):
    add_parts(parts, tot)
    whole_gain(tot, 0, dgain, dbias)
    debias[...] = jnp.concatenate([tot[k : k + 1, :] for k in range(4, 8)], axis=1).reshape(2048)
    dsbias[...] = tot[8:9, 0:128].reshape(128)
    sl = slice(0, 512)
    mean, scale = coefs(tot2, 0, sl, fs, INV_OUT)
    x = (pre2[...] - mean) * scale
    a, bb = means(tot, 0, sl, fs, INV_OUT)
    d = low((do2[...] - a - x * bb) * (scale * gb[2:3, :]) * keep[...])
    d2[...] = d
    dcol[0] = d
    dcol[1] = low(mm(sh[5], d))
    dcol[2] = low(mm(sh[7], d))
    dcol[3] = low(mm(sh[8], d))
    terms = (
        ((0, 4),),
        ((0, 5), (1, 3)),
        ((0, 7), (2, 1)),
        ((0, 8), (1, 6), (2, 2), (3, 0)),
    )
    st[...] = jnp.zeros((4, 512), F32)
    for k in range(4):
        acc = 0.0
        for which, t in terms[k]:
            acc = acc + mm_nt(dcol[which], ws[t])
        x = x1[k]
        o = x * gb[0:1, :] + gb[1:2, :]
        d = acc * keep1[k] * slope(o)
        do1[k] = d
        rows = back_rows(d, x, fs)
        for r in range(4):
            st[r : r + 1, :] += rows[r]


def deal(isc, full, rows, keep, send, at):
    for p in range(16):
        tile = full[pl.ds(pl.multiple_of(isc[DEST + p] * rows, rows), rows), :]
        (keep if p < 8 else send)[p % 8, at_rows(at, rows), :] = tile


def back_one_kernel(
    fs, isc, parts, tot1, x1, do1, xp, keep1, gb, d1, gkeep, gsend, dgain, dbias, tot, dn, full
):
    n = isc[NARROW]
    add_parts(parts, tot)
    whole_gain(tot, 0, dgain, dbias)
    sl = slice(0, 512)
    scale = coefs(tot1, 0, sl, fs, INV_IN)[1] * gb[0:1, :]
    a, bb = means(tot, 0, sl, fs, INV_IN)
    planes = []
    for k in range(4):
        d = (do1[k] - a - x1[k] * bb) * scale * keep1[k]
        planes.append(d)
        dn[k] = low(d)
    for b in range(B):
        d1[b] = low(jnp.concatenate([d[b * POS : (b + 1) * POS] for d in planes], axis=0))

    def body(c):
        g = 0.0
        for k in range(4):
            g = g + mm_tn(xp[k, :, cols(c)], dn[k, :, cols(n)])
        full[cols(c), :] = low(g)

    loop(4, body)
    deal(isc, full, 64, gkeep, gsend, 0)


def image_kernel(own, pick_own, spread, d1, dproj, keep, w1, wp, out, dc, cc):
    for b in range(B):
        dc[b * HALF : (b + 1) * HALF, :] = low(mm(own[...], d1[b]))
    cc[...] = low(mm(pick_own[...], dproj[...]))

    def body(c):
        sl = cols(c)
        hi, lo = split2(mm_nt(cc[...], wp[sl, :]))
        v = mm_nt(dc[...], w1[sl, :]) + mm(spread[...], hi) + mm(spread[...], lo)
        out[:, sl] = v * keep[...]

    loop(4, body)


def grads_a_kernel(isc, h5, d6, col4, d5, gkeep, gsend, wider, full):
    n = isc[NARROW]

    def expand2(c):
        wider[:, cols(c)] = low(mm_tn(h5[:, cols(n)], d6[:, cols(c)]))

    loop(8, expand2)
    for p in range(16):
        sl = cols(isc[DEST + p], 128)
        for k in range(2):
            (gkeep if p < 8 else gsend)[p % 8, 0:128, k * 128 : (k + 1) * 128] = wider[
                k * 128 : (k + 1) * 128, sl
            ]

    def spatial(t):
        full[...] = low(mm_tn(col4[t], d5[:, cols(n)]))
        deal(isc, full, 32, gkeep, gsend, 128 + t * 32)

    loop(9, spatial)


def gate_grads(isc, n, c, at, squeezed, pooled, de, ds, gkeep, gsend, q, e):
    sl = cols(n * 4 + c)
    q[...] = outer(ds[...], pooled[:, sl])
    e[...] = outer(squeezed[...], de[:, sl])
    for p in range(16):
        rows = pl.ds(pl.multiple_of(isc[DEST + p] * 8, 8), 8)
        both = jnp.concatenate([q[rows, :], e[rows, :]], axis=0)
        (gkeep if p < 8 else gsend)[p % 8, at_rows(at + c * 16, 16), :] = low(both)


def grads_b_kernel(isc, d4, lows, squeezed, pooled, de, ds, gkeep, gsend, full, q, e):
    n = isc[NARROW]

    def body(c):
        full[...] = low(mm_tn(d4[...], lows[:, cols(n * 4 + c)]))
        deal(isc, full, 32, gkeep, gsend, c * 32)
        gate_grads(isc, n, c, 128, squeezed, pooled, de, ds, gkeep, gsend, q, e)

    loop(4, body)


def grads_c_kernel(
    isc, h2, d3, strided, dproj, sp, pooled, de, ds, gkeep, gsend, full, taller, q, e, squeezed
):
    n = isc[NARROW]
    squeezed[...] = sp[...] * sigmoid(sp[...])

    def body(c):
        sl = cols(n * 4 + c)
        full[...] = low(mm_tn(h2[...], d3[:, sl]))
        deal(isc, full, 32, gkeep, gsend, c * 32)
        taller[...] = low(mm_tn(strided[...], dproj[:, sl]))
        deal(isc, taller, 64, gkeep, gsend, 128 + c * 64)
        gate_grads(isc, n, c, 384, squeezed, pooled, de, ds, gkeep, gsend, q, e)

    loop(4, body)


def grads_d_kernel(isc, col1, d2, gkeep, gsend, full):
    n = isc[NARROW]

    def spatial(t):
        full[...] = low(mm_tn(col1[t], d2[:, cols(n)]))
        deal(isc, full, 32, gkeep, gsend, t * 32)

    loop(9, spatial)


def joined(v, out, at, rows):
    for c in range(4):
        out[:, c * 256 : (c + 1) * 256] = v[at + c * rows : at + (c + 1) * rows, :]


def unpack_gates(v, at, squeeze, excite):
    for c in range(4):
        part = v[at + c * 16 : at + (c + 1) * 16, :]
        squeeze[:, c * 256 : (c + 1) * 256] = part[0:8]
        excite[:, c * 256 : (c + 1) * 256] = part[8:16]


def unpack_a_kernel(a, b, expand2, spatial2):
    v = f32(a[0]) + f32(b[0])
    expand2[0:128, :] = v[0:128, 0:128]
    expand2[128:256, :] = v[0:128, 128:256]
    spatial2[...] = v[128:416, :]


def unpack_b_kernel(a, b, reduce2, squeeze2, excite2):
    v = f32(a[0]) + f32(b[0])
    joined(v, reduce2, 0, 32)
    unpack_gates(v, 128, squeeze2, excite2)


def unpack_c_kernel(a, b, expand1, project1, squeeze1, excite1):
    v = f32(a[0]) + f32(b[0])
    joined(v, expand1, 0, 32)
    joined(v, project1, 128, 64)
    unpack_gates(v, 384, squeeze1, excite1)


def unpack_d_kernel(a, b, spatial1):
    spatial1[...] = f32(a[0]) + f32(b[0])


REST = PACK_ROWS - W6_AT


def pack_kernel(
    isc, w5, w4, w6, ex, sq,
    g1, b1, g2, b2, g4, b4, g3, b3, gp, bp, eb1, sqb1, sqb2, g5, b5, g6, b6, eb2,
    out, w4_half, gb, vec1, sqb, vown, rest, rows, sems,
):
    core = isc[CORE]
    copies = copy_all(
        [
            (w4.at[at_rows(core * 512, 512)], w4_half),
            (w5.at[at_rows(core * 2304, 2304)], out.at[0:W6_AT]),
        ],
        sems,
    )

    def row(v):
        return f32(v[...]).reshape(1, v.shape[0])

    for k, v in enumerate((g1, b1, g2, b2, g4, b4)):
        gb[k : k + 1, :] = row(v)
    for k, v in enumerate((g3, b3, gp, bp, eb1)):
        vec1[k : k + 1, :] = row(v)
    for k, v in enumerate((sqb1, sqb2)):
        sqb[k : k + 1, :] = row(v)
    rows[...] = jnp.zeros((16, 256), F32)
    at = 0
    for v in (g5, b5, g6, b6, eb2):
        r = row(v)
        for c in range(v.shape[0] // 256):
            rows[at : at + 1, :] = r[:, c * 256 : (c + 1) * 256]
            at += 1
    vown[...] = low(rows[...])
    for c in range(8):
        rest[c * 128 : (c + 1) * 128, :] = w6[at_rows(core * 128, 128), c * 256 : (c + 1) * 256]
    for c in range(4):
        start = EX_AT - W6_AT + c * 64
        rest[start : start + 64, :] = ex[at_rows(core * 64, 64), c * 256 : (c + 1) * 256]
    for k in range(2):
        rest[SQ_AT - W6_AT : SQ_AT - W6_AT + 256, k * 128 : (k + 1) * 128] = sq[
            at_rows(core * 512 + k * 256, 256), :
        ]
    rest[VEC_AT - W6_AT : REST, :] = vown[...]
    last = pltpu.make_async_copy(rest, out.at[W6_AT:PACK_ROWS], sems.at[2])
    last.start()
    last.wait()
    wait_all(copies)


def call(body, outs, args, scratch=(), flops=1e8, size=5e6, name=None, vmem=LIMIT):
    specs, values = [], []
    for a in args:
        kind, v = a if isinstance(a, tuple) else (VMEM, a)
        specs.append(kind)
        values.append(v)
    return pl.pallas_call(
        body,
        out_shape=tuple(jax.ShapeDtypeStruct(o[0], o[1]) for o in outs),
        in_specs=specs,
        out_specs=tuple(o[2] if len(o) > 2 else VMEM for o in outs),
        scratch_shapes=list(scratch),
        compiler_params=pltpu.CompilerParams(vmem_limit_bytes=vmem * 2**20),
        cost_estimate=pl.CostEstimate(
            flops=int(flops), bytes_accessed=int(size), transcendentals=0
        ),
        name=name,
    )(*values)


def constants():
    perm = np.zeros((2, M, HALF), np.float32)
    for r in range(16):
        for c in range(14):
            place = (2 * (r % 2) + c % 2) * POS + (c // 2) * 8 + r // 2
            perm[r // 8, place, c * 8 + r % 8] = 1
    shift = np.zeros((9, M, M), np.float32)
    for di in range(3):
        for dj in range(3):
            for b in range(B):
                for i in range(8):
                    for j in range(7):
                        si, sj = i + di - 1, j + dj - 1
                        if 0 <= si < 8 and 0 <= sj < 7:
                            shift[3 * di + dj, b * POS + j * 8 + i, b * POS + sj * 8 + si] = 1
    pick_own = np.zeros((2, HALF, M), np.float32)
    spread = np.zeros((HROWS, HALF), np.float32)
    for b in range(B):
        for j in range(7):
            for i in range(4):
                for n in range(2):
                    pick_own[n, b * 28 + j * 4 + i, b * POS + j * 8 + n * 4 + i] = 1
                spread[b * HALF + 2 * j * 8 + 2 * i, b * 28 + j * 4 + i] = 1
    return perm, shift, pick_own, spread


def swap(v, axis, pairs):
    return lax.ppermute(v, axis, pairs)


def after(v, *others):
    return lax.optimization_barrier((v,) + others)[0]


def local(
    images, crop, micro,
    first_reduce, first_reduce_gain, first_reduce_bias,
    first_spatial, first_spatial_gain, first_spatial_bias,
    first_expand, first_expand_gain, first_expand_bias,
    first_project, first_project_gain, first_project_bias,
    first_squeeze, first_squeeze_bias, first_excite, first_excite_bias,
    second_reduce, second_reduce_gain, second_reduce_bias,
    second_spatial, second_spatial_gain, second_spatial_bias,
    second_expand, second_expand_gain, second_expand_bias,
    second_squeeze, second_squeeze_bias, second_excite, second_excite_bias,
    out_grad,
):
    wide = lax.axis_size("wide")
    n = lax.axis_index("narrow")
    exact = wide == 16
    near = [(i, i ^ 1) for i in range(wide)]
    pair = [(0, 1), (1, 0)]
    groups = [list(range(k, wide, 2)) for k in range(2)]
    V = pltpu.VMEM
    D = pltpu.SemaphoreType.DMA
    f = lambda *shape: (shape, F32)
    h = lambda *shape: (shape, BF)

    def across(x):
        x = x + swap(x, "wide", near)
        sent = jnp.broadcast_to(x[None], (wide // 2,) + x.shape)
        got = lax.all_to_all(sent, "wide", 0, 0, axis_index_groups=groups, tiled=True)
        return got if exact else jnp.sum(got, axis=0, keepdims=True)

    def steps(x):
        step = 1
        while step < wide:
            x = x + swap(x, "wide", [(i, i ^ step) for i in range(wide)])
            step *= 2
        return x[None]

    perm_np, shift_np, pick_np, spread_np = constants()
    perm, sh = jnp.asarray(perm_np, BF), jnp.asarray(shift_np, BF)

    own_px = images.transpose(0, 2, 1, 3).reshape(B, HALF, 1024)
    other_px = swap(own_px, "narrow", pair)

    fs_, isc_, keep, keep1, keep_half = call(
        functools.partial(setup_kernel, exact),
        [((13,), F32, SMEM), ((18,), jnp.int32, SMEM), f(M, 1), f(4, M, 1), f(HROWS, 1)],
        [(SMEM, crop), (SMEM, micro)], name="setup",
    )
    fs, isc = (SMEM, fs_), (SMEM, isc_)
    st1 = call(
        one_half_kernel, [f(4, 512)], [fs, own_px.reshape(HROWS, 1024), keep_half, first_reduce],
        flops=5e8, name="one_half",
    )[0]
    part = jnp.sum(across(st1), axis=0)
    part_other = swap(part, "narrow", pair)

    w5_own = second_spatial.reshape(9 * 512, 256)
    pack, w4_half, gb, vec1, sqb, vown = call(
        pack_kernel,
        [
            ((PACK_ROWS, 256), BF, ANY), ((512, 512), BF, ANY), f(8, 512), f(8, 2048), f(8, 128), h(16, 256),
        ],
        [
            (SMEM, after(isc_, st1)), (ANY, w5_own), (ANY, second_reduce), second_expand, second_excite, second_squeeze,
            first_reduce_gain, first_reduce_bias, first_spatial_gain, first_spatial_bias,
            second_reduce_gain, second_reduce_bias, first_expand_gain, first_expand_bias,
            first_project_gain, first_project_bias, first_excite_bias,
            first_squeeze_bias, second_squeeze_bias,
            second_spatial_gain, second_spatial_bias, second_expand_gain, second_expand_bias, second_excite_bias,
        ],
        [V((REST, 256), BF), V((16, 256), F32), D((3,))],
        size=1e7, name="pack",
    )
    w4_r1 = swap(after(w4_half, other_px, part_other), "narrow", pair)
    pk1 = swap(after(pack, other_px, part_other), "narrow", pair)
    og_own = out_grad.transpose(0, 2, 1, 3).reshape(M, 1024)
    ws = first_spatial.reshape(9, 512, 512)

    xp, strided, x1, col1, pre2, st2, tot1 = call(
        stage_two_kernel,
        [h(4, M, 1024), h(M, 1024), f(4, M, 512), h(9, M, 512), f(M, 512), f(4, 512), f(4, 512)],
        [
            fs, isc, (ANY, own_px), (ANY, other_px), part, part_other, perm, keep1, keep,
            first_reduce, ws, gb, sh,
        ],
        [V((2, B, HALF, 1024), BF), V((4, M, 256), F32), V((4, M, 512), BF), V((4, 512), F32), D((2,))],
        flops=4e9, size=2e7, name="stage_two",
    )
    parts2 = across(st2)
    w4_r2 = swap(after(w4_r1, st2), "wide", near)
    w4_refs = [(ANY, second_reduce), (ANY, w4_r1), (ANY, w4_r2)]
    prep, stp = call(
        project_kernel, [f(M, 2048), f(4, 2048)], [fs, after(strided, w4_r1), keep, first_project],
        flops=1e9, size=8e6, name="project",
    )
    h2, pre3, st3, tot2 = call(
        stage_three_kernel, [h(M, 512), f(M, 2048), f(8, 2048), f(4, 512)],
        [fs, parts2, pre2, stp, keep, first_expand, gb], [V((4, 512), F32)],
        flops=1e9, size=6e6, name="stage_three",
    )
    parts3 = steps(st3)
    lows, pre4, st4, tot3, gate1, sp1, pooled1, squares = call(
        stage_four_kernel,
        [
            h(M, 2048), f(M, 512), f(4, 512), f(8, 2048), f(8, 2048), f(8, 128), f(8, 2048), f(8, 256),
        ],
        [fs, isc, parts3, pre3, prep, keep, vec1, sqb, first_squeeze, first_excite] + w4_refs,
        [V((M, 2048), F32), V((M, 2048), F32), V((2048, 512), BF), V((M, 512), F32), V((8, 2048), F32), D((3,))],
        flops=1e9, size=1e7, name="stage_four",
    )
    parts4 = across(st4)
    pk2 = swap(after(pk1, st4), "wide", near)
    og_other = swap(after(og_own, pk1, st4), "narrow", pair)
    w5_refs = [(ANY, w5_own), (ANY, pk1), (ANY, pk2)]
    w6_refs = [(ANY, second_expand), (ANY, pk1), (ANY, pk2)]
    col4, pre5, st5, tot4, gain5, vec2 = call(
        stage_five_kernel,
        [h(9, M, 512), f(M, 512), f(4, 512), f(4, 512), f(2, 512), f(3, 2048)],
        [fs, isc, parts4, pre4, keep, gb, sh, vown] + w5_refs,
        [V((2, 4608, 256), BF), V((4, 512), F32), V((16, 256), BF), D((4,))],
        flops=2e9, size=1e7, name="stage_five",
    )
    parts5 = across(st5)
    h5, pre6, st6, tot5 = call(
        stage_six_kernel, [h(M, 512), f(M, 2048), f(4, 2048), f(4, 512)],
        [fs, isc, parts5, pre5, keep, gain5] + w6_refs,
        [V((512, 2048), BF), V((4, 512), F32), D((17,))],
        flops=1e9, size=6e6, name="stage_six",
    )
    parts6 = across(st6)
    result, dj2, pay6, extra6, tot6, gate2, dp2, pooled2, de2, ds2, sq2 = call(
        turn_kernel,
        [
            h(M, 1024), f(M, 2048), f(4, 2048), f(8, 512), f(4, 2048), f(8, 2048),
            f(8, 2048), f(8, 2048), f(8, 2048), f(8, 128), f(8, 128),
        ],
        [
            fs, isc, parts6, pre6, keep, lows, vec2, sqb, squares,
            (ANY, second_squeeze), (ANY, second_excite), (ANY, pk1), (ANY, pk2), (ANY, og_own), (ANY, og_other),
        ],
        [
            V((M, 2048), F32), V((2, M, 1024), BF), V((2, M, 1024), BF), V((2048, 128), BF),
            V((2, 128, 1024), BF), V((4, 2048), F32), V((8, 128), F32), D((16,)),
        ],
        flops=1e9, size=1e7, name="turn",
    )
    back6 = across(pay6)
    d6, do5, bt5, dgain6, dbias6 = call(
        back_six_kernel, [h(M, 2048), f(M, 512), f(12, 512), f(1024), f(1024)],
        [fs, isc, back6, tot6, pre6, dj2, gate2, dp2, pre5, tot5, extra6, keep, vec2, gain5] + w6_refs,
        [V((512, 2048), BF), V((4, 2048), F32), V((M, 512), F32), D((17,))],
        flops=1e9, size=1e7, name="back_six",
    )
    back5 = across(bt5)
    d5, do4, bt4, dgain5, dbias5, debias2, dsbias2, norms = call(
        back_five_kernel,
        [h(M, 512), f(M, 512), f(4, 512), f(256), f(256), f(1024), f(128), ((5,), F32, SMEM)],
        [fs, isc, back5, tot5, pre5, do5, pre4, tot4, keep, gb, gain5, sh] + w5_refs,
        [V((2, 4608, 256), BF), V((12, 512), F32), D((3,))],
        flops=2e9, size=1e7, name="back_five",
    )
    back4 = across(bt4)

    def step(g, k):
        if not exact:
            return g
        partner = [(i, i ^ (1 << k)) for i in range(wide)]
        if k == 0:
            return g[0] + swap(g[1], "wide", partner)
        half = g.shape[0] // 2
        return g[:half] + swap(g[half:], "wide", partner)

    def last_step(g):
        return g[:1], swap(g[1:], "wide", [(i, i ^ 8) for i in range(wide)])

    ga = call(
        grads_a_kernel, [h(8, 416, 256)] * 2, [isc, h5, d6, col4, d5],
        [V((256, 2048), BF), V((512, 256), BF)], flops=2e9, size=1e7, name="grads_a",
    )
    back4, ga = lax.optimization_barrier((back4, ga))
    d4, dj1, bt3, dgain4, dbias4, dp1, de1, ds1, bias1 = call(
        back_four_kernel,
        [
            h(M, 512), f(M, 2048), f(8, 2048), f(512), f(512), f(8, 2048),
            f(8, 2048), f(8, 128), f(8, 512),
        ],
        [
            fs, isc, back4, tot4, pre4, do4, dj2, tot3, pre3, prep, gate1, sp1, keep, gb, vec1,
            first_squeeze, first_excite,
        ] + w4_refs,
        [V((2048, 512), BF), V((4, 512), F32), D((3,))],
        flops=1e9, size=1e7, name="back_four",
    )
    back3 = steps(bt3)
    ga = step(ga, 0)
    gb1 = call(
        grads_b_kernel, [h(8, 192, 256)] * 2, [isc, d4, lows, sq2, pooled2, de2, ds2],
        [V((512, 256), BF), V((128, 256), F32), V((128, 256), F32)],
        flops=1e9, size=4e6, name="grads_b",
    )
    back3, ga, gb1 = lax.optimization_barrier((back3, ga, gb1))
    d3, dproj, do2, bt2, dgain3, dbias3, dgainp, dbiasp = call(
        back_three_kernel,
        [h(M, 2048), h(M, 2048), f(M, 512), f(12, 512), f(2048), f(2048), f(2048), f(2048)],
        [fs, back3, tot3, pre3, prep, dj1, gate1, dp1, bias1, pre2, tot2, keep, vec1, gb, first_expand],
        [V((8, 2048), F32), V((M, 512), F32)],
        flops=1e9, size=1e7, name="back_three",
    )
    back2 = across(bt2)
    ga, gb1 = step(ga, 1), step(gb1, 0)
    gc = call(
        grads_c_kernel, [h(8, 448, 256)] * 2,
        [isc, h2, d3, strided, dproj, sp1, pooled1, de1, ds1],
        [V((512, 256), BF), V((1024, 256), BF), V((128, 256), F32), V((128, 256), F32), V((8, 128), F32)],
        flops=3e9, size=1e7, name="grads_c",
    )
    back2, ga, gb1, gc = lax.optimization_barrier((back2, ga, gb1, gc))
    d2, do1, bt1, dgain2, dbias2, debias1, dsbias1 = call(
        back_two_kernel,
        [h(M, 512), f(4, M, 512), f(4, 512), f(512), f(512), f(2048), f(128)],
        [fs, back2, tot2, pre2, do2, x1, keep1, keep, gb, sh, ws],
        [V((12, 512), F32), V((4, M, 512), BF)],
        flops=2e9, size=1e7, name="back_two",
    )
    back1 = across(bt1)
    ga, gb1, gc = step(ga, 2), step(gb1, 1), step(gc, 0)
    gd = call(
        grads_d_kernel, [h(8, 288, 256)] * 2, [isc, col1, d2], [V((512, 256), BF)],
        flops=2e9, size=6e6, name="grads_d",
    )
    back1, ga, gb1, gc, gd = lax.optimization_barrier((back1, ga, gb1, gc, gd))
    d1, ge_keep, ge_send, dgain1, dbias1 = call(
        back_one_kernel, [h(B, M, 512), h(8, 64, 256), h(8, 64, 256), f(512), f(512)],
        [fs, isc, back1, tot1, x1, do1, xp, keep1, gb],
        [V((4, 512), F32), V((4, M, 512), BF), V((1024, 256), BF)],
        flops=1e9, size=6e6, name="back_one",
    )
    ge = (ge_keep, ge_send)
    dimg = call(
        image_kernel, [f(HROWS, 1024)],
        [
            perm.transpose(0, 2, 1)[n], jnp.asarray(pick_np, BF)[n], jnp.asarray(spread_np, BF),
            d1, dproj, keep_half, first_reduce, first_project,
        ],
        [V((HROWS, 512), BF), V((HALF, 2048), BF)],
        flops=1e9, size=1e7, name="image",
    )[0]

    if exact:
        for k in range(1, 4):
            gb1 = step(gb1, k) if k == 2 else gb1
            gc = step(gc, k) if k < 3 else gc
        gd, ge = step(step(gd, 0), 1), step(ge, 0)
        gd, ge, dimg = lax.optimization_barrier((gd, ge, dimg))
        gd, ge = step(gd, 2), step(step(ge, 1), 2)
        expand2, spatial2 = call(
            unpack_a_kernel, [f(256, 128), f(288, 256)], list(last_step(ga)), name="unpack_a"
        )
        reduce2, squeeze2, excite2 = call(
            unpack_b_kernel, [f(32, 1024), f(8, 1024), f(8, 1024)], list(last_step(gb1)), name="unpack_b"
        )
        expand1, project1, squeeze1, excite1 = call(
            unpack_c_kernel, [f(32, 1024), f(64, 1024), f(8, 1024), f(8, 1024)], list(last_step(gc)),
            name="unpack_c",
        )
        spatial1 = call(unpack_d_kernel, [f(288, 256)], list(last_step(gd)), name="unpack_d")[0]
        reduce1 = call(unpack_d_kernel, [f(64, 256)], list(last_step(ge)), name="unpack_e")[0]
    else:
        finer = wide // 16

        def summed(g):
            return lax.psum_scatter(g, "wide", scatter_dimension=0, tiled=True)

        def blocks(g, start, count, rows):
            p = g[:, start : start + count * rows].reshape(16, count, finer, rows // finer, 256)
            p = summed(p.transpose(0, 2, 1, 3, 4).reshape(wide, count, rows // finer, 256))[0]
            return f32(p).transpose(1, 0, 2).reshape(rows // finer, count * 256)

        def both(g, start):
            p = g[:, start : start + 64].reshape(16, 4, 2, finer, 8 // finer, 256)
            p = f32(summed(p.transpose(0, 3, 1, 2, 4, 5).reshape(wide, 4, 2, -1, 256))[0])
            return [p[:, k].transpose(1, 0, 2).reshape(-1, 1024) for k in range(2)]

        def taps(g, start):
            p = g[:, start : start + 288].reshape(16, 9, finer, 32 // finer, 256)
            return f32(summed(p.transpose(0, 2, 1, 3, 4).reshape(wide, 9, -1, 256))[0]).reshape(-1, 256)

        ga, gb1, gc, gd, ge = (jnp.concatenate(g) for g in (ga, gb1, gc, gd, ge))
        e2 = ga[:, 0:128].reshape(16, 128, 2, finer, 128 // finer).transpose(0, 3, 1, 2, 4)
        e2 = summed(e2.reshape(wide, 1, -1)).reshape(128, 2, -1)
        expand2 = f32(e2.transpose(1, 0, 2).reshape(256, -1))
        spatial2 = taps(ga, 128)
        reduce2 = blocks(gb1, 0, 4, 32)
        squeeze2, excite2 = both(gb1, 128)
        expand1, project1 = blocks(gc, 0, 4, 32), blocks(gc, 128, 4, 64)
        squeeze1, excite1 = both(gc, 384)
        spatial1, reduce1 = taps(gd, 0), blocks(ge, 0, 1, 64)
    return (
        result.reshape(B, 7, 8, 1024).transpose(0, 2, 1, 3),
        dimg.reshape(B, 14, 8, 1024).transpose(0, 2, 1, 3),
        reduce1, dgain1, dbias1,
        spatial1.reshape(3, 3, -1, 256), dgain2, dbias2,
        expand1, dgain3, dbias3,
        project1, dgainp, dbiasp,
        squeeze1.T, dsbias1, excite1, debias1,
        reduce2.T, dgain4, dbias4,
        spatial2.reshape(3, 3, -1, 256), dgain5, dbias5,
        expand2, dgain6, dbias6,
        squeeze2.T, dsbias2, excite2, debias2,
        norms,
    )


def solution(mesh):
    rep, nar = P(), P("narrow")
    return jax.shard_map(
        local,
        mesh=mesh,
        in_specs=(P("wide", "narrow", None, None),) + (rep,) * 18 + (
            P("narrow", None), rep, rep,
            P(None, None, None, "narrow"), nar, nar,
            P("narrow", None), nar, nar,
            P("narrow", None), rep, P(None, "narrow"), nar,
            P("wide", None, None, "narrow"),
        ),
        out_specs=(
            P("wide", None, None, "narrow"), P("wide", "narrow", None, None),
            P("wide", "narrow"), rep, rep,
            P(None, None, "wide", "narrow"), rep, rep,
            P("wide", "narrow"), rep, rep,
            P("wide", "narrow"), rep, rep,
            P("narrow", "wide"), rep, P("wide", "narrow"), rep,
            P("narrow", "wide"), rep, rep,
            P(None, None, "wide", "narrow"), nar, nar,
            P("narrow", "wide"), nar, nar,
            P("narrow", "wide"), rep, P("wide", "narrow"), nar,
            rep,
        ),
        check_vma=False,
    )
```

time: 1930 us -> 428 us (0.22)
  waiting for transfers between devices: 979 us -> 109 us
  blocking collectives: 468 us -> 43.9 us
  matrix products: 158 us -> 0 us
  local copies, waits for them, and re-layouts: 198 us -> 99.1 us
  Pallas kernels: 0 us -> 93 us
  other arithmetic: 85.6 us -> 17.1 us
  starting transfers between devices: 7.01 us -> 61.9 us
    reduce_scatter x18 -> x0, waiting for transfers between devices: 706 us -> none  [the longest x1 114 us: wide_totals(): lax.psum_scatter(spatial_grad, 'wide', scatter_dimension=2, tiled=True)]
    psum x14 -> x0, blocking collectives: 439 us -> none  [the longest x6 246 us: total_wide(): return lax.psum(flattened, 'wide')]
    psum x4 -> x0, waiting for transfers between devices: 272 us -> none  [the longest x2 231 us: total_all(): return lax.psum(flattened, ('wide', 'narrow'))]
    dot_general x137 -> x0, matrix products: 158 us -> none  [the longest x23 32.9 us: pointwise(): jnp.einsum('brci,io->brco', values, weights, preferred_element_type=jnp.f...]
    ppermute x2 -> x45, waiting for transfers between devices: 0.01 us -> 99 us  [swap(): return lax.ppermute(v, axis, pairs)]
    pallas_call x0 -> x26, Pallas kernels: none -> 93 us  [call(): pl.pallas_call(body, out_shape=tuple((jax.ShapeDtypeStruct(o[0], o[1]) fo...]
    pad x10 -> x0, local copies, waits for them, and re-layouts: 53.9 us -> none  [the longest x9 47.5 us: taps_input(): lax.pad(product_term, zero_value, ((0, 0, 0), (offset_row, padded_rows -...]
    convert_element_type x45 -> x0, other arithmetic: 34.5 us -> none  [the longest x6 8.83 us: pair_totals(): return (lax.psum_scatter(reduce_grad.astype(jnp.bfloat16), 'narrow', scat...]
  transfers between devices with their start and end apart: 24 -> 51, of which waited for: 17 -> 25; matrix products, arithmetic and copies ran while one was open for 10% -> 7% of each run, Pallas kernels for 0% -> 16%
where the time goes in v1:
time: 428 us; the launch traced here: 425 us
  waiting for transfers between devices  109 us (25%)
  local copies, waits for them, and re-layouts  99.1 us (23%)
  Pallas kernels  93 us (22%)
  starting transfers between devices  61.9 us (14%)
  blocking collectives  43.9 us (10%)
  other arithmetic  17.1 us (4%)
    ppermute x45, waiting for transfers between devices, swap(): return lax.ppermute(v, axis, pairs)  99 us
    pallas_call x26, Pallas kernels, call(): pl.pallas_call(body, out_shape=tuple((jax.ShapeDtypeStruct(o[0], o[1]) fo...  93 us
    unnamed x328, local copies, waits for them, and re-layouts  84.3 us
    all_to_all x4, blocking collectives, across(): lax.all_to_all(sent, 'wide', 0, 0, axis_index_groups=groups, tiled=True)  43.9 us
    ppermute x45, starting transfers between devices, swap(): return lax.ppermute(v, axis, pairs)  35.5 us
    all_to_all x6, starting transfers between devices, across(): lax.all_to_all(sent, 'wide', 0, 0, axis_index_groups=groups, tiled=True)  26.3 us
    all_to_all x6, waiting for transfers between devices, across(): lax.all_to_all(sent, 'wide', 0, 0, axis_index_groups=groups, tiled=True)  9.59 us
  transfers between devices with their start and end apart: 51, of which 25 were waited for; matrix products, arithmetic and copies ran while one was open for 7% of the time, Pallas kernels for 16%

profile of v1, /device:TPU:0, one launch (start us, length us, event | category | flops | bytes accessed | tf_op | source)
XLA Modules:
  0.0 425.4 jit_solution(15333868653389803456)
XLA Ops:
  0.7 3.0 collective-permute-start
  5.0 2.1 setup.1
  13.1 5.8 %all-to-all-start = ((f32[8,4,512]{2,1,0:T(4,128)}), f32[8,4,512]{2,1,0:T(4,128)}, u32[]{:S(2)}, u32[]{:S(2)}) async-start(f32[8,4,512]{2,1,0:T(4,128)} %broadcast_in_dim.24), calls=%async_computation | async-start | bytes 131072 | tf_op jit(solution)/shard_map/all_to_all | solution.py:1030
  18.9 7.0 %all-to-all-done = f32[8,4,512]{2,1,0:T(4,128)} async-done(((f32[8,4,512]{2,1,0:T(4,128)}), f32[8,4,512]{2,1,0:T(4,128)}, u32[]{:S(2)}, u32[]{:S(2)}) %all-to-all-start) | async-done | bytes 65568 | tf_op jit(solution)/shard_map/all_to_all | solution.py:1030
  40.2 2.1 pack.1
  45.6 2.3 copy-done.31
  47.9 8.3 %stage_two.1 = (bf16[4,224,1024]{2,1,0:T(8,128)(2,1)S(1)}, bf16[224,1024]{1,0:T(8,128)(2,1)S(1)}, f32[4,224,512]{2,1,0:T(8,128)S(1)}, bf16[9,224,512]{2,1,0:T(8,...) custom-call(f32[13]{0:T(128)S(1)} %get-tuple-element.172.fs, ...), custom_call_target="tpu_custom_call" | custom-call | flops 4000000000 | bytes 20000000 | tf_op jit(solution)/shard_map/stage_two/pallas_call | solution.py:955
  64.2 3.4 all-to-all-start.1
  67.5 30.8 %collective-permute-done.4.r1 = bf16[512,512]{1,0:T(8,128)(2,1)S(1)} collective-permute-done((bf16[512,512]{1,0:T(8,128)(2,1)}, bf16[512,512]{1,0:T(8,128)(2,1)S(1)}, u32[]{:S(2)}, u32[]{:S(2)}) %collective-permute-start.4) | collective-permute-done | bytes 524320 | tf_op jit(solution)/shard_map/ppermute | solution.py:996
  98.4 2.4 copy-done.6
  101.8 3.1 project.1
  106.1 1.6 copy-done.41
  108.7 2.8 stage_three.1
  114.0 3.9 collective-permute-done.6
  118.1 4.0 collective-permute-done.7
  122.9 4.8 %collective-permute-done.8 = f32[8,2048]{1,0:T(8,128)S(1)} collective-permute-done((f32[8,2048]{1,0:T(8,128)S(1)}, f32[8,2048]{1,0:T(8,128)S(1)}, u32[]{:S(2)}, u32[]{:S(2)}) %collective-permute-start.8) | collective-permute-done | bytes 65568 | tf_op jit(solution)/shard_map/ppermute | solution.py:996
  127.9 5.2 %stage_four.1 = (bf16[224,2048]{1,0:T(8,128)(2,1)S(1)}, f32[224,512]{1,0:T(8,128)S(1)}, f32[4,512]{1,0:T(4,128)S(1)}, f32[8,2048]{1,0:T(8,128)S(1)}, f32[8,2048]...) custom-call(f32[13]{0:T(128)S(1)} %get-tuple-element.172.fs, ...), custom_call_target="tpu_custom_call" | custom-call | flops 1000000000 | bytes 10000000 | tf_op jit(solution)/shard_map/stage_four/pallas_call | solution.py:955
  136.7 3.5 collective-permute-done.10
  140.2 9.4 %all_to_all.50.parts = f32[8,4,512]{2,1,0:T(4,128)S(1)} all-to-all(f32[8,4,512]{2,1,0:T(4,128)S(1)} %broadcast_in_dim.27), channel_id=1, replica_groups={{0,4,8,12,16,20,24,28},{2,6,10,14,18,22,26,30},{1,5,9,13,17,21,25,29},{..., dimensions={0} | all-to-all | bytes 131072 | tf_op jit(solution)/shard_map/all_to_all | solution.py:1030
  149.6 3.6 stage_five.1
  155.7 9.3 %all_to_all.51.parts = f32[8,4,512]{2,1,0:T(4,128)S(1)} all-to-all(f32[8,4,512]{2,1,0:T(4,128)S(1)} %broadcast_in_dim.28), channel_id=1, replica_groups={{0,4,8,12,16,20,24,28},{2,6,10,14,18,22,26,30},{1,5,9,13,17,21,25,29},{..., dimensions={0} | all-to-all | bytes 131072 | tf_op jit(solution)/shard_map/all_to_all | solution.py:1030
  165.0 3.2 stage_six.1
  172.3 4.1 all-to-all-start.4
  176.3 7.0 %collective-permute-done.15.ogother = bf16[224,1024]{1,0:T(8,128)(2,1)} collective-permute-done((bf16[224,1024]{1,0:T(8,128)(2,1)}, bf16[224,1024]{1,0:T(8,128)(2,1)}, u32[]{:S(2)}, u32[]{:S(2)}) %collective-permute-start.15) | collective-permute-done | bytes 458784 | tf_op jit(solution)/shard_map/ppermute | solution.py:996
  183.4 2.6 all-to-all-done.4.parts
  191.8 8.4 %turn.1 = (bf16[224,1024]{1,0:T(8,128)(2,1)}, f32[224,2048]{1,0:T(8,128)S(1)}, f32[4,2048]{1,0:T(4,128)S(1)}, f32[8,512]{1,0:T(8,128)S(1)}, f32[4,2048]{1,0:T(4,...) custom-call(f32[13]{0:T(128)S(1)} %get-tuple-element.172.fs, ...), custom_call_target="tpu_custom_call" | custom-call | flops 1000000000 | bytes 10000000 | tf_op jit(solution)/shard_map/turn/pallas_call | solution.py:955
  203.3 12.6 %all_to_all.52.parts = f32[8,4,2048]{2,1,0:T(4,128)S(1)} all-to-all(f32[8,4,2048]{2,1,0:T(4,128)S(1)} %broadcast_in_dim.30), channel_id=1, replica_groups={{0,4,8,12,16,20,24,28},{2,6,10,14,18,22,26,30},{1,5,9,13,17,21,25,29},{..., dimensions={0} | all-to-all | bytes 524288 | tf_op jit(solution)/shard_map/all_to_all | solution.py:1030
  216.0 4.0 back_six.1
  221.4 12.7 %all_to_all.53.parts = f32[8,12,512]{2,1,0:T(8,128)S(1)} all-to-all(f32[8,12,512]{2,1,0:T(8,128)S(1)} %broadcast_in_dim.31), channel_id=1, replica_groups={{0,4,8,12,16,20,24,28},{2,6,10,14,18,22,26,30},{1,5,9,13,17,21,25,29},{..., dimensions={0} | all-to-all | bytes 393216 | tf_op jit(solution)/shard_map/all_to_all | solution.py:1030
  234.1 4.7 %back_five.1 = (bf16[224,512]{1,0:T(8,128)(2,1)S(1)}, f32[224,512]{1,0:T(8,128)S(1)}, f32[4,512]{1,0:T(4,128)S(1)}, f32[256]{0:T(256)}, f32[256]{0:T(256)}, /*index=5*/f32[1024]{0:T(1024)}, f32[128]{0:T(128)}, f32[5]{0:T(128)}) custom-call(f32[13]{0:T(128)S(1)} %get-tuple-element.172.fs, s32[18]{0:T(128)S(1)} %get-tuple-element.177.isc, ...), custom_call_target="tpu_custom_call" | custom-call | flops 2000000000 | bytes 10000000 | tf_op jit(solution)/shard_map/back_five/pallas_call | solution.py:955
  242.0 4.0 all-to-all-start.7
  250.6 5.3 %grads_a.1 = (bf16[8,416,256]{2,1,0:T(8,128)(2,1)S(1)}, bf16[8,416,256]{2,1,0:T(8,128)(2,1)S(1)}) custom-call(s32[18]{0:T(128)S(1)} %get-tuple-element.177.isc, bf16[224,512]{1,0:T(8,128)(2,1)S(1)} %copy-done.136, bf16[224,2048]{1,0:T(8,128)(2,1)S(1)} %copy-done.132, bf16[9,224,512]{2,1,0:T(8,128)(2,1)S(1)} %copy-done.127, bf16[224,512]{1,0:T(8,128)(2,1)S(1)} %copy-done.138), custom_call_target="tpu_custom_call" | custom-call | flops 2000000000 | bytes 10000000 | tf_op jit(solution)/shard_map/grads_a/pallas_call | solution.py:955
  269.9 7.9 %back_four.1 = (bf16[224,512]{1,0:T(8,128)(2,1)S(1)}, f32[224,2048]{1,0:T(8,128)S(1)}, f32[8,2048]{1,0:T(8,128)S(1)}, f32[512]{0:T(512)}, f32[512]{0:T(512)}, /*...) custom-call(f32[13]{0:T(128)S(1)} %get-tuple-element.172.fs, ...), custom_call_target="tpu_custom_call" | custom-call | flops 1000000000 | bytes 10000000 | tf_op jit(solution)/shard_map/back_four/pallas_call | solution.py:955
  279.1 1.9 collective-permute-start.20
  281.1 2.6 collective-permute-done.20
  283.7 1.8 collective-permute-start.21
  285.5 2.5 collective-permute-done.21
  288.0 2.7 collective-permute-start.22
  290.8 3.0 grads_b.1
  298.0 4.5 %back_three.1 = (bf16[224,2048]{1,0:T(8,128)(2,1)S(1)}, bf16[224,2048]{1,0:T(8,128)(2,1)S(1)}, f32[224,512]{1,0:T(8,128)S(1)}, f32[12,512]{1,0:T(8,128)S(1)}, f3...) custom-call(f32[13]{0:T(128)S(1)} %get-tuple-element.172.fs, ...), custom_call_target="tpu_custom_call" | custom-call | flops 1000000000 | bytes 10000000 | tf_op jit(solution)/shard_map/back_three/pallas_call | solution.py:955
  307.1 4.9 %all-to-all-start.8 = ((f32[8,12,512]{2,1,0:T(8,128)}), f32[8,12,512]{2,1,0:T(8,128)S(1)}, u32[]{:S(2)}, u32[]{:S(2)}) async-start(f32[8,12,512]{2,1,0:T(8,128)} %broadcast_in_dim.34), calls=%async_computation.8 | async-start | bytes 524288 | tf_op jit(solution)/shard_map/all_to_all | solution.py:1030
  315.4 2.9 grads_c.1
  319.5 2.9 add.122
  322.4 2.4 slice_add_fusion.1
  324.8 1.8 slice.95
  326.6 2.0 collective-permute-start.29
  328.6 1.8 slice.93
  333.4 2.3 copy-done.32
  335.7 3.6 back_two.1
  339.3 3.2 grads_d.1
  344.2 4.2 all-to-all-start.9
  348.4 1.9 slice_add_fusion.5
  350.4 1.9 slice_add_fusion.4
  352.3 3.2 add.126
  356.1 2.2 slice.109
  365.0 2.5 collective-permute-start.44
  370.5 3.4 back_one.1
  374.0 6.8 %image.1 = f32[448,1024]{1,0:T(8,128)} custom-call(bf16[112,224]{1,0:T(8,128)(2,1)S(1)} %dynamic-slice_bitcast_fusion.1.own, bf16[112,224]{1,0:T(8,128)(2,1)S(1)} %dynamic-slice_bitcast_fusion.pick_own, bf16[448,112]{1,0:T(8,128)(2,1)S(1)} %copy-done.94, bf16[4,224,512]{2,1,0:T(8,128)(2,1)S(1)} %get-tuple-element.277.d1, bf16[224,2048]{1,0:T(8,128)(2,1)S(1)} %copy-done.74, ...), custom_call_target="tpu_custom_call" | custom-call | flops 1000000000 | bytes 10000000 | tf_op jit(solution)/shard_map/image/pallas_call | solution.py:955
  380.8 1.7 add.127
  386.6 11.7 %collective-permute-done.32 = bf16[4,288,256]{2,1,0:T(8,128)(2,1)S(1)} collective-permute-done((bf16[4,288,256]{2,1,0:T(8,128)(2,1)S(1)}, bf16[4,288,256]{2,1,0:T(8,128)(2,1)S(1)}, u32[]{:S(2)}, u32[]{:S(2)}) %collective-permute-start.32) | collective-permute-done | bytes 589856 | tf_op jit(solution)/shard_map/ppermute | solution.py:996
  399.8 3.8 collective-permute-done.34
  404.9 6.9 %collective-permute-done.35 = bf16[2,64,256]{2,1,0:T(8,128)(2,1)S(1)} collective-permute-done((bf16[2,64,256]{2,1,0:T(8,128)(2,1)S(1)}, bf16[2,64,256]{2,1,0:T(8,128)(2,1)S(1)}, u32[]{:S(2)}, u32[]{:S(2)}) %collective-permute-start.35) | collective-permute-done | bytes 65568 | tf_op jit(solution)/shard_map/ppermute | solution.py:996
  412.0 2.9 collective-permute-start.36
  416.4 5.5 %collective-permute-done.41.b = bf16[1,448,256]{2,1,0:T(8,128)(2,1)S(1)} collective-permute-done((bf16[1,448,256]{2,1,0:T(8,128)(2,1)S(1)}, bf16[1,448,256]{2,1,0:T(8,128)(2,1)S(1)}, u32[]{:S(2)}, u32[]{:S(2)}) %collective-permute-start.41) | collective-permute-done | bytes 229408 | tf_op jit(solution)/shard_map/ppermute | solution.py:996
  (457 shorter events, 123.2 us)
Async XLA Ops:
  0.7 26.8 %copy-start.3 = (bf16[3,3,512,256]{3,2,1,0:T(8,128)(2,1)S(1)}, bf16[3,3,512,256]{3,2,1,0:T(8,128)(2,1)}, u32[]{:S(2)}) copy-start(bf16[3,3,512,256]{3,2,1,0:T(8,128)(2,1)} %param.59) | copy-start | bytes 7077892
  0.7 42.8 %collective-permute-start = (bf16[4,112,1024]{2,1,0:T(8,128)(2,1)}, bf16[4,112,1024]{2,1,0:T(8,128)(2,1)}, u32[]{:S(2)}, u32[]{:S(2)}) collective-permute-start(bf16[4,112,1024]{2,1,0:T(8,128)(2,1)} %bitcast.36), channel_id=1, source_target_pairs={{0,1},{1,0},{2,3},{3,2},{4,5},{5,4},{6,7},{7,6},{8,9},{9,8},{10,11... | collective-permute-start | bytes 2752520 | tf_op jit(solution)/shard_map/ppermute | solution.py:996
  7.2 38.4 %copy-start.52 = (f32[4,224,1]{2,1,0:T(8,128)}, f32[4,224,1]{2,1,0:T(8,128)S(1)}, u32[]{:S(2)}) copy-start(f32[4,224,1]{2,1,0:T(8,128)S(1)} %get-tuple-element.175.keep1) | copy-start | bytes 10756
  11.2 1.2 collective-permute-start.1
  13.1 12.8 %all-to-all-start = ((f32[8,4,512]{2,1,0:T(4,128)}), f32[8,4,512]{2,1,0:T(4,128)}, u32[]{:S(2)}, u32[]{:S(2)}) async-start(f32[8,4,512]{2,1,0:T(4,128)} %broadcast_in_dim.24), calls=%async_computation | async-start | bytes 131072 | tf_op jit(solution)/shard_map/all_to_all | solution.py:1030
  26.8 16.7 %collective-permute-start.2 = (f32[4,512]{1,0:T(4,128)S(1)}, f32[4,512]{1,0:T(4,128)S(1)}, u32[]{:S(2)}, u32[]{:S(2)}) collective-permute-start(f32[4,512]{1,0:T(4,128)S(1)} %reduce_sum.9.part), channel_id=1, source_target_pairs={{0,1},{1,0},{2,3},{3,2},{4,5},{5,4},{6,7},{7,6},{8,9},{9,8},{10,11... | collective-permute-start | bytes 24584 | tf_op jit(solution)/shard_map/ppermute | solution.py:996
  43.5 92.7 %collective-permute-start.11 = (bf16[3856,256]{1,0:T(8,128)(2,1)}, bf16[3856,256]{1,0:T(8,128)(2,1)S(1)}, u32[]{:S(2)}, u32[]{:S(2)}) collective-permute-start(bf16[3856,256]{1,0:T(8,128)(2,1)} %get-tuple-element.196), channel_id=1, source_target_pairs={{0,1},{1,0},{2,3},{3,2},{4,5},{5,4},{6,7},{7,6},{8,9},{9,8},{10,11... | collective-permute-start | bytes 5922824 | tf_op jit(solution)/shard_map/ppermute | solution.py:996
  44.9 53.4 %collective-permute-start.4 = (bf16[512,512]{1,0:T(8,128)(2,1)}, bf16[512,512]{1,0:T(8,128)(2,1)S(1)}, u32[]{:S(2)}, u32[]{:S(2)}) collective-permute-start(bf16[512,512]{1,0:T(8,128)(2,1)} %get-tuple-element.183), channel_id=1, source_target_pairs={{0,1},{1,0},{2,3},{3,2},{4,5},{5,4},{6,7},{7,6},{8,9},{9,8},{10,11... | collective-permute-start | bytes 1572872 | tf_op jit(solution)/shard_map/ppermute | solution.py:996
  62.4 1.2 collective-permute-start.3
  64.2 41.9 %all-to-all-start.1 = ((f32[8,4,512]{2,1,0:T(4,128)}), f32[8,4,512]{2,1,0:T(4,128)S(1)}, u32[]{:S(2)}, u32[]{:S(2)}) async-start(f32[8,4,512]{2,1,0:T(4,128)} %broadcast_in_dim.25), calls=%async_computation.1 | async-start | bytes 131072 | tf_op jit(solution)/shard_map/all_to_all | solution.py:1030
  101.8 26.0 %copy-start.82 = (f32[8,2048]{1,0:T(8,128)S(1)}, f32[8,2048]{1,0:T(8,128)}, u32[]{:S(2)}) copy-start(f32[8,2048]{1,0:T(8,128)} %copy-done.81) | copy-start | bytes 196612
  112.2 20.9 %copy-start.11 = (f32[224,2048]{1,0:T(8,128)}, f32[224,2048]{1,0:T(8,128)S(1)}, u32[]{:S(2)}) copy-start(f32[224,2048]{1,0:T(8,128)S(1)} %get-tuple-element.187.pre3) | copy-start | bytes 5505028
  112.2 1.3 collective-permute-start.5
  113.5 4.3 %collective-permute-start.6 = (f32[8,2048]{1,0:T(8,128)S(1)}, f32[8,2048]{1,0:T(8,128)S(1)}, u32[]{:S(2)}, u32[]{:S(2)}) collective-permute-start(f32[8,2048]{1,0:T(8,128)S(1)} %add.105), channel_id=1, source_target_pairs={{0,4},{2,6},{4,0},{6,2},{8,12},{10,14},{12,8},{14,10},{16,20},{18,... | collective-permute-start | bytes 196616 | tf_op jit(solution)/shard_map/ppermute | solution.py:996
  117.8 4.3 %collective-permute-start.7 = (f32[8,2048]{1,0:T(8,128)S(1)}, f32[8,2048]{1,0:T(8,128)S(1)}, u32[]{:S(2)}, u32[]{:S(2)}) collective-permute-start(f32[8,2048]{1,0:T(8,128)S(1)} %add.106), channel_id=1, source_target_pairs={{0,8},{2,10},{4,12},{6,14},{8,0},{10,2},{12,4},{14,6},{16,24},{18,... | collective-permute-start | bytes 196616 | tf_op jit(solution)/shard_map/ppermute | solution.py:996
  118.1 9.7 %collective-permute-start.9 = (bf16[512,512]{1,0:T(8,128)(2,1)}, bf16[512,512]{1,0:T(8,128)(2,1)S(1)}, u32[]{:S(2)}, u32[]{:S(2)}) collective-permute-start(bf16[512,512]{1,0:T(8,128)(2,1)} %copy-done.47), channel_id=1, source_target_pairs={{0,2},{2,0},{4,6},{6,4},{8,10},{10,8},{12,14},{14,12},{16,18},{18,... | collective-permute-start | bytes 1572872 | tf_op jit(solution)/shard_map/ppermute | solution.py:996
  122.2 5.6 %collective-permute-start.8 = (f32[8,2048]{1,0:T(8,128)S(1)}, f32[8,2048]{1,0:T(8,128)S(1)}, u32[]{:S(2)}, u32[]{:S(2)}) collective-permute-start(f32[8,2048]{1,0:T(8,128)S(1)} %add.107), channel_id=1, source_target_pairs={{0,16},{2,18},{4,20},{6,22},{8,24},{10,26},{12,28},{14,30},{16,0},... | collective-permute-start | bytes 196616 | tf_op jit(solution)/shard_map/ppermute | solution.py:996
  127.9 21.7 %copy-start.4 = (bf16[3,3,512,256]{3,2,1,0:T(8,128)(2,1)S(1)}, bf16[3,3,512,256]{3,2,1,0:T(8,128)(2,1)}, u32[]{:S(2)}) copy-start(bf16[3,3,512,256]{3,2,1,0:T(8,128)(2,1)} %param.59) | copy-start | bytes 7077892
  127.9 21.7 %copy-start.20 = (bf16[9,224,224]{2,1,0:T(8,128)(2,1)S(1)}, bf16[9,224,224]{2,1,0:T(8,128)(2,1)}, u32[]{:S(2)}) copy-start(bf16[9,224,224]{2,1,0:T(8,128)(2,1)} %constant.19.clone.sh) | copy-start | bytes 2709508
  127.9 21.7 %copy-start.102 = (bf16[16,256]{1,0:T(8,128)(2,1)S(1)}, bf16[16,256]{1,0:T(8,128)(2,1)}, u32[]{:S(2)}) copy-start(bf16[16,256]{1,0:T(8,128)(2,1)} %copy-done.101) | copy-start | bytes 24580
  136.2 13.4 %collective-permute-start.12 = (bf16[3856,256]{1,0:T(8,128)(2,1)S(1)}, bf16[3856,256]{1,0:T(8,128)(2,1)S(1)}, u32[]{:S(2)}, u32[]{:S(2)}) collective-permute-start(bf16[3856,256]{1,0:T(8,128)(2,1)S(1)} %collective-permute-done.11.r1), channel_id=1, source_target_pairs={{0,2},{2,0},{4,6},{6,4},{8,10},{10,8},{12,14},{14,12},{16,18},{18,... | collective-permute-start | bytes 5922824 | tf_op jit(solution)/shard_map/ppermute | solution.py:996
  136.2 4.0 collective-permute-start.10
  154.5 79.5 %copy-start.95 = (f32[4,512]{1,0:T(4,128)}, f32[4,512]{1,0:T(4,128)S(1)}, u32[]{:S(2)}) copy-start(f32[4,512]{1,0:T(4,128)S(1)} %get-tuple-element.217.tot4) | copy-start | bytes 24580
  154.5 1.2 collective-permute-start.13
  165.0 20.9 %copy-start.66 = (bf16[128,1024]{1,0:T(8,128)(2,1)S(1)}, bf16[128,1024]{1,0:T(8,128)(2,1)}, u32[]{:S(2)}) copy-start(bf16[128,1024]{1,0:T(8,128)(2,1)} %exown.1) | copy-start | bytes 786436
  170.1 1.4 collective-permute-start.14
  170.1 13.2 %collective-permute-start.15 = (bf16[224,1024]{1,0:T(8,128)(2,1)}, bf16[224,1024]{1,0:T(8,128)(2,1)}, u32[]{:S(2)}, u32[]{:S(2)}) collective-permute-start(bf16[224,1024]{1,0:T(8,128)(2,1)} %bitcast.8.ogown), channel_id=1, source_target_pairs={{0,1},{1,0},{2,3},{3,2},{4,5},{5,4},{6,7},{7,6},{8,9},{9,8},{10,11... | collective-permute-start | bytes 1376264 | tf_op jit(solution)/shard_map/ppermute | solution.py:996
  172.3 13.7 %all-to-all-start.4 = ((f32[8,4,2048]{2,1,0:T(4,128)}), f32[8,4,2048]{2,1,0:T(4,128)}, u32[]{:S(2)}, u32[]{:S(2)}) async-start(f32[8,4,2048]{2,1,0:T(4,128)} %broadcast_in_dim.29), calls=%async_computation.4 | async-start | bytes 524288 | tf_op jit(solution)/shard_map/all_to_all | solution.py:1030
  191.8 24.1 %copy-start.18 = (bf16[256,2048]{1,0:T(8,128)(2,1)S(1)}, bf16[256,2048]{1,0:T(8,128)(2,1)}, u32[]{:S(2)}) copy-start(bf16[256,2048]{1,0:T(8,128)(2,1)} %w6own.3) | copy-start | bytes 3145732
  191.8 24.1 %copy-start.25 = (f32[224,2048]{1,0:T(8,128)S(1)}, f32[224,2048]{1,0:T(8,128)}, u32[]{:S(2)}) copy-start(f32[224,2048]{1,0:T(8,128)} %copy-done.23) | copy-start | bytes 5505028
  191.8 24.1 %copy-start.40 = (f32[224,512]{1,0:T(8,128)S(1)}, f32[224,512]{1,0:T(8,128)}, u32[]{:S(2)}) copy-start(f32[224,512]{1,0:T(8,128)} %copy-done.39) | copy-start | bytes 1376260
  202.1 1.2 collective-permute-start.16
  220.1 1.3 collective-permute-start.17
  240.2 1.2 collective-permute-start.18
  242.0 16.4 %all-to-all-start.7 = ((f32[8,4,512]{2,1,0:T(4,128)}), f32[8,4,512]{2,1,0:T(4,128)}, u32[]{:S(2)}, u32[]{:S(2)}) async-start(f32[8,4,512]{2,1,0:T(4,128)} %broadcast_in_dim.32), calls=%async_computation.7 | async-start | bytes 131072 | tf_op jit(solution)/shard_map/all_to_all | solution.py:1030
  258.5 36.3 %collective-permute-start.23 = (bf16[8,416,256]{2,1,0:T(8,128)(2,1)}, bf16[8,416,256]{2,1,0:T(8,128)(2,1)S(1)}, u32[]{:S(2)}, u32[]{:S(2)}) collective-permute-start(bf16[8,416,256]{2,1,0:T(8,128)(2,1)} %copy-done.129), channel_id=1, source_target_pairs={{0,2},{2,0},{4,6},{6,4},{8,10},{10,8},{12,14},{14,12},{16,18},{18,... | collective-permute-start | bytes 5111816 | tf_op jit(solution)/shard_map/ppermute | solution.py:996
  269.9 20.9 %copy-start.150 = (f32[8,128]{1,0:T(8,128)S(1)}, f32[8,128]{1,0:T(8,128)}, u32[]{:S(2)}) copy-start(f32[8,128]{1,0:T(8,128)} %copy-done.149) | copy-start | bytes 12292
  277.8 1.3 collective-permute-start.19
  279.1 4.6 %collective-permute-start.20 = (f32[8,2048]{1,0:T(8,128)S(1)}, f32[8,2048]{1,0:T(8,128)S(1)}, u32[]{:S(2)}, u32[]{:S(2)}) collective-permute-start(f32[8,2048]{1,0:T(8,128)S(1)} %add.115), channel_id=1, source_target_pairs={{0,4},{2,6},{4,0},{6,2},{8,12},{10,14},{12,8},{14,10},{16,20},{18,... | collective-permute-start | bytes 196616 | tf_op jit(solution)/shard_map/ppermute | solution.py:996
  283.7 4.3 %collective-permute-start.21 = (f32[8,2048]{1,0:T(8,128)S(1)}, f32[8,2048]{1,0:T(8,128)S(1)}, u32[]{:S(2)}, u32[]{:S(2)}) collective-permute-start(f32[8,2048]{1,0:T(8,128)S(1)} %add.116), channel_id=1, source_target_pairs={{0,8},{2,10},{4,12},{6,14},{8,0},{10,2},{12,4},{14,6},{16,24},{18,... | collective-permute-start | bytes 196616 | tf_op jit(solution)/shard_map/ppermute | solution.py:996
  288.0 6.7 %collective-permute-start.22 = (f32[8,2048]{1,0:T(8,128)S(1)}, f32[8,2048]{1,0:T(8,128)S(1)}, u32[]{:S(2)}, u32[]{:S(2)}) collective-permute-start(f32[8,2048]{1,0:T(8,128)S(1)} %add.117), channel_id=1, source_target_pairs={{0,16},{2,18},{4,20},{6,22},{8,24},{10,26},{12,28},{14,30},{16,0},... | collective-permute-start | bytes 196616 | tf_op jit(solution)/shard_map/ppermute | solution.py:996
  296.3 26.1 %collective-permute-start.25 = (bf16[4,416,256]{2,1,0:T(8,128)(2,1)}, bf16[4,416,256]{2,1,0:T(8,128)(2,1)}, u32[]{:S(2)}, u32[]{:S(2)}) collective-permute-start(bf16[4,416,256]{2,1,0:T(8,128)(2,1)} %slice.91), channel_id=1, source_target_pairs={{0,4},{2,6},{4,0},{6,2},{8,12},{10,14},{12,8},{14,10},{16,20},{18,... | collective-permute-start | bytes 2555912 | tf_op jit(solution)/shard_map/ppermute | solution.py:996
  297.8 21.7 %collective-permute-start.26 = (bf16[8,192,256]{2,1,0:T(8,128)(2,1)}, bf16[8,192,256]{2,1,0:T(8,128)(2,1)}, u32[]{:S(2)}, u32[]{:S(2)}) collective-permute-start(bf16[8,192,256]{2,1,0:T(8,128)(2,1)} %get-tuple-element.248), channel_id=1, source_target_pairs={{0,2},{2,0},{4,6},{6,4},{8,10},{10,8},{12,14},{14,12},{16,18},{18,... | collective-permute-start | bytes 2359304 | tf_op jit(solution)/shard_map/ppermute | solution.py:996
  305.1 1.2 collective-permute-start.24
  307.1 17.7 %all-to-all-start.8 = ((f32[8,12,512]{2,1,0:T(8,128)}), f32[8,12,512]{2,1,0:T(8,128)S(1)}, u32[]{:S(2)}, u32[]{:S(2)}) async-start(f32[8,12,512]{2,1,0:T(8,128)} %broadcast_in_dim.34), calls=%async_computation.8 | async-start | bytes 524288 | tf_op jit(solution)/shard_map/all_to_all | solution.py:1030
  324.8 27.5 %collective-permute-start.30 = (bf16[8,448,256]{2,1,0:T(8,128)(2,1)}, bf16[8,448,256]{2,1,0:T(8,128)(2,1)}, u32[]{:S(2)}, u32[]{:S(2)}) collective-permute-start(bf16[8,448,256]{2,1,0:T(8,128)(2,1)} %copy-done.128), channel_id=1, source_target_pairs={{0,2},{2,0},{4,6},{6,4},{8,10},{10,8},{12,14},{14,12},{16,18},{18,... | collective-permute-start | bytes 5505032 | tf_op jit(solution)/shard_map/ppermute | solution.py:996
  326.6 21.8 %collective-permute-start.29 = (bf16[4,192,256]{2,1,0:T(8,128)(2,1)}, bf16[4,192,256]{2,1,0:T(8,128)(2,1)}, u32[]{:S(2)}, u32[]{:S(2)}) collective-permute-start(bf16[4,192,256]{2,1,0:T(8,128)(2,1)} %slice.95), channel_id=1, source_target_pairs={{0,4},{2,6},{4,0},{6,2},{8,12},{10,14},{12,8},{14,10},{16,20},{18,... | collective-permute-start | bytes 1179656 | tf_op jit(solution)/shard_map/ppermute | solution.py:996
  330.4 19.9 %collective-permute-start.28 = (bf16[2,416,256]{2,1,0:T(8,128)(2,1)}, bf16[2,416,256]{2,1,0:T(8,128)(2,1)}, u32[]{:S(2)}, u32[]{:S(2)}) collective-permute-start(bf16[2,416,256]{2,1,0:T(8,128)(2,1)} %slice.93), channel_id=1, source_target_pairs={{0,8},{2,10},{4,12},{6,14},{8,0},{10,2},{12,4},{14,6},{16,24},{18,... | collective-permute-start | bytes 1277960 | tf_op jit(solution)/shard_map/ppermute | solution.py:996
  339.3 3.2 collective-permute-start.27
  344.2 11.3 %all-to-all-start.9 = ((f32[8,4,512]{2,1,0:T(4,128)}), f32[8,4,512]{2,1,0:T(4,128)}, u32[]{:S(2)}, u32[]{:S(2)}) async-start(f32[8,4,512]{2,1,0:T(4,128)} %broadcast_in_dim.35), calls=%async_computation.9 | async-start | bytes 131072 | tf_op jit(solution)/shard_map/all_to_all | solution.py:1030
  355.5 25.3 %collective-permute-start.31 = (bf16[8,288,256]{2,1,0:T(8,128)(2,1)}, bf16[8,288,256]{2,1,0:T(8,128)(2,1)}, u32[]{:S(2)}, u32[]{:S(2)}) collective-permute-start(bf16[8,288,256]{2,1,0:T(8,128)(2,1)} %copy-done.130), channel_id=1, source_target_pairs={{0,2},{2,0},{4,6},{6,4},{8,10},{10,8},{12,14},{14,12},{16,18},{18,... | collective-permute-start | bytes 3538952 | tf_op jit(solution)/shard_map/ppermute | solution.py:996
  358.2 25.0 %collective-permute-start.39 = (bf16[4,448,256]{2,1,0:T(8,128)(2,1)}, bf16[4,448,256]{2,1,0:T(8,128)(2,1)}, u32[]{:S(2)}, u32[]{:S(2)}) collective-permute-start(bf16[4,448,256]{2,1,0:T(8,128)(2,1)} %slice.109), channel_id=1, source_target_pairs={{0,4},{2,6},{4,0},{6,2},{8,12},{10,14},{12,8},{14,10},{16,20},{18,... | collective-permute-start | bytes 2752520 | tf_op jit(solution)/shard_map/ppermute | solution.py:996
  362.4 20.8 %collective-permute-start.42 = (bf16[2,192,256]{2,1,0:T(8,128)(2,1)S(1)}, bf16[2,192,256]{2,1,0:T(8,128)(2,1)S(1)}, u32[]{:S(2)}, u32[]{:S(2)}) collective-permute-start(bf16[2,192,256]{2,1,0:T(8,128)(2,1)S(1)} %slice.115), channel_id=1, source_target_pairs={{0,8},{2,10},{4,12},{6,14},{8,0},{10,2},{12,4},{14,6},{16,24},{18,... | collective-permute-start | bytes 589832 | tf_op jit(solution)/shard_map/ppermute | solution.py:996
  365.0 49.9 %collective-permute-start.44 = (bf16[1,416,256]{2,1,0:T(8,128)(2,1)S(1)}, bf16[1,416,256]{2,1,0:T(8,128)(2,1)S(1)}, u32[]{:S(2)}, u32[]{:S(2)}) collective-permute-start(bf16[1,416,256]{2,1,0:T(8,128)(2,1)S(1)} %get-tuple-element.314), channel_id=1, source_target_pairs={{0,16},{2,18},{4,20},{6,22},{8,24},{10,26},{12,28},{14,30},{16,0},... | collective-permute-start | bytes 638984 | tf_op jit(solution)/shard_map/ppermute | solution.py:996
  373.9 12.6 %collective-permute-start.33 = (bf16[8,64,256]{2,1,0:T(8,128)(2,1)S(1)}, bf16[8,64,256]{2,1,0:T(8,128)(2,1)S(1)}, u32[]{:S(2)}, u32[]{:S(2)}) collective-permute-start(bf16[8,64,256]{2,1,0:T(8,128)(2,1)S(1)} %get-tuple-element.276), channel_id=1, source_target_pairs={{0,2},{2,0},{4,6},{6,4},{8,10},{10,8},{12,14},{14,12},{16,18},{18,... | collective-permute-start | bytes 786440 | tf_op jit(solution)/shard_map/ppermute | solution.py:996
  382.6 15.8 %collective-permute-start.32 = (bf16[4,288,256]{2,1,0:T(8,128)(2,1)S(1)}, bf16[4,288,256]{2,1,0:T(8,128)(2,1)S(1)}, u32[]{:S(2)}, u32[]{:S(2)}) collective-permute-start(bf16[4,288,256]{2,1,0:T(8,128)(2,1)S(1)} %slice.121), channel_id=1, source_target_pairs={{0,4},{2,6},{4,0},{6,2},{8,12},{10,14},{12,8},{14,10},{16,20},{18,... | collective-permute-start | bytes 1769480 | tf_op jit(solution)/shard_map/ppermute | solution.py:996
  384.6 14.8 %collective-permute-start.40 = (bf16[2,448,256]{2,1,0:T(8,128)(2,1)S(1)}, bf16[2,448,256]{2,1,0:T(8,128)(2,1)S(1)}, u32[]{:S(2)}, u32[]{:S(2)}) collective-permute-start(bf16[2,448,256]{2,1,0:T(8,128)(2,1)S(1)} %slice.129), channel_id=1, source_target_pairs={{0,8},{2,10},{4,12},{6,14},{8,0},{10,2},{12,4},{14,6},{16,24},{18,... | collective-permute-start | bytes 1376264 | tf_op jit(solution)/shard_map/ppermute | solution.py:996
  385.2 30.4 %collective-permute-start.43 = (bf16[1,192,256]{2,1,0:T(8,128)(2,1)S(1)}, bf16[1,192,256]{2,1,0:T(8,128)(2,1)S(1)}, u32[]{:S(2)}, u32[]{:S(2)}) collective-permute-start(bf16[1,192,256]{2,1,0:T(8,128)(2,1)S(1)} %get-tuple-element.318), channel_id=1, source_target_pairs={{0,16},{2,18},{4,20},{6,22},{8,24},{10,26},{12,28},{14,30},{16,0},... | collective-permute-start | bytes 294920 | tf_op jit(solution)/shard_map/ppermute | solution.py:996
  398.5 5.2 %collective-permute-start.34 = (bf16[4,64,256]{2,1,0:T(8,128)(2,1)S(1)}, bf16[4,64,256]{2,1,0:T(8,128)(2,1)S(1)}, u32[]{:S(2)}, u32[]{:S(2)}) collective-permute-start(bf16[4,64,256]{2,1,0:T(8,128)(2,1)S(1)} %slice.99), channel_id=1, source_target_pairs={{0,4},{2,6},{4,0},{6,2},{8,12},{10,14},{12,8},{14,10},{16,20},{18,... | collective-permute-start | bytes 393224 | tf_op jit(solution)/shard_map/ppermute | solution.py:996
  399.5 12.3 %collective-permute-start.37 = (bf16[2,288,256]{2,1,0:T(8,128)(2,1)S(1)}, bf16[2,288,256]{2,1,0:T(8,128)(2,1)S(1)}, u32[]{:S(2)}, u32[]{:S(2)}) collective-permute-start(bf16[2,288,256]{2,1,0:T(8,128)(2,1)S(1)} %slice.105), channel_id=1, source_target_pairs={{0,8},{2,10},{4,12},{6,14},{8,0},{10,2},{12,4},{14,6},{16,24},{18,... | collective-permute-start | bytes 884744 | tf_op jit(solution)/shard_map/ppermute | solution.py:996
  403.7 8.1 %collective-permute-start.35 = (bf16[2,64,256]{2,1,0:T(8,128)(2,1)S(1)}, bf16[2,64,256]{2,1,0:T(8,128)(2,1)S(1)}, u32[]{:S(2)}, u32[]{:S(2)}) collective-permute-start(bf16[2,64,256]{2,1,0:T(8,128)(2,1)S(1)} %slice.123), channel_id=1, source_target_pairs={{0,8},{2,10},{4,12},{6,14},{8,0},{10,2},{12,4},{14,6},{16,24},{18,... | collective-permute-start | bytes 196616 | tf_op jit(solution)/shard_map/ppermute | solution.py:996
  404.3 17.5 %collective-permute-start.41 = (bf16[1,448,256]{2,1,0:T(8,128)(2,1)S(1)}, bf16[1,448,256]{2,1,0:T(8,128)(2,1)S(1)}, u32[]{:S(2)}, u32[]{:S(2)}) collective-permute-start(bf16[1,448,256]{2,1,0:T(8,128)(2,1)S(1)} %get-tuple-element.312), channel_id=1, source_target_pairs={{0,16},{2,18},{4,20},{6,22},{8,24},{10,26},{12,28},{14,30},{16,0},... | collective-permute-start | bytes 688136 | tf_op jit(solution)/shard_map/ppermute | solution.py:996
  411.9 12.7 %collective-permute-start.38 = (bf16[1,288,256]{2,1,0:T(8,128)(2,1)S(1)}, bf16[1,288,256]{2,1,0:T(8,128)(2,1)S(1)}, u32[]{:S(2)}, u32[]{:S(2)}) collective-permute-start(bf16[1,288,256]{2,1,0:T(8,128)(2,1)S(1)} %get-tuple-element.316), channel_id=1, source_target_pairs={{0,16},{2,18},{4,20},{6,22},{8,24},{10,26},{12,28},{14,30},{16,0},... | collective-permute-start | bytes 442376 | tf_op jit(solution)/shard_map/ppermute | solution.py:996
  412.0 12.0 %collective-permute-start.36 = (bf16[1,64,256]{2,1,0:T(8,128)(2,1)S(1)}, bf16[1,64,256]{2,1,0:T(8,128)(2,1)S(1)}, u32[]{:S(2)}, u32[]{:S(2)}) collective-permute-start(bf16[1,64,256]{2,1,0:T(8,128)(2,1)S(1)} %get-tuple-element.320), channel_id=1, source_target_pairs={{0,16},{2,18},{4,20},{6,22},{8,24},{10,26},{12,28},{14,30},{16,0},... | collective-permute-start | bytes 98312 | tf_op jit(solution)/shard_map/ppermute | solution.py:996
  (151 other events, 867.1 us)

commit v2 on v1

--- a/solution.py
+++ b/solution.py
@@ -13,7 +13,7 @@
 F32 = jnp.float32
 B = 4
 POS = 56
-LIMIT = 24
+LIMIT = 14
 M = B * POS
 HALF = 112
 HROWS = B * HALF
@@ -148,6 +148,10 @@
     lax.fori_loop(0, count, lambda c, _: (body(c), 0)[1], 0)
 
 
+def loop_from(first, last, body):
+    lax.fori_loop(first, last, lambda c, _: (body(c), 0)[1], 0)
+
+
 def copy_all(pairs, sems):
     copies = [pltpu.make_async_copy(s, d, sems.at[k]) for k, (s, d) in enumerate(pairs)]
     for c in copies:
@@ -168,7 +172,7 @@
     return (p & 1) * 8 + (p & 2) * 2 + (p & 4) // 2 + (p & 8) // 8
 
 
-def setup_kernel(exact, crop, micro, fs, isc, keep, keep1, keep_half):
+def setup_kernel(exact, crop, micro, fs, isc, keep, keep1, keep_half, sh, perm):
     n = lax.axis_index("narrow").astype(jnp.int32)
     w = lax.axis_index("wide").astype(jnp.int32)
     isc[NARROW] = n
@@ -205,12 +209,37 @@
         for k in range(4):
             keep1[k, b * POS : (b + 1) * POS, :] = inside(2 * i8 + k // 2, 2 * j7 + k % 2, side_in)
         keep_half[b * HALF : (b + 1) * HALF, :] = inside(r8, c14, side_in)
-
-
-def one_half_kernel(fs, x, keep, w1, st):
+    place = lax.broadcasted_iota(jnp.int32, (POS, M), 1)
+    it = lax.broadcasted_iota(jnp.int32, (POS, M), 0)
+    for t in range(9):
+        di, dj = t // 3 - 1, t % 3 - 1
+        i, j = (it & 7) + di, (it >> 3) + dj
+        fits = (i >= 0) & (i < 8) & (j >= 0) & (j < 7)
+        sh[t] = low(jnp.concatenate([
+            jnp.where(fits & (place == b * POS + j * 8 + i), 1.0, 0.0) for b in range(B)
+        ], axis=0))
+    place = lax.broadcasted_iota(jnp.int32, (POS, HALF), 1)
+    it = lax.broadcasted_iota(jnp.int32, (POS, HALF), 0)
+    for half in range(2):
+        planes = []
+        for k in range(4):
+            r, c = 2 * (it & 7) + k // 2, 2 * (it >> 3) + k % 2
+            planes.append(
+                jnp.where(((r >> 3) == half) & (place == c * 8 + (r & 7)), 1.0, 0.0)
+            )
+        perm[half] = low(jnp.concatenate(planes, axis=0))
+
+
+def one_half_kernel(fs, px, keep, w1_far, st, x, w1, flat, sems):
+    copies = copy_all([(px, x), (w1_far, w1)], sems)
+    copies[0].wait()
+    for b in range(B):
+        flat[b * HALF : (b + 1) * HALF, :] = x[b]
+    copies[1].wait()
+
     def body(c):
         sl = cols(c)
-        v = mm(x[...], w1[:, sl]) * keep[...]
+        v = mm(flat[...], w1[:, sl]) * keep[...]
         sums = [jnp.sum(v[b * HALF : (b + 1) * HALF], axis=0, keepdims=True) for b in range(B)]
         v2 = v * v
         sq = [jnp.sum(v2[b * HALF : (b + 1) * HALF], axis=0, keepdims=True) for b in range(B)]
@@ -224,18 +253,16 @@
 
 def stage_two_kernel(
     fs, isc, own, other, part, part_other, perm, keep1, keep, w1, ws, gb, sh,
-    xp, strided, x1, col, pre2, st, tot1, xs, tmp, hid, tot, sems,
+    xp, strided, x1, col, pre2, st, tot1, tmp, hid, tot,
 ):
     n = isc[NARROW]
-    copies = copy_all([(own, xs.at[n]), (other, xs.at[1 - n])], sems)
     tot[...] = part[...] + part_other[...]
     tot1[...] = tot[...]
-    wait_all(copies)
 
     def permute(c):
         sl = cols(c)
         for b in range(B):
-            r = mm(perm[0], xs[0, b, :, sl]) + mm(perm[1], xs[1, b, :, sl])
+            r = mm(perm[n], own[b, :, sl]) + mm(perm[1 - n], other[b, :, sl])
             for k in range(4):
                 tmp[k, b * POS : (b + 1) * POS, :] = r[k * POS : (k + 1) * POS]
         for k in range(4):
@@ -271,14 +298,25 @@
     loop(2, second)
 
 
-def project_kernel(fs, x, keep, wp, prep, st):
+def project_kernel(fs, x, keep, wp_far, w3_far, prep, st, w3, wp, sems):
+    copies = []
+    for c in range(4):
+        sl = slice(c * 512, (c + 1) * 512)
+        copies.append(pltpu.make_async_copy(wp_far.at[:, sl], wp.at[:, sl], sems.at[c]))
+    copies.append(pltpu.make_async_copy(w3_far, w3, sems.at[4]))
+    for c in copies:
+        c.start()
+
     def body(c):
         sl = cols(c)
         v = mm(x[...], wp[:, sl])
         prep[:, sl] = v
         put(st, 0, stat_rows(v, keep[...], fs), sl)
 
-    loop(8, body)
+    for c in range(4):
+        copies[c].wait()
+        loop_from(2 * c, 2 * c + 2, body)
+    copies[4].wait()
 
 
 def stage_three_kernel(fs, parts, pre2, stp, keep, w3, gb, h2, pre3, st, tot2, tot):
@@ -299,20 +337,24 @@
     loop(8, body)
 
 
-def stage_four_kernel(
-    fs, isc, parts, pre3, prep, keep, vec, sqb, sq, ex, w4own, r1, r2,
-    lows, pre4, st, tot3, gate, sp, pooled, squares, unit, short, w4, acc, tot, sems,
-):
+def fetch_four_kernel(isc, own, r1, r2, w4, sems):
     n, core = isc[NARROW], isc[CORE]
     away = (1 - n) * 1024
-    copies = copy_all(
+    wait_all(copy_all(
         [
-            (w4own, w4.at[at_rows(n * 1024, 1024)]),
+            (own, w4.at[at_rows(n * 1024, 1024)]),
             (r1, w4.at[at_rows(away + core * 512, 512)]),
             (r2, w4.at[at_rows(away + (1 - core) * 512, 512)]),
         ],
         sems,
-    )
+    ))
+
+
+def stage_four_kernel(
+    fs, parts, pre3, prep, keep, vec, sqb, sq_far, ex_far, w4,
+    lows, pre4, st, tot3, gate, sp, pooled, squares, unit, short, acc, tot, sq, ex, sems,
+):
+    copies = copy_all([(sq_far, sq), (ex_far, ex)], sems)
     add_parts(parts, tot)
     tot3[...] = tot[...]
     pooled[...] = jnp.zeros((8, 2048), F32)
@@ -329,12 +371,12 @@
         short[:, sl] = s
 
     loop(8, units)
+    wait_all(copies)
     sp[...] = dot3(pooled[...], sq[...]) + sqb[0:1, :]
     squeezed = sp[...] * sigmoid(sp[...])
     gate[...] = sigmoid(dot3(squeezed, ex[...]) + vec[4:5, :])
     squares[...] = jnp.zeros((8, 256), F32)
     acc[...] = jnp.zeros((M, 512), F32)
-    wait_all(copies)
 
     def streams(c):
         sl = cols(c)
@@ -353,22 +395,20 @@
     put(st, 0, stat_rows(acc[...], keep[...], fs), slice(0, 512))
 
 
-def w5_copies(isc, own, r1, r2, w5):
+def fetch_five_kernel(isc, own, r1, r2, w5, vaway, sems):
     n, core = isc[NARROW], isc[CORE]
-    return [
+    wait_all(copy_all([
+        (r1.at[VEC_AT:PACK_ROWS], vaway),
         (own, w5.at[n]),
         (r1.at[0:2304], w5.at[1 - n, at_rows(core * 2304, 2304)]),
         (r2.at[0:2304], w5.at[1 - n, at_rows((1 - core) * 2304, 2304)]),
-    ]
+    ], sems))
 
 
 def stage_five_kernel(
-    fs, isc, parts, pre4, keep, gb, sh, vown, w5own, r1, r2,
-    col, pre5, st, tot4, gain5, vec2, w5, tot, vaway, sems,
+    fs, isc, parts, pre4, keep, gb, sh, vown, vaway, w5, col, pre5, st, tot4, gain5, vec2, tot,
 ):
     n = isc[NARROW]
-    pairs = w5_copies(isc, w5own, r1, r2, w5) + [(r1.at[VEC_AT:PACK_ROWS], vaway)]
-    copies = copy_all(pairs, sems)
     add_parts(parts, tot)
     tot4[...] = tot[...]
     mean, scale = coefs(tot, 0, slice(0, 512), fs, INV_OUT)
@@ -376,7 +416,6 @@
     h = low(o * sigmoid(o) * keep[...])
     for t in range(9):
         col[t] = h if t == 4 else low(mm(sh[t], h))
-    wait_all(copies)
     for side, v in ((n, f32(vown[...])), (1 - n, f32(vaway[...]))):
         for k in range(2):
             gain5[k : k + 1, cols(side)] = v[k : k + 1]
@@ -395,7 +434,7 @@
     loop(2, body)
 
 
-def w6_copies(isc, own, r1, r2, w6):
+def fetch_six_kernel(isc, own, r1, r2, w6, sems):
     n, core = isc[NARROW], isc[CORE]
     pairs = [(own, w6.at[at_rows(n * 256, 256)])]
     for r, h in ((r1, core), (r2, 1 - core)):
@@ -406,19 +445,17 @@
                     w6.at[at_rows((1 - n) * 256 + h * 128, 128), c * 256 : (c + 1) * 256],
                 )
             )
-    return pairs
+    wait_all(copy_all(pairs, sems))
 
 
 def stage_six_kernel(
-    fs, isc, parts, pre5, keep, gain5, w6own, r1, r2, h5, pre6, st, tot5, w6, tot, sems
+    fs, parts, pre5, keep, gain5, w6, h5, pre6, st, tot5, tot
 ):
-    copies = copy_all(w6_copies(isc, w6own, r1, r2, w6), sems)
     add_parts(parts, tot)
     tot5[...] = tot[...]
     mean, scale = coefs(tot, 0, slice(0, 512), fs, INV_OUT)
     o = (pre5[...] - mean) * scale * gain5[0:1, :] + gain5[1:2, :]
     h5[...] = low(o * sigmoid(o) * keep[...])
-    wait_all(copies)
 
     def body(c):
         sl = cols(c)
@@ -429,11 +466,7 @@
     loop(8, body)
 
 
-def turn_kernel(
-    fs, isc, parts, pre6, keep, lows, vec, sqb, sq1s, sqown, exown, r1, r2, ogown, ogother,
-    result, dj2, pay, extra, tot6, gate, dp, pooled, de, ds, squeezed,
-    unit, og, res, sq, ex, tot, sp, sems,
-):
+def fetch_turn_kernel(isc, sqown, exown, r1, r2, ogown, ogother, sq, ex, og, sems):
     n, core = isc[NARROW], isc[CORE]
     pairs = [
         (sqown, sq.at[at_rows(n * 1024, 1024)]),
@@ -456,7 +489,14 @@
                     ex.at[1 - n, at_rows(h * 64, 64), c * 256 : (c + 1) * 256],
                 )
             )
-    copies = copy_all(pairs, sems)
+    wait_all(copy_all(pairs, sems))
+
+
+def turn_kernel(
+    fs, isc, parts, pre6, keep, lows, vec, sqb, sq1s, sq, ex, og,
+    result, dj2, pay, extra, tot6, gate, dp, pooled, de, ds, squeezed, unit, res, tot, sp,
+):
+    n = isc[NARROW]
     add_parts(parts, tot)
     tot6[...] = tot[...]
     pooled[...] = jnp.zeros((8, 2048), F32)
@@ -471,7 +511,6 @@
             pooled[b : b + 1, sl] = r * fs[CELLS + b]
 
     loop(8, units)
-    wait_all(copies)
     sp[...] = dot3(pooled[...], sq[...]) + sqb[1:2, :]
     squeezed[...] = sp[...] * sigmoid(sp[...])
     for h in range(2):
@@ -537,14 +576,12 @@
 
 
 def back_six_kernel(
-    fs, isc, parts, tot6, pre6, dj2, gate, dp, pre5, tot5, extra, keep, vec, gain5, w6own, r1, r2,
-    d6, do5, st, dgain, dbias, w6, tot, acc, sems,
+    fs, isc, parts, tot6, pre6, dj2, gate, dp, pre5, tot5, extra, keep, vec, gain5, w6,
+    d6, do5, st, dgain, dbias, tot, acc,
 ):
-    copies = copy_all(w6_copies(isc, w6own, r1, r2, w6), sems)
     add_parts(parts, tot)
     half_gain(tot, isc[NARROW], dgain, dbias)
     acc[...] = jnp.zeros((M, 512), F32)
-    wait_all(copies)
 
     def body(c):
         sl = cols(c)
@@ -570,11 +607,10 @@
 
 
 def back_five_kernel(
-    fs, isc, parts, tot5, pre5, do5, pre4, tot4, keep, gb, gain5, sh, w5own, r1, r2,
-    d5, do4, st, dgain, dbias, debias, dsbias, norms, w5, tot, sems,
+    fs, isc, parts, tot5, pre5, do5, pre4, tot4, keep, gb, gain5, sh, w5,
+    d5, do4, st, dgain, dbias, debias, dsbias, norms, tot,
 ):
     n = isc[NARROW]
-    copies = copy_all(w5_copies(isc, w5own, r1, r2, w5), sems)
     add_parts(parts, tot)
     half_gain(tot, n, dgain, dbias)
     excite = jnp.concatenate([tot[pl.ds(4 + 2 * n, 1), :], tot[pl.ds(5 + 2 * n, 1), :]], axis=1)
@@ -589,7 +625,6 @@
     a, bb = means(tot, 0, sl, fs, INV_OUT)
     d = low((do5[...] - a - x * bb) * (scale * gain5[0:1, :]) * keep[...])
     d5[...] = d
-    wait_all(copies)
     acc = 0.0
     for t in range(9):
         dc = d if t == 4 else low(mm(sh[8 - t], d))
@@ -604,20 +639,10 @@
 
 
 def back_four_kernel(
-    fs, isc, parts, tot4, pre4, do4, dj2, tot3, pre3, prep, gate, sp, keep, gb, vec, sq, ex,
-    w4own, r1, r2,
-    d4, dj1, st, dgain, dbias, dp, de, ds, bias, w4, tot, sems,
+    fs, parts, tot4, pre4, do4, dj2, tot3, pre3, prep, gate, sp, keep, gb, vec, sq_far, ex_far, w4,
+    d4, dj1, st, dgain, dbias, dp, de, ds, bias, tot, sq, ex, sems,
 ):
-    n, core = isc[NARROW], isc[CORE]
-    away = (1 - n) * 1024
-    copies = copy_all(
-        [
-            (w4own, w4.at[at_rows(n * 1024, 1024)]),
-            (r1, w4.at[at_rows(away + core * 512, 512)]),
-            (r2, w4.at[at_rows(away + (1 - core) * 512, 512)]),
-        ],
-        sems,
-    )
+    copies = copy_all([(sq_far, sq), (ex_far, ex)], sems)
     add_parts(parts, tot)
     whole_gain(tot, 0, dgain, dbias)
     de[...] = jnp.zeros((8, 2048), F32)
@@ -625,7 +650,6 @@
     x = (pre4[...] - mean) * scale
     a, bb = means(tot, 0, slice(0, 512), fs, INV_OUT)
     d4[...] = low((do4[...] - a - x * bb) * (scale * gb[4:5, :]) * keep[...])
-    wait_all(copies)
 
     def joins(c):
         sl = cols(c)
@@ -641,6 +665,7 @@
             de[b : b + 1, sl] = r
 
     loop(8, joins)
+    wait_all(copies)
     de[...] = de[...] * gate[...] * (1.0 - gate[...])
     ds[...] = dot3_nt(de[...], ex[...]) * slope(sp[...])
     dp[...] = dot3_nt(ds[...], sq[...])
@@ -704,6 +729,10 @@
     do2[...] = d
     put(st, 0, back_rows(d, x, fs), sl)
     st[4:12, :] = bias[...]
+
+
+def fetch_two_kernel(far, ws, sems):
+    wait_all(copy_all([(far.at[3 * k : 3 * k + 3], ws.at[3 * k : 3 * k + 3]) for k in range(3)], sems))
 
 
 def back_two_kernel(
@@ -777,9 +806,26 @@
     deal(isc, full, 64, gkeep, gsend, 0)
 
 
-def image_kernel(own, pick_own, spread, d1, dproj, keep, w1, wp, out, dc, cc):
+def image_kernel(isc, perm, d1, dproj, keep, w1, wp_far, out, dc, cc, pick_own, spread, wp, sems):
+    n = isc[NARROW]
+    copies = [
+        pltpu.make_async_copy(wp_far.at[cut], wp.at[cut], sems.at[k])
+        for k, cut in enumerate(slice(256 * k, 256 * (k + 1)) for k in range(4))
+    ]
+    for c in copies:
+        c.start()
     for b in range(B):
-        dc[b * HALF : (b + 1) * HALF, :] = low(mm(own[...], d1[b]))
+        dc[b * HALF : (b + 1) * HALF, :] = low(mm_tn(perm[n], d1[b]))
+        place = lax.broadcasted_iota(jnp.int32, (32, M), 1)
+        it = lax.broadcasted_iota(jnp.int32, (32, M), 0)
+        pick_own[b * 32 : (b + 1) * 32, :] = low(jnp.where(
+            (place == b * POS + (it >> 2) * 8 + n * 4 + (it & 3)) & (it < 28), 1.0, 0.0
+        ))
+        place = lax.broadcasted_iota(jnp.int32, (HALF, 128), 1)
+        it = lax.broadcasted_iota(jnp.int32, (HALF, 128), 0)
+        spread[b * HALF : (b + 1) * HALF, :] = low(jnp.where(
+            ((it & 9) == 0) & (place == b * 32 + (it >> 4) * 4 + ((it & 7) >> 1)), 1.0, 0.0
+        ))
     cc[...] = low(mm(pick_own[...], dproj[...]))
 
     def body(c):
@@ -788,7 +834,9 @@
         v = mm_nt(dc[...], w1[sl, :]) + mm(spread[...], hi) + mm(spread[...], lo)
         out[:, sl] = v * keep[...]
 
-    loop(4, body)
+    for c in range(4):
+        copies[c].wait()
+        body(c)
 
 
 def grads_a_kernel(isc, h5, d6, col4, d5, gkeep, gsend, wider, full):
@@ -896,54 +944,50 @@
     spatial1[...] = f32(a[0]) + f32(b[0])
 
 
-REST = PACK_ROWS - W6_AT
-
-
-def pack_kernel(
-    isc, w5, w4, w6, ex, sq,
-    g1, b1, g2, b2, g4, b4, g3, b3, gp, bp, eb1, sqb1, sqb2, g5, b5, g6, b6, eb2,
-    out, w4_half, gb, vec1, sqb, vown, rest, rows, sems,
-):
+VECTORS = (512,) * 6 + (2048,) * 5 + (128,) * 2 + (256,) * 2 + (1024,) * 3
+
+
+def pack_kernel(isc, w5, w4, w6, ex, sq, ws_far, *refs):
+    far, refs = refs[:18], refs[18:]
+    out, w4_half, gb, vec1, sqb, vown, ws, w6v, exv, sqv, rows = refs[:11]
+    vecs, sems = refs[11:29], refs[29]
     core = isc[CORE]
-    copies = copy_all(
-        [
-            (w4.at[at_rows(core * 512, 512)], w4_half),
-            (w5.at[at_rows(core * 2304, 2304)], out.at[0:W6_AT]),
-        ],
-        sems,
-    )
+    pairs = [(f, v) for f, v in zip(far, vecs)] + [
+        (w6.at[at_rows(core * 128, 128)], w6v),
+        (ex.at[at_rows(core * 64, 64)], exv),
+        (sq.at[at_rows(core * 512, 512)], sqv),
+        (w4.at[at_rows(core * 512, 512)], w4_half),
+        (w5.at[at_rows(core * 2304, 2304)], out.at[0:W6_AT]),
+        (ws_far, ws),
+    ]
+    copies = copy_all(pairs, sems)
+    wait_all(copies[:21])
 
     def row(v):
         return f32(v[...]).reshape(1, v.shape[0])
 
-    for k, v in enumerate((g1, b1, g2, b2, g4, b4)):
-        gb[k : k + 1, :] = row(v)
-    for k, v in enumerate((g3, b3, gp, bp, eb1)):
-        vec1[k : k + 1, :] = row(v)
-    for k, v in enumerate((sqb1, sqb2)):
-        sqb[k : k + 1, :] = row(v)
+    for k in range(6):
+        gb[k : k + 1, :] = row(vecs[k])
+    for k in range(5):
+        vec1[k : k + 1, :] = row(vecs[6 + k])
+    for k in range(2):
+        sqb[k : k + 1, :] = row(vecs[11 + k])
     rows[...] = jnp.zeros((16, 256), F32)
     at = 0
-    for v in (g5, b5, g6, b6, eb2):
+    for v in vecs[13:18]:
         r = row(v)
         for c in range(v.shape[0] // 256):
             rows[at : at + 1, :] = r[:, c * 256 : (c + 1) * 256]
             at += 1
     vown[...] = low(rows[...])
     for c in range(8):
-        rest[c * 128 : (c + 1) * 128, :] = w6[at_rows(core * 128, 128), c * 256 : (c + 1) * 256]
+        out[W6_AT + c * 128 : W6_AT + (c + 1) * 128, :] = w6v[:, c * 256 : (c + 1) * 256]
     for c in range(4):
-        start = EX_AT - W6_AT + c * 64
-        rest[start : start + 64, :] = ex[at_rows(core * 64, 64), c * 256 : (c + 1) * 256]
+        out[EX_AT + c * 64 : EX_AT + (c + 1) * 64, :] = exv[:, c * 256 : (c + 1) * 256]
     for k in range(2):
-        rest[SQ_AT - W6_AT : SQ_AT - W6_AT + 256, k * 128 : (k + 1) * 128] = sq[
-            at_rows(core * 512 + k * 256, 256), :
-        ]
-    rest[VEC_AT - W6_AT : REST, :] = vown[...]
-    last = pltpu.make_async_copy(rest, out.at[W6_AT:PACK_ROWS], sems.at[2])
-    last.start()
-    last.wait()
-    wait_all(copies)
+        out[SQ_AT : SQ_AT + 256, k * 128 : (k + 1) * 128] = sqv[k * 256 : (k + 1) * 256, :]
+    out[VEC_AT:PACK_ROWS, :] = vown[...]
+    wait_all(copies[21:])
 
 
 def call(body, outs, args, scratch=(), flops=1e8, size=5e6, name=None, vmem=LIMIT):
@@ -954,9 +998,9 @@
         values.append(v)
     return pl.pallas_call(
         body,
-        out_shape=tuple(jax.ShapeDtypeStruct(o[0], o[1]) for o in outs),
+        out_shape=tuple(o if hasattr(o, "memory_space") else jax.ShapeDtypeStruct(o[0], o[1]) for o in outs),
         in_specs=specs,
-        out_specs=tuple(o[2] if len(o) > 2 else VMEM for o in outs),
+        out_specs=tuple(o[2] if isinstance(o, tuple) and len(o) > 2 else pl.BlockSpec(memory_space=getattr(o, "memory_space", pltpu.VMEM)) for o in outs),
         scratch_shapes=list(scratch),
         compiler_params=pltpu.CompilerParams(vmem_limit_bytes=vmem * 2**20),
         cost_estimate=pl.CostEstimate(
@@ -964,32 +1008,6 @@
         ),
         name=name,
     )(*values)
-
-
-def constants():
-    perm = np.zeros((2, M, HALF), np.float32)
-    for r in range(16):
-        for c in range(14):
-            place = (2 * (r % 2) + c % 2) * POS + (c // 2) * 8 + r // 2
-            perm[r // 8, place, c * 8 + r % 8] = 1
-    shift = np.zeros((9, M, M), np.float32)
-    for di in range(3):
-        for dj in range(3):
-            for b in range(B):
-                for i in range(8):
-                    for j in range(7):
-                        si, sj = i + di - 1, j + dj - 1
-                        if 0 <= si < 8 and 0 <= sj < 7:
-                            shift[3 * di + dj, b * POS + j * 8 + i, b * POS + sj * 8 + si] = 1
-    pick_own = np.zeros((2, HALF, M), np.float32)
-    spread = np.zeros((HROWS, HALF), np.float32)
-    for b in range(B):
-        for j in range(7):
-            for i in range(4):
-                for n in range(2):
-                    pick_own[n, b * 28 + j * 4 + i, b * POS + j * 8 + n * 4 + i] = 1
-                spread[b * HALF + 2 * j * 8 + 2 * i, b * 28 + j * 4 + i] = 1
-    return perm, shift, pick_own, spread
 
 
 def swap(v, axis, pairs):
@@ -1014,15 +1032,16 @@
     out_grad,
 ):
     wide = lax.axis_size("wide")
-    n = lax.axis_index("narrow")
     exact = wide == 16
     near = [(i, i ^ 1) for i in range(wide)]
     pair = [(0, 1), (1, 0)]
     groups = [list(range(k, wide, 2)) for k in range(2)]
     V = pltpu.VMEM
     D = pltpu.SemaphoreType.DMA
-    f = lambda *shape: (shape, F32)
-    h = lambda *shape: (shape, BF)
+    out = lambda *shape: (shape, F32)
+    f = lambda *shape: V(shape, F32)
+    h = lambda *shape: V(shape, BF)
+    far = lambda v: (ANY, pltpu.with_memory_space_constraint(v, pltpu.HBM))
 
     def across(x):
         x = x + swap(x, "wide", near)
@@ -1037,143 +1056,160 @@
             step *= 2
         return x[None]
 
-    perm_np, shift_np, pick_np, spread_np = constants()
-    perm, sh = jnp.asarray(perm_np, BF), jnp.asarray(shift_np, BF)
-
     own_px = images.transpose(0, 2, 1, 3).reshape(B, HALF, 1024)
     other_px = swap(own_px, "narrow", pair)
-
-    fs_, isc_, keep, keep1, keep_half = call(
+    ws_far = first_spatial.reshape(9, 512, 512)
+
+    fs_, isc_, keep, keep1, keep_half, sh, perm = call(
         functools.partial(setup_kernel, exact),
-        [((13,), F32, SMEM), ((18,), jnp.int32, SMEM), f(M, 1), f(4, M, 1), f(HROWS, 1)],
-        [(SMEM, crop), (SMEM, micro)], name="setup",
+        [
+            pltpu.SMEM((13,), F32), pltpu.SMEM((18,), jnp.int32), f(M, 1), f(4, M, 1), f(HROWS, 1),
+            h(9, M, M), h(2, M, HALF),
+        ],
+        [(SMEM, far(crop)[1]), (SMEM, far(micro)[1])], name="setup",
     )
     fs, isc = (SMEM, fs_), (SMEM, isc_)
-    st1 = call(
-        one_half_kernel, [f(4, 512)], [fs, own_px.reshape(HROWS, 1024), keep_half, first_reduce],
-        flops=5e8, name="one_half",
-    )[0]
-    part = jnp.sum(across(st1), axis=0)
-    part_other = swap(part, "narrow", pair)
+    st1, xown, w1 = call(
+        one_half_kernel, [f(4, 512), h(B, HALF, 1024), h(1024, 512)],
+        [fs, far(own_px), keep_half, far(first_reduce)],
+        [V((HROWS, 1024), BF), D((2,))], flops=5e8, name="one_half",
+    )
+    part = steps(st1)[0]
 
     w5_own = second_spatial.reshape(9 * 512, 256)
-    pack, w4_half, gb, vec1, sqb, vown = call(
+    vectors = [
+        first_reduce_gain, first_reduce_bias, first_spatial_gain, first_spatial_bias,
+        second_reduce_gain, second_reduce_bias, first_expand_gain, first_expand_bias,
+        first_project_gain, first_project_bias, first_excite_bias,
+        first_squeeze_bias, second_squeeze_bias,
+        second_spatial_gain, second_spatial_bias, second_expand_gain, second_expand_bias, second_excite_bias,
+    ]
+    pack, w4_half, gb, vec1, sqb, vown, ws = call(
         pack_kernel,
         [
-            ((PACK_ROWS, 256), BF, ANY), ((512, 512), BF, ANY), f(8, 512), f(8, 2048), f(8, 128), h(16, 256),
+            ((PACK_ROWS, 256), BF), ((512, 512), BF), f(8, 512), f(8, 2048), f(8, 128), h(16, 256),
+            h(9, 512, 512),
         ],
         [
-            (SMEM, after(isc_, st1)), (ANY, w5_own), (ANY, second_reduce), second_expand, second_excite, second_squeeze,
-            first_reduce_gain, first_reduce_bias, first_spatial_gain, first_spatial_bias,
-            second_reduce_gain, second_reduce_bias, first_expand_gain, first_expand_bias,
-            first_project_gain, first_project_bias, first_excite_bias,
-            first_squeeze_bias, second_squeeze_bias,
-            second_spatial_gain, second_spatial_bias, second_expand_gain, second_expand_bias, second_excite_bias,
-        ],
-        [V((REST, 256), BF), V((16, 256), F32), D((3,))],
-        size=1e7, name="pack",
-    )
+            (SMEM, after(isc_, st1)), far(w5_own), far(second_reduce), far(second_expand), far(second_excite),
+            far(second_squeeze), far(ws_far),
+        ] + [far(v) for v in vectors],
+        [V((128, 2048), BF), V((64, 1024), BF), V((512, 128), BF), V((16, 256), F32)]
+        + [V((size,), BF) for size in VECTORS] + [D((24,))],
+        size=2e7, name="pack",
+    )
+    part = after(part, gb)
+    part_other = swap(part, "narrow", pair)
     w4_r1 = swap(after(w4_half, other_px, part_other), "narrow", pair)
-    pk1 = swap(after(pack, other_px, part_other), "narrow", pair)
     og_own = out_grad.transpose(0, 2, 1, 3).reshape(M, 1024)
-    ws = first_spatial.reshape(9, 512, 512)
 
     xp, strided, x1, col1, pre2, st2, tot1 = call(
         stage_two_kernel,
         [h(4, M, 1024), h(M, 1024), f(4, M, 512), h(9, M, 512), f(M, 512), f(4, 512), f(4, 512)],
-        [
-            fs, isc, (ANY, own_px), (ANY, other_px), part, part_other, perm, keep1, keep,
-            first_reduce, ws, gb, sh,
-        ],
-        [V((2, B, HALF, 1024), BF), V((4, M, 256), F32), V((4, M, 512), BF), V((4, 512), F32), D((2,))],
+        [fs, isc, xown, other_px, part, part_other, perm, keep1, keep, w1, ws, gb, sh],
+        [V((4, M, 256), F32), V((4, M, 512), BF), V((4, 512), F32)],
         flops=4e9, size=2e7, name="stage_two",
     )
-    parts2 = across(st2)
+    parts2 = steps(st2)
     w4_r2 = swap(after(w4_r1, st2), "wide", near)
-    w4_refs = [(ANY, second_reduce), (ANY, w4_r1), (ANY, w4_r2)]
-    prep, stp = call(
-        project_kernel, [f(M, 2048), f(4, 2048)], [fs, after(strided, w4_r1), keep, first_project],
-        flops=1e9, size=8e6, name="project",
+    pk1 = swap(after(pack, w4_r1, st2), "narrow", pair)
+    prep, stp, w3 = call(
+        project_kernel, [f(M, 2048), f(4, 2048), h(512, 2048)],
+        [fs, after(strided, w4_r1), keep, far(first_project), far(first_expand)],
+        [V((1024, 2048), BF), D((5,))], flops=1e9, size=8e6, name="project",
     )
     h2, pre3, st3, tot2 = call(
         stage_three_kernel, [h(M, 512), f(M, 2048), f(8, 2048), f(4, 512)],
-        [fs, parts2, pre2, stp, keep, first_expand, gb], [V((4, 512), F32)],
+        [fs, parts2, pre2, stp, keep, w3, gb], [V((4, 512), F32)],
         flops=1e9, size=6e6, name="stage_three",
     )
     parts3 = steps(st3)
+    w4 = call(
+        fetch_four_kernel, [h(2048, 512)],
+        [(SMEM, after(isc_, st3)), far(second_reduce), far(w4_r1), far(w4_r2)], [D((3,))],
+        size=4e6, name="fetch_four",
+    )[0]
     lows, pre4, st4, tot3, gate1, sp1, pooled1, squares = call(
         stage_four_kernel,
         [
             h(M, 2048), f(M, 512), f(4, 512), f(8, 2048), f(8, 2048), f(8, 128), f(8, 2048), f(8, 256),
         ],
-        [fs, isc, parts3, pre3, prep, keep, vec1, sqb, first_squeeze, first_excite] + w4_refs,
-        [V((M, 2048), F32), V((M, 2048), F32), V((2048, 512), BF), V((M, 512), F32), V((8, 2048), F32), D((3,))],
+        [fs, parts3, pre3, prep, keep, vec1, sqb, far(first_squeeze), far(first_excite), w4],
+        [
+            V((M, 2048), F32), V((M, 2048), F32), V((M, 512), F32), V((8, 2048), F32),
+            V((2048, 128), BF), V((128, 2048), BF), D((2,)),
+        ],
         flops=1e9, size=1e7, name="stage_four",
     )
-    parts4 = across(st4)
+    parts4 = steps(st4)
     pk2 = swap(after(pk1, st4), "wide", near)
     og_other = swap(after(og_own, pk1, st4), "narrow", pair)
-    w5_refs = [(ANY, w5_own), (ANY, pk1), (ANY, pk2)]
-    w6_refs = [(ANY, second_expand), (ANY, pk1), (ANY, pk2)]
+    pk1, pk2 = far(pk1), far(pk2)
+    w5, vaway = call(
+        fetch_five_kernel, [h(2, 4608, 256), h(16, 256)],
+        [(SMEM, after(isc_, st4)), far(w5_own), pk1, pk2], [D((4,))], size=8e6, name="fetch_five",
+    )
     col4, pre5, st5, tot4, gain5, vec2 = call(
         stage_five_kernel,
         [h(9, M, 512), f(M, 512), f(4, 512), f(4, 512), f(2, 512), f(3, 2048)],
-        [fs, isc, parts4, pre4, keep, gb, sh, vown] + w5_refs,
-        [V((2, 4608, 256), BF), V((4, 512), F32), V((16, 256), BF), D((4,))],
+        [fs, isc, parts4, pre4, keep, gb, sh, vown, vaway, w5], [V((4, 512), F32)],
         flops=2e9, size=1e7, name="stage_five",
     )
-    parts5 = across(st5)
+    parts5 = steps(st5)
+    w6 = call(
+        fetch_six_kernel, [h(512, 2048)],
+        [(SMEM, after(isc_, st5)), far(second_expand), pk1, pk2], [D((17,))], size=4e6, name="fetch_six",
+    )[0]
     h5, pre6, st6, tot5 = call(
         stage_six_kernel, [h(M, 512), f(M, 2048), f(4, 2048), f(4, 512)],
-        [fs, isc, parts5, pre5, keep, gain5] + w6_refs,
-        [V((512, 2048), BF), V((4, 512), F32), D((17,))],
+        [fs, parts5, pre5, keep, gain5, w6], [V((4, 512), F32)],
         flops=1e9, size=6e6, name="stage_six",
     )
-    parts6 = across(st6)
+    parts6 = steps(st6)
+    sq, ex, og = call(
+        fetch_turn_kernel, [h(2048, 128), h(2, 128, 1024), h(2, M, 1024)],
+        [
+            (SMEM, after(isc_, st6)), far(second_squeeze), far(second_excite), pk1, pk2,
+            far(og_own), far(og_other),
+        ],
+        [D((16,))], size=4e6, name="fetch_turn",
+    )
     result, dj2, pay6, extra6, tot6, gate2, dp2, pooled2, de2, ds2, sq2 = call(
         turn_kernel,
         [
-            h(M, 1024), f(M, 2048), f(4, 2048), f(8, 512), f(4, 2048), f(8, 2048),
+            ((M, 1024), BF), f(M, 2048), f(4, 2048), f(8, 512), f(4, 2048), f(8, 2048),
             f(8, 2048), f(8, 2048), f(8, 2048), f(8, 128), f(8, 128),
         ],
-        [
-            fs, isc, parts6, pre6, keep, lows, vec2, sqb, squares,
-            (ANY, second_squeeze), (ANY, second_excite), (ANY, pk1), (ANY, pk2), (ANY, og_own), (ANY, og_other),
-        ],
-        [
-            V((M, 2048), F32), V((2, M, 1024), BF), V((2, M, 1024), BF), V((2048, 128), BF),
-            V((2, 128, 1024), BF), V((4, 2048), F32), V((8, 128), F32), D((16,)),
-        ],
+        [fs, isc, parts6, pre6, keep, lows, vec2, sqb, squares, sq, ex, og],
+        [V((M, 2048), F32), V((2, M, 1024), BF), V((4, 2048), F32), V((8, 128), F32)],
         flops=1e9, size=1e7, name="turn",
     )
     back6 = across(pay6)
     d6, do5, bt5, dgain6, dbias6 = call(
-        back_six_kernel, [h(M, 2048), f(M, 512), f(12, 512), f(1024), f(1024)],
-        [fs, isc, back6, tot6, pre6, dj2, gate2, dp2, pre5, tot5, extra6, keep, vec2, gain5] + w6_refs,
-        [V((512, 2048), BF), V((4, 2048), F32), V((M, 512), F32), D((17,))],
+        back_six_kernel, [h(M, 2048), f(M, 512), f(12, 512), out(1024), out(1024)],
+        [fs, isc, back6, tot6, pre6, dj2, gate2, dp2, pre5, tot5, extra6, keep, vec2, gain5, w6],
+        [V((4, 2048), F32), V((M, 512), F32)],
         flops=1e9, size=1e7, name="back_six",
     )
     back5 = across(bt5)
     d5, do4, bt4, dgain5, dbias5, debias2, dsbias2, norms = call(
         back_five_kernel,
-        [h(M, 512), f(M, 512), f(4, 512), f(256), f(256), f(1024), f(128), ((5,), F32, SMEM)],
-        [fs, isc, back5, tot5, pre5, do5, pre4, tot4, keep, gb, gain5, sh] + w5_refs,
-        [V((2, 4608, 256), BF), V((12, 512), F32), D((3,))],
+        [h(M, 512), f(M, 512), f(4, 512), out(256), out(256), out(1024), out(128), ((5,), F32, SMEM)],
+        [fs, isc, back5, tot5, pre5, do5, pre4, tot4, keep, gb, gain5, sh, w5],
+        [V((12, 512), F32)],
         flops=2e9, size=1e7, name="back_five",
     )
-    back4 = across(bt4)
+    back4 = steps(bt4)
 
     def step(g, k):
         if not exact:
             return g
-        partner = [(i, i ^ (1 << k)) for i in range(wide)]
-        if k == 0:
-            return g[0] + swap(g[1], "wide", partner)
-        half = g.shape[0] // 2
-        return g[:half] + swap(g[half:], "wide", partner)
-
-    def last_step(g):
-        return g[:1], swap(g[1:], "wide", [(i, i ^ 8) for i in range(wide)])
+        kept, sent = g
+        got = swap(sent, "wide", [(i, i ^ (1 << k)) for i in range(wide)])
+        if k == 3:
+            return kept, got
+        half = kept.shape[0] // 2
+        return kept[:half] + got[:half], kept[half:] + got[half:]
 
     ga = call(
         grads_a_kernel, [h(8, 416, 256)] * 2, [isc, h5, d6, col4, d5],
@@ -1183,14 +1219,14 @@
     d4, dj1, bt3, dgain4, dbias4, dp1, de1, ds1, bias1 = call(
         back_four_kernel,
         [
-            h(M, 512), f(M, 2048), f(8, 2048), f(512), f(512), f(8, 2048),
+            h(M, 512), f(M, 2048), f(8, 2048), out(512), out(512), f(8, 2048),
             f(8, 2048), f(8, 128), f(8, 512),
         ],
         [
-            fs, isc, back4, tot4, pre4, do4, dj2, tot3, pre3, prep, gate1, sp1, keep, gb, vec1,
-            first_squeeze, first_excite,
-        ] + w4_refs,
-        [V((2048, 512), BF), V((4, 512), F32), D((3,))],
+            fs, back4, tot4, pre4, do4, dj2, tot3, pre3, prep, gate1, sp1, keep, gb, vec1,
+            far(first_squeeze), far(first_excite), w4,
+        ],
+        [V((4, 512), F32), V((2048, 128), BF), V((128, 2048), BF), D((2,))],
         flops=1e9, size=1e7, name="back_four",
     )
     back3 = steps(bt3)
@@ -1203,12 +1239,12 @@
     back3, ga, gb1 = lax.optimization_barrier((back3, ga, gb1))
     d3, dproj, do2, bt2, dgain3, dbias3, dgainp, dbiasp = call(
         back_three_kernel,
-        [h(M, 2048), h(M, 2048), f(M, 512), f(12, 512), f(2048), f(2048), f(2048), f(2048)],
-        [fs, back3, tot3, pre3, prep, dj1, gate1, dp1, bias1, pre2, tot2, keep, vec1, gb, first_expand],
+        [h(M, 2048), h(M, 2048), f(M, 512), f(12, 512), out(2048), out(2048), out(2048), out(2048)],
+        [fs, back3, tot3, pre3, prep, dj1, gate1, dp1, bias1, pre2, tot2, keep, vec1, gb, w3],
         [V((8, 2048), F32), V((M, 512), F32)],
         flops=1e9, size=1e7, name="back_three",
     )
-    back2 = across(bt2)
+    back2 = steps(bt2)
     ga, gb1 = step(ga, 1), step(gb1, 0)
     gc = call(
         grads_c_kernel, [h(8, 448, 256)] * 2,
@@ -1216,57 +1252,60 @@
         [V((512, 256), BF), V((1024, 256), BF), V((128, 256), F32), V((128, 256), F32), V((8, 128), F32)],
         flops=3e9, size=1e7, name="grads_c",
     )
+    gc = step(gc, 0)
     back2, ga, gb1, gc = lax.optimization_barrier((back2, ga, gb1, gc))
+    ws_back = call(
+        fetch_two_kernel, [h(9, 512, 512)], [far(after(ws_far, bt2))], [D((3,))], size=9e6, name="fetch_two",
+    )[0]
     d2, do1, bt1, dgain2, dbias2, debias1, dsbias1 = call(
         back_two_kernel,
-        [h(M, 512), f(4, M, 512), f(4, 512), f(512), f(512), f(2048), f(128)],
-        [fs, back2, tot2, pre2, do2, x1, keep1, keep, gb, sh, ws],
+        [h(M, 512), f(4, M, 512), f(4, 512), out(512), out(512), out(2048), out(128)],
+        [fs, back2, tot2, pre2, do2, x1, keep1, keep, gb, sh, ws_back],
         [V((12, 512), F32), V((4, M, 512), BF)],
         flops=2e9, size=1e7, name="back_two",
     )
-    back1 = across(bt1)
-    ga, gb1, gc = step(ga, 2), step(gb1, 1), step(gc, 0)
+    back1 = steps(bt1)
+    ga, gb1, gc = step(ga, 2), step(gb1, 1), step(gc, 1)
     gd = call(
         grads_d_kernel, [h(8, 288, 256)] * 2, [isc, col1, d2], [V((512, 256), BF)],
         flops=2e9, size=6e6, name="grads_d",
     )
+    gd = step(gd, 0)
     back1, ga, gb1, gc, gd = lax.optimization_barrier((back1, ga, gb1, gc, gd))
     d1, ge_keep, ge_send, dgain1, dbias1 = call(
-        back_one_kernel, [h(B, M, 512), h(8, 64, 256), h(8, 64, 256), f(512), f(512)],
+        back_one_kernel, [h(B, M, 512), h(8, 64, 256), h(8, 64, 256), out(512), out(512)],
         [fs, isc, back1, tot1, x1, do1, xp, keep1, gb],
         [V((4, 512), F32), V((4, M, 512), BF), V((1024, 256), BF)],
         flops=1e9, size=6e6, name="back_one",
     )
     ge = (ge_keep, ge_send)
     dimg = call(
-        image_kernel, [f(HROWS, 1024)],
+        image_kernel, [out(HROWS, 1024)],
+        [isc, perm, d1, dproj, keep_half, w1, far(after(first_project, bt1))],
         [
-            perm.transpose(0, 2, 1)[n], jnp.asarray(pick_np, BF)[n], jnp.asarray(spread_np, BF),
-            d1, dproj, keep_half, first_reduce, first_project,
+            V((HROWS, 512), BF), V((128, 2048), BF), V((128, M), BF), V((HROWS, 128), BF),
+            V((1024, 2048), BF), D((4,)),
         ],
-        [V((HROWS, 512), BF), V((HALF, 2048), BF)],
         flops=1e9, size=1e7, name="image",
     )[0]
 
     if exact:
-        for k in range(1, 4):
-            gb1 = step(gb1, k) if k == 2 else gb1
-            gc = step(gc, k) if k < 3 else gc
-        gd, ge = step(step(gd, 0), 1), step(ge, 0)
+        ge, gd = step(ge, 0), step(gd, 1)
         gd, ge, dimg = lax.optimization_barrier((gd, ge, dimg))
-        gd, ge = step(gd, 2), step(step(ge, 1), 2)
+        ge = step(step(ge, 1), 2)
+        gd, gb1, gc = step(gd, 2), step(gb1, 2), step(gc, 2)
         expand2, spatial2 = call(
-            unpack_a_kernel, [f(256, 128), f(288, 256)], list(last_step(ga)), name="unpack_a"
+            unpack_a_kernel, [out(256, 128), out(288, 256)], list(step(ga, 3)), name="unpack_a"
         )
         reduce2, squeeze2, excite2 = call(
-            unpack_b_kernel, [f(32, 1024), f(8, 1024), f(8, 1024)], list(last_step(gb1)), name="unpack_b"
+            unpack_b_kernel, [out(32, 1024), out(8, 1024), out(8, 1024)], list(step(gb1, 3)), name="unpack_b"
         )
         expand1, project1, squeeze1, excite1 = call(
-            unpack_c_kernel, [f(32, 1024), f(64, 1024), f(8, 1024), f(8, 1024)], list(last_step(gc)),
+            unpack_c_kernel, [out(32, 1024), out(64, 1024), out(8, 1024), out(8, 1024)], list(step(gc, 3)),
             name="unpack_c",
         )
-        spatial1 = call(unpack_d_kernel, [f(288, 256)], list(last_step(gd)), name="unpack_d")[0]
-        reduce1 = call(unpack_d_kernel, [f(64, 256)], list(last_step(ge)), name="unpack_e")[0]
+        spatial1 = call(unpack_d_kernel, [out(288, 256)], list(step(gd, 3)), name="unpack_d")[0]
+        reduce1 = call(unpack_d_kernel, [out(64, 256)], list(step(ge, 3)), name="unpack_e")[0]
     else:
         finer = wide // 16
 

time: 428 us -> 341 us (0.80)
  local copies, waits for them, and re-layouts: 99.1 us -> 2.95 us
  waiting for transfers between devices: 109 us -> 146 us
  blocking collectives: 43.9 us -> 27.8 us
  other arithmetic: 17.1 us -> 1.5 us
  starting transfers between devices: 61.9 us -> 69.3 us
    unnamed x328 -> x12, local copies, waits for them, and re-layouts: 84.3 us -> 2.89 us
    ppermute x45 -> x69, waiting for transfers between devices: 99 us -> 146 us  [swap(): return lax.ppermute(v, axis, pairs)]
    ppermute x45 -> x69, starting transfers between devices: 35.5 us -> 69.3 us  [swap(): return lax.ppermute(v, axis, pairs)]
    all_to_all x6 -> x0, starting transfers between devices: 26.3 us -> none  [across(): lax.all_to_all(sent, 'wide', 0, 0, axis_index_groups=groups, tiled=True)]
    all_to_all x4 -> x2, blocking collectives: 43.9 us -> 27.8 us  [across(): lax.all_to_all(sent, 'wide', 0, 0, axis_index_groups=groups, tiled=True)]
    add x15, other arithmetic: 16.1 us -> 1.23 us  [step(): return (kept[:half] + got[:half], kept[half:] + got[half:])]
    all_to_all x6 -> x0, waiting for transfers between devices: 9.59 us -> none  [across(): lax.all_to_all(sent, 'wide', 0, 0, axis_index_groups=groups, tiled=True)]
    slice x15 -> x0, local copies, waits for them, and re-layouts: 9.05 us -> none  [the longest x10 7.91 us: step(): return g[:half] + swap(g[half:], 'wide', partner)]
  transfers between devices with their start and end apart: 51 -> 69, of which waited for: 25 -> 47; matrix products, arithmetic and copies ran while one was open for 7% -> 0% of each run, Pallas kernels for 16% -> 20%
where the time goes in v2:
time: 341 us
  waiting for transfers between devices  146 us (43%)
  Pallas kernels  91.8 us (27%)
  starting transfers between devices  69.3 us (20%)
  blocking collectives  27.8 us (8%)
    ppermute x69, waiting for transfers between devices, swap(): return lax.ppermute(v, axis, pairs)  146 us
    pallas_call x31, Pallas kernels, call(): pl.pallas_call(body, out_shape=tuple((o if hasattr(o, 'memory_space') els...  91.8 us
    ppermute x69, starting transfers between devices, swap(): return lax.ppermute(v, axis, pairs)  69.3 us
    all_to_all x2, blocking collectives, across(): lax.all_to_all(sent, 'wide', 0, 0, axis_index_groups=groups, tiled=True)  27.8 us
  transfers between devices with their start and end apart: 69, of which 47 were waited for; matrix products, arithmetic and copies ran while one was open for 0% of the time, Pallas kernels for 20%

profile of v2, /device:TPU:0, one launch (start us, length us, event | category | flops | bytes accessed | tf_op | source)
XLA Modules:
  0.0 340.7 jit_solution(9255854553609248863)
XLA Ops:
  0.7 3.0 collective-permute-start
  3.7 2.1 setup.1
  5.8 2.4 one_half.1
  10.9 2.2 collective-permute-done.2
  14.6 2.1 collective-permute-done.3
  16.7 2.6 collective-permute-start.4
  19.3 3.5 %pack.1 = (bf16[3856,256]{1,0:T(8,128)(2,1)S(1)}, bf16[512,512]{1,0:T(8,128)(2,1)S(1)}, f32[8,512]{1,0:T(8,128)S(1)}, f32[8,2048]{1,0:T(8,128)S(1)}, f32[8,128]{...) custom-call(s32[18]{0:T(128)S(4)} %get-tuple-element.246.isc, ...), custom_call_target="tpu_custom_call" | custom-call | flops 100000000 | bytes 20000000 | tf_op jit(solution)/shard_map/pack/pallas_call | solution.py:999
  23.4 3.1 collective-permute-done.5.part_other
  27.0 6.3 %stage_two.1 = (bf16[4,224,1024]{2,1,0:T(8,128)(2,1)S(1)}, bf16[224,1024]{1,0:T(8,128)(2,1)S(1)}, f32[4,224,512]{2,1,0:T(8,128)S(1)}, bf16[9,224,512]{2,1,0:T(8,...) custom-call(f32[13]{0:T(128)S(4)} %get-tuple-element.199.fs, ...), custom_call_target="tpu_custom_call" | custom-call | flops 4000000000 | bytes 20000000 | tf_op jit(solution)/shard_map/stage_two/pallas_call | solution.py:999
  33.4 5.2 %collective-permute-done.10.r1 = bf16[512,512]{1,0:T(8,128)(2,1)S(1)} collective-permute-done((bf16[512,512]{1,0:T(8,128)(2,1)S(1)}, bf16[512,512]{1,0:T(8,128)(2,1)S(1)}, u32[]{:S(2)}, u32[]{:S(2)}) %collective-permute-start.10) | collective-permute-done | bytes 524320 | tf_op jit(solution)/shard_map/ppermute | solution.py:1014
  41.8 2.2 collective-permute-done.7
  45.5 2.1 collective-permute-done.8
  47.6 2.5 collective-permute-start.9
  50.1 2.1 collective-permute-done.9
  52.2 3.8 %project.1 = (f32[224,2048]{1,0:T(8,128)S(1)}, f32[4,2048]{1,0:T(4,128)S(1)}, bf16[512,2048]{1,0:T(8,128)(2,1)S(1)}) custom-call(f32[13]{0:T(128)S(4)} %get-tuple-element.199.fs, bf16[224,1024]{1,0:T(8,128)(2,1)S(1)} %get-tuple-element.218.x.strided, f32[224,1]{1,0:T(8,128)S(1)} %get-tuple-element.209.keep, bf16[1024,2048]{1,0:T(8,128)(2,1)} %wp_far.2, ...), custom_call_target="tpu_custom_call" | custom-call | flops 1000000000 | bytes 8000000 | tf_op jit(solution)/shard_map/project/pallas_call | solution.py:999
  56.0 2.2 stage_three.1
  61.1 2.8 collective-permute-done.12
  65.5 2.7 collective-permute-done.13
  68.2 2.5 collective-permute-start.14
  70.7 2.7 collective-permute-done.14
  75.8 4.5 %stage_four.1 = (bf16[224,2048]{1,0:T(8,128)(2,1)S(1)}, f32[224,512]{1,0:T(8,128)S(1)}, f32[4,512]{1,0:T(4,128)S(1)}, f32[8,2048]{1,0:T(8,128)S(1)}, f32[8,2048]...) custom-call(f32[13]{0:T(128)S(4)} %get-tuple-element.199.fs, ...), custom_call_target="tpu_custom_call" | custom-call | flops 1000000000 | bytes 10000000 | tf_op jit(solution)/shard_map/stage_four/pallas_call | solution.py:999
  81.0 3.5 %collective-permute-done.16 = f32[4,512]{1,0:T(4,128)S(1)} collective-permute-done((f32[4,512]{1,0:T(4,128)S(1)}, f32[4,512]{1,0:T(4,128)S(1)}, u32[]{:S(2)}, u32[]{:S(2)}) %collective-permute-start.16) | collective-permute-done | bytes 8224 | tf_op jit(solution)/shard_map/ppermute | solution.py:1014
  85.9 2.2 collective-permute-done.17
  89.7 2.1 collective-permute-done.18
  91.8 2.6 collective-permute-start.19
  94.4 2.0 collective-permute-done.19
  97.6 2.4 fetch_five.1
  100.0 2.3 stage_five.1
  108.9 1.9 collective-permute-done.24
  110.9 2.6 collective-permute-start.25
  115.4 2.2 stage_six.1
  120.5 2.4 collective-permute-done.27
  124.7 2.2 collective-permute-done.28
  127.0 2.7 collective-permute-start.29
  132.0 6.8 %turn.1 = (bf16[224,1024]{1,0:T(8,128)(2,1)}, f32[224,2048]{1,0:T(8,128)S(1)}, f32[4,2048]{1,0:T(4,128)S(1)}, f32[8,512]{1,0:T(8,128)S(1)}, f32[4,2048]{1,0:T(4,...) custom-call(f32[13]{0:T(128)S(4)} %get-tuple-element.199.fs, ...), custom_call_target="tpu_custom_call" | custom-call | flops 1000000000 | bytes 10000000 | tf_op jit(solution)/shard_map/turn/pallas_call | solution.py:999
  140.1 15.2 %all_to_all.10.parts = f32[8,4,2048]{2,1,0:T(4,128)S(1)} all-to-all(f32[8,4,2048]{2,1,0:T(4,128)S(1)} %broadcast_in_dim.44), channel_id=1, replica_groups={{0,4,8,12,16,20,24,28},{2,6,10,14,18,22,26,30},{1,5,9,13,17,21,25,29},{..., dimensions={0} | all-to-all | bytes 524288 | tf_op jit(solution)/shard_map/all_to_all | solution.py:1049
  155.3 3.4 back_six.1
  159.9 12.6 %all_to_all.11.parts = f32[8,12,512]{2,1,0:T(8,128)S(1)} all-to-all(f32[8,12,512]{2,1,0:T(8,128)S(1)} %broadcast_in_dim.45), channel_id=1, replica_groups={{0,4,8,12,16,20,24,28},{2,6,10,14,18,22,26,30},{1,5,9,13,17,21,25,29},{..., dimensions={0} | all-to-all | bytes 393216 | tf_op jit(solution)/shard_map/all_to_all | solution.py:1049
  172.5 3.5 %back_five.1 = (bf16[224,512]{1,0:T(8,128)(2,1)S(1)}, f32[224,512]{1,0:T(8,128)S(1)}, f32[4,512]{1,0:T(4,128)S(1)}, f32[256]{0:T(256)}, f32[256]{0:T(256)}, /*index=5*/f32[1024]{0:T(1024)}, f32[128]{0:T(128)}, f32[5]{0:T(128)}) custom-call(f32[13]{0:T(128)S(4)} %get-tuple-element.199.fs, s32[18]{0:T(128)S(4)} %get-tuple-element.246.isc, ...), custom_call_target="tpu_custom_call" | custom-call | flops 2000000000 | bytes 10000000 | tf_op jit(solution)/shard_map/back_five/pallas_call | solution.py:999
  178.7 2.2 collective-permute-done.34
  182.0 2.6 collective-permute-done.35
  185.6 4.8 %grads_a.1 = (bf16[8,416,256]{2,1,0:T(8,128)(2,1)S(1)}, bf16[8,416,256]{2,1,0:T(8,128)(2,1)S(1)}) custom-call(s32[18]{0:T(128)S(4)} %get-tuple-element.246.isc, bf16[224,512]{1,0:T(8,128)(2,1)S(1)} %get-tuple-element.263.h5, bf16[224,2048]{1,0:T(8,128)(2,1)S(1)} %get-tuple-element.264.d6, bf16[9,224,512]{2,1,0:T(8,128)(2,1)S(1)} %get-tuple-element.265.col4, ...), custom_call_target="tpu_custom_call" | custom-call | flops 2000000000 | bytes 10000000 | tf_op jit(solution)/shard_map/grads_a/pallas_call | solution.py:999
  190.5 6.8 %back_four.1 = (bf16[224,512]{1,0:T(8,128)(2,1)S(1)}, f32[224,2048]{1,0:T(8,128)S(1)}, f32[8,2048]{1,0:T(8,128)S(1)}, f32[512]{0:T(512)}, f32[512]{0:T(512)}, /*...) custom-call(f32[13]{0:T(128)S(4)} %get-tuple-element.199.fs, ...), custom_call_target="tpu_custom_call" | custom-call | flops 1000000000 | bytes 10000000 | tf_op jit(solution)/shard_map/back_four/pallas_call | solution.py:999
  199.2 4.0 %collective-permute-done.38 = f32[8,2048]{1,0:T(8,128)S(1)} collective-permute-done((f32[8,2048]{1,0:T(8,128)S(1)}, f32[8,2048]{1,0:T(8,128)S(1)}, u32[]{:S(2)}, u32[]{:S(2)}) %collective-permute-start.38) | collective-permute-done | bytes 65568 | tf_op jit(solution)/shard_map/ppermute | solution.py:1014
  203.9 3.6 %collective-permute-done.39 = f32[8,2048]{1,0:T(8,128)S(1)} collective-permute-done((f32[8,2048]{1,0:T(8,128)S(1)}, f32[8,2048]{1,0:T(8,128)S(1)}, u32[]{:S(2)}, u32[]{:S(2)}) %collective-permute-start.39) | collective-permute-done | bytes 65568 | tf_op jit(solution)/shard_map/ppermute | solution.py:1014
  211.1 2.4 collective-permute-done.40
  213.7 3.9 %back_three.1 = (bf16[224,2048]{1,0:T(8,128)(2,1)S(1)}, bf16[224,2048]{1,0:T(8,128)(2,1)S(1)}, f32[224,512]{1,0:T(8,128)S(1)}, f32[12,512]{1,0:T(8,128)S(1)}, f3...) custom-call(f32[13]{0:T(128)S(4)} %get-tuple-element.199.fs, ...), custom_call_target="tpu_custom_call" | custom-call | flops 1000000000 | bytes 10000000 | tf_op jit(solution)/shard_map/back_three/pallas_call | solution.py:999
  217.6 2.3 grads_c.1
  220.6 4.4 %collective-permute-done.42 = f32[12,512]{1,0:T(8,128)S(1)} collective-permute-done((f32[12,512]{1,0:T(8,128)S(1)}, f32[12,512]{1,0:T(8,128)S(1)}, u32[]{:S(2)}, u32[]{:S(2)}) %collective-permute-start.42) | collective-permute-done | bytes 24608 | tf_op jit(solution)/shard_map/ppermute | solution.py:1014
  225.0 17.2 %collective-permute-done.43 = f32[12,512]{1,0:T(8,128)S(1)} collective-permute-done((f32[12,512]{1,0:T(8,128)S(1)}, f32[12,512]{1,0:T(8,128)S(1)}, u32[]{:S(2)}, u32[]{:S(2)}) %collective-permute-start.43) | collective-permute-done | bytes 24608 | tf_op jit(solution)/shard_map/ppermute | solution.py:1014
  242.2 3.9 %collective-permute-done.44 = f32[12,512]{1,0:T(8,128)S(1)} collective-permute-done((f32[12,512]{1,0:T(8,128)S(1)}, f32[12,512]{1,0:T(8,128)S(1)}, u32[]{:S(2)}, u32[]{:S(2)}) %collective-permute-start.44) | collective-permute-done | bytes 24608 | tf_op jit(solution)/shard_map/ppermute | solution.py:1014
  247.3 2.4 fetch_two.1.ws
  251.7 3.1 back_two.1
  254.8 2.6 grads_d.1
  262.1 17.2 %collective-permute-done.50 = f32[4,512]{1,0:T(4,128)S(1)} collective-permute-done((f32[4,512]{1,0:T(4,128)S(1)}, f32[4,512]{1,0:T(4,128)S(1)}, u32[]{:S(2)}, u32[]{:S(2)}) %collective-permute-start.50) | collective-permute-done | bytes 8224 | tf_op jit(solution)/shard_map/ppermute | solution.py:1014
  280.7 2.4 collective-permute-done.51
  287.7 9.1 %collective-permute-done.53 = bf16[2,416,256]{2,1,0:T(8,128)(2,1)S(1)} collective-permute-done((bf16[2,416,256]{2,1,0:T(8,128)(2,1)S(1)}, bf16[2,416,256]{2,1,0:T(8,128)(2,1)S(1)}, u32[]{:S(2)}, u32[]{:S(2)}) %collective-permute-start.53) | collective-permute-done | bytes 426016 | tf_op jit(solution)/shard_map/ppermute | solution.py:1014
  297.7 2.4 collective-permute-start.68
  300.8 2.7 back_one.1
  303.6 8.0 %image.1 = f32[448,1024]{1,0:T(8,128)} custom-call(s32[18]{0:T(128)S(4)} %get-tuple-element.246.isc, bf16[2,224,112]{2,1,0:T(8,128)(2,1)S(1)} %get-tuple-element.207.perm, bf16[4,224,512]{2,1,0:T(8,128)(2,1)S(1)} %get-tuple-element.325.d1, bf16[224,2048]{1,0:T(8,128)(2,1)S(1)} %get-tuple-element.296.dproj, f32[448,1]{1,0:T(8,128)S(1)} %get-tuple-element.201.keep, ...), custom_call_target="tpu_custom_call" | custom-call | flops 1000000000 | bytes 10000000 | tf_op jit(solution)/shard_map/image/pallas_call | solution.py:999
  311.6 2.6 collective-permute-start.67
  315.7 2.4 collective-permute-done.64
  320.5 9.4 %collective-permute-done.62 = bf16[2,288,256]{2,1,0:T(8,128)(2,1)S(1)} collective-permute-done((bf16[2,288,256]{2,1,0:T(8,128)(2,1)S(1)}, bf16[2,288,256]{2,1,0:T(8,128)(2,1)S(1)}, u32[]{:S(2)}, u32[]{:S(2)}) %collective-permute-start.62) | collective-permute-done | bytes 294944 | tf_op jit(solution)/shard_map/ppermute | solution.py:1014
  335.2 4.1 %collective-permute-done.61.b = bf16[1,64,256]{2,1,0:T(8,128)(2,1)S(1)} collective-permute-done((bf16[1,64,256]{2,1,0:T(8,128)(2,1)S(1)}, bf16[1,64,256]{2,1,0:T(8,128)(2,1)S(1)}, u32[]{:S(2)}, u32[]{:S(2)}) %collective-permute-start.61) | collective-permute-done | bytes 32800 | tf_op jit(solution)/shard_map/ppermute | solution.py:1014
  (178 shorter events, 78.2 us)
Async XLA Ops:
  0.7 25.8 %collective-permute-start = (bf16[4,112,1024]{2,1,0:T(8,128)(2,1)}, bf16[4,112,1024]{2,1,0:T(8,128)(2,1)S(1)}, u32[]{:S(2)}, u32[]{:S(2)}) collective-permute-start(bf16[4,112,1024]{2,1,0:T(8,128)(2,1)} %bitcast.42), channel_id=1, source_target_pairs={{0,1},{1,0},{2,3},{3,2},{4,5},{5,4},{6,7},{7,6},{8,9},{9,8},{10,11... | collective-permute-start | bytes 2752520 | tf_op jit(solution)/shard_map/ppermute | solution.py:1014
  9.4 3.7 %collective-permute-start.2 = (f32[4,512]{1,0:T(4,128)S(1)}, f32[4,512]{1,0:T(4,128)S(1)}, u32[]{:S(2)}, u32[]{:S(2)}) collective-permute-start(f32[4,512]{1,0:T(4,128)S(1)} %add.216), channel_id=1, source_target_pairs={{0,4},{2,6},{4,0},{6,2},{8,12},{10,14},{12,8},{14,10},{16,20},{18,... | collective-permute-start | bytes 24584 | tf_op jit(solution)/shard_map/ppermute | solution.py:1014
  13.0 3.7 %collective-permute-start.3 = (f32[4,512]{1,0:T(4,128)S(1)}, f32[4,512]{1,0:T(4,128)S(1)}, u32[]{:S(2)}, u32[]{:S(2)}) collective-permute-start(f32[4,512]{1,0:T(4,128)S(1)} %add.217), channel_id=1, source_target_pairs={{0,8},{2,10},{4,12},{6,14},{8,0},{10,2},{12,4},{14,6},{16,24},{18,... | collective-permute-start | bytes 24584 | tf_op jit(solution)/shard_map/ppermute | solution.py:1014
  16.7 6.1 %collective-permute-start.4 = (f32[4,512]{1,0:T(4,128)S(1)}, f32[4,512]{1,0:T(4,128)S(1)}, u32[]{:S(2)}, u32[]{:S(2)}) collective-permute-start(f32[4,512]{1,0:T(4,128)S(1)} %add.218), channel_id=1, source_target_pairs={{0,16},{2,18},{4,20},{6,22},{8,24},{10,26},{12,28},{14,30},{16,0},... | collective-permute-start | bytes 24584 | tf_op jit(solution)/shard_map/ppermute | solution.py:1014
  22.8 3.7 %collective-permute-start.5 = (f32[4,512]{1,0:T(4,128)S(1)}, f32[4,512]{1,0:T(4,128)S(1)}, u32[]{:S(2)}, u32[]{:S(2)}) collective-permute-start(f32[4,512]{1,0:T(4,128)S(1)} %add.219.part), channel_id=1, source_target_pairs={{0,1},{1,0},{2,3},{3,2},{4,5},{5,4},{6,7},{7,6},{8,9},{9,8},{10,11... | collective-permute-start | bytes 24584 | tf_op jit(solution)/shard_map/ppermute | solution.py:1014
  26.5 12.0 %collective-permute-start.10 = (bf16[512,512]{1,0:T(8,128)(2,1)S(1)}, bf16[512,512]{1,0:T(8,128)(2,1)S(1)}, u32[]{:S(2)}, u32[]{:S(2)}) collective-permute-start(bf16[512,512]{1,0:T(8,128)(2,1)S(1)} %get-tuple-element.217), channel_id=1, source_target_pairs={{0,1},{1,0},{2,3},{3,2},{4,5},{5,4},{6,7},{7,6},{8,9},{9,8},{10,11... | collective-permute-start | bytes 1572872 | tf_op jit(solution)/shard_map/ppermute | solution.py:1014
  38.5 41.8 %collective-permute-start.20 = (bf16[3856,256]{1,0:T(8,128)(2,1)S(1)}, bf16[3856,256]{1,0:T(8,128)(2,1)S(1)}, u32[]{:S(2)}, u32[]{:S(2)}) collective-permute-start(bf16[3856,256]{1,0:T(8,128)(2,1)S(1)} %get-tuple-element.233), channel_id=1, source_target_pairs={{0,1},{1,0},{2,3},{3,2},{4,5},{5,4},{6,7},{7,6},{8,9},{9,8},{10,11... | collective-permute-start | bytes 5922824 | tf_op jit(solution)/shard_map/ppermute | solution.py:1014
  40.3 3.7 %collective-permute-start.7 = (f32[4,512]{1,0:T(4,128)S(1)}, f32[4,512]{1,0:T(4,128)S(1)}, u32[]{:S(2)}, u32[]{:S(2)}) collective-permute-start(f32[4,512]{1,0:T(4,128)S(1)} %add.220), channel_id=1, source_target_pairs={{0,4},{2,6},{4,0},{6,2},{8,12},{10,14},{12,8},{14,10},{16,20},{18,... | collective-permute-start | bytes 24584 | tf_op jit(solution)/shard_map/ppermute | solution.py:1014
  43.9 3.7 %collective-permute-start.8 = (f32[4,512]{1,0:T(4,128)S(1)}, f32[4,512]{1,0:T(4,128)S(1)}, u32[]{:S(2)}, u32[]{:S(2)}) collective-permute-start(f32[4,512]{1,0:T(4,128)S(1)} %add.221), channel_id=1, source_target_pairs={{0,8},{2,10},{4,12},{6,14},{8,0},{10,2},{12,4},{14,6},{16,24},{18,... | collective-permute-start | bytes 24584 | tf_op jit(solution)/shard_map/ppermute | solution.py:1014
  47.6 4.5 %collective-permute-start.9 = (f32[4,512]{1,0:T(4,128)S(1)}, f32[4,512]{1,0:T(4,128)S(1)}, u32[]{:S(2)}, u32[]{:S(2)}) collective-permute-start(f32[4,512]{1,0:T(4,128)S(1)} %add.222), channel_id=1, source_target_pairs={{0,16},{2,18},{4,20},{6,22},{8,24},{10,26},{12,28},{14,30},{16,0},... | collective-permute-start | bytes 24584 | tf_op jit(solution)/shard_map/ppermute | solution.py:1014
  58.2 1.3 collective-permute-start.11
  59.5 4.3 %collective-permute-start.12 = (f32[8,2048]{1,0:T(8,128)S(1)}, f32[8,2048]{1,0:T(8,128)S(1)}, u32[]{:S(2)}, u32[]{:S(2)}) collective-permute-start(f32[8,2048]{1,0:T(8,128)S(1)} %add.224), channel_id=1, source_target_pairs={{0,4},{2,6},{4,0},{6,2},{8,12},{10,14},{12,8},{14,10},{16,20},{18,... | collective-permute-start | bytes 196616 | tf_op jit(solution)/shard_map/ppermute | solution.py:1014
  63.9 4.3 %collective-permute-start.13 = (f32[8,2048]{1,0:T(8,128)S(1)}, f32[8,2048]{1,0:T(8,128)S(1)}, u32[]{:S(2)}, u32[]{:S(2)}) collective-permute-start(f32[8,2048]{1,0:T(8,128)S(1)} %add.225), channel_id=1, source_target_pairs={{0,8},{2,10},{4,12},{6,14},{8,0},{10,2},{12,4},{14,6},{16,24},{18,... | collective-permute-start | bytes 196616 | tf_op jit(solution)/shard_map/ppermute | solution.py:1014
  65.5 8.0 %collective-permute-start.15 = (bf16[512,512]{1,0:T(8,128)(2,1)S(1)}, bf16[512,512]{1,0:T(8,128)(2,1)S(1)}, u32[]{:S(2)}, u32[]{:S(2)}) collective-permute-start(bf16[512,512]{1,0:T(8,128)(2,1)S(1)} %collective-permute-done.10.r1), channel_id=1, source_target_pairs={{0,2},{2,0},{4,6},{6,4},{8,10},{10,8},{12,14},{14,12},{16,18},{18,... | collective-permute-start | bytes 1572872 | tf_op jit(solution)/shard_map/ppermute | solution.py:1014
  68.2 5.2 %collective-permute-start.14 = (f32[8,2048]{1,0:T(8,128)S(1)}, f32[8,2048]{1,0:T(8,128)S(1)}, u32[]{:S(2)}, u32[]{:S(2)}) collective-permute-start(f32[8,2048]{1,0:T(8,128)S(1)} %add.226), channel_id=1, source_target_pairs={{0,16},{2,18},{4,20},{6,22},{8,24},{10,26},{12,28},{14,30},{16,0},... | collective-permute-start | bytes 196616 | tf_op jit(solution)/shard_map/ppermute | solution.py:1014
  80.4 15.9 %collective-permute-start.21 = (bf16[3856,256]{1,0:T(8,128)(2,1)S(1)}, bf16[3856,256]{1,0:T(8,128)(2,1)S(1)}, u32[]{:S(2)}, u32[]{:S(2)}) collective-permute-start(bf16[3856,256]{1,0:T(8,128)(2,1)S(1)} %collective-permute-done.20.r1), channel_id=1, source_target_pairs={{0,2},{2,0},{4,6},{6,4},{8,10},{10,8},{12,14},{14,12},{16,18},{18,... | collective-permute-start | bytes 5922824 | tf_op jit(solution)/shard_map/ppermute | solution.py:1014
  80.5 4.0 %collective-permute-start.16 = (f32[4,512]{1,0:T(4,128)S(1)}, f32[4,512]{1,0:T(4,128)S(1)}, u32[]{:S(2)}, u32[]{:S(2)}) collective-permute-start(f32[4,512]{1,0:T(4,128)S(1)} %get-tuple-element.228), channel_id=1, source_target_pairs={{0,2},{2,0},{4,6},{6,4},{8,10},{10,8},{12,14},{14,12},{16,18},{18,... | collective-permute-start | bytes 24584 | tf_op jit(solution)/shard_map/ppermute | solution.py:1014
  84.4 3.7 %collective-permute-start.17 = (f32[4,512]{1,0:T(4,128)S(1)}, f32[4,512]{1,0:T(4,128)S(1)}, u32[]{:S(2)}, u32[]{:S(2)}) collective-permute-start(f32[4,512]{1,0:T(4,128)S(1)} %add.228), channel_id=1, source_target_pairs={{0,4},{2,6},{4,0},{6,2},{8,12},{10,14},{12,8},{14,10},{16,20},{18,... | collective-permute-start | bytes 24584 | tf_op jit(solution)/shard_map/ppermute | solution.py:1014
  88.1 3.7 %collective-permute-start.18 = (f32[4,512]{1,0:T(4,128)S(1)}, f32[4,512]{1,0:T(4,128)S(1)}, u32[]{:S(2)}, u32[]{:S(2)}) collective-permute-start(f32[4,512]{1,0:T(4,128)S(1)} %add.229), channel_id=1, source_target_pairs={{0,8},{2,10},{4,12},{6,14},{8,0},{10,2},{12,4},{14,6},{16,24},{18,... | collective-permute-start | bytes 24584 | tf_op jit(solution)/shard_map/ppermute | solution.py:1014
  91.8 4.5 %collective-permute-start.19 = (f32[4,512]{1,0:T(4,128)S(1)}, f32[4,512]{1,0:T(4,128)S(1)}, u32[]{:S(2)}, u32[]{:S(2)}) collective-permute-start(f32[4,512]{1,0:T(4,128)S(1)} %add.230), channel_id=1, source_target_pairs={{0,16},{2,18},{4,20},{6,22},{8,24},{10,26},{12,28},{14,30},{16,0},... | collective-permute-start | bytes 24584 | tf_op jit(solution)/shard_map/ppermute | solution.py:1014
  102.3 1.2 collective-permute-start.22
  103.6 3.7 %collective-permute-start.23 = (f32[4,512]{1,0:T(4,128)S(1)}, f32[4,512]{1,0:T(4,128)S(1)}, u32[]{:S(2)}, u32[]{:S(2)}) collective-permute-start(f32[4,512]{1,0:T(4,128)S(1)} %add.232), channel_id=1, source_target_pairs={{0,4},{2,6},{4,0},{6,2},{8,12},{10,14},{12,8},{14,10},{16,20},{18,... | collective-permute-start | bytes 24584 | tf_op jit(solution)/shard_map/ppermute | solution.py:1014
  105.1 24.6 %collective-permute-start.30 = (bf16[224,1024]{1,0:T(8,128)(2,1)S(1)}, bf16[224,1024]{1,0:T(8,128)(2,1)S(1)}, u32[]{:S(2)}, u32[]{:S(2)}) collective-permute-start(bf16[224,1024]{1,0:T(8,128)(2,1)S(1)} %bitcast.45), channel_id=1, source_target_pairs={{0,1},{1,0},{2,3},{3,2},{4,5},{5,4},{6,7},{7,6},{8,9},{9,8},{10,11... | collective-permute-start | bytes 1376264 | tf_op jit(solution)/shard_map/ppermute | solution.py:1014
  107.2 3.7 %collective-permute-start.24 = (f32[4,512]{1,0:T(4,128)S(1)}, f32[4,512]{1,0:T(4,128)S(1)}, u32[]{:S(2)}, u32[]{:S(2)}) collective-permute-start(f32[4,512]{1,0:T(4,128)S(1)} %add.233), channel_id=1, source_target_pairs={{0,8},{2,10},{4,12},{6,14},{8,0},{10,2},{12,4},{14,6},{16,24},{18,... | collective-permute-start | bytes 24584 | tf_op jit(solution)/shard_map/ppermute | solution.py:1014
  110.9 4.5 %collective-permute-start.25 = (f32[4,512]{1,0:T(4,128)S(1)}, f32[4,512]{1,0:T(4,128)S(1)}, u32[]{:S(2)}, u32[]{:S(2)}) collective-permute-start(f32[4,512]{1,0:T(4,128)S(1)} %add.234), channel_id=1, source_target_pairs={{0,16},{2,18},{4,20},{6,22},{8,24},{10,26},{12,28},{14,30},{16,0},... | collective-permute-start | bytes 24584 | tf_op jit(solution)/shard_map/ppermute | solution.py:1014
  117.7 1.3 collective-permute-start.26
  119.0 4.0 %collective-permute-start.27 = (f32[4,2048]{1,0:T(4,128)S(1)}, f32[4,2048]{1,0:T(4,128)S(1)}, u32[]{:S(2)}, u32[]{:S(2)}) collective-permute-start(f32[4,2048]{1,0:T(4,128)S(1)} %add.236), channel_id=1, source_target_pairs={{0,4},{2,6},{4,0},{6,2},{8,12},{10,14},{12,8},{14,10},{16,20},{18,... | collective-permute-start | bytes 98312 | tf_op jit(solution)/shard_map/ppermute | solution.py:1014
  123.0 4.0 %collective-permute-start.28 = (f32[4,2048]{1,0:T(4,128)S(1)}, f32[4,2048]{1,0:T(4,128)S(1)}, u32[]{:S(2)}, u32[]{:S(2)}) collective-permute-start(f32[4,2048]{1,0:T(4,128)S(1)} %add.237), channel_id=1, source_target_pairs={{0,8},{2,10},{4,12},{6,14},{8,0},{10,2},{12,4},{14,6},{16,24},{18,... | collective-permute-start | bytes 98312 | tf_op jit(solution)/shard_map/ppermute | solution.py:1014
  127.0 5.0 %collective-permute-start.29 = (f32[4,2048]{1,0:T(4,128)S(1)}, f32[4,2048]{1,0:T(4,128)S(1)}, u32[]{:S(2)}, u32[]{:S(2)}) collective-permute-start(f32[4,2048]{1,0:T(4,128)S(1)} %add.238), channel_id=1, source_target_pairs={{0,16},{2,18},{4,20},{6,22},{8,24},{10,26},{12,28},{14,30},{16,0},... | collective-permute-start | bytes 98312 | tf_op jit(solution)/shard_map/ppermute | solution.py:1014
  176.0 1.2 collective-permute-start.33
  177.3 3.7 %collective-permute-start.34 = (f32[4,512]{1,0:T(4,128)S(1)}, f32[4,512]{1,0:T(4,128)S(1)}, u32[]{:S(2)}, u32[]{:S(2)}) collective-permute-start(f32[4,512]{1,0:T(4,128)S(1)} %add.242), channel_id=1, source_target_pairs={{0,4},{2,6},{4,0},{6,2},{8,12},{10,14},{12,8},{14,10},{16,20},{18,... | collective-permute-start | bytes 24584 | tf_op jit(solution)/shard_map/ppermute | solution.py:1014
  180.9 3.7 %collective-permute-start.35 = (f32[4,512]{1,0:T(4,128)S(1)}, f32[4,512]{1,0:T(4,128)S(1)}, u32[]{:S(2)}, u32[]{:S(2)}) collective-permute-start(f32[4,512]{1,0:T(4,128)S(1)} %add.243), channel_id=1, source_target_pairs={{0,8},{2,10},{4,12},{6,14},{8,0},{10,2},{12,4},{14,6},{16,24},{18,... | collective-permute-start | bytes 24584 | tf_op jit(solution)/shard_map/ppermute | solution.py:1014
  184.6 5.8 %collective-permute-start.36 = (f32[4,512]{1,0:T(4,128)S(1)}, f32[4,512]{1,0:T(4,128)S(1)}, u32[]{:S(2)}, u32[]{:S(2)}) collective-permute-start(f32[4,512]{1,0:T(4,128)S(1)} %add.244), channel_id=1, source_target_pairs={{0,16},{2,18},{4,20},{6,22},{8,24},{10,26},{12,28},{14,30},{16,0},... | collective-permute-start | bytes 24584 | tf_op jit(solution)/shard_map/ppermute | solution.py:1014
  190.4 23.0 %collective-permute-start.41 = (bf16[8,416,256]{2,1,0:T(8,128)(2,1)S(1)}, bf16[8,416,256]{2,1,0:T(8,128)(2,1)S(1)}, u32[]{:S(2)}, u32[]{:S(2)}) collective-permute-start(bf16[8,416,256]{2,1,0:T(8,128)(2,1)S(1)} %get-tuple-element.276), channel_id=1, source_target_pairs={{0,2},{2,0},{4,6},{6,4},{8,10},{10,8},{12,14},{14,12},{16,18},{18,... | collective-permute-start | bytes 5111816 | tf_op jit(solution)/shard_map/ppermute | solution.py:1014
  197.3 1.5 collective-permute-start.37
  198.8 4.4 %collective-permute-start.38 = (f32[8,2048]{1,0:T(8,128)S(1)}, f32[8,2048]{1,0:T(8,128)S(1)}, u32[]{:S(2)}, u32[]{:S(2)}) collective-permute-start(f32[8,2048]{1,0:T(8,128)S(1)} %add.246), channel_id=1, source_target_pairs={{0,4},{2,6},{4,0},{6,2},{8,12},{10,14},{12,8},{14,10},{16,20},{18,... | collective-permute-start | bytes 196616 | tf_op jit(solution)/shard_map/ppermute | solution.py:1014
  203.2 4.3 %collective-permute-start.39 = (f32[8,2048]{1,0:T(8,128)S(1)}, f32[8,2048]{1,0:T(8,128)S(1)}, u32[]{:S(2)}, u32[]{:S(2)}) collective-permute-start(f32[8,2048]{1,0:T(8,128)S(1)} %add.247), channel_id=1, source_target_pairs={{0,8},{2,10},{4,12},{6,14},{8,0},{10,2},{12,4},{14,6},{16,24},{18,... | collective-permute-start | bytes 196616 | tf_op jit(solution)/shard_map/ppermute | solution.py:1014
  207.5 5.9 %collective-permute-start.40 = (f32[8,2048]{1,0:T(8,128)S(1)}, f32[8,2048]{1,0:T(8,128)S(1)}, u32[]{:S(2)}, u32[]{:S(2)}) collective-permute-start(f32[8,2048]{1,0:T(8,128)S(1)} %add.248), channel_id=1, source_target_pairs={{0,16},{2,18},{4,20},{6,22},{8,24},{10,26},{12,28},{14,30},{16,0},... | collective-permute-start | bytes 196616 | tf_op jit(solution)/shard_map/ppermute | solution.py:1014
  219.9 31.2 %collective-permute-start.48 = (bf16[8,448,256]{2,1,0:T(8,128)(2,1)S(1)}, bf16[8,448,256]{2,1,0:T(8,128)(2,1)S(1)}, u32[]{:S(2)}, u32[]{:S(2)}) collective-permute-start(bf16[8,448,256]{2,1,0:T(8,128)(2,1)S(1)} %get-tuple-element.301), channel_id=1, source_target_pairs={{0,2},{2,0},{4,6},{6,4},{8,10},{10,8},{12,14},{14,12},{16,18},{18,... | collective-permute-start | bytes 5505032 | tf_op jit(solution)/shard_map/ppermute | solution.py:1014
  220.0 30.9 %collective-permute-start.47 = (bf16[8,192,256]{2,1,0:T(8,128)(2,1)S(1)}, bf16[8,192,256]{2,1,0:T(8,128)(2,1)S(1)}, u32[]{:S(2)}, u32[]{:S(2)}) collective-permute-start(bf16[8,192,256]{2,1,0:T(8,128)(2,1)S(1)} %get-tuple-element.293), channel_id=1, source_target_pairs={{0,2},{2,0},{4,6},{6,4},{8,10},{10,8},{12,14},{14,12},{16,18},{18,... | collective-permute-start | bytes 2359304 | tf_op jit(solution)/shard_map/ppermute | solution.py:1014
  220.5 30.5 %collective-permute-start.46 = (bf16[4,416,256]{2,1,0:T(8,128)(2,1)S(1)}, bf16[4,416,256]{2,1,0:T(8,128)(2,1)S(1)}, u32[]{:S(2)}, u32[]{:S(2)}) collective-permute-start(bf16[4,416,256]{2,1,0:T(8,128)(2,1)S(1)} %get-tuple-element.291), channel_id=1, source_target_pairs={{0,4},{2,6},{4,0},{6,2},{8,12},{10,14},{12,8},{14,10},{16,20},{18,... | collective-permute-start | bytes 2555912 | tf_op jit(solution)/shard_map/ppermute | solution.py:1014
  220.5 4.4 %collective-permute-start.42 = (f32[12,512]{1,0:T(8,128)S(1)}, f32[12,512]{1,0:T(8,128)S(1)}, u32[]{:S(2)}, u32[]{:S(2)}) collective-permute-start(f32[12,512]{1,0:T(8,128)S(1)} %get-tuple-element.289), channel_id=1, source_target_pairs={{0,2},{2,0},{4,6},{6,4},{8,10},{10,8},{12,14},{14,12},{16,18},{18,... | collective-permute-start | bytes 73736 | tf_op jit(solution)/shard_map/ppermute | solution.py:1014
  225.0 17.2 %collective-permute-start.43 = (f32[12,512]{1,0:T(8,128)S(1)}, f32[12,512]{1,0:T(8,128)S(1)}, u32[]{:S(2)}, u32[]{:S(2)}) collective-permute-start(f32[12,512]{1,0:T(8,128)S(1)} %add.252), channel_id=1, source_target_pairs={{0,4},{2,6},{4,0},{6,2},{8,12},{10,14},{12,8},{14,10},{16,20},{18,... | collective-permute-start | bytes 73736 | tf_op jit(solution)/shard_map/ppermute | solution.py:1014
  242.1 3.9 %collective-permute-start.44 = (f32[12,512]{1,0:T(8,128)S(1)}, f32[12,512]{1,0:T(8,128)S(1)}, u32[]{:S(2)}, u32[]{:S(2)}) collective-permute-start(f32[12,512]{1,0:T(8,128)S(1)} %add.253), channel_id=1, source_target_pairs={{0,8},{2,10},{4,12},{6,14},{8,0},{10,2},{12,4},{14,6},{16,24},{18,... | collective-permute-start | bytes 73736 | tf_op jit(solution)/shard_map/ppermute | solution.py:1014
  246.1 4.8 %collective-permute-start.45 = (f32[12,512]{1,0:T(8,128)S(1)}, f32[12,512]{1,0:T(8,128)S(1)}, u32[]{:S(2)}, u32[]{:S(2)}) collective-permute-start(f32[12,512]{1,0:T(8,128)S(1)} %add.254), channel_id=1, source_target_pairs={{0,16},{2,18},{4,20},{6,22},{8,24},{10,26},{12,28},{14,30},{16,0},... | collective-permute-start | bytes 73736 | tf_op jit(solution)/shard_map/ppermute | solution.py:1014
  251.4 45.5 %collective-permute-start.55 = (bf16[4,448,256]{2,1,0:T(8,128)(2,1)S(1)}, bf16[4,448,256]{2,1,0:T(8,128)(2,1)S(1)}, u32[]{:S(2)}, u32[]{:S(2)}) collective-permute-start(bf16[4,448,256]{2,1,0:T(8,128)(2,1)S(1)} %get-tuple-element.312), channel_id=1, source_target_pairs={{0,4},{2,6},{4,0},{6,2},{8,12},{10,14},{12,8},{14,10},{16,20},{18,... | collective-permute-start | bytes 2752520 | tf_op jit(solution)/shard_map/ppermute | solution.py:1014
  257.4 39.6 %collective-permute-start.56 = (bf16[8,288,256]{2,1,0:T(8,128)(2,1)S(1)}, bf16[8,288,256]{2,1,0:T(8,128)(2,1)S(1)}, u32[]{:S(2)}, u32[]{:S(2)}) collective-permute-start(bf16[8,288,256]{2,1,0:T(8,128)(2,1)S(1)} %get-tuple-element.316), channel_id=1, source_target_pairs={{0,2},{2,0},{4,6},{6,4},{8,10},{10,8},{12,14},{14,12},{16,18},{18,... | collective-permute-start | bytes 3538952 | tf_op jit(solution)/shard_map/ppermute | solution.py:1014
  257.5 30.1 %collective-permute-start.54 = (bf16[4,192,256]{2,1,0:T(8,128)(2,1)S(1)}, bf16[4,192,256]{2,1,0:T(8,128)(2,1)S(1)}, u32[]{:S(2)}, u32[]{:S(2)}) collective-permute-start(bf16[4,192,256]{2,1,0:T(8,128)(2,1)S(1)} %get-tuple-element.310), channel_id=1, source_target_pairs={{0,4},{2,6},{4,0},{6,2},{8,12},{10,14},{12,8},{14,10},{16,20},{18,... | collective-permute-start | bytes 1179656 | tf_op jit(solution)/shard_map/ppermute | solution.py:1014
  260.5 18.8 %collective-permute-start.50 = (f32[4,512]{1,0:T(4,128)S(1)}, f32[4,512]{1,0:T(4,128)S(1)}, u32[]{:S(2)}, u32[]{:S(2)}) collective-permute-start(f32[4,512]{1,0:T(4,128)S(1)} %add.262), channel_id=1, source_target_pairs={{0,4},{2,6},{4,0},{6,2},{8,12},{10,14},{12,8},{14,10},{16,20},{18,... | collective-permute-start | bytes 24584 | tf_op jit(solution)/shard_map/ppermute | solution.py:1014
  279.3 3.7 %collective-permute-start.51 = (f32[4,512]{1,0:T(4,128)S(1)}, f32[4,512]{1,0:T(4,128)S(1)}, u32[]{:S(2)}, u32[]{:S(2)}) collective-permute-start(f32[4,512]{1,0:T(4,128)S(1)} %add.263), channel_id=1, source_target_pairs={{0,8},{2,10},{4,12},{6,14},{8,0},{10,2},{12,4},{14,6},{16,24},{18,... | collective-permute-start | bytes 24584 | tf_op jit(solution)/shard_map/ppermute | solution.py:1014
  283.1 4.5 %collective-permute-start.52 = (f32[4,512]{1,0:T(4,128)S(1)}, f32[4,512]{1,0:T(4,128)S(1)}, u32[]{:S(2)}, u32[]{:S(2)}) collective-permute-start(f32[4,512]{1,0:T(4,128)S(1)} %add.264), channel_id=1, source_target_pairs={{0,16},{2,18},{4,20},{6,22},{8,24},{10,26},{12,28},{14,30},{16,0},... | collective-permute-start | bytes 24584 | tf_op jit(solution)/shard_map/ppermute | solution.py:1014
  284.3 12.5 %collective-permute-start.53 = (bf16[2,416,256]{2,1,0:T(8,128)(2,1)S(1)}, bf16[2,416,256]{2,1,0:T(8,128)(2,1)S(1)}, u32[]{:S(2)}, u32[]{:S(2)}) collective-permute-start(bf16[2,416,256]{2,1,0:T(8,128)(2,1)S(1)} %get-tuple-element.308), channel_id=1, source_target_pairs={{0,8},{2,10},{4,12},{6,14},{8,0},{10,2},{12,4},{14,6},{16,24},{18,... | collective-permute-start | bytes 1277960 | tf_op jit(solution)/shard_map/ppermute | solution.py:1014
  297.2 14.4 %collective-permute-start.66 = (bf16[2,192,256]{2,1,0:T(8,128)(2,1)S(1)}, bf16[2,192,256]{2,1,0:T(8,128)(2,1)S(1)}, u32[]{:S(2)}, u32[]{:S(2)}) collective-permute-start(bf16[2,192,256]{2,1,0:T(8,128)(2,1)S(1)} %get-tuple-element.349), channel_id=1, source_target_pairs={{0,8},{2,10},{4,12},{6,14},{8,0},{10,2},{12,4},{14,6},{16,24},{18,... | collective-permute-start | bytes 589832 | tf_op jit(solution)/shard_map/ppermute | solution.py:1014
  297.7 35.2 %collective-permute-start.68 = (bf16[1,416,256]{2,1,0:T(8,128)(2,1)S(1)}, bf16[1,416,256]{2,1,0:T(8,128)(2,1)S(1)}, u32[]{:S(2)}, u32[]{:S(2)}) collective-permute-start(bf16[1,416,256]{2,1,0:T(8,128)(2,1)S(1)} %get-tuple-element.354), channel_id=1, source_target_pairs={{0,16},{2,18},{4,20},{6,22},{8,24},{10,26},{12,28},{14,30},{16,0},... | collective-permute-start | bytes 638984 | tf_op jit(solution)/shard_map/ppermute | solution.py:1014
  300.1 14.2 %collective-permute-start.57 = (bf16[4,288,256]{2,1,0:T(8,128)(2,1)S(1)}, bf16[4,288,256]{2,1,0:T(8,128)(2,1)S(1)}, u32[]{:S(2)}, u32[]{:S(2)}) collective-permute-start(bf16[4,288,256]{2,1,0:T(8,128)(2,1)S(1)} %get-tuple-element.318), channel_id=1, source_target_pairs={{0,4},{2,6},{4,0},{6,2},{8,12},{10,14},{12,8},{14,10},{16,20},{18,... | collective-permute-start | bytes 1769480 | tf_op jit(solution)/shard_map/ppermute | solution.py:1014
  303.5 10.7 %collective-permute-start.58 = (bf16[8,64,256]{2,1,0:T(8,128)(2,1)S(1)}, bf16[8,64,256]{2,1,0:T(8,128)(2,1)S(1)}, u32[]{:S(2)}, u32[]{:S(2)}) collective-permute-start(bf16[8,64,256]{2,1,0:T(8,128)(2,1)S(1)} %get-tuple-element.324), channel_id=1, source_target_pairs={{0,2},{2,0},{4,6},{6,4},{8,10},{10,8},{12,14},{14,12},{16,18},{18,... | collective-permute-start | bytes 786440 | tf_op jit(solution)/shard_map/ppermute | solution.py:1014
  303.5 14.6 %collective-permute-start.64 = (bf16[2,448,256]{2,1,0:T(8,128)(2,1)S(1)}, bf16[2,448,256]{2,1,0:T(8,128)(2,1)S(1)}, u32[]{:S(2)}, u32[]{:S(2)}) collective-permute-start(bf16[2,448,256]{2,1,0:T(8,128)(2,1)S(1)} %get-tuple-element.337), channel_id=1, source_target_pairs={{0,8},{2,10},{4,12},{6,14},{8,0},{10,2},{12,4},{14,6},{16,24},{18,... | collective-permute-start | bytes 1376264 | tf_op jit(solution)/shard_map/ppermute | solution.py:1014
  311.6 22.2 %collective-permute-start.67 = (bf16[1,192,256]{2,1,0:T(8,128)(2,1)S(1)}, bf16[1,192,256]{2,1,0:T(8,128)(2,1)S(1)}, u32[]{:S(2)}, u32[]{:S(2)}) collective-permute-start(bf16[1,192,256]{2,1,0:T(8,128)(2,1)S(1)} %get-tuple-element.390), channel_id=1, source_target_pairs={{0,16},{2,18},{4,20},{6,22},{8,24},{10,26},{12,28},{14,30},{16,0},... | collective-permute-start | bytes 294920 | tf_op jit(solution)/shard_map/ppermute | solution.py:1014
  314.3 5.4 %collective-permute-start.59 = (bf16[4,64,256]{2,1,0:T(8,128)(2,1)S(1)}, bf16[4,64,256]{2,1,0:T(8,128)(2,1)S(1)}, u32[]{:S(2)}, u32[]{:S(2)}) collective-permute-start(bf16[4,64,256]{2,1,0:T(8,128)(2,1)S(1)} %get-tuple-element.329), channel_id=1, source_target_pairs={{0,4},{2,6},{4,0},{6,2},{8,12},{10,14},{12,8},{14,10},{16,20},{18,... | collective-permute-start | bytes 393224 | tf_op jit(solution)/shard_map/ppermute | solution.py:1014
  315.1 14.7 %collective-permute-start.62 = (bf16[2,288,256]{2,1,0:T(8,128)(2,1)S(1)}, bf16[2,288,256]{2,1,0:T(8,128)(2,1)S(1)}, u32[]{:S(2)}, u32[]{:S(2)}) collective-permute-start(bf16[2,288,256]{2,1,0:T(8,128)(2,1)S(1)} %get-tuple-element.333), channel_id=1, source_target_pairs={{0,8},{2,10},{4,12},{6,14},{8,0},{10,2},{12,4},{14,6},{16,24},{18,... | collective-permute-start | bytes 884744 | tf_op jit(solution)/shard_map/ppermute | solution.py:1014
  318.1 16.3 %collective-permute-start.65 = (bf16[1,448,256]{2,1,0:T(8,128)(2,1)S(1)}, bf16[1,448,256]{2,1,0:T(8,128)(2,1)S(1)}, u32[]{:S(2)}, u32[]{:S(2)}) collective-permute-start(bf16[1,448,256]{2,1,0:T(8,128)(2,1)S(1)} %get-tuple-element.380), channel_id=1, source_target_pairs={{0,16},{2,18},{4,20},{6,22},{8,24},{10,26},{12,28},{14,30},{16,0},... | collective-permute-start | bytes 688136 | tf_op jit(solution)/shard_map/ppermute | solution.py:1014
  319.8 11.6 %collective-permute-start.60 = (bf16[2,64,256]{2,1,0:T(8,128)(2,1)S(1)}, bf16[2,64,256]{2,1,0:T(8,128)(2,1)S(1)}, u32[]{:S(2)}, u32[]{:S(2)}) collective-permute-start(bf16[2,64,256]{2,1,0:T(8,128)(2,1)S(1)} %get-tuple-element.393), channel_id=1, source_target_pairs={{0,8},{2,10},{4,12},{6,14},{8,0},{10,2},{12,4},{14,6},{16,24},{18,... | collective-permute-start | bytes 196616 | tf_op jit(solution)/shard_map/ppermute | solution.py:1014
  329.9 10.0 %collective-permute-start.63 = (bf16[1,288,256]{2,1,0:T(8,128)(2,1)S(1)}, bf16[1,288,256]{2,1,0:T(8,128)(2,1)S(1)}, u32[]{:S(2)}, u32[]{:S(2)}) collective-permute-start(bf16[1,288,256]{2,1,0:T(8,128)(2,1)S(1)} %get-tuple-element.386), channel_id=1, source_target_pairs={{0,16},{2,18},{4,20},{6,22},{8,24},{10,26},{12,28},{14,30},{16,0},... | collective-permute-start | bytes 442376 | tf_op jit(solution)/shard_map/ppermute | solution.py:1014
  331.4 7.9 %collective-permute-start.61 = (bf16[1,64,256]{2,1,0:T(8,128)(2,1)S(1)}, bf16[1,64,256]{2,1,0:T(8,128)(2,1)S(1)}, u32[]{:S(2)}, u32[]{:S(2)}) collective-permute-start(bf16[1,64,256]{2,1,0:T(8,128)(2,1)S(1)} %get-tuple-element.394), channel_id=1, source_target_pairs={{0,16},{2,18},{4,20},{6,22},{8,24},{10,26},{12,28},{14,30},{16,0},... | collective-permute-start | bytes 98312 | tf_op jit(solution)/shard_map/ppermute | solution.py:1014
  (11 other events, 56.9 us)

commit v3 on v2

--- a/solution.py
+++ b/solution.py
@@ -14,6 +14,8 @@
 B = 4
 POS = 56
 LIMIT = 14
+SCALE = 0.01
+UNROLL = 2
 M = B * POS
 HALF = 112
 HROWS = B * HALF
@@ -22,7 +24,7 @@
 ANY = pl.BlockSpec(memory_space=pl.ANY)
 INV_IN, INV_OUT, CELLS, MICRO, INV_ALL = 0, 2, 4, 8, 12
 NARROW, CORE, DEST = 0, 1, 2
-W6_AT, EX_AT, SQ_AT, VEC_AT, PACK_ROWS = 2304, 3328, 3584, 3840, 3856
+W6_AT, EX_AT, SQ_AT, VEC_AT, PACK_ROWS = 0, 1024, 1280, 1536, 1552
 
 
 def mm(a, b):
@@ -145,11 +147,12 @@
 
 
 def loop(count, body):
-    lax.fori_loop(0, count, lambda c, _: (body(c), 0)[1], 0)
+    lax.fori_loop(0, count, lambda c, _: (body(c), 0)[1], 0, unroll=UNROLL)
 
 
 def loop_from(first, last, body):
-    lax.fori_loop(first, last, lambda c, _: (body(c), 0)[1], 0)
+    for c in range(first, last):
+        body(c)
 
 
 def copy_all(pairs, sems):
@@ -395,20 +398,18 @@
     put(st, 0, stat_rows(acc[...], keep[...], fs), slice(0, 512))
 
 
-def fetch_five_kernel(isc, own, r1, r2, w5, vaway, sems):
+def fetch_five_kernel(isc, own, r1, r2, w5, sems):
     n, core = isc[NARROW], isc[CORE]
     wait_all(copy_all([
-        (r1.at[VEC_AT:PACK_ROWS], vaway),
         (own, w5.at[n]),
-        (r1.at[0:2304], w5.at[1 - n, at_rows(core * 2304, 2304)]),
-        (r2.at[0:2304], w5.at[1 - n, at_rows((1 - core) * 2304, 2304)]),
+        (r1, w5.at[1 - n, at_rows(core * 2304, 2304)]),
+        (r2, w5.at[1 - n, at_rows((1 - core) * 2304, 2304)]),
     ], sems))
 
 
 def stage_five_kernel(
-    fs, isc, parts, pre4, keep, gb, sh, vown, vaway, w5, col, pre5, st, tot4, gain5, vec2, tot,
+    fs, parts, pre4, keep, gb, sh, w5, col, pre5, st, tot4, tot
 ):
-    n = isc[NARROW]
     add_parts(parts, tot)
     tot4[...] = tot[...]
     mean, scale = coefs(tot, 0, slice(0, 512), fs, INV_OUT)
@@ -416,14 +417,6 @@
     h = low(o * sigmoid(o) * keep[...])
     for t in range(9):
         col[t] = h if t == 4 else low(mm(sh[t], h))
-    for side, v in ((n, f32(vown[...])), (1 - n, f32(vaway[...]))):
-        for k in range(2):
-            gain5[k : k + 1, cols(side)] = v[k : k + 1]
-        for k in range(3):
-            for c in range(4):
-                at = 2 + 4 * k + c
-                vec2[k : k + 1, cols(side * 4 + c)] = v[at : at + 1]
-
     def body(c):
         v = 0.0
         for t in range(9):
@@ -434,9 +427,9 @@
     loop(2, body)
 
 
-def fetch_six_kernel(isc, own, r1, r2, w6, sems):
+def fetch_six_kernel(isc, own, r1, r2, vown, w6, gain5, vec2, vaway, sems):
     n, core = isc[NARROW], isc[CORE]
-    pairs = [(own, w6.at[at_rows(n * 256, 256)])]
+    pairs = [(r1.at[VEC_AT:PACK_ROWS], vaway), (own, w6.at[at_rows(n * 256, 256)])]
     for r, h in ((r1, core), (r2, 1 - core)):
         for c in range(8):
             pairs.append(
@@ -445,7 +438,16 @@
                     w6.at[at_rows((1 - n) * 256 + h * 128, 128), c * 256 : (c + 1) * 256],
                 )
             )
-    wait_all(copy_all(pairs, sems))
+    copies = copy_all(pairs, sems)
+    copies[0].wait()
+    for side, v in ((n, f32(vown[...])), (1 - n, f32(vaway[...]))):
+        for k in range(2):
+            gain5[k : k + 1, cols(side)] = v[k : k + 1]
+        for k in range(3):
+            for c in range(4):
+                at = 2 + 4 * k + c
+                vec2[k : k + 1, cols(side * 4 + c)] = v[at : at + 1]
+    wait_all(copies[1:])
 
 
 def stage_six_kernel(
@@ -806,7 +808,7 @@
     deal(isc, full, 64, gkeep, gsend, 0)
 
 
-def image_kernel(isc, perm, d1, dproj, keep, w1, wp_far, out, dc, cc, pick_own, spread, wp, sems):
+def placed_kernel(isc, dproj, wp_far, out, cc, pick_own, spread, wp, sems):
     n = isc[NARROW]
     copies = [
         pltpu.make_async_copy(wp_far.at[cut], wp.at[cut], sems.at[k])
@@ -815,7 +817,6 @@
     for c in copies:
         c.start()
     for b in range(B):
-        dc[b * HALF : (b + 1) * HALF, :] = low(mm_tn(perm[n], d1[b]))
         place = lax.broadcasted_iota(jnp.int32, (32, M), 1)
         it = lax.broadcasted_iota(jnp.int32, (32, M), 0)
         pick_own[b * 32 : (b + 1) * 32, :] = low(jnp.where(
@@ -827,16 +828,20 @@
             ((it & 9) == 0) & (place == b * 32 + (it >> 4) * 4 + ((it & 7) >> 1)), 1.0, 0.0
         ))
     cc[...] = low(mm(pick_own[...], dproj[...]))
-
-    def body(c):
-        sl = cols(c)
+    for c in range(4):
+        sl = cols(c)
+        copies[c].wait()
         hi, lo = split2(mm_nt(cc[...], wp[sl, :]))
-        v = mm_nt(dc[...], w1[sl, :]) + mm(spread[...], hi) + mm(spread[...], lo)
-        out[:, sl] = v * keep[...]
-
+        out[:, sl] = mm(spread[...], hi) + mm(spread[...], lo)
+
+
+def image_kernel(isc, perm, d1, placed, keep, w1, out, dc):
+    n = isc[NARROW]
+    for b in range(B):
+        dc[b * HALF : (b + 1) * HALF, :] = low(mm_tn(perm[n], d1[b]))
     for c in range(4):
-        copies[c].wait()
-        body(c)
+        sl = cols(c)
+        out[:, sl] = (mm_nt(dc[...], w1[sl, :]) + placed[:, sl]) * keep[...]
 
 
 def grads_a_kernel(isc, h5, d6, col4, d5, gkeep, gsend, wider, full):
@@ -870,22 +875,23 @@
         (gkeep if p < 8 else gsend)[p % 8, at_rows(at + c * 16, 16), :] = low(both)
 
 
-def grads_b_kernel(isc, d4, lows, squeezed, pooled, de, ds, gkeep, gsend, full, q, e):
+def grads_b_kernel(
+    isc, d4, lows, sq2, pooled2, de2, ds2, sp1, pooled1, de1, ds1, gkeep, gsend, full, q, e, sq1
+):
     n = isc[NARROW]
+    sq1[...] = sp1[...] * sigmoid(sp1[...])
 
     def body(c):
         full[...] = low(mm_tn(d4[...], lows[:, cols(n * 4 + c)]))
         deal(isc, full, 32, gkeep, gsend, c * 32)
-        gate_grads(isc, n, c, 128, squeezed, pooled, de, ds, gkeep, gsend, q, e)
+        gate_grads(isc, n, c, 128, sq2, pooled2, de2, ds2, gkeep, gsend, q, e)
+        gate_grads(isc, n, c, 192, sq1, pooled1, de1, ds1, gkeep, gsend, q, e)
 
     loop(4, body)
 
 
-def grads_c_kernel(
-    isc, h2, d3, strided, dproj, sp, pooled, de, ds, gkeep, gsend, full, taller, q, e, squeezed
-):
+def grads_c_kernel(isc, h2, d3, strided, dproj, gkeep, gsend, full, taller):
     n = isc[NARROW]
-    squeezed[...] = sp[...] * sigmoid(sp[...])
 
     def body(c):
         sl = cols(n * 4 + c)
@@ -893,7 +899,6 @@
         deal(isc, full, 32, gkeep, gsend, c * 32)
         taller[...] = low(mm_tn(strided[...], dproj[:, sl]))
         deal(isc, taller, 64, gkeep, gsend, 128 + c * 64)
-        gate_grads(isc, n, c, 384, squeezed, pooled, de, ds, gkeep, gsend, q, e)
 
     loop(4, body)
 
@@ -927,17 +932,17 @@
     spatial2[...] = v[128:416, :]
 
 
-def unpack_b_kernel(a, b, reduce2, squeeze2, excite2):
+def unpack_b_kernel(a, b, reduce2, squeeze2, excite2, squeeze1, excite1):
     v = f32(a[0]) + f32(b[0])
     joined(v, reduce2, 0, 32)
     unpack_gates(v, 128, squeeze2, excite2)
-
-
-def unpack_c_kernel(a, b, expand1, project1, squeeze1, excite1):
+    unpack_gates(v, 192, squeeze1, excite1)
+
+
+def unpack_c_kernel(a, b, expand1, project1):
     v = f32(a[0]) + f32(b[0])
     joined(v, expand1, 0, 32)
     joined(v, project1, 128, 64)
-    unpack_gates(v, 384, squeeze1, excite1)
 
 
 def unpack_d_kernel(a, b, spatial1):
@@ -949,15 +954,15 @@
 
 def pack_kernel(isc, w5, w4, w6, ex, sq, ws_far, *refs):
     far, refs = refs[:18], refs[18:]
-    out, w4_half, gb, vec1, sqb, vown, ws, w6v, exv, sqv, rows = refs[:11]
-    vecs, sems = refs[11:29], refs[29]
+    out, w5_half, w4_half, gb, vec1, sqb, vown, ws, w6v, exv, sqv, rows = refs[:12]
+    vecs, sems = refs[12:30], refs[30]
     core = isc[CORE]
     pairs = [(f, v) for f, v in zip(far, vecs)] + [
         (w6.at[at_rows(core * 128, 128)], w6v),
         (ex.at[at_rows(core * 64, 64)], exv),
         (sq.at[at_rows(core * 512, 512)], sqv),
         (w4.at[at_rows(core * 512, 512)], w4_half),
-        (w5.at[at_rows(core * 2304, 2304)], out.at[0:W6_AT]),
+        (w5.at[at_rows(core * 2304, 2304)], w5_half),
         (ws_far, ws),
     ]
     copies = copy_all(pairs, sems)
@@ -1004,7 +1009,7 @@
         scratch_shapes=list(scratch),
         compiler_params=pltpu.CompilerParams(vmem_limit_bytes=vmem * 2**20),
         cost_estimate=pl.CostEstimate(
-            flops=int(flops), bytes_accessed=int(size), transcendentals=0
+            flops=int(flops * SCALE), bytes_accessed=int(size * SCALE), transcendentals=0
         ),
         name=name,
     )(*values)
@@ -1035,7 +1040,6 @@
     exact = wide == 16
     near = [(i, i ^ 1) for i in range(wide)]
     pair = [(0, 1), (1, 0)]
-    groups = [list(range(k, wide, 2)) for k in range(2)]
     V = pltpu.VMEM
     D = pltpu.SemaphoreType.DMA
     out = lambda *shape: (shape, F32)
@@ -1043,18 +1047,15 @@
     h = lambda *shape: V(shape, BF)
     far = lambda v: (ANY, pltpu.with_memory_space_constraint(v, pltpu.HBM))
 
-    def across(x):
-        x = x + swap(x, "wide", near)
-        sent = jnp.broadcast_to(x[None], (wide // 2,) + x.shape)
-        got = lax.all_to_all(sent, "wide", 0, 0, axis_index_groups=groups, tiled=True)
-        return got if exact else jnp.sum(got, axis=0, keepdims=True)
-
-    def steps(x):
-        step = 1
+    def steps(x, *first, before=None):
+        results, step = [], 1
+        x = after(x, *first)
         while step < wide:
-            x = x + swap(x, "wide", [(i, i ^ step) for i in range(wide)])
+            y = after(x, *(before or {}).get(len(results), ()))
+            x = x + swap(y, "wide", [(i, i ^ step) for i in range(wide)])
+            results.append(x)
             step *= 2
-        return x[None]
+        return x[None], results
 
     own_px = images.transpose(0, 2, 1, 3).reshape(B, HALF, 1024)
     other_px = swap(own_px, "narrow", pair)
@@ -1074,7 +1075,7 @@
         [fs, far(own_px), keep_half, far(first_reduce)],
         [V((HROWS, 1024), BF), D((2,))], flops=5e8, name="one_half",
     )
-    part = steps(st1)[0]
+    part = steps(st1)[0][0]
 
     w5_own = second_spatial.reshape(9 * 512, 256)
     vectors = [
@@ -1084,10 +1085,10 @@
         first_squeeze_bias, second_squeeze_bias,
         second_spatial_gain, second_spatial_bias, second_expand_gain, second_expand_bias, second_excite_bias,
     ]
-    pack, w4_half, gb, vec1, sqb, vown, ws = call(
+    pack, w5_half, w4_half, gb, vec1, sqb, vown, ws = call(
         pack_kernel,
         [
-            ((PACK_ROWS, 256), BF), ((512, 512), BF), f(8, 512), f(8, 2048), f(8, 128), h(16, 256),
+            ((PACK_ROWS, 256), BF), ((2304, 256), BF), ((512, 512), BF), f(8, 512), f(8, 2048), f(8, 128), h(16, 256),
             h(9, 512, 512),
         ],
         [
@@ -1110,12 +1111,12 @@
         [V((4, M, 256), F32), V((4, M, 512), BF), V((4, 512), F32)],
         flops=4e9, size=2e7, name="stage_two",
     )
-    parts2 = steps(st2)
-    w4_r2 = swap(after(w4_r1, st2), "wide", near)
-    pk1 = swap(after(pack, w4_r1, st2), "narrow", pair)
+    parts2, sent2 = steps(st2, before={3: (w4_r1,)})
+    w4_r2 = swap(after(w4_r1, sent2[1]), "wide", near)
+    w5_r1 = swap(after(w5_half, w4_r1, sent2[1]), "narrow", pair)
     prep, stp, w3 = call(
         project_kernel, [f(M, 2048), f(4, 2048), h(512, 2048)],
-        [fs, after(strided, w4_r1), keep, far(first_project), far(first_expand)],
+        [fs, strided, keep, far(first_project), far(first_expand)],
         [V((1024, 2048), BF), D((5,))], flops=1e9, size=8e6, name="project",
     )
     h2, pre3, st3, tot2 = call(
@@ -1123,10 +1124,12 @@
         [fs, parts2, pre2, stp, keep, w3, gb], [V((4, 512), F32)],
         flops=1e9, size=6e6, name="stage_three",
     )
-    parts3 = steps(st3)
+    parts3, _ = steps(st3, before={3: (w4_r2,)})
+    w5_r2 = swap(after(w5_r1, parts3), "wide", near)
+    pk1 = swap(after(pack, w5_r1, parts3), "narrow", pair)
     w4 = call(
         fetch_four_kernel, [h(2048, 512)],
-        [(SMEM, after(isc_, st3)), far(second_reduce), far(w4_r1), far(w4_r2)], [D((3,))],
+        [(SMEM, after(isc_, st3)), far(second_reduce), (ANY, w4_r1), (ANY, w4_r2)], [D((3,))],
         size=4e6, name="fetch_four",
     )[0]
     lows, pre4, st4, tot3, gate1, sp1, pooled1, squares = call(
@@ -1141,36 +1144,37 @@
         ],
         flops=1e9, size=1e7, name="stage_four",
     )
-    parts4 = steps(st4)
-    pk2 = swap(after(pk1, st4), "wide", near)
-    og_other = swap(after(og_own, pk1, st4), "narrow", pair)
-    pk1, pk2 = far(pk1), far(pk2)
-    w5, vaway = call(
-        fetch_five_kernel, [h(2, 4608, 256), h(16, 256)],
-        [(SMEM, after(isc_, st4)), far(w5_own), pk1, pk2], [D((4,))], size=8e6, name="fetch_five",
-    )
-    col4, pre5, st5, tot4, gain5, vec2 = call(
-        stage_five_kernel,
-        [h(9, M, 512), f(M, 512), f(4, 512), f(4, 512), f(2, 512), f(3, 2048)],
-        [fs, isc, parts4, pre4, keep, gb, sh, vown, vaway, w5], [V((4, 512), F32)],
+    parts4, _ = steps(st4, before={3: (w5_r2,)})
+    w5 = call(
+        fetch_five_kernel, [h(2, 4608, 256)],
+        [(SMEM, after(isc_, st4)), far(w5_own), (ANY, w5_r1), (ANY, w5_r2)], [D((3,))],
+        size=8e6, name="fetch_five",
+    )[0]
+    col4, pre5, st5, tot4 = call(
+        stage_five_kernel, [h(9, M, 512), f(M, 512), f(4, 512), f(4, 512)],
+        [fs, parts4, pre4, keep, gb, sh, w5], [V((4, 512), F32)],
         flops=2e9, size=1e7, name="stage_five",
     )
-    parts5 = steps(st5)
-    w6 = call(
-        fetch_six_kernel, [h(512, 2048)],
-        [(SMEM, after(isc_, st5)), far(second_expand), pk1, pk2], [D((17,))], size=4e6, name="fetch_six",
-    )[0]
+    pk2 = swap(after(pk1, st5), "wide", near)
+    parts5, _ = steps(st5, before={3: (pk2,)})
+    og_other = swap(after(og_own, pk1, st5), "narrow", pair)
+    pk1, pk2 = (ANY, pk1), (ANY, pk2)
+    w6, gain5, vec2 = call(
+        fetch_six_kernel, [h(512, 2048), f(2, 512), f(3, 2048)],
+        [(SMEM, after(isc_, st5)), far(second_expand), pk1, pk2, vown],
+        [V((16, 256), BF), D((18,))], size=4e6, name="fetch_six",
+    )
     h5, pre6, st6, tot5 = call(
         stage_six_kernel, [h(M, 512), f(M, 2048), f(4, 2048), f(4, 512)],
         [fs, parts5, pre5, keep, gain5, w6], [V((4, 512), F32)],
         flops=1e9, size=6e6, name="stage_six",
     )
-    parts6 = steps(st6)
+    parts6, _ = steps(st6)
     sq, ex, og = call(
         fetch_turn_kernel, [h(2048, 128), h(2, 128, 1024), h(2, M, 1024)],
         [
             (SMEM, after(isc_, st6)), far(second_squeeze), far(second_excite), pk1, pk2,
-            far(og_own), far(og_other),
+            far(og_own), (ANY, og_other),
         ],
         [D((16,))], size=4e6, name="fetch_turn",
     )
@@ -1184,14 +1188,14 @@
         [V((M, 2048), F32), V((2, M, 1024), BF), V((4, 2048), F32), V((8, 128), F32)],
         flops=1e9, size=1e7, name="turn",
     )
-    back6 = across(pay6)
+    back6, _ = steps(pay6)
     d6, do5, bt5, dgain6, dbias6 = call(
         back_six_kernel, [h(M, 2048), f(M, 512), f(12, 512), out(1024), out(1024)],
         [fs, isc, back6, tot6, pre6, dj2, gate2, dp2, pre5, tot5, extra6, keep, vec2, gain5, w6],
         [V((4, 2048), F32), V((M, 512), F32)],
         flops=1e9, size=1e7, name="back_six",
     )
-    back5 = across(bt5)
+    back5, _ = steps(bt5)
     d5, do4, bt4, dgain5, dbias5, debias2, dsbias2, norms = call(
         back_five_kernel,
         [h(M, 512), f(M, 512), f(4, 512), out(256), out(256), out(1024), out(128), ((5,), F32, SMEM)],
@@ -1199,23 +1203,25 @@
         [V((12, 512), F32)],
         flops=2e9, size=1e7, name="back_five",
     )
-    back4 = steps(bt4)
-
-    def step(g, k):
+
+    def step(g, k, *ties):
         if not exact:
-            return g
+            return g, ()
         kept, sent = g
-        got = swap(sent, "wide", [(i, i ^ (1 << k)) for i in range(wide)])
+        got = swap(after(sent, *ties), "wide", [(i, i ^ (1 << k)) for i in range(wide)])
         if k == 3:
-            return kept, got
+            return (kept, got), (got,)
         half = kept.shape[0] // 2
-        return kept[:half] + got[:half], kept[half:] + got[half:]
+        return (kept[:half] + got[:half], kept[half:] + got[half:]), (got,)
 
     ga = call(
         grads_a_kernel, [h(8, 416, 256)] * 2, [isc, h5, d6, col4, d5],
         [V((256, 2048), BF), V((512, 256), BF)], flops=2e9, size=1e7, name="grads_a",
     )
-    back4, ga = lax.optimization_barrier((back4, ga))
+    back4, sent4 = steps(bt4, *ga)
+    ga, _ = step(ga, 0, sent4[0])
+    back4 = after(back4, *ga)
+    ga, xa = step(ga, 1, sent4[1])
     d4, dj1, bt3, dgain4, dbias4, dp1, de1, ds1, bias1 = call(
         back_four_kernel,
         [
@@ -1229,14 +1235,16 @@
         [V((4, 512), F32), V((2048, 128), BF), V((128, 2048), BF), D((2,))],
         flops=1e9, size=1e7, name="back_four",
     )
-    back3 = steps(bt3)
-    ga = step(ga, 0)
     gb1 = call(
-        grads_b_kernel, [h(8, 192, 256)] * 2, [isc, d4, lows, sq2, pooled2, de2, ds2],
-        [V((512, 256), BF), V((128, 256), F32), V((128, 256), F32)],
+        grads_b_kernel, [h(8, 256, 256)] * 2,
+        [isc, d4, lows, sq2, pooled2, de2, ds2, sp1, pooled1, de1, ds1],
+        [V((512, 256), BF), V((128, 256), F32), V((128, 256), F32), V((8, 128), F32)],
         flops=1e9, size=4e6, name="grads_b",
     )
-    back3, ga, gb1 = lax.optimization_barrier((back3, ga, gb1))
+    back3, sent3 = steps(bt3, *gb1, before={1: xa})
+    gb1, _ = step(gb1, 0, sent3[0])
+    back3 = after(back3, *gb1)
+    ga, za = step(ga, 2, sent3[3])
     d3, dproj, do2, bt2, dgain3, dbias3, dgainp, dbiasp = call(
         back_three_kernel,
         [h(M, 2048), h(M, 2048), f(M, 512), f(12, 512), out(2048), out(2048), out(2048), out(2048)],
@@ -1244,16 +1252,15 @@
         [V((8, 2048), F32), V((M, 512), F32)],
         flops=1e9, size=1e7, name="back_three",
     )
-    back2 = steps(bt2)
-    ga, gb1 = step(ga, 1), step(gb1, 0)
     gc = call(
-        grads_c_kernel, [h(8, 448, 256)] * 2,
-        [isc, h2, d3, strided, dproj, sp1, pooled1, de1, ds1],
-        [V((512, 256), BF), V((1024, 256), BF), V((128, 256), F32), V((128, 256), F32), V((8, 128), F32)],
+        grads_c_kernel, [h(8, 384, 256)] * 2, [isc, h2, d3, strided, dproj],
+        [V((512, 256), BF), V((1024, 256), BF)],
         flops=3e9, size=1e7, name="grads_c",
     )
-    gc = step(gc, 0)
-    back2, ga, gb1, gc = lax.optimization_barrier((back2, ga, gb1, gc))
+    back2, sent2 = steps(bt2, *gc, *za)
+    gc, _ = step(gc, 0, sent2[0])
+    back2 = after(back2, *gc)
+    gc, xc = step(gc, 1, sent2[1])
     ws_back = call(
         fetch_two_kernel, [h(9, 512, 512)], [far(after(ws_far, bt2))], [D((3,))], size=9e6, name="fetch_two",
     )[0]
@@ -1264,14 +1271,24 @@
         [V((12, 512), F32), V((4, M, 512), BF)],
         flops=2e9, size=1e7, name="back_two",
     )
-    back1 = steps(bt1)
-    ga, gb1, gc = step(ga, 2), step(gb1, 1), step(gc, 1)
     gd = call(
         grads_d_kernel, [h(8, 288, 256)] * 2, [isc, col1, d2], [V((512, 256), BF)],
         flops=2e9, size=6e6, name="grads_d",
     )
-    gd = step(gd, 0)
-    back1, ga, gb1, gc, gd = lax.optimization_barrier((back1, ga, gb1, gc, gd))
+    back1, sent1 = steps(bt1, *gd, before={1: xc})
+    gd, _ = step(gd, 0)
+    gd0 = gd
+    gd, xd = step(gd, 1, sent1[2])
+    gb1, _ = step(gb1, 1, sent1[2])
+    gc, _ = step(gc, 2, sent1[3])
+    ga, _ = step(ga, 3, sent1[3])
+    back1 = after(back1, *gd0)
+    placed = call(
+        placed_kernel, [f(HROWS, 1024)], [(SMEM, after(isc_, sent1[2])), dproj, far(first_project)],
+        [V((128, 2048), BF), V((128, M), BF), V((HROWS, 128), BF), V((1024, 2048), BF), D((4,))],
+        flops=1e9, size=1e7, name="placed",
+    )[0]
+    back1, placed = lax.optimization_barrier((back1, placed))
     d1, ge_keep, ge_send, dgain1, dbias1 = call(
         back_one_kernel, [h(B, M, 512), h(8, 64, 256), h(8, 64, 256), out(512), out(512)],
         [fs, isc, back1, tot1, x1, do1, xp, keep1, gb],
@@ -1280,32 +1297,32 @@
     )
     ge = (ge_keep, ge_send)
     dimg = call(
-        image_kernel, [out(HROWS, 1024)],
-        [isc, perm, d1, dproj, keep_half, w1, far(after(first_project, bt1))],
-        [
-            V((HROWS, 512), BF), V((128, 2048), BF), V((128, M), BF), V((HROWS, 128), BF),
-            V((1024, 2048), BF), D((4,)),
-        ],
-        flops=1e9, size=1e7, name="image",
+        image_kernel, [out(HROWS, 1024)], [isc, perm, d1, placed, keep_half, w1],
+        [V((HROWS, 512), BF)], flops=1e9, size=1e7, name="image",
     )[0]
 
     if exact:
-        ge, gd = step(ge, 0), step(gd, 1)
-        gd, ge, dimg = lax.optimization_barrier((gd, ge, dimg))
-        ge = step(step(ge, 1), 2)
-        gd, gb1, gc = step(gd, 2), step(gb1, 2), step(gc, 2)
+        ge, _ = step(ge, 0)
+        dimg, *ge = lax.optimization_barrier((dimg,) + ge)
+        gb1, _ = step(gb1, 2)
+        gd, _ = step(gd, 2)
+        gc, _ = step(gc, 3)
+        gb1, _ = step(gb1, 3)
+        ge, _ = step(ge, 1)
+        ge, _ = step(ge, 2)
+        gd, _ = step(gd, 3)
+        ge, _ = step(ge, 3)
         expand2, spatial2 = call(
-            unpack_a_kernel, [out(256, 128), out(288, 256)], list(step(ga, 3)), name="unpack_a"
+            unpack_a_kernel, [out(256, 128), out(288, 256)], list(ga), name="unpack_a"
         )
-        reduce2, squeeze2, excite2 = call(
-            unpack_b_kernel, [out(32, 1024), out(8, 1024), out(8, 1024)], list(step(gb1, 3)), name="unpack_b"
+        reduce2, squeeze2, excite2, squeeze1, excite1 = call(
+            unpack_b_kernel, [out(32, 1024)] + [out(8, 1024)] * 4, list(gb1), name="unpack_b"
         )
-        expand1, project1, squeeze1, excite1 = call(
-            unpack_c_kernel, [out(32, 1024), out(64, 1024), out(8, 1024), out(8, 1024)], list(step(gc, 3)),
-            name="unpack_c",
+        expand1, project1 = call(
+            unpack_c_kernel, [out(32, 1024), out(64, 1024)], list(gc), name="unpack_c"
         )
-        spatial1 = call(unpack_d_kernel, [out(288, 256)], list(step(gd, 3)), name="unpack_d")[0]
-        reduce1 = call(unpack_d_kernel, [out(64, 256)], list(step(ge, 3)), name="unpack_e")[0]
+        spatial1 = call(unpack_d_kernel, [out(288, 256)], list(gd), name="unpack_d")[0]
+        reduce1 = call(unpack_d_kernel, [out(64, 256)], list(ge), name="unpack_e")[0]
     else:
         finer = wide // 16
 
@@ -1334,7 +1351,7 @@
         reduce2 = blocks(gb1, 0, 4, 32)
         squeeze2, excite2 = both(gb1, 128)
         expand1, project1 = blocks(gc, 0, 4, 32), blocks(gc, 128, 4, 64)
-        squeeze1, excite1 = both(gc, 384)
+        squeeze1, excite1 = both(gb1, 192)
         spatial1, reduce1 = taps(gd, 0), blocks(ge, 0, 1, 64)
     return (
         result.reshape(B, 7, 8, 1024).transpose(0, 2, 1, 3),

time: 341 us -> 302 us (0.89)
  blocking collectives: 27.8 us -> 0 us
  starting transfers between devices: 69.3 us -> 88.9 us
  waiting for transfers between devices: 146 us -> 129 us
  Pallas kernels: 91.8 us -> 80.4 us
    all_to_all x2 -> x0, blocking collectives: 27.8 us -> none  [across(): lax.all_to_all(sent, 'wide', 0, 0, axis_index_groups=groups, tiled=True)]
    ppermute x69 -> x77, starting transfers between devices: 69.3 us -> 88.9 us  [swap(): return lax.ppermute(v, axis, pairs)]
    ppermute x69 -> x77, waiting for transfers between devices: 146 us -> 129 us  [swap(): return lax.ppermute(v, axis, pairs)]
    pallas_call x31 -> x32, Pallas kernels: 91.8 us -> 80.4 us  [call(): pl.pallas_call(body, out_shape=tuple((o if hasattr(o, 'memory_space') els...]
  transfers between devices with their start and end apart: 69 -> 77, of which waited for: 47 -> 55; matrix products, arithmetic and copies ran while one was open for 0% -> 0% of each run, Pallas kernels for 20% -> 21%
where the time goes in v3:
time: 302 us; the launch traced here: 301 us
  waiting for transfers between devices  129 us (43%)
  starting transfers between devices  88.9 us (29%)
  Pallas kernels  80.4 us (27%)
    ppermute x77, waiting for transfers between devices, swap(): return lax.ppermute(v, axis, pairs)  129 us
    ppermute x77, starting transfers between devices, swap(): return lax.ppermute(v, axis, pairs)  88.9 us
    pallas_call x32, Pallas kernels, call(): pl.pallas_call(body, out_shape=tuple((o if hasattr(o, 'memory_space') els...  80.4 us
  transfers between devices with their start and end apart: 77, of which 55 were waited for; matrix products, arithmetic and copies ran while one was open for 0% of the time, Pallas kernels for 21%

profile of v3, /device:TPU:0, one launch (start us, length us, event | category | flops | bytes accessed | tf_op | source)
XLA Modules:
  0.0 301.2 jit_solution(10640758153965371431)
XLA Ops:
  0.7 3.0 %collective-permute-start = (bf16[4,112,1024]{2,1,0:T(8,128)(2,1)}, bf16[4,112,1024]{2,1,0:T(8,128)(2,1)S(1)}, u32[]{:S(2)}, u32[]{:S(2)}) collective-permute-start(bf16[4,112,1024]{2,1,0:T(8,128)(2,1)} %bitcast.46), channel_id=1, source_target_pairs={{0,1},{1,0},{2,3},{3,2},{4,5},{5,4},{6,7},{7,6},{8,9},{9,8},{10,11... | collective-permute-start | bytes 2752520 | tf_op jit(solution)/shard_map/ppermute | solution.py:1019
  3.7 2.1 setup.1
  5.8 2.2 one_half.1
  10.7 2.2 collective-permute-done.2
  14.5 2.1 collective-permute-done.3
  16.5 2.6 collective-permute-start.4
  19.1 3.5 %pack.1 = (bf16[1552,256]{1,0:T(8,128)(2,1)S(1)}, bf16[2304,256]{1,0:T(8,128)(2,1)S(1)}, bf16[512,512]{1,0:T(8,128)(2,1)S(1)}, f32[8,512]{1,0:T(8,128)S(1)}, f32...) custom-call(s32[18]{0:T(128)S(4)} %get-tuple-element.324.isc, ...), custom_call_target="tpu_custom_call" | custom-call | flops 1000000 | bytes 200000 | tf_op jit(solution)/shard_map/pack/pallas_call | solution.py:1004
  23.2 3.1 %collective-permute-done.5.part_other = f32[4,512]{1,0:T(4,128)S(1)} collective-permute-done((f32[4,512]{1,0:T(4,128)S(1)}, f32[4,512]{1,0:T(4,128)S(1)}, u32[]{:S(2)}, u32[]{:S(2)}) %collective-permute-start.5) | collective-permute-done | bytes 8224 | tf_op jit(solution)/shard_map/ppermute | solution.py:1019
  26.9 5.2 %stage_two.1 = (bf16[4,224,1024]{2,1,0:T(8,128)(2,1)S(1)}, bf16[224,1024]{1,0:T(8,128)(2,1)S(1)}, f32[4,224,512]{2,1,0:T(8,128)S(1)}, bf16[9,224,512]{2,1,0:T(8,...) custom-call(f32[13]{0:T(128)S(4)} %get-tuple-element.200.fs, ...), custom_call_target="tpu_custom_call" | custom-call | flops 40000000 | bytes 200000 | tf_op jit(solution)/shard_map/stage_two/pallas_call | solution.py:1004
  34.8 2.2 collective-permute-done.7
  40.6 2.1 collective-permute-done.8
  42.6 2.6 collective-permute-start.10
  45.2 3.1 %project.1 = (f32[224,2048]{1,0:T(8,128)S(1)}, f32[4,2048]{1,0:T(4,128)S(1)}, bf16[512,2048]{1,0:T(8,128)(2,1)S(1)}) custom-call(f32[13]{0:T(128)S(4)} %get-tuple-element.200.fs, bf16[224,1024]{1,0:T(8,128)(2,1)S(1)} %get-tuple-element.219.x.strided, f32[224,1]{1,0:T(8,128)S(1)} %get-tuple-element.210.keep, bf16[1024,2048]{1,0:T(8,128)(2,1)} %wp_far.3, ...), custom_call_target="tpu_custom_call" | custom-call | flops 10000000 | bytes 80000 | tf_op jit(solution)/shard_map/project/pallas_call | solution.py:1004
  48.4 1.7 stage_three.1
  53.0 2.8 collective-permute-done.12
  57.4 2.7 collective-permute-done.13
  61.6 3.8 %collective-permute-done.15 = f32[8,2048]{1,0:T(8,128)S(1)} collective-permute-done((f32[8,2048]{1,0:T(8,128)S(1)}, f32[8,2048]{1,0:T(8,128)S(1)}, u32[]{:S(2)}, u32[]{:S(2)}) %collective-permute-start.15) | collective-permute-done | bytes 65568 | tf_op jit(solution)/shard_map/ppermute | solution.py:1019
  67.3 3.9 %stage_four.1 = (bf16[224,2048]{1,0:T(8,128)(2,1)S(1)}, f32[224,512]{1,0:T(8,128)S(1)}, f32[4,512]{1,0:T(4,128)S(1)}, f32[8,2048]{1,0:T(8,128)S(1)}, f32[8,2048]...) custom-call(f32[13]{0:T(128)S(4)} %get-tuple-element.200.fs, ...), custom_call_target="tpu_custom_call" | custom-call | flops 10000000 | bytes 100000 | tf_op jit(solution)/shard_map/stage_four/pallas_call | solution.py:1004
  74.0 2.2 collective-permute-done.17
  77.7 2.1 collective-permute-done.18
  84.4 1.9 stage_five.1
  90.7 2.2 collective-permute-done.23
  94.5 2.1 collective-permute-done.24
  101.2 1.7 stage_six.1
  105.7 2.4 collective-permute-done.29
  109.8 2.3 collective-permute-done.30
  115.1 1.9 collective-permute-done.31
  117.1 6.4 %turn.1 = (bf16[224,1024]{1,0:T(8,128)(2,1)}, f32[224,2048]{1,0:T(8,128)S(1)}, f32[4,2048]{1,0:T(4,128)S(1)}, f32[8,512]{1,0:T(8,128)S(1)}, f32[4,2048]{1,0:T(4,...) custom-call(f32[13]{0:T(128)S(4)} %get-tuple-element.200.fs, ...), custom_call_target="tpu_custom_call" | custom-call | flops 10000000 | bytes 100000 | tf_op jit(solution)/shard_map/turn/pallas_call | solution.py:1004
  126.2 2.4 collective-permute-done.34
  130.3 2.3 collective-permute-done.35
  134.3 3.3 %collective-permute-done.36 = f32[4,2048]{1,0:T(4,128)S(1)} collective-permute-done((f32[4,2048]{1,0:T(4,128)S(1)}, f32[4,2048]{1,0:T(4,128)S(1)}, u32[]{:S(2)}, u32[]{:S(2)}) %collective-permute-start.36) | collective-permute-done | bytes 32800 | tf_op jit(solution)/shard_map/ppermute | solution.py:1019
  137.5 2.5 back_six.1
  142.8 2.4 collective-permute-done.38
  146.8 2.3 collective-permute-done.39
  150.7 3.3 %collective-permute-done.40 = f32[12,512]{1,0:T(8,128)S(1)} collective-permute-done((f32[12,512]{1,0:T(8,128)S(1)}, f32[12,512]{1,0:T(8,128)S(1)}, u32[]{:S(2)}, u32[]{:S(2)}) %collective-permute-start.40) | collective-permute-done | bytes 24608 | tf_op jit(solution)/shard_map/ppermute | solution.py:1019
  153.9 3.5 %back_five.1 = (bf16[224,512]{1,0:T(8,128)(2,1)S(1)}, f32[224,512]{1,0:T(8,128)S(1)}, f32[4,512]{1,0:T(4,128)S(1)}, f32[256]{0:T(256)}, f32[256]{0:T(256)}, /*index=5*/f32[1024]{0:T(1024)}, f32[128]{0:T(128)}, f32[5]{0:T(128)}) custom-call(f32[13]{0:T(128)S(4)} %get-tuple-element.200.fs, s32[18]{0:T(128)S(4)} %get-tuple-element.324.isc, ...), custom_call_target="tpu_custom_call" | custom-call | flops 20000000 | bytes 100000 | tf_op jit(solution)/shard_map/back_five/pallas_call | solution.py:1004
  157.4 3.2 %grads_a.1 = (bf16[8,416,256]{2,1,0:T(8,128)(2,1)S(1)}, bf16[8,416,256]{2,1,0:T(8,128)(2,1)S(1)}) custom-call(s32[18]{0:T(128)S(4)} %get-tuple-element.324.isc, bf16[224,512]{1,0:T(8,128)(2,1)S(1)} %get-tuple-element.269.h5, bf16[224,2048]{1,0:T(8,128)(2,1)S(1)} %get-tuple-element.270.d6, bf16[9,224,512]{2,1,0:T(8,128)(2,1)S(1)} %get-tuple-element.271.col4, ...), custom_call_target="tpu_custom_call" | custom-call | flops 20000000 | bytes 100000 | tf_op jit(solution)/shard_map/grads_a/pallas_call | solution.py:1004
  163.6 2.2 collective-permute-done.42
  169.1 2.1 collective-permute-done.43
  172.7 3.0 collective-permute-done.44
  175.7 6.5 %back_four.1 = (bf16[224,512]{1,0:T(8,128)(2,1)S(1)}, f32[224,2048]{1,0:T(8,128)S(1)}, f32[8,2048]{1,0:T(8,128)S(1)}, f32[512]{0:T(512)}, f32[512]{0:T(512)}, /*...) custom-call(f32[13]{0:T(128)S(4)} %get-tuple-element.200.fs, ...), custom_call_target="tpu_custom_call" | custom-call | flops 10000000 | bytes 100000 | tf_op jit(solution)/shard_map/back_four/pallas_call | solution.py:1004
  188.3 2.8 collective-permute-done.48
  192.7 2.7 collective-permute-done.49
  197.2 3.6 %collective-permute-done.50 = f32[8,2048]{1,0:T(8,128)S(1)} collective-permute-done((f32[8,2048]{1,0:T(8,128)S(1)}, f32[8,2048]{1,0:T(8,128)S(1)}, u32[]{:S(2)}, u32[]{:S(2)}) %collective-permute-start.50) | collective-permute-done | bytes 65568 | tf_op jit(solution)/shard_map/ppermute | solution.py:1019
  200.8 2.6 collective-permute-start.52
  203.5 3.3 %back_three.1 = (bf16[224,2048]{1,0:T(8,128)(2,1)S(1)}, bf16[224,2048]{1,0:T(8,128)(2,1)S(1)}, f32[224,512]{1,0:T(8,128)S(1)}, f32[12,512]{1,0:T(8,128)S(1)}, f3...) custom-call(f32[13]{0:T(128)S(4)} %get-tuple-element.200.fs, f32[1,8,2048]{2,1,0:T(8,128)S(1)} %bitcast.39, ...), custom_call_target="tpu_custom_call" | custom-call | flops 10000000 | bytes 100000 | tf_op jit(solution)/shard_map/back_three/pallas_call | solution.py:1004
  206.7 1.9 grads_c.1
  212.3 2.5 collective-permute-done.54
  214.8 2.0 collective-permute-start.55
  216.8 2.4 fetch_two.1.ws
  224.1 3.0 back_two.1
  227.1 1.8 grads_d.1
  229.5 2.3 collective-permute-done.58
  231.8 7.2 %collective-permute-done.59 = bf16[4,384,256]{2,1,0:T(8,128)(2,1)S(1)} collective-permute-done((bf16[4,384,256]{2,1,0:T(8,128)(2,1)S(1)}, bf16[4,384,256]{2,1,0:T(8,128)(2,1)S(1)}, u32[]{:S(2)}, u32[]{:S(2)}) %collective-permute-start.59) | collective-permute-done | bytes 786464 | tf_op jit(solution)/shard_map/ppermute | solution.py:1019
  240.5 2.2 collective-permute-done.60
  243.4 3.0 collective-permute-done.61
  247.9 3.1 %collective-permute-done.62 = f32[4,512]{1,0:T(4,128)S(1)} collective-permute-done((f32[4,512]{1,0:T(4,128)S(1)}, f32[4,512]{1,0:T(4,128)S(1)}, u32[]{:S(2)}, u32[]{:S(2)}) %collective-permute-start.62) | collective-permute-done | bytes 8224 | tf_op jit(solution)/shard_map/ppermute | solution.py:1019
  253.3 5.7 %placed.1 = f32[448,1024]{1,0:T(8,128)S(1)} custom-call(s32[18]{0:T(128)S(4)} %get-tuple-element.324.isc, bf16[224,2048]{1,0:T(8,128)(2,1)S(1)} %get-tuple-element.305.dproj, bf16[1024,2048]{1,0:T(8,128)(2,1)} %wp_far.3), custom_call_target="tpu_custom_call" | custom-call | flops 10000000 | bytes 100000 | tf_op jit(solution)/shard_map/placed/pallas_call | solution.py:1004
  260.6 2.0 back_one.1
  263.2 2.1 image.1
  270.0 8.8 %collective-permute-done.68 = bf16[4,288,256]{2,1,0:T(8,128)(2,1)S(1)} collective-permute-done((bf16[4,288,256]{2,1,0:T(8,128)(2,1)S(1)}, bf16[4,288,256]{2,1,0:T(8,128)(2,1)S(1)}, u32[]{:S(2)}, u32[]{:S(2)}) %collective-permute-start.68) | collective-permute-done | bytes 589856 | tf_op jit(solution)/shard_map/ppermute | solution.py:1019
  284.2 7.5 %collective-permute-done.69 = bf16[2,288,256]{2,1,0:T(8,128)(2,1)S(1)} collective-permute-done((bf16[2,288,256]{2,1,0:T(8,128)(2,1)S(1)}, bf16[2,288,256]{2,1,0:T(8,128)(2,1)S(1)}, u32[]{:S(2)}, u32[]{:S(2)}) %collective-permute-start.69) | collective-permute-done | bytes 294944 | tf_op jit(solution)/shard_map/ppermute | solution.py:1019
  292.4 2.4 collective-permute-start.67
  296.4 2.8 collective-permute-done.67.b
  (187 shorter events, 107.9 us)
Async XLA Ops:
  0.7 25.7 %collective-permute-start = (bf16[4,112,1024]{2,1,0:T(8,128)(2,1)}, bf16[4,112,1024]{2,1,0:T(8,128)(2,1)S(1)}, u32[]{:S(2)}, u32[]{:S(2)}) collective-permute-start(bf16[4,112,1024]{2,1,0:T(8,128)(2,1)} %bitcast.46), channel_id=1, source_target_pairs={{0,1},{1,0},{2,3},{3,2},{4,5},{5,4},{6,7},{7,6},{8,9},{9,8},{10,11... | collective-permute-start | bytes 2752520 | tf_op jit(solution)/shard_map/ppermute | solution.py:1019
  9.2 3.7 %collective-permute-start.2 = (f32[4,512]{1,0:T(4,128)S(1)}, f32[4,512]{1,0:T(4,128)S(1)}, u32[]{:S(2)}, u32[]{:S(2)}) collective-permute-start(f32[4,512]{1,0:T(4,128)S(1)} %add.234), channel_id=1, source_target_pairs={{0,4},{2,6},{4,0},{6,2},{8,12},{10,14},{12,8},{14,10},{16,20},{18,... | collective-permute-start | bytes 24584 | tf_op jit(solution)/shard_map/ppermute | solution.py:1019
  12.9 3.7 %collective-permute-start.3 = (f32[4,512]{1,0:T(4,128)S(1)}, f32[4,512]{1,0:T(4,128)S(1)}, u32[]{:S(2)}, u32[]{:S(2)}) collective-permute-start(f32[4,512]{1,0:T(4,128)S(1)} %add.235), channel_id=1, source_target_pairs={{0,8},{2,10},{4,12},{6,14},{8,0},{10,2},{12,4},{14,6},{16,24},{18,... | collective-permute-start | bytes 24584 | tf_op jit(solution)/shard_map/ppermute | solution.py:1019
  16.5 6.1 %collective-permute-start.4 = (f32[4,512]{1,0:T(4,128)S(1)}, f32[4,512]{1,0:T(4,128)S(1)}, u32[]{:S(2)}, u32[]{:S(2)}) collective-permute-start(f32[4,512]{1,0:T(4,128)S(1)} %add.236), channel_id=1, source_target_pairs={{0,16},{2,18},{4,20},{6,22},{8,24},{10,26},{12,28},{14,30},{16,0},... | collective-permute-start | bytes 24584 | tf_op jit(solution)/shard_map/ppermute | solution.py:1019
  22.6 3.7 %collective-permute-start.5 = (f32[4,512]{1,0:T(4,128)S(1)}, f32[4,512]{1,0:T(4,128)S(1)}, u32[]{:S(2)}, u32[]{:S(2)}) collective-permute-start(f32[4,512]{1,0:T(4,128)S(1)} %add.237.part), channel_id=1, source_target_pairs={{0,1},{1,0},{2,3},{3,2},{4,5},{5,4},{6,7},{7,6},{8,9},{9,8},{10,11... | collective-permute-start | bytes 24584 | tf_op jit(solution)/shard_map/ppermute | solution.py:1019
  26.3 11.3 %collective-permute-start.9 = (bf16[512,512]{1,0:T(8,128)(2,1)S(1)}, bf16[512,512]{1,0:T(8,128)(2,1)S(1)}, u32[]{:S(2)}, u32[]{:S(2)}) collective-permute-start(bf16[512,512]{1,0:T(8,128)(2,1)S(1)} %get-tuple-element.216), channel_id=1, source_target_pairs={{0,1},{1,0},{2,3},{3,2},{4,5},{5,4},{6,7},{7,6},{8,9},{9,8},{10,11... | collective-permute-start | bytes 1572872 | tf_op jit(solution)/shard_map/ppermute | solution.py:1019
  33.3 3.7 %collective-permute-start.7 = (f32[4,512]{1,0:T(4,128)S(1)}, f32[4,512]{1,0:T(4,128)S(1)}, u32[]{:S(2)}, u32[]{:S(2)}) collective-permute-start(f32[4,512]{1,0:T(4,128)S(1)} %add.238), channel_id=1, source_target_pairs={{0,4},{2,6},{4,0},{6,2},{8,12},{10,14},{12,8},{14,10},{16,20},{18,... | collective-permute-start | bytes 24584 | tf_op jit(solution)/shard_map/ppermute | solution.py:1019
  37.7 27.7 %collective-permute-start.19 = (bf16[2304,256]{1,0:T(8,128)(2,1)S(1)}, bf16[2304,256]{1,0:T(8,128)(2,1)S(1)}, u32[]{:S(2)}, u32[]{:S(2)}) collective-permute-start(bf16[2304,256]{1,0:T(8,128)(2,1)S(1)} %get-tuple-element.232), channel_id=1, source_target_pairs={{0,1},{1,0},{2,3},{3,2},{4,5},{5,4},{6,7},{7,6},{8,9},{9,8},{10,11... | collective-permute-start | bytes 3538952 | tf_op jit(solution)/shard_map/ppermute | solution.py:1019
  39.0 21.1 %collective-permute-start.14 = (bf16[512,512]{1,0:T(8,128)(2,1)S(1)}, bf16[512,512]{1,0:T(8,128)(2,1)S(1)}, u32[]{:S(2)}, u32[]{:S(2)}) collective-permute-start(bf16[512,512]{1,0:T(8,128)(2,1)S(1)} %collective-permute-done.9.r1), channel_id=1, source_target_pairs={{0,2},{2,0},{4,6},{6,4},{8,10},{10,8},{12,14},{14,12},{16,18},{18,... | collective-permute-start | bytes 1572872 | tf_op jit(solution)/shard_map/ppermute | solution.py:1019
  39.0 3.7 %collective-permute-start.8 = (f32[4,512]{1,0:T(4,128)S(1)}, f32[4,512]{1,0:T(4,128)S(1)}, u32[]{:S(2)}, u32[]{:S(2)}) collective-permute-start(f32[4,512]{1,0:T(4,128)S(1)} %add.239), channel_id=1, source_target_pairs={{0,8},{2,10},{4,12},{6,14},{8,0},{10,2},{12,4},{14,6},{16,24},{18,... | collective-permute-start | bytes 24584 | tf_op jit(solution)/shard_map/ppermute | solution.py:1019
  42.6 5.7 %collective-permute-start.10 = (f32[4,512]{1,0:T(4,128)S(1)}, f32[4,512]{1,0:T(4,128)S(1)}, u32[]{:S(2)}, u32[]{:S(2)}) collective-permute-start(f32[4,512]{1,0:T(4,128)S(1)} %add.240), channel_id=1, source_target_pairs={{0,16},{2,18},{4,20},{6,22},{8,24},{10,26},{12,28},{14,30},{16,0},... | collective-permute-start | bytes 24584 | tf_op jit(solution)/shard_map/ppermute | solution.py:1019
  51.4 4.3 %collective-permute-start.12 = (f32[8,2048]{1,0:T(8,128)S(1)}, f32[8,2048]{1,0:T(8,128)S(1)}, u32[]{:S(2)}, u32[]{:S(2)}) collective-permute-start(f32[8,2048]{1,0:T(8,128)S(1)} %add.242), channel_id=1, source_target_pairs={{0,4},{2,6},{4,0},{6,2},{8,12},{10,14},{12,8},{14,10},{16,20},{18,... | collective-permute-start | bytes 196616 | tf_op jit(solution)/shard_map/ppermute | solution.py:1019
  55.8 4.3 %collective-permute-start.13 = (f32[8,2048]{1,0:T(8,128)S(1)}, f32[8,2048]{1,0:T(8,128)S(1)}, u32[]{:S(2)}, u32[]{:S(2)}) collective-permute-start(f32[8,2048]{1,0:T(8,128)S(1)} %add.243), channel_id=1, source_target_pairs={{0,8},{2,10},{4,12},{6,14},{8,0},{10,2},{12,4},{14,6},{16,24},{18,... | collective-permute-start | bytes 196616 | tf_op jit(solution)/shard_map/ppermute | solution.py:1019
  60.1 5.2 %collective-permute-start.15 = (f32[8,2048]{1,0:T(8,128)S(1)}, f32[8,2048]{1,0:T(8,128)S(1)}, u32[]{:S(2)}, u32[]{:S(2)}) collective-permute-start(f32[8,2048]{1,0:T(8,128)S(1)} %add.244), channel_id=1, source_target_pairs={{0,16},{2,18},{4,20},{6,22},{8,24},{10,26},{12,28},{14,30},{16,0},... | collective-permute-start | bytes 196616 | tf_op jit(solution)/shard_map/ppermute | solution.py:1019
  65.4 14.4 %collective-permute-start.20 = (bf16[2304,256]{1,0:T(8,128)(2,1)S(1)}, bf16[2304,256]{1,0:T(8,128)(2,1)S(1)}, u32[]{:S(2)}, u32[]{:S(2)}) collective-permute-start(bf16[2304,256]{1,0:T(8,128)(2,1)S(1)} %collective-permute-done.19.r1), channel_id=1, source_target_pairs={{0,2},{2,0},{4,6},{6,4},{8,10},{10,8},{12,14},{14,12},{16,18},{18,... | collective-permute-start | bytes 3538952 | tf_op jit(solution)/shard_map/ppermute | solution.py:1019
  65.4 20.9 %collective-permute-start.25 = (bf16[1552,256]{1,0:T(8,128)(2,1)S(1)}, bf16[1552,256]{1,0:T(8,128)(2,1)S(1)}, u32[]{:S(2)}, u32[]{:S(2)}) collective-permute-start(bf16[1552,256]{1,0:T(8,128)(2,1)S(1)} %get-tuple-element.239), channel_id=1, source_target_pairs={{0,1},{1,0},{2,3},{3,2},{4,5},{5,4},{6,7},{7,6},{8,9},{9,8},{10,11... | collective-permute-start | bytes 2383880 | tf_op jit(solution)/shard_map/ppermute | solution.py:1019
  72.5 3.7 %collective-permute-start.17 = (f32[4,512]{1,0:T(4,128)S(1)}, f32[4,512]{1,0:T(4,128)S(1)}, u32[]{:S(2)}, u32[]{:S(2)}) collective-permute-start(f32[4,512]{1,0:T(4,128)S(1)} %add.246), channel_id=1, source_target_pairs={{0,4},{2,6},{4,0},{6,2},{8,12},{10,14},{12,8},{14,10},{16,20},{18,... | collective-permute-start | bytes 24584 | tf_op jit(solution)/shard_map/ppermute | solution.py:1019
  76.1 3.7 %collective-permute-start.18 = (f32[4,512]{1,0:T(4,128)S(1)}, f32[4,512]{1,0:T(4,128)S(1)}, u32[]{:S(2)}, u32[]{:S(2)}) collective-permute-start(f32[4,512]{1,0:T(4,128)S(1)} %add.247), channel_id=1, source_target_pairs={{0,8},{2,10},{4,12},{6,14},{8,0},{10,2},{12,4},{14,6},{16,24},{18,... | collective-permute-start | bytes 24584 | tf_op jit(solution)/shard_map/ppermute | solution.py:1019
  79.8 4.6 %collective-permute-start.21 = (f32[4,512]{1,0:T(4,128)S(1)}, f32[4,512]{1,0:T(4,128)S(1)}, u32[]{:S(2)}, u32[]{:S(2)}) collective-permute-start(f32[4,512]{1,0:T(4,128)S(1)} %add.248), channel_id=1, source_target_pairs={{0,16},{2,18},{4,20},{6,22},{8,24},{10,26},{12,28},{14,30},{16,0},... | collective-permute-start | bytes 24584 | tf_op jit(solution)/shard_map/ppermute | solution.py:1019
  86.4 10.2 %collective-permute-start.26 = (bf16[1552,256]{1,0:T(8,128)(2,1)S(1)}, bf16[1552,256]{1,0:T(8,128)(2,1)S(1)}, u32[]{:S(2)}, u32[]{:S(2)}) collective-permute-start(bf16[1552,256]{1,0:T(8,128)(2,1)S(1)} %collective-permute-done.25.r1), channel_id=1, source_target_pairs={{0,2},{2,0},{4,6},{6,4},{8,10},{10,8},{12,14},{14,12},{16,18},{18,... | collective-permute-start | bytes 2383880 | tf_op jit(solution)/shard_map/ppermute | solution.py:1019
  86.5 27.3 %collective-permute-start.32 = (bf16[224,1024]{1,0:T(8,128)(2,1)S(1)}, bf16[224,1024]{1,0:T(8,128)(2,1)S(1)}, u32[]{:S(2)}, u32[]{:S(2)}) collective-permute-start(bf16[224,1024]{1,0:T(8,128)(2,1)S(1)} %bitcast.49), channel_id=1, source_target_pairs={{0,1},{1,0},{2,3},{3,2},{4,5},{5,4},{6,7},{7,6},{8,9},{9,8},{10,11... | collective-permute-start | bytes 1376264 | tf_op jit(solution)/shard_map/ppermute | solution.py:1019
  89.2 3.7 %collective-permute-start.23 = (f32[4,512]{1,0:T(4,128)S(1)}, f32[4,512]{1,0:T(4,128)S(1)}, u32[]{:S(2)}, u32[]{:S(2)}) collective-permute-start(f32[4,512]{1,0:T(4,128)S(1)} %add.250), channel_id=1, source_target_pairs={{0,4},{2,6},{4,0},{6,2},{8,12},{10,14},{12,8},{14,10},{16,20},{18,... | collective-permute-start | bytes 24584 | tf_op jit(solution)/shard_map/ppermute | solution.py:1019
  92.9 3.7 %collective-permute-start.24 = (f32[4,512]{1,0:T(4,128)S(1)}, f32[4,512]{1,0:T(4,128)S(1)}, u32[]{:S(2)}, u32[]{:S(2)}) collective-permute-start(f32[4,512]{1,0:T(4,128)S(1)} %add.251), channel_id=1, source_target_pairs={{0,8},{2,10},{4,12},{6,14},{8,0},{10,2},{12,4},{14,6},{16,24},{18,... | collective-permute-start | bytes 24584 | tf_op jit(solution)/shard_map/ppermute | solution.py:1019
  96.6 4.6 %collective-permute-start.27 = (f32[4,512]{1,0:T(4,128)S(1)}, f32[4,512]{1,0:T(4,128)S(1)}, u32[]{:S(2)}, u32[]{:S(2)}) collective-permute-start(f32[4,512]{1,0:T(4,128)S(1)} %add.252), channel_id=1, source_target_pairs={{0,16},{2,18},{4,20},{6,22},{8,24},{10,26},{12,28},{14,30},{16,0},... | collective-permute-start | bytes 24584 | tf_op jit(solution)/shard_map/ppermute | solution.py:1019
  104.2 4.0 %collective-permute-start.29 = (f32[4,2048]{1,0:T(4,128)S(1)}, f32[4,2048]{1,0:T(4,128)S(1)}, u32[]{:S(2)}, u32[]{:S(2)}) collective-permute-start(f32[4,2048]{1,0:T(4,128)S(1)} %add.254), channel_id=1, source_target_pairs={{0,4},{2,6},{4,0},{6,2},{8,12},{10,14},{12,8},{14,10},{16,20},{18,... | collective-permute-start | bytes 98312 | tf_op jit(solution)/shard_map/ppermute | solution.py:1019
  108.2 4.0 %collective-permute-start.30 = (f32[4,2048]{1,0:T(4,128)S(1)}, f32[4,2048]{1,0:T(4,128)S(1)}, u32[]{:S(2)}, u32[]{:S(2)}) collective-permute-start(f32[4,2048]{1,0:T(4,128)S(1)} %add.255), channel_id=1, source_target_pairs={{0,8},{2,10},{4,12},{6,14},{8,0},{10,2},{12,4},{14,6},{16,24},{18,... | collective-permute-start | bytes 98312 | tf_op jit(solution)/shard_map/ppermute | solution.py:1019
  112.2 4.9 %collective-permute-start.31 = (f32[4,2048]{1,0:T(4,128)S(1)}, f32[4,2048]{1,0:T(4,128)S(1)}, u32[]{:S(2)}, u32[]{:S(2)}) collective-permute-start(f32[4,2048]{1,0:T(4,128)S(1)} %add.256), channel_id=1, source_target_pairs={{0,16},{2,18},{4,20},{6,22},{8,24},{10,26},{12,28},{14,30},{16,0},... | collective-permute-start | bytes 98312 | tf_op jit(solution)/shard_map/ppermute | solution.py:1019
  124.6 4.0 %collective-permute-start.34 = (f32[4,2048]{1,0:T(4,128)S(1)}, f32[4,2048]{1,0:T(4,128)S(1)}, u32[]{:S(2)}, u32[]{:S(2)}) collective-permute-start(f32[4,2048]{1,0:T(4,128)S(1)} %add.258), channel_id=1, source_target_pairs={{0,4},{2,6},{4,0},{6,2},{8,12},{10,14},{12,8},{14,10},{16,20},{18,... | collective-permute-start | bytes 98312 | tf_op jit(solution)/shard_map/ppermute | solution.py:1019
  128.6 4.0 %collective-permute-start.35 = (f32[4,2048]{1,0:T(4,128)S(1)}, f32[4,2048]{1,0:T(4,128)S(1)}, u32[]{:S(2)}, u32[]{:S(2)}) collective-permute-start(f32[4,2048]{1,0:T(4,128)S(1)} %add.259), channel_id=1, source_target_pairs={{0,8},{2,10},{4,12},{6,14},{8,0},{10,2},{12,4},{14,6},{16,24},{18,... | collective-permute-start | bytes 98312 | tf_op jit(solution)/shard_map/ppermute | solution.py:1019
  132.6 4.9 %collective-permute-start.36 = (f32[4,2048]{1,0:T(4,128)S(1)}, f32[4,2048]{1,0:T(4,128)S(1)}, u32[]{:S(2)}, u32[]{:S(2)}) collective-permute-start(f32[4,2048]{1,0:T(4,128)S(1)} %add.260), channel_id=1, source_target_pairs={{0,16},{2,18},{4,20},{6,22},{8,24},{10,26},{12,28},{14,30},{16,0},... | collective-permute-start | bytes 98312 | tf_op jit(solution)/shard_map/ppermute | solution.py:1019
  141.3 3.9 %collective-permute-start.38 = (f32[12,512]{1,0:T(8,128)S(1)}, f32[12,512]{1,0:T(8,128)S(1)}, u32[]{:S(2)}, u32[]{:S(2)}) collective-permute-start(f32[12,512]{1,0:T(8,128)S(1)} %add.262), channel_id=1, source_target_pairs={{0,4},{2,6},{4,0},{6,2},{8,12},{10,14},{12,8},{14,10},{16,20},{18,... | collective-permute-start | bytes 73736 | tf_op jit(solution)/shard_map/ppermute | solution.py:1019
  145.2 3.9 %collective-permute-start.39 = (f32[12,512]{1,0:T(8,128)S(1)}, f32[12,512]{1,0:T(8,128)S(1)}, u32[]{:S(2)}, u32[]{:S(2)}) collective-permute-start(f32[12,512]{1,0:T(8,128)S(1)} %add.263), channel_id=1, source_target_pairs={{0,8},{2,10},{4,12},{6,14},{8,0},{10,2},{12,4},{14,6},{16,24},{18,... | collective-permute-start | bytes 73736 | tf_op jit(solution)/shard_map/ppermute | solution.py:1019
  149.1 4.8 %collective-permute-start.40 = (f32[12,512]{1,0:T(8,128)S(1)}, f32[12,512]{1,0:T(8,128)S(1)}, u32[]{:S(2)}, u32[]{:S(2)}) collective-permute-start(f32[12,512]{1,0:T(8,128)S(1)} %add.264), channel_id=1, source_target_pairs={{0,16},{2,18},{4,20},{6,22},{8,24},{10,26},{12,28},{14,30},{16,0},... | collective-permute-start | bytes 73736 | tf_op jit(solution)/shard_map/ppermute | solution.py:1019
  161.9 3.8 %collective-permute-start.45 = (bf16[8,416,256]{2,1,0:T(8,128)(2,1)S(1)}, bf16[8,416,256]{2,1,0:T(8,128)(2,1)S(1)}, u32[]{:S(2)}, u32[]{:S(2)}) collective-permute-start(bf16[8,416,256]{2,1,0:T(8,128)(2,1)S(1)} %get-tuple-element.276), channel_id=1, source_target_pairs={{0,2},{2,0},{4,6},{6,4},{8,10},{10,8},{12,14},{14,12},{16,18},{18,... | collective-permute-start | bytes 5111816 | tf_op jit(solution)/shard_map/ppermute | solution.py:1019
  162.1 3.7 %collective-permute-start.42 = (f32[4,512]{1,0:T(4,128)S(1)}, f32[4,512]{1,0:T(4,128)S(1)}, u32[]{:S(2)}, u32[]{:S(2)}) collective-permute-start(f32[4,512]{1,0:T(4,128)S(1)} %add.266), channel_id=1, source_target_pairs={{0,4},{2,6},{4,0},{6,2},{8,12},{10,14},{12,8},{14,10},{16,20},{18,... | collective-permute-start | bytes 24584 | tf_op jit(solution)/shard_map/ppermute | solution.py:1019
  165.9 20.9 %collective-permute-start.47 = (bf16[4,416,256]{2,1,0:T(8,128)(2,1)S(1)}, bf16[4,416,256]{2,1,0:T(8,128)(2,1)S(1)}, u32[]{:S(2)}, u32[]{:S(2)}) collective-permute-start(bf16[4,416,256]{2,1,0:T(8,128)(2,1)S(1)} %get-tuple-element.294), channel_id=1, source_target_pairs={{0,4},{2,6},{4,0},{6,2},{8,12},{10,14},{12,8},{14,10},{16,20},{18,... | collective-permute-start | bytes 2555912 | tf_op jit(solution)/shard_map/ppermute | solution.py:1019
  167.5 3.7 %collective-permute-start.43 = (f32[4,512]{1,0:T(4,128)S(1)}, f32[4,512]{1,0:T(4,128)S(1)}, u32[]{:S(2)}, u32[]{:S(2)}) collective-permute-start(f32[4,512]{1,0:T(4,128)S(1)} %add.267), channel_id=1, source_target_pairs={{0,8},{2,10},{4,12},{6,14},{8,0},{10,2},{12,4},{14,6},{16,24},{18,... | collective-permute-start | bytes 24584 | tf_op jit(solution)/shard_map/ppermute | solution.py:1019
  171.2 4.5 %collective-permute-start.44 = (f32[4,512]{1,0:T(4,128)S(1)}, f32[4,512]{1,0:T(4,128)S(1)}, u32[]{:S(2)}, u32[]{:S(2)}) collective-permute-start(f32[4,512]{1,0:T(4,128)S(1)} %add.268), channel_id=1, source_target_pairs={{0,16},{2,18},{4,20},{6,22},{8,24},{10,26},{12,28},{14,30},{16,0},... | collective-permute-start | bytes 24584 | tf_op jit(solution)/shard_map/ppermute | solution.py:1019
  185.1 18.3 %collective-permute-start.51 = (bf16[8,256,256]{2,1,0:T(8,128)(2,1)S(1)}, bf16[8,256,256]{2,1,0:T(8,128)(2,1)S(1)}, u32[]{:S(2)}, u32[]{:S(2)}) collective-permute-start(bf16[8,256,256]{2,1,0:T(8,128)(2,1)S(1)} %get-tuple-element.296), channel_id=1, source_target_pairs={{0,2},{2,0},{4,6},{6,4},{8,10},{10,8},{12,14},{14,12},{16,18},{18,... | collective-permute-start | bytes 3145736 | tf_op jit(solution)/shard_map/ppermute | solution.py:1019
  186.8 4.3 %collective-permute-start.48 = (f32[8,2048]{1,0:T(8,128)S(1)}, f32[8,2048]{1,0:T(8,128)S(1)}, u32[]{:S(2)}, u32[]{:S(2)}) collective-permute-start(f32[8,2048]{1,0:T(8,128)S(1)} %add.272), channel_id=1, source_target_pairs={{0,4},{2,6},{4,0},{6,2},{8,12},{10,14},{12,8},{14,10},{16,20},{18,... | collective-permute-start | bytes 196616 | tf_op jit(solution)/shard_map/ppermute | solution.py:1019
  191.1 4.3 %collective-permute-start.49 = (f32[8,2048]{1,0:T(8,128)S(1)}, f32[8,2048]{1,0:T(8,128)S(1)}, u32[]{:S(2)}, u32[]{:S(2)}) collective-permute-start(f32[8,2048]{1,0:T(8,128)S(1)} %add.273), channel_id=1, source_target_pairs={{0,8},{2,10},{4,12},{6,14},{8,0},{10,2},{12,4},{14,6},{16,24},{18,... | collective-permute-start | bytes 196616 | tf_op jit(solution)/shard_map/ppermute | solution.py:1019
  195.4 5.3 %collective-permute-start.50 = (f32[8,2048]{1,0:T(8,128)S(1)}, f32[8,2048]{1,0:T(8,128)S(1)}, u32[]{:S(2)}, u32[]{:S(2)}) collective-permute-start(f32[8,2048]{1,0:T(8,128)S(1)} %add.274), channel_id=1, source_target_pairs={{0,16},{2,18},{4,20},{6,22},{8,24},{10,26},{12,28},{14,30},{16,0},... | collective-permute-start | bytes 196616 | tf_op jit(solution)/shard_map/ppermute | solution.py:1019
  200.8 8.7 %collective-permute-start.52 = (bf16[2,416,256]{2,1,0:T(8,128)(2,1)S(1)}, bf16[2,416,256]{2,1,0:T(8,128)(2,1)S(1)}, u32[]{:S(2)}, u32[]{:S(2)}) collective-permute-start(bf16[2,416,256]{2,1,0:T(8,128)(2,1)S(1)} %get-tuple-element.308), channel_id=1, source_target_pairs={{0,8},{2,10},{4,12},{6,14},{8,0},{10,2},{12,4},{14,6},{16,24},{18,... | collective-permute-start | bytes 1277960 | tf_op jit(solution)/shard_map/ppermute | solution.py:1019
  210.7 10.1 %collective-permute-start.57 = (bf16[8,384,256]{2,1,0:T(8,128)(2,1)S(1)}, bf16[8,384,256]{2,1,0:T(8,128)(2,1)S(1)}, u32[]{:S(2)}, u32[]{:S(2)}) collective-permute-start(bf16[8,384,256]{2,1,0:T(8,128)(2,1)S(1)} %get-tuple-element.310), channel_id=1, source_target_pairs={{0,2},{2,0},{4,6},{6,4},{8,10},{10,8},{12,14},{14,12},{16,18},{18,... | collective-permute-start | bytes 4718600 | tf_op jit(solution)/shard_map/ppermute | solution.py:1019
  210.8 3.9 %collective-permute-start.54 = (f32[12,512]{1,0:T(8,128)S(1)}, f32[12,512]{1,0:T(8,128)S(1)}, u32[]{:S(2)}, u32[]{:S(2)}) collective-permute-start(f32[12,512]{1,0:T(8,128)S(1)} %add.279), channel_id=1, source_target_pairs={{0,4},{2,6},{4,0},{6,2},{8,12},{10,14},{12,8},{14,10},{16,20},{18,... | collective-permute-start | bytes 73736 | tf_op jit(solution)/shard_map/ppermute | solution.py:1019
  214.8 4.4 %collective-permute-start.55 = (f32[12,512]{1,0:T(8,128)S(1)}, f32[12,512]{1,0:T(8,128)S(1)}, u32[]{:S(2)}, u32[]{:S(2)}) collective-permute-start(f32[12,512]{1,0:T(8,128)S(1)} %add.280), channel_id=1, source_target_pairs={{0,8},{2,10},{4,12},{6,14},{8,0},{10,2},{12,4},{14,6},{16,24},{18,... | collective-permute-start | bytes 73736 | tf_op jit(solution)/shard_map/ppermute | solution.py:1019
  219.2 4.9 %collective-permute-start.56 = (f32[12,512]{1,0:T(8,128)S(1)}, f32[12,512]{1,0:T(8,128)S(1)}, u32[]{:S(2)}, u32[]{:S(2)}) collective-permute-start(f32[12,512]{1,0:T(8,128)S(1)} %add.281), channel_id=1, source_target_pairs={{0,16},{2,18},{4,20},{6,22},{8,24},{10,26},{12,28},{14,30},{16,0},... | collective-permute-start | bytes 73736 | tf_op jit(solution)/shard_map/ppermute | solution.py:1019
  220.9 18.1 %collective-permute-start.59 = (bf16[4,384,256]{2,1,0:T(8,128)(2,1)S(1)}, bf16[4,384,256]{2,1,0:T(8,128)(2,1)S(1)}, u32[]{:S(2)}, u32[]{:S(2)}) collective-permute-start(bf16[4,384,256]{2,1,0:T(8,128)(2,1)S(1)} %get-tuple-element.321), channel_id=1, source_target_pairs={{0,4},{2,6},{4,0},{6,2},{8,12},{10,14},{12,8},{14,10},{16,20},{18,... | collective-permute-start | bytes 2359304 | tf_op jit(solution)/shard_map/ppermute | solution.py:1019
  228.9 31.6 %collective-permute-start.63 = (bf16[8,288,256]{2,1,0:T(8,128)(2,1)S(1)}, bf16[8,288,256]{2,1,0:T(8,128)(2,1)S(1)}, u32[]{:S(2)}, u32[]{:S(2)}) collective-permute-start(bf16[8,288,256]{2,1,0:T(8,128)(2,1)S(1)} %get-tuple-element.319), channel_id=1, source_target_pairs={{0,2},{2,0},{4,6},{6,4},{8,10},{10,8},{12,14},{14,12},{16,18},{18,... | collective-permute-start | bytes 3538952 | tf_op jit(solution)/shard_map/ppermute | solution.py:1019
  239.0 3.7 %collective-permute-start.60 = (f32[4,512]{1,0:T(4,128)S(1)}, f32[4,512]{1,0:T(4,128)S(1)}, u32[]{:S(2)}, u32[]{:S(2)}) collective-permute-start(f32[4,512]{1,0:T(4,128)S(1)} %add.285), channel_id=1, source_target_pairs={{0,4},{2,6},{4,0},{6,2},{8,12},{10,14},{12,8},{14,10},{16,20},{18,... | collective-permute-start | bytes 24584 | tf_op jit(solution)/shard_map/ppermute | solution.py:1019
  246.4 4.7 %collective-permute-start.62 = (f32[4,512]{1,0:T(4,128)S(1)}, f32[4,512]{1,0:T(4,128)S(1)}, u32[]{:S(2)}, u32[]{:S(2)}) collective-permute-start(f32[4,512]{1,0:T(4,128)S(1)} %add.287), channel_id=1, source_target_pairs={{0,16},{2,18},{4,20},{6,22},{8,24},{10,26},{12,28},{14,30},{16,0},... | collective-permute-start | bytes 24584 | tf_op jit(solution)/shard_map/ppermute | solution.py:1019
  251.0 14.3 %collective-permute-start.71 = (bf16[2,384,256]{2,1,0:T(8,128)(2,1)S(1)}, bf16[2,384,256]{2,1,0:T(8,128)(2,1)S(1)}, u32[]{:S(2)}, u32[]{:S(2)}) collective-permute-start(bf16[2,384,256]{2,1,0:T(8,128)(2,1)S(1)} %get-tuple-element.341), channel_id=1, source_target_pairs={{0,8},{2,10},{4,12},{6,14},{8,0},{10,2},{12,4},{14,6},{16,24},{18,... | collective-permute-start | bytes 1179656 | tf_op jit(solution)/shard_map/ppermute | solution.py:1019
  251.8 15.2 %collective-permute-start.73 = (bf16[4,256,256]{2,1,0:T(8,128)(2,1)S(1)}, bf16[4,256,256]{2,1,0:T(8,128)(2,1)S(1)}, u32[]{:S(2)}, u32[]{:S(2)}) collective-permute-start(bf16[4,256,256]{2,1,0:T(8,128)(2,1)S(1)} %get-tuple-element.348), channel_id=1, source_target_pairs={{0,4},{2,6},{4,0},{6,2},{8,12},{10,14},{12,8},{14,10},{16,20},{18,... | collective-permute-start | bytes 1572872 | tf_op jit(solution)/shard_map/ppermute | solution.py:1019
  259.0 35.8 %collective-permute-start.76 = (bf16[1,416,256]{2,1,0:T(8,128)(2,1)S(1)}, bf16[1,416,256]{2,1,0:T(8,128)(2,1)S(1)}, u32[]{:S(2)}, u32[]{:S(2)}) collective-permute-start(bf16[1,416,256]{2,1,0:T(8,128)(2,1)S(1)} %get-tuple-element.356), channel_id=1, source_target_pairs={{0,16},{2,18},{4,20},{6,22},{8,24},{10,26},{12,28},{14,30},{16,0},... | collective-permute-start | bytes 638984 | tf_op jit(solution)/shard_map/ppermute | solution.py:1019
  262.6 5.8 %collective-permute-start.64 = (bf16[8,64,256]{2,1,0:T(8,128)(2,1)S(1)}, bf16[8,64,256]{2,1,0:T(8,128)(2,1)S(1)}, u32[]{:S(2)}, u32[]{:S(2)}) collective-permute-start(bf16[8,64,256]{2,1,0:T(8,128)(2,1)S(1)} %get-tuple-element.332), channel_id=1, source_target_pairs={{0,2},{2,0},{4,6},{6,4},{8,10},{10,8},{12,14},{14,12},{16,18},{18,... | collective-permute-start | bytes 786440 | tf_op jit(solution)/shard_map/ppermute | solution.py:1019
  262.6 16.1 %collective-permute-start.68 = (bf16[4,288,256]{2,1,0:T(8,128)(2,1)S(1)}, bf16[4,288,256]{2,1,0:T(8,128)(2,1)S(1)}, u32[]{:S(2)}, u32[]{:S(2)}) collective-permute-start(bf16[4,288,256]{2,1,0:T(8,128)(2,1)S(1)} %get-tuple-element.338), channel_id=1, source_target_pairs={{0,4},{2,6},{4,0},{6,2},{8,12},{10,14},{12,8},{14,10},{16,20},{18,... | collective-permute-start | bytes 1769480 | tf_op jit(solution)/shard_map/ppermute | solution.py:1019
  265.3 30.2 %collective-permute-start.72 = (bf16[1,384,256]{2,1,0:T(8,128)(2,1)S(1)}, bf16[1,384,256]{2,1,0:T(8,128)(2,1)S(1)}, u32[]{:S(2)}, u32[]{:S(2)}) collective-permute-start(bf16[1,384,256]{2,1,0:T(8,128)(2,1)S(1)} %get-tuple-element.386), channel_id=1, source_target_pairs={{0,16},{2,18},{4,20},{6,22},{8,24},{10,26},{12,28},{14,30},{16,0},... | collective-permute-start | bytes 589832 | tf_op jit(solution)/shard_map/ppermute | solution.py:1019
  267.0 15.7 %collective-permute-start.74 = (bf16[2,256,256]{2,1,0:T(8,128)(2,1)S(1)}, bf16[2,256,256]{2,1,0:T(8,128)(2,1)S(1)}, u32[]{:S(2)}, u32[]{:S(2)}) collective-permute-start(bf16[2,256,256]{2,1,0:T(8,128)(2,1)S(1)} %get-tuple-element.383), channel_id=1, source_target_pairs={{0,8},{2,10},{4,12},{6,14},{8,0},{10,2},{12,4},{14,6},{16,24},{18,... | collective-permute-start | bytes 786440 | tf_op jit(solution)/shard_map/ppermute | solution.py:1019
  268.4 12.8 %collective-permute-start.65 = (bf16[4,64,256]{2,1,0:T(8,128)(2,1)S(1)}, bf16[4,64,256]{2,1,0:T(8,128)(2,1)S(1)}, u32[]{:S(2)}, u32[]{:S(2)}) collective-permute-start(bf16[4,64,256]{2,1,0:T(8,128)(2,1)S(1)} %get-tuple-element.335), channel_id=1, source_target_pairs={{0,4},{2,6},{4,0},{6,2},{8,12},{10,14},{12,8},{14,10},{16,20},{18,... | collective-permute-start | bytes 393224 | tf_op jit(solution)/shard_map/ppermute | solution.py:1019
  278.8 12.9 %collective-permute-start.69 = (bf16[2,288,256]{2,1,0:T(8,128)(2,1)S(1)}, bf16[2,288,256]{2,1,0:T(8,128)(2,1)S(1)}, u32[]{:S(2)}, u32[]{:S(2)}) collective-permute-start(bf16[2,288,256]{2,1,0:T(8,128)(2,1)S(1)} %get-tuple-element.381), channel_id=1, source_target_pairs={{0,8},{2,10},{4,12},{6,14},{8,0},{10,2},{12,4},{14,6},{16,24},{18,... | collective-permute-start | bytes 884744 | tf_op jit(solution)/shard_map/ppermute | solution.py:1019
  281.2 11.2 %collective-permute-start.66 = (bf16[2,64,256]{2,1,0:T(8,128)(2,1)S(1)}, bf16[2,64,256]{2,1,0:T(8,128)(2,1)S(1)}, u32[]{:S(2)}, u32[]{:S(2)}) collective-permute-start(bf16[2,64,256]{2,1,0:T(8,128)(2,1)S(1)} %get-tuple-element.395), channel_id=1, source_target_pairs={{0,8},{2,10},{4,12},{6,14},{8,0},{10,2},{12,4},{14,6},{16,24},{18,... | collective-permute-start | bytes 196616 | tf_op jit(solution)/shard_map/ppermute | solution.py:1019
  282.7 17.1 %collective-permute-start.75 = (bf16[1,256,256]{2,1,0:T(8,128)(2,1)S(1)}, bf16[1,256,256]{2,1,0:T(8,128)(2,1)S(1)}, u32[]{:S(2)}, u32[]{:S(2)}) collective-permute-start(bf16[1,256,256]{2,1,0:T(8,128)(2,1)S(1)} %get-tuple-element.390), channel_id=1, source_target_pairs={{0,16},{2,18},{4,20},{6,22},{8,24},{10,26},{12,28},{14,30},{16,0},... | collective-permute-start | bytes 393224 | tf_op jit(solution)/shard_map/ppermute | solution.py:1019
  291.7 8.8 %collective-permute-start.70 = (bf16[1,288,256]{2,1,0:T(8,128)(2,1)S(1)}, bf16[1,288,256]{2,1,0:T(8,128)(2,1)S(1)}, u32[]{:S(2)}, u32[]{:S(2)}) collective-permute-start(bf16[1,288,256]{2,1,0:T(8,128)(2,1)S(1)} %get-tuple-element.388), channel_id=1, source_target_pairs={{0,16},{2,18},{4,20},{6,22},{8,24},{10,26},{12,28},{14,30},{16,0},... | collective-permute-start | bytes 442376 | tf_op jit(solution)/shard_map/ppermute | solution.py:1019
  292.4 6.8 %collective-permute-start.67 = (bf16[1,64,256]{2,1,0:T(8,128)(2,1)S(1)}, bf16[1,64,256]{2,1,0:T(8,128)(2,1)S(1)}, u32[]{:S(2)}, u32[]{:S(2)}) collective-permute-start(bf16[1,64,256]{2,1,0:T(8,128)(2,1)S(1)} %get-tuple-element.396), channel_id=1, source_target_pairs={{0,16},{2,18},{4,20},{6,22},{8,24},{10,26},{12,28},{14,30},{16,0},... | collective-permute-start | bytes 98312 | tf_op jit(solution)/shard_map/ppermute | solution.py:1019
  (14 other events, 22.2 us)

commit v4 on v3

--- a/solution.py
+++ b/solution.py
@@ -24,7 +24,7 @@
 ANY = pl.BlockSpec(memory_space=pl.ANY)
 INV_IN, INV_OUT, CELLS, MICRO, INV_ALL = 0, 2, 4, 8, 12
 NARROW, CORE, DEST = 0, 1, 2
-W6_AT, EX_AT, SQ_AT, VEC_AT, PACK_ROWS = 0, 1024, 1280, 1536, 1552
+W6_AT, EX_AT, SQ_AT, VE2, PACK_ROWS = 0, 1024, 1280, 1536, 1552
 
 
 def mm(a, b):
@@ -429,7 +429,7 @@
 
 def fetch_six_kernel(isc, own, r1, r2, vown, w6, gain5, vec2, vaway, sems):
     n, core = isc[NARROW], isc[CORE]
-    pairs = [(r1.at[VEC_AT:PACK_ROWS], vaway), (own, w6.at[at_rows(n * 256, 256)])]
+    pairs = [(r1.at[VE2:PACK_ROWS], vaway), (own, w6.at[at_rows(n * 256, 256)])]
     for r, h in ((r1, core), (r2, 1 - core)):
         for c in range(8):
             pairs.append(
@@ -925,28 +925,24 @@
         excite[:, c * 256 : (c + 1) * 256] = part[8:16]
 
 
-def unpack_a_kernel(a, b, expand2, spatial2):
+def unpack_kernel(
+    a, b, c, d, expand2, spatial2, reduce2, squeeze2, excite2, squeeze1, excite1, expand1, project1
+):
     v = f32(a[0]) + f32(b[0])
     expand2[0:128, :] = v[0:128, 0:128]
     expand2[128:256, :] = v[0:128, 128:256]
     spatial2[...] = v[128:416, :]
-
-
-def unpack_b_kernel(a, b, reduce2, squeeze2, excite2, squeeze1, excite1):
-    v = f32(a[0]) + f32(b[0])
-    joined(v, reduce2, 0, 32)
-    unpack_gates(v, 128, squeeze2, excite2)
-    unpack_gates(v, 192, squeeze1, excite1)
-
-
-def unpack_c_kernel(a, b, expand1, project1):
-    v = f32(a[0]) + f32(b[0])
+    joined(v, reduce2, 416, 32)
+    unpack_gates(v, 544, squeeze2, excite2)
+    unpack_gates(v, 608, squeeze1, excite1)
+    v = f32(c[0]) + f32(d[0])
     joined(v, expand1, 0, 32)
     joined(v, project1, 128, 64)
 
 
-def unpack_d_kernel(a, b, spatial1):
+def unpack_last_kernel(a, b, c, d, spatial1, reduce1):
     spatial1[...] = f32(a[0]) + f32(b[0])
+    reduce1[...] = f32(c[0]) + f32(d[0])
 
 
 VECTORS = (512,) * 6 + (2048,) * 5 + (128,) * 2 + (256,) * 2 + (1024,) * 3
@@ -991,7 +987,7 @@
         out[EX_AT + c * 64 : EX_AT + (c + 1) * 64, :] = exv[:, c * 256 : (c + 1) * 256]
     for k in range(2):
         out[SQ_AT : SQ_AT + 256, k * 128 : (k + 1) * 128] = sqv[k * 256 : (k + 1) * 256, :]
-    out[VEC_AT:PACK_ROWS, :] = vown[...]
+    out[VE2:PACK_ROWS, :] = vown[...]
     wait_all(copies[21:])
 
 
@@ -1051,7 +1047,8 @@
         results, step = [], 1
         x = after(x, *first)
         while step < wide:
-            y = after(x, *(before or {}).get(len(results), ()))
+            due = (before or {}).get(len(results), ())
+            y = after(x, *(due(results) if callable(due) else due))
             x = x + swap(y, "wide", [(i, i ^ step) for i in range(wide)])
             results.append(x)
             step *= 2
@@ -1218,10 +1215,17 @@
         grads_a_kernel, [h(8, 416, 256)] * 2, [isc, h5, d6, col4, d5],
         [V((256, 2048), BF), V((512, 256), BF)], flops=2e9, size=1e7, name="grads_a",
     )
-    back4, sent4 = steps(bt4, *ga)
-    ga, _ = step(ga, 0, sent4[0])
-    back4 = after(back4, *ga)
-    ga, xa = step(ga, 1, sent4[1])
+    held = {}
+
+    def core_step(name, g, tied=True):
+        def due(results):
+            held[name], _ = step(g, 0, *(results[:1] if tied else ()))
+            return held[name] if exact else ()
+
+        return due
+
+    back4, sent4 = steps(bt4, *ga, before={2: core_step("a", ga)})
+    ga, xa = step(held["a"], 1, sent4[1])
     d4, dj1, bt3, dgain4, dbias4, dp1, de1, ds1, bias1 = call(
         back_four_kernel,
         [
@@ -1241,9 +1245,12 @@
         [V((512, 256), BF), V((128, 256), F32), V((128, 256), F32), V((8, 128), F32)],
         flops=1e9, size=4e6, name="grads_b",
     )
-    back3, sent3 = steps(bt3, *gb1, before={1: xa})
-    gb1, _ = step(gb1, 0, sent3[0])
-    back3 = after(back3, *gb1)
+    ws_back = call(
+        fetch_two_kernel, [h(9, 512, 512)], [far(after(ws_far, bt4))], [D((3,))], size=9e6, name="fetch_two",
+    )[0]
+    back3, sent3 = steps(bt3, *gb1, *xa, ws_back, before={3: core_step("b", gb1, True)})
+    gb1 = held["b"]
+    gb1, xb = step(gb1, 1, sent3[3])
     ga, za = step(ga, 2, sent3[3])
     d3, dproj, do2, bt2, dgain3, dbias3, dgainp, dbiasp = call(
         back_three_kernel,
@@ -1257,13 +1264,8 @@
         [V((512, 256), BF), V((1024, 256), BF)],
         flops=3e9, size=1e7, name="grads_c",
     )
-    back2, sent2 = steps(bt2, *gc, *za)
-    gc, _ = step(gc, 0, sent2[0])
-    back2 = after(back2, *gc)
-    gc, xc = step(gc, 1, sent2[1])
-    ws_back = call(
-        fetch_two_kernel, [h(9, 512, 512)], [far(after(ws_far, bt2))], [D((3,))], size=9e6, name="fetch_two",
-    )[0]
+    back2, sent2 = steps(bt2, *gc, *za, *xb, before={2: core_step("c", gc)})
+    gc, xc = step(held["c"], 1, sent2[1])
     d2, do1, bt1, dgain2, dbias2, debias1, dsbias1 = call(
         back_two_kernel,
         [h(M, 512), f(4, M, 512), f(4, 512), out(512), out(512), out(2048), out(128)],
@@ -1275,20 +1277,17 @@
         grads_d_kernel, [h(8, 288, 256)] * 2, [isc, col1, d2], [V((512, 256), BF)],
         flops=2e9, size=6e6, name="grads_d",
     )
-    back1, sent1 = steps(bt1, *gd, before={1: xc})
-    gd, _ = step(gd, 0)
-    gd0 = gd
-    gd, xd = step(gd, 1, sent1[2])
-    gb1, _ = step(gb1, 1, sent1[2])
-    gc, _ = step(gc, 2, sent1[3])
-    ga, _ = step(ga, 3, sent1[3])
-    back1 = after(back1, *gd0)
     placed = call(
-        placed_kernel, [f(HROWS, 1024)], [(SMEM, after(isc_, sent1[2])), dproj, far(first_project)],
+        placed_kernel, [f(HROWS, 1024)], [(SMEM, after(isc_, bt2)), dproj, far(first_project)],
         [V((128, 2048), BF), V((128, M), BF), V((HROWS, 128), BF), V((1024, 2048), BF), D((4,))],
         flops=1e9, size=1e7, name="placed",
     )[0]
-    back1, placed = lax.optimization_barrier((back1, placed))
+    back1, sent1 = steps(bt1, *gd, *xc, placed)
+    gd, _ = step(gd, 0, sent1[0])
+    gd0 = gd
+    gd, xd = step(gd, 1, sent1[2])
+    gc, _ = step(gc, 2, sent1[3])
+    back1 = after(back1, *gd0)
     d1, ge_keep, ge_send, dgain1, dbias1 = call(
         back_one_kernel, [h(B, M, 512), h(8, 64, 256), h(8, 64, 256), out(512), out(512)],
         [fs, isc, back1, tot1, x1, do1, xp, keep1, gb],
@@ -1303,26 +1302,26 @@
 
     if exact:
         ge, _ = step(ge, 0)
-        dimg, *ge = lax.optimization_barrier((dimg,) + ge)
+        dimg, *gd = lax.optimization_barrier((dimg,) + gd)
         gb1, _ = step(gb1, 2)
+        gab = tuple(jnp.concatenate(p, axis=1) for p in zip(ga, gb1))
+        gab, _ = step(gab, 3)
         gd, _ = step(gd, 2)
         gc, _ = step(gc, 3)
-        gb1, _ = step(gb1, 3)
         ge, _ = step(ge, 1)
         ge, _ = step(ge, 2)
         gd, _ = step(gd, 3)
         ge, _ = step(ge, 3)
-        expand2, spatial2 = call(
-            unpack_a_kernel, [out(256, 128), out(288, 256)], list(ga), name="unpack_a"
+        (
+            expand2, spatial2, reduce2, squeeze2, excite2, squeeze1, excite1, expand1, project1,
+        ) = call(
+            unpack_kernel,
+            [out(256, 128), out(288, 256), out(32, 1024)] + [out(8, 1024)] * 4 + [out(32, 1024), out(64, 1024)],
+            list(gab + gc), name="unpack",
         )
-        reduce2, squeeze2, excite2, squeeze1, excite1 = call(
-            unpack_b_kernel, [out(32, 1024)] + [out(8, 1024)] * 4, list(gb1), name="unpack_b"
+        spatial1, reduce1 = call(
+            unpack_last_kernel, [out(288, 256), out(64, 256)], list(gd + ge), name="unpack_last"
         )
-        expand1, project1 = call(
-            unpack_c_kernel, [out(32, 1024), out(64, 1024)], list(gc), name="unpack_c"
-        )
-        spatial1 = call(unpack_d_kernel, [out(288, 256)], list(gd), name="unpack_d")[0]
-        reduce1 = call(unpack_d_kernel, [out(64, 256)], list(ge), name="unpack_e")[0]
     else:
         finer = wide // 16
 

time: 302 us -> 294 us (0.974)
  waiting for transfers between devices: 129 us -> 124 us
    ppermute x77 -> x76, waiting for transfers between devices: 129 us -> 124 us  [swap(): return lax.ppermute(v, axis, pairs)]
    pallas_call x32 -> x29, Pallas kernels: 80.4 us -> 78.5 us  [call(): pl.pallas_call(body, out_shape=tuple((o if hasattr(o, 'memory_space') els...]
    ppermute x77 -> x76, starting transfers between devices: 88.9 us -> 88.4 us  [swap(): return lax.ppermute(v, axis, pairs)]
  transfers between devices with their start and end apart: 77 -> 76, of which waited for: 55 -> 57; matrix products, arithmetic and copies ran while one was open for 0% -> 0% of each run, Pallas kernels for 21% -> 21%
where the time goes in v4:
time: 294 us
  waiting for transfers between devices  124 us (42%)
  starting transfers between devices  88.4 us (30%)
  Pallas kernels  78.5 us (27%)
    ppermute x76, waiting for transfers between devices, swap(): return lax.ppermute(v, axis, pairs)  124 us
    ppermute x76, starting transfers between devices, swap(): return lax.ppermute(v, axis, pairs)  88.4 us
    pallas_call x29, Pallas kernels, call(): pl.pallas_call(body, out_shape=tuple((o if hasattr(o, 'memory_space') els...  78.5 us
  transfers between devices with their start and end apart: 76, of which 57 were waited for; matrix products, arithmetic and copies ran while one was open for 0% of the time, Pallas kernels for 21%

profile of v4, /device:TPU:0, one launch (start us, length us, event | category | flops | bytes accessed | tf_op | source)
XLA Modules:
  0.0 293.5 jit_solution(1951864750071225420)
XLA Ops:
  0.7 3.0 %collective-permute-start = (bf16[4,112,1024]{2,1,0:T(8,128)(2,1)}, bf16[4,112,1024]{2,1,0:T(8,128)(2,1)S(1)}, u32[]{:S(2)}, u32[]{:S(2)}) collective-permute-start(bf16[4,112,1024]{2,1,0:T(8,128)(2,1)} %bitcast.46), channel_id=1, source_target_pairs={{0,1},{1,0},{2,3},{3,2},{4,5},{5,4},{6,7},{7,6},{8,9},{9,8},{10,11... | collective-permute-start | bytes 2752520 | tf_op jit(solution)/shard_map/ppermute | solution.py:1015
  3.7 2.1 setup.1
  5.8 2.2 one_half.1
  10.7 2.2 collective-permute-done.2
  14.5 2.1 collective-permute-done.3
  16.5 2.6 collective-permute-start.4
  19.1 3.5 %pack.1 = (bf16[1552,256]{1,0:T(8,128)(2,1)S(1)}, bf16[2304,256]{1,0:T(8,128)(2,1)S(1)}, bf16[512,512]{1,0:T(8,128)(2,1)S(1)}, f32[8,512]{1,0:T(8,128)S(1)}, f32...) custom-call(s32[18]{0:T(128)S(4)} %get-tuple-element.319.isc, ...), custom_call_target="tpu_custom_call" | custom-call | flops 1000000 | bytes 200000 | tf_op jit(solution)/shard_map/pack/pallas_call | solution.py:1000
  23.2 3.1 %collective-permute-done.5.part_other = f32[4,512]{1,0:T(4,128)S(1)} collective-permute-done((f32[4,512]{1,0:T(4,128)S(1)}, f32[4,512]{1,0:T(4,128)S(1)}, u32[]{:S(2)}, u32[]{:S(2)}) %collective-permute-start.5) | collective-permute-done | bytes 8224 | tf_op jit(solution)/shard_map/ppermute | solution.py:1015
  26.9 5.2 %stage_two.1 = (bf16[4,224,1024]{2,1,0:T(8,128)(2,1)S(1)}, bf16[224,1024]{1,0:T(8,128)(2,1)S(1)}, f32[4,224,512]{2,1,0:T(8,128)S(1)}, bf16[9,224,512]{2,1,0:T(8,...) custom-call(f32[13]{0:T(128)S(4)} %get-tuple-element.198.fs, ...), custom_call_target="tpu_custom_call" | custom-call | flops 40000000 | bytes 200000 | tf_op jit(solution)/shard_map/stage_two/pallas_call | solution.py:1000
  34.8 2.2 collective-permute-done.7
  40.6 2.1 collective-permute-done.8
  42.6 2.6 collective-permute-start.10
  45.2 3.1 %project.1 = (f32[224,2048]{1,0:T(8,128)S(1)}, f32[4,2048]{1,0:T(4,128)S(1)}, bf16[512,2048]{1,0:T(8,128)(2,1)S(1)}) custom-call(f32[13]{0:T(128)S(4)} %get-tuple-element.198.fs, bf16[224,1024]{1,0:T(8,128)(2,1)S(1)} %get-tuple-element.217.x.strided, f32[224,1]{1,0:T(8,128)S(1)} %get-tuple-element.208.keep, bf16[1024,2048]{1,0:T(8,128)(2,1)} %wp_far.3, ...), custom_call_target="tpu_custom_call" | custom-call | flops 10000000 | bytes 80000 | tf_op jit(solution)/shard_map/project/pallas_call | solution.py:1000
  53.0 2.8 collective-permute-done.12
  57.4 2.7 collective-permute-done.13
  61.6 3.8 %collective-permute-done.15 = f32[8,2048]{1,0:T(8,128)S(1)} collective-permute-done((f32[8,2048]{1,0:T(8,128)S(1)}, f32[8,2048]{1,0:T(8,128)S(1)}, u32[]{:S(2)}, u32[]{:S(2)}) %collective-permute-start.15) | collective-permute-done | bytes 65568 | tf_op jit(solution)/shard_map/ppermute | solution.py:1015
  67.3 3.9 %stage_four.1 = (bf16[224,2048]{1,0:T(8,128)(2,1)S(1)}, f32[224,512]{1,0:T(8,128)S(1)}, f32[4,512]{1,0:T(4,128)S(1)}, f32[8,2048]{1,0:T(8,128)S(1)}, f32[8,2048]...) custom-call(f32[13]{0:T(128)S(4)} %get-tuple-element.198.fs, ...), custom_call_target="tpu_custom_call" | custom-call | flops 10000000 | bytes 100000 | tf_op jit(solution)/shard_map/stage_four/pallas_call | solution.py:1000
  74.0 2.2 collective-permute-done.17
  77.7 2.1 collective-permute-done.18
  84.4 1.9 stage_five.1
  90.7 2.2 collective-permute-done.23
  94.5 2.1 collective-permute-done.24
  105.7 2.4 collective-permute-done.29
  109.8 2.3 collective-permute-done.30
  115.1 1.9 collective-permute-done.31
  117.1 6.4 %turn.1 = (bf16[224,1024]{1,0:T(8,128)(2,1)}, f32[224,2048]{1,0:T(8,128)S(1)}, f32[4,2048]{1,0:T(4,128)S(1)}, f32[8,512]{1,0:T(8,128)S(1)}, f32[4,2048]{1,0:T(4,...) custom-call(f32[13]{0:T(128)S(4)} %get-tuple-element.198.fs, ...), custom_call_target="tpu_custom_call" | custom-call | flops 10000000 | bytes 100000 | tf_op jit(solution)/shard_map/turn/pallas_call | solution.py:1000
  126.2 2.4 collective-permute-done.34
  130.3 2.3 collective-permute-done.35
  134.3 3.3 %collective-permute-done.36 = f32[4,2048]{1,0:T(4,128)S(1)} collective-permute-done((f32[4,2048]{1,0:T(4,128)S(1)}, f32[4,2048]{1,0:T(4,128)S(1)}, u32[]{:S(2)}, u32[]{:S(2)}) %collective-permute-start.36) | collective-permute-done | bytes 32800 | tf_op jit(solution)/shard_map/ppermute | solution.py:1015
  137.5 2.5 back_six.1
  142.8 2.4 collective-permute-done.38
  146.8 2.3 collective-permute-done.39
  150.7 3.3 %collective-permute-done.40 = f32[12,512]{1,0:T(8,128)S(1)} collective-permute-done((f32[12,512]{1,0:T(8,128)S(1)}, f32[12,512]{1,0:T(8,128)S(1)}, u32[]{:S(2)}, u32[]{:S(2)}) %collective-permute-start.40) | collective-permute-done | bytes 24608 | tf_op jit(solution)/shard_map/ppermute | solution.py:1015
  153.9 3.5 %back_five.1 = (bf16[224,512]{1,0:T(8,128)(2,1)S(1)}, f32[224,512]{1,0:T(8,128)S(1)}, f32[4,512]{1,0:T(4,128)S(1)}, f32[256]{0:T(256)}, f32[256]{0:T(256)}, /*index=5*/f32[1024]{0:T(1024)}, f32[128]{0:T(128)}, f32[5]{0:T(128)}) custom-call(f32[13]{0:T(128)S(4)} %get-tuple-element.198.fs, s32[18]{0:T(128)S(4)} %get-tuple-element.319.isc, ...), custom_call_target="tpu_custom_call" | custom-call | flops 20000000 | bytes 100000 | tf_op jit(solution)/shard_map/back_five/pallas_call | solution.py:1000
  157.4 3.2 %grads_a.1 = (bf16[8,416,256]{2,1,0:T(8,128)(2,1)S(1)}, bf16[8,416,256]{2,1,0:T(8,128)(2,1)S(1)}) custom-call(s32[18]{0:T(128)S(4)} %get-tuple-element.319.isc, bf16[224,512]{1,0:T(8,128)(2,1)S(1)} %get-tuple-element.267.h5, bf16[224,2048]{1,0:T(8,128)(2,1)S(1)} %get-tuple-element.268.d6, bf16[9,224,512]{2,1,0:T(8,128)(2,1)S(1)} %get-tuple-element.269.col4, ...), custom_call_target="tpu_custom_call" | custom-call | flops 20000000 | bytes 100000 | tf_op jit(solution)/shard_map/grads_a/pallas_call | solution.py:1000
  163.6 2.2 collective-permute-done.42
  169.1 2.1 collective-permute-done.44
  172.7 2.4 fetch_two.1.ws
  175.7 6.5 %back_four.1 = (bf16[224,512]{1,0:T(8,128)(2,1)S(1)}, f32[224,2048]{1,0:T(8,128)S(1)}, f32[8,2048]{1,0:T(8,128)S(1)}, f32[512]{0:T(512)}, f32[512]{0:T(512)}, /*...) custom-call(f32[13]{0:T(128)S(4)} %get-tuple-element.198.fs, ...), custom_call_target="tpu_custom_call" | custom-call | flops 10000000 | bytes 100000 | tf_op jit(solution)/shard_map/back_four/pallas_call | solution.py:1000
  183.8 3.0 %collective-permute-done.46 = bf16[4,416,256]{2,1,0:T(8,128)(2,1)S(1)} collective-permute-done((bf16[4,416,256]{2,1,0:T(8,128)(2,1)S(1)}, bf16[4,416,256]{2,1,0:T(8,128)(2,1)S(1)}, u32[]{:S(2)}, u32[]{:S(2)}) %collective-permute-start.46) | collective-permute-done | bytes 852000 | tf_op jit(solution)/shard_map/ppermute | solution.py:1015
  189.8 2.9 collective-permute-done.48
  194.3 2.7 collective-permute-done.49
  198.7 3.6 %collective-permute-done.51 = f32[8,2048]{1,0:T(8,128)S(1)} collective-permute-done((f32[8,2048]{1,0:T(8,128)S(1)}, f32[8,2048]{1,0:T(8,128)S(1)}, u32[]{:S(2)}, u32[]{:S(2)}) %collective-permute-start.51) | collective-permute-done | bytes 65568 | tf_op jit(solution)/shard_map/ppermute | solution.py:1015
  205.7 3.2 %back_three.1 = (bf16[224,2048]{1,0:T(8,128)(2,1)S(1)}, bf16[224,2048]{1,0:T(8,128)(2,1)S(1)}, f32[224,512]{1,0:T(8,128)S(1)}, f32[12,512]{1,0:T(8,128)S(1)}, f3...) custom-call(f32[13]{0:T(128)S(4)} %get-tuple-element.198.fs, f32[1,8,2048]{2,1,0:T(8,128)S(1)} %bitcast.39, ...), custom_call_target="tpu_custom_call" | custom-call | flops 10000000 | bytes 100000 | tf_op jit(solution)/shard_map/back_three/pallas_call | solution.py:1000
  208.9 1.9 grads_c.1
  210.8 2.0 collective-permute-done.52
  216.4 2.4 collective-permute-done.55
  222.1 2.3 collective-permute-done.57
  224.5 2.0 collective-permute-start.58
  226.5 5.7 %placed.1 = f32[448,1024]{1,0:T(8,128)S(1)} custom-call(s32[18]{0:T(128)S(4)} %get-tuple-element.319.isc, bf16[224,2048]{1,0:T(8,128)(2,1)S(1)} %get-tuple-element.303.dproj, bf16[1024,2048]{1,0:T(8,128)(2,1)} %wp_far.3), custom_call_target="tpu_custom_call" | custom-call | flops 10000000 | bytes 100000 | tf_op jit(solution)/shard_map/placed/pallas_call | solution.py:1000
  232.2 3.0 %back_two.1 = (bf16[224,512]{1,0:T(8,128)(2,1)S(1)}, f32[4,224,512]{2,1,0:T(8,128)S(1)}, f32[4,512]{1,0:T(4,128)S(1)}, f32[512]{0:T(512)}, f32[512]{0:T(512)}, /*index=5*/f32[2048]{0:T(1024)}, f32[128]{0:T(128)}) custom-call(f32[13]{0:T(128)S(4)} %get-tuple-element.198.fs, f32[1,12,512]{2,1,0:T(8,128)S(1)} %add_bitcast_fusion.1.parts, ...), custom_call_target="tpu_custom_call" | custom-call | flops 20000000 | bytes 100000 | tf_op jit(solution)/shard_map/back_two/pallas_call | solution.py:1000
  242.6 2.1 collective-permute-done.61
  245.1 3.0 %collective-permute-done.72 = bf16[2,256,256]{2,1,0:T(8,128)(2,1)S(1)} collective-permute-done((bf16[2,256,256]{2,1,0:T(8,128)(2,1)S(1)}, bf16[2,256,256]{2,1,0:T(8,128)(2,1)S(1)}, u32[]{:S(2)}, u32[]{:S(2)}) %collective-permute-start.72) | collective-permute-done | bytes 262176 | tf_op jit(solution)/shard_map/ppermute | solution.py:1015
  248.4 2.4 collective-permute-start.63
  253.1 2.0 back_one.1
  256.7 2.1 image.1
  260.3 6.6 %collective-permute-done.65 = bf16[4,288,256]{2,1,0:T(8,128)(2,1)S(1)} collective-permute-done((bf16[4,288,256]{2,1,0:T(8,128)(2,1)S(1)}, bf16[4,288,256]{2,1,0:T(8,128)(2,1)S(1)}, u32[]{:S(2)}, u32[]{:S(2)}) %collective-permute-start.65) | collective-permute-done | bytes 589856 | tf_op jit(solution)/shard_map/ppermute | solution.py:1015
  268.4 5.1 %collective-permute-done.74 = bf16[2,384,256]{2,1,0:T(8,128)(2,1)S(1)} collective-permute-done((bf16[2,384,256]{2,1,0:T(8,128)(2,1)S(1)}, bf16[2,384,256]{2,1,0:T(8,128)(2,1)S(1)}, u32[]{:S(2)}, u32[]{:S(2)}) %collective-permute-start.74) | collective-permute-done | bytes 393248 | tf_op jit(solution)/shard_map/ppermute | solution.py:1015
  273.6 2.3 collective-permute-start.75
  276.0 2.5 collective-permute-start.70
  278.5 3.3 %collective-permute-done.66 = bf16[2,288,256]{2,1,0:T(8,128)(2,1)S(1)} collective-permute-done((bf16[2,288,256]{2,1,0:T(8,128)(2,1)S(1)}, bf16[2,288,256]{2,1,0:T(8,128)(2,1)S(1)}, u32[]{:S(2)}, u32[]{:S(2)}) %collective-permute-start.66) | collective-permute-done | bytes 294944 | tf_op jit(solution)/shard_map/ppermute | solution.py:1015
  282.8 2.6 collective-permute-done.70
  285.9 3.0 %collective-permute-done.75.d = bf16[1,384,256]{2,1,0:T(8,128)(2,1)S(1)} collective-permute-done((bf16[1,384,256]{2,1,0:T(8,128)(2,1)S(1)}, bf16[1,384,256]{2,1,0:T(8,128)(2,1)S(1)}, u32[]{:S(2)}, u32[]{:S(2)}) %collective-permute-start.75) | collective-permute-done | bytes 196640 | tf_op jit(solution)/shard_map/ppermute | solution.py:1015
  290.0 2.8 collective-permute-done.71.d
  (184 shorter events, 107.0 us)
Async XLA Ops:
  0.7 25.7 %collective-permute-start = (bf16[4,112,1024]{2,1,0:T(8,128)(2,1)}, bf16[4,112,1024]{2,1,0:T(8,128)(2,1)S(1)}, u32[]{:S(2)}, u32[]{:S(2)}) collective-permute-start(bf16[4,112,1024]{2,1,0:T(8,128)(2,1)} %bitcast.46), channel_id=1, source_target_pairs={{0,1},{1,0},{2,3},{3,2},{4,5},{5,4},{6,7},{7,6},{8,9},{9,8},{10,11... | collective-permute-start | bytes 2752520 | tf_op jit(solution)/shard_map/ppermute | solution.py:1015
  9.2 3.7 %collective-permute-start.2 = (f32[4,512]{1,0:T(4,128)S(1)}, f32[4,512]{1,0:T(4,128)S(1)}, u32[]{:S(2)}, u32[]{:S(2)}) collective-permute-start(f32[4,512]{1,0:T(4,128)S(1)} %add.234), channel_id=1, source_target_pairs={{0,4},{2,6},{4,0},{6,2},{8,12},{10,14},{12,8},{14,10},{16,20},{18,... | collective-permute-start | bytes 24584 | tf_op jit(solution)/shard_map/ppermute | solution.py:1015
  12.9 3.7 %collective-permute-start.3 = (f32[4,512]{1,0:T(4,128)S(1)}, f32[4,512]{1,0:T(4,128)S(1)}, u32[]{:S(2)}, u32[]{:S(2)}) collective-permute-start(f32[4,512]{1,0:T(4,128)S(1)} %add.235), channel_id=1, source_target_pairs={{0,8},{2,10},{4,12},{6,14},{8,0},{10,2},{12,4},{14,6},{16,24},{18,... | collective-permute-start | bytes 24584 | tf_op jit(solution)/shard_map/ppermute | solution.py:1015
  16.5 6.1 %collective-permute-start.4 = (f32[4,512]{1,0:T(4,128)S(1)}, f32[4,512]{1,0:T(4,128)S(1)}, u32[]{:S(2)}, u32[]{:S(2)}) collective-permute-start(f32[4,512]{1,0:T(4,128)S(1)} %add.236), channel_id=1, source_target_pairs={{0,16},{2,18},{4,20},{6,22},{8,24},{10,26},{12,28},{14,30},{16,0},... | collective-permute-start | bytes 24584 | tf_op jit(solution)/shard_map/ppermute | solution.py:1015
  22.6 3.7 %collective-permute-start.5 = (f32[4,512]{1,0:T(4,128)S(1)}, f32[4,512]{1,0:T(4,128)S(1)}, u32[]{:S(2)}, u32[]{:S(2)}) collective-permute-start(f32[4,512]{1,0:T(4,128)S(1)} %add.237.part), channel_id=1, source_target_pairs={{0,1},{1,0},{2,3},{3,2},{4,5},{5,4},{6,7},{7,6},{8,9},{9,8},{10,11... | collective-permute-start | bytes 24584 | tf_op jit(solution)/shard_map/ppermute | solution.py:1015
  26.3 11.3 %collective-permute-start.9 = (bf16[512,512]{1,0:T(8,128)(2,1)S(1)}, bf16[512,512]{1,0:T(8,128)(2,1)S(1)}, u32[]{:S(2)}, u32[]{:S(2)}) collective-permute-start(bf16[512,512]{1,0:T(8,128)(2,1)S(1)} %get-tuple-element.214), channel_id=1, source_target_pairs={{0,1},{1,0},{2,3},{3,2},{4,5},{5,4},{6,7},{7,6},{8,9},{9,8},{10,11... | collective-permute-start | bytes 1572872 | tf_op jit(solution)/shard_map/ppermute | solution.py:1015
  33.3 3.7 %collective-permute-start.7 = (f32[4,512]{1,0:T(4,128)S(1)}, f32[4,512]{1,0:T(4,128)S(1)}, u32[]{:S(2)}, u32[]{:S(2)}) collective-permute-start(f32[4,512]{1,0:T(4,128)S(1)} %add.238), channel_id=1, source_target_pairs={{0,4},{2,6},{4,0},{6,2},{8,12},{10,14},{12,8},{14,10},{16,20},{18,... | collective-permute-start | bytes 24584 | tf_op jit(solution)/shard_map/ppermute | solution.py:1015
  37.7 27.7 %collective-permute-start.19 = (bf16[2304,256]{1,0:T(8,128)(2,1)S(1)}, bf16[2304,256]{1,0:T(8,128)(2,1)S(1)}, u32[]{:S(2)}, u32[]{:S(2)}) collective-permute-start(bf16[2304,256]{1,0:T(8,128)(2,1)S(1)} %get-tuple-element.230), channel_id=1, source_target_pairs={{0,1},{1,0},{2,3},{3,2},{4,5},{5,4},{6,7},{7,6},{8,9},{9,8},{10,11... | collective-permute-start | bytes 3538952 | tf_op jit(solution)/shard_map/ppermute | solution.py:1015
  39.0 21.1 %collective-permute-start.14 = (bf16[512,512]{1,0:T(8,128)(2,1)S(1)}, bf16[512,512]{1,0:T(8,128)(2,1)S(1)}, u32[]{:S(2)}, u32[]{:S(2)}) collective-permute-start(bf16[512,512]{1,0:T(8,128)(2,1)S(1)} %collective-permute-done.9.r1), channel_id=1, source_target_pairs={{0,2},{2,0},{4,6},{6,4},{8,10},{10,8},{12,14},{14,12},{16,18},{18,... | collective-permute-start | bytes 1572872 | tf_op jit(solution)/shard_map/ppermute | solution.py:1015
  39.0 3.7 %collective-permute-start.8 = (f32[4,512]{1,0:T(4,128)S(1)}, f32[4,512]{1,0:T(4,128)S(1)}, u32[]{:S(2)}, u32[]{:S(2)}) collective-permute-start(f32[4,512]{1,0:T(4,128)S(1)} %add.239), channel_id=1, source_target_pairs={{0,8},{2,10},{4,12},{6,14},{8,0},{10,2},{12,4},{14,6},{16,24},{18,... | collective-permute-start | bytes 24584 | tf_op jit(solution)/shard_map/ppermute | solution.py:1015
  42.6 5.7 %collective-permute-start.10 = (f32[4,512]{1,0:T(4,128)S(1)}, f32[4,512]{1,0:T(4,128)S(1)}, u32[]{:S(2)}, u32[]{:S(2)}) collective-permute-start(f32[4,512]{1,0:T(4,128)S(1)} %add.240), channel_id=1, source_target_pairs={{0,16},{2,18},{4,20},{6,22},{8,24},{10,26},{12,28},{14,30},{16,0},... | collective-permute-start | bytes 24584 | tf_op jit(solution)/shard_map/ppermute | solution.py:1015
  51.4 4.3 %collective-permute-start.12 = (f32[8,2048]{1,0:T(8,128)S(1)}, f32[8,2048]{1,0:T(8,128)S(1)}, u32[]{:S(2)}, u32[]{:S(2)}) collective-permute-start(f32[8,2048]{1,0:T(8,128)S(1)} %add.242), channel_id=1, source_target_pairs={{0,4},{2,6},{4,0},{6,2},{8,12},{10,14},{12,8},{14,10},{16,20},{18,... | collective-permute-start | bytes 196616 | tf_op jit(solution)/shard_map/ppermute | solution.py:1015
  55.8 4.3 %collective-permute-start.13 = (f32[8,2048]{1,0:T(8,128)S(1)}, f32[8,2048]{1,0:T(8,128)S(1)}, u32[]{:S(2)}, u32[]{:S(2)}) collective-permute-start(f32[8,2048]{1,0:T(8,128)S(1)} %add.243), channel_id=1, source_target_pairs={{0,8},{2,10},{4,12},{6,14},{8,0},{10,2},{12,4},{14,6},{16,24},{18,... | collective-permute-start | bytes 196616 | tf_op jit(solution)/shard_map/ppermute | solution.py:1015
  60.1 5.2 %collective-permute-start.15 = (f32[8,2048]{1,0:T(8,128)S(1)}, f32[8,2048]{1,0:T(8,128)S(1)}, u32[]{:S(2)}, u32[]{:S(2)}) collective-permute-start(f32[8,2048]{1,0:T(8,128)S(1)} %add.244), channel_id=1, source_target_pairs={{0,16},{2,18},{4,20},{6,22},{8,24},{10,26},{12,28},{14,30},{16,0},... | collective-permute-start | bytes 196616 | tf_op jit(solution)/shard_map/ppermute | solution.py:1015
  65.4 14.4 %collective-permute-start.20 = (bf16[2304,256]{1,0:T(8,128)(2,1)S(1)}, bf16[2304,256]{1,0:T(8,128)(2,1)S(1)}, u32[]{:S(2)}, u32[]{:S(2)}) collective-permute-start(bf16[2304,256]{1,0:T(8,128)(2,1)S(1)} %collective-permute-done.19.r1), channel_id=1, source_target_pairs={{0,2},{2,0},{4,6},{6,4},{8,10},{10,8},{12,14},{14,12},{16,18},{18,... | collective-permute-start | bytes 3538952 | tf_op jit(solution)/shard_map/ppermute | solution.py:1015
  65.4 20.9 %collective-permute-start.25 = (bf16[1552,256]{1,0:T(8,128)(2,1)S(1)}, bf16[1552,256]{1,0:T(8,128)(2,1)S(1)}, u32[]{:S(2)}, u32[]{:S(2)}) collective-permute-start(bf16[1552,256]{1,0:T(8,128)(2,1)S(1)} %get-tuple-element.237), channel_id=1, source_target_pairs={{0,1},{1,0},{2,3},{3,2},{4,5},{5,4},{6,7},{7,6},{8,9},{9,8},{10,11... | collective-permute-start | bytes 2383880 | tf_op jit(solution)/shard_map/ppermute | solution.py:1015
  72.5 3.7 %collective-permute-start.17 = (f32[4,512]{1,0:T(4,128)S(1)}, f32[4,512]{1,0:T(4,128)S(1)}, u32[]{:S(2)}, u32[]{:S(2)}) collective-permute-start(f32[4,512]{1,0:T(4,128)S(1)} %add.246), channel_id=1, source_target_pairs={{0,4},{2,6},{4,0},{6,2},{8,12},{10,14},{12,8},{14,10},{16,20},{18,... | collective-permute-start | bytes 24584 | tf_op jit(solution)/shard_map/ppermute | solution.py:1015
  76.1 3.7 %collective-permute-start.18 = (f32[4,512]{1,0:T(4,128)S(1)}, f32[4,512]{1,0:T(4,128)S(1)}, u32[]{:S(2)}, u32[]{:S(2)}) collective-permute-start(f32[4,512]{1,0:T(4,128)S(1)} %add.247), channel_id=1, source_target_pairs={{0,8},{2,10},{4,12},{6,14},{8,0},{10,2},{12,4},{14,6},{16,24},{18,... | collective-permute-start | bytes 24584 | tf_op jit(solution)/shard_map/ppermute | solution.py:1015
  79.8 4.6 %collective-permute-start.21 = (f32[4,512]{1,0:T(4,128)S(1)}, f32[4,512]{1,0:T(4,128)S(1)}, u32[]{:S(2)}, u32[]{:S(2)}) collective-permute-start(f32[4,512]{1,0:T(4,128)S(1)} %add.248), channel_id=1, source_target_pairs={{0,16},{2,18},{4,20},{6,22},{8,24},{10,26},{12,28},{14,30},{16,0},... | collective-permute-start | bytes 24584 | tf_op jit(solution)/shard_map/ppermute | solution.py:1015
  86.4 10.2 %collective-permute-start.26 = (bf16[1552,256]{1,0:T(8,128)(2,1)S(1)}, bf16[1552,256]{1,0:T(8,128)(2,1)S(1)}, u32[]{:S(2)}, u32[]{:S(2)}) collective-permute-start(bf16[1552,256]{1,0:T(8,128)(2,1)S(1)} %collective-permute-done.25.r1), channel_id=1, source_target_pairs={{0,2},{2,0},{4,6},{6,4},{8,10},{10,8},{12,14},{14,12},{16,18},{18,... | collective-permute-start | bytes 2383880 | tf_op jit(solution)/shard_map/ppermute | solution.py:1015
  86.5 27.3 %collective-permute-start.32 = (bf16[224,1024]{1,0:T(8,128)(2,1)S(1)}, bf16[224,1024]{1,0:T(8,128)(2,1)S(1)}, u32[]{:S(2)}, u32[]{:S(2)}) collective-permute-start(bf16[224,1024]{1,0:T(8,128)(2,1)S(1)} %bitcast.49), channel_id=1, source_target_pairs={{0,1},{1,0},{2,3},{3,2},{4,5},{5,4},{6,7},{7,6},{8,9},{9,8},{10,11... | collective-permute-start | bytes 1376264 | tf_op jit(solution)/shard_map/ppermute | solution.py:1015
  89.2 3.7 %collective-permute-start.23 = (f32[4,512]{1,0:T(4,128)S(1)}, f32[4,512]{1,0:T(4,128)S(1)}, u32[]{:S(2)}, u32[]{:S(2)}) collective-permute-start(f32[4,512]{1,0:T(4,128)S(1)} %add.250), channel_id=1, source_target_pairs={{0,4},{2,6},{4,0},{6,2},{8,12},{10,14},{12,8},{14,10},{16,20},{18,... | collective-permute-start | bytes 24584 | tf_op jit(solution)/shard_map/ppermute | solution.py:1015
  92.9 3.7 %collective-permute-start.24 = (f32[4,512]{1,0:T(4,128)S(1)}, f32[4,512]{1,0:T(4,128)S(1)}, u32[]{:S(2)}, u32[]{:S(2)}) collective-permute-start(f32[4,512]{1,0:T(4,128)S(1)} %add.251), channel_id=1, source_target_pairs={{0,8},{2,10},{4,12},{6,14},{8,0},{10,2},{12,4},{14,6},{16,24},{18,... | collective-permute-start | bytes 24584 | tf_op jit(solution)/shard_map/ppermute | solution.py:1015
  96.6 4.6 %collective-permute-start.27 = (f32[4,512]{1,0:T(4,128)S(1)}, f32[4,512]{1,0:T(4,128)S(1)}, u32[]{:S(2)}, u32[]{:S(2)}) collective-permute-start(f32[4,512]{1,0:T(4,128)S(1)} %add.252), channel_id=1, source_target_pairs={{0,16},{2,18},{4,20},{6,22},{8,24},{10,26},{12,28},{14,30},{16,0},... | collective-permute-start | bytes 24584 | tf_op jit(solution)/shard_map/ppermute | solution.py:1015
  104.2 4.0 %collective-permute-start.29 = (f32[4,2048]{1,0:T(4,128)S(1)}, f32[4,2048]{1,0:T(4,128)S(1)}, u32[]{:S(2)}, u32[]{:S(2)}) collective-permute-start(f32[4,2048]{1,0:T(4,128)S(1)} %add.254), channel_id=1, source_target_pairs={{0,4},{2,6},{4,0},{6,2},{8,12},{10,14},{12,8},{14,10},{16,20},{18,... | collective-permute-start | bytes 98312 | tf_op jit(solution)/shard_map/ppermute | solution.py:1015
  108.2 4.0 %collective-permute-start.30 = (f32[4,2048]{1,0:T(4,128)S(1)}, f32[4,2048]{1,0:T(4,128)S(1)}, u32[]{:S(2)}, u32[]{:S(2)}) collective-permute-start(f32[4,2048]{1,0:T(4,128)S(1)} %add.255), channel_id=1, source_target_pairs={{0,8},{2,10},{4,12},{6,14},{8,0},{10,2},{12,4},{14,6},{16,24},{18,... | collective-permute-start | bytes 98312 | tf_op jit(solution)/shard_map/ppermute | solution.py:1015
  112.2 4.9 %collective-permute-start.31 = (f32[4,2048]{1,0:T(4,128)S(1)}, f32[4,2048]{1,0:T(4,128)S(1)}, u32[]{:S(2)}, u32[]{:S(2)}) collective-permute-start(f32[4,2048]{1,0:T(4,128)S(1)} %add.256), channel_id=1, source_target_pairs={{0,16},{2,18},{4,20},{6,22},{8,24},{10,26},{12,28},{14,30},{16,0},... | collective-permute-start | bytes 98312 | tf_op jit(solution)/shard_map/ppermute | solution.py:1015
  124.6 4.0 %collective-permute-start.34 = (f32[4,2048]{1,0:T(4,128)S(1)}, f32[4,2048]{1,0:T(4,128)S(1)}, u32[]{:S(2)}, u32[]{:S(2)}) collective-permute-start(f32[4,2048]{1,0:T(4,128)S(1)} %add.258), channel_id=1, source_target_pairs={{0,4},{2,6},{4,0},{6,2},{8,12},{10,14},{12,8},{14,10},{16,20},{18,... | collective-permute-start | bytes 98312 | tf_op jit(solution)/shard_map/ppermute | solution.py:1015
  128.6 4.0 %collective-permute-start.35 = (f32[4,2048]{1,0:T(4,128)S(1)}, f32[4,2048]{1,0:T(4,128)S(1)}, u32[]{:S(2)}, u32[]{:S(2)}) collective-permute-start(f32[4,2048]{1,0:T(4,128)S(1)} %add.259), channel_id=1, source_target_pairs={{0,8},{2,10},{4,12},{6,14},{8,0},{10,2},{12,4},{14,6},{16,24},{18,... | collective-permute-start | bytes 98312 | tf_op jit(solution)/shard_map/ppermute | solution.py:1015
  132.6 4.9 %collective-permute-start.36 = (f32[4,2048]{1,0:T(4,128)S(1)}, f32[4,2048]{1,0:T(4,128)S(1)}, u32[]{:S(2)}, u32[]{:S(2)}) collective-permute-start(f32[4,2048]{1,0:T(4,128)S(1)} %add.260), channel_id=1, source_target_pairs={{0,16},{2,18},{4,20},{6,22},{8,24},{10,26},{12,28},{14,30},{16,0},... | collective-permute-start | bytes 98312 | tf_op jit(solution)/shard_map/ppermute | solution.py:1015
  141.3 3.9 %collective-permute-start.38 = (f32[12,512]{1,0:T(8,128)S(1)}, f32[12,512]{1,0:T(8,128)S(1)}, u32[]{:S(2)}, u32[]{:S(2)}) collective-permute-start(f32[12,512]{1,0:T(8,128)S(1)} %add.262), channel_id=1, source_target_pairs={{0,4},{2,6},{4,0},{6,2},{8,12},{10,14},{12,8},{14,10},{16,20},{18,... | collective-permute-start | bytes 73736 | tf_op jit(solution)/shard_map/ppermute | solution.py:1015
  145.2 3.9 %collective-permute-start.39 = (f32[12,512]{1,0:T(8,128)S(1)}, f32[12,512]{1,0:T(8,128)S(1)}, u32[]{:S(2)}, u32[]{:S(2)}) collective-permute-start(f32[12,512]{1,0:T(8,128)S(1)} %add.263), channel_id=1, source_target_pairs={{0,8},{2,10},{4,12},{6,14},{8,0},{10,2},{12,4},{14,6},{16,24},{18,... | collective-permute-start | bytes 73736 | tf_op jit(solution)/shard_map/ppermute | solution.py:1015
  149.1 4.8 %collective-permute-start.40 = (f32[12,512]{1,0:T(8,128)S(1)}, f32[12,512]{1,0:T(8,128)S(1)}, u32[]{:S(2)}, u32[]{:S(2)}) collective-permute-start(f32[12,512]{1,0:T(8,128)S(1)} %add.264), channel_id=1, source_target_pairs={{0,16},{2,18},{4,20},{6,22},{8,24},{10,26},{12,28},{14,30},{16,0},... | collective-permute-start | bytes 73736 | tf_op jit(solution)/shard_map/ppermute | solution.py:1015
  161.9 3.8 %collective-permute-start.43 = (bf16[8,416,256]{2,1,0:T(8,128)(2,1)S(1)}, bf16[8,416,256]{2,1,0:T(8,128)(2,1)S(1)}, u32[]{:S(2)}, u32[]{:S(2)}) collective-permute-start(bf16[8,416,256]{2,1,0:T(8,128)(2,1)S(1)} %get-tuple-element.274), channel_id=1, source_target_pairs={{0,2},{2,0},{4,6},{6,4},{8,10},{10,8},{12,14},{14,12},{16,18},{18,... | collective-permute-start | bytes 5111816 | tf_op jit(solution)/shard_map/ppermute | solution.py:1015
  162.1 3.7 %collective-permute-start.42 = (f32[4,512]{1,0:T(4,128)S(1)}, f32[4,512]{1,0:T(4,128)S(1)}, u32[]{:S(2)}, u32[]{:S(2)}) collective-permute-start(f32[4,512]{1,0:T(4,128)S(1)} %add.266), channel_id=1, source_target_pairs={{0,4},{2,6},{4,0},{6,2},{8,12},{10,14},{12,8},{14,10},{16,20},{18,... | collective-permute-start | bytes 24584 | tf_op jit(solution)/shard_map/ppermute | solution.py:1015
  165.9 20.9 %collective-permute-start.46 = (bf16[4,416,256]{2,1,0:T(8,128)(2,1)S(1)}, bf16[4,416,256]{2,1,0:T(8,128)(2,1)S(1)}, u32[]{:S(2)}, u32[]{:S(2)}) collective-permute-start(bf16[4,416,256]{2,1,0:T(8,128)(2,1)S(1)} %get-tuple-element.291), channel_id=1, source_target_pairs={{0,4},{2,6},{4,0},{6,2},{8,12},{10,14},{12,8},{14,10},{16,20},{18,... | collective-permute-start | bytes 2555912 | tf_op jit(solution)/shard_map/ppermute | solution.py:1015
  167.5 3.7 %collective-permute-start.44 = (f32[4,512]{1,0:T(4,128)S(1)}, f32[4,512]{1,0:T(4,128)S(1)}, u32[]{:S(2)}, u32[]{:S(2)}) collective-permute-start(f32[4,512]{1,0:T(4,128)S(1)} %add.267), channel_id=1, source_target_pairs={{0,8},{2,10},{4,12},{6,14},{8,0},{10,2},{12,4},{14,6},{16,24},{18,... | collective-permute-start | bytes 24584 | tf_op jit(solution)/shard_map/ppermute | solution.py:1015
  171.2 4.5 %collective-permute-start.45 = (f32[4,512]{1,0:T(4,128)S(1)}, f32[4,512]{1,0:T(4,128)S(1)}, u32[]{:S(2)}, u32[]{:S(2)}) collective-permute-start(f32[4,512]{1,0:T(4,128)S(1)} %add.270), channel_id=1, source_target_pairs={{0,16},{2,18},{4,20},{6,22},{8,24},{10,26},{12,28},{14,30},{16,0},... | collective-permute-start | bytes 24584 | tf_op jit(solution)/shard_map/ppermute | solution.py:1015
  188.1 8.9 %collective-permute-start.50 = (bf16[8,256,256]{2,1,0:T(8,128)(2,1)S(1)}, bf16[8,256,256]{2,1,0:T(8,128)(2,1)S(1)}, u32[]{:S(2)}, u32[]{:S(2)}) collective-permute-start(bf16[8,256,256]{2,1,0:T(8,128)(2,1)S(1)} %get-tuple-element.294), channel_id=1, source_target_pairs={{0,2},{2,0},{4,6},{6,4},{8,10},{10,8},{12,14},{14,12},{16,18},{18,... | collective-permute-start | bytes 3145736 | tf_op jit(solution)/shard_map/ppermute | solution.py:1015
  188.3 4.4 %collective-permute-start.48 = (f32[8,2048]{1,0:T(8,128)S(1)}, f32[8,2048]{1,0:T(8,128)S(1)}, u32[]{:S(2)}, u32[]{:S(2)}) collective-permute-start(f32[8,2048]{1,0:T(8,128)S(1)} %add.272), channel_id=1, source_target_pairs={{0,4},{2,6},{4,0},{6,2},{8,12},{10,14},{12,8},{14,10},{16,20},{18,... | collective-permute-start | bytes 196616 | tf_op jit(solution)/shard_map/ppermute | solution.py:1015
  192.6 4.3 %collective-permute-start.49 = (f32[8,2048]{1,0:T(8,128)S(1)}, f32[8,2048]{1,0:T(8,128)S(1)}, u32[]{:S(2)}, u32[]{:S(2)}) collective-permute-start(f32[8,2048]{1,0:T(8,128)S(1)} %add.273), channel_id=1, source_target_pairs={{0,8},{2,10},{4,12},{6,14},{8,0},{10,2},{12,4},{14,6},{16,24},{18,... | collective-permute-start | bytes 196616 | tf_op jit(solution)/shard_map/ppermute | solution.py:1015
  197.1 5.2 %collective-permute-start.51 = (f32[8,2048]{1,0:T(8,128)S(1)}, f32[8,2048]{1,0:T(8,128)S(1)}, u32[]{:S(2)}, u32[]{:S(2)}) collective-permute-start(f32[8,2048]{1,0:T(8,128)S(1)} %add.274), channel_id=1, source_target_pairs={{0,16},{2,18},{4,20},{6,22},{8,24},{10,26},{12,28},{14,30},{16,0},... | collective-permute-start | bytes 196616 | tf_op jit(solution)/shard_map/ppermute | solution.py:1015
  202.4 11.1 %collective-permute-start.53 = (bf16[4,256,256]{2,1,0:T(8,128)(2,1)S(1)}, bf16[4,256,256]{2,1,0:T(8,128)(2,1)S(1)}, u32[]{:S(2)}, u32[]{:S(2)}) collective-permute-start(bf16[4,256,256]{2,1,0:T(8,128)(2,1)S(1)} %get-tuple-element.307), channel_id=1, source_target_pairs={{0,4},{2,6},{4,0},{6,2},{8,12},{10,14},{12,8},{14,10},{16,20},{18,... | collective-permute-start | bytes 1572872 | tf_op jit(solution)/shard_map/ppermute | solution.py:1015
  204.0 8.8 %collective-permute-start.52 = (bf16[2,416,256]{2,1,0:T(8,128)(2,1)S(1)}, bf16[2,416,256]{2,1,0:T(8,128)(2,1)S(1)}, u32[]{:S(2)}, u32[]{:S(2)}) collective-permute-start(bf16[2,416,256]{2,1,0:T(8,128)(2,1)S(1)} %get-tuple-element.306), channel_id=1, source_target_pairs={{0,8},{2,10},{4,12},{6,14},{8,0},{10,2},{12,4},{14,6},{16,24},{18,... | collective-permute-start | bytes 1277960 | tf_op jit(solution)/shard_map/ppermute | solution.py:1015
  214.7 4.1 %collective-permute-start.56 = (bf16[8,384,256]{2,1,0:T(8,128)(2,1)S(1)}, bf16[8,384,256]{2,1,0:T(8,128)(2,1)S(1)}, u32[]{:S(2)}, u32[]{:S(2)}) collective-permute-start(bf16[8,384,256]{2,1,0:T(8,128)(2,1)S(1)} %get-tuple-element.309), channel_id=1, source_target_pairs={{0,2},{2,0},{4,6},{6,4},{8,10},{10,8},{12,14},{14,12},{16,18},{18,... | collective-permute-start | bytes 4718600 | tf_op jit(solution)/shard_map/ppermute | solution.py:1015
  214.9 3.9 %collective-permute-start.55 = (f32[12,512]{1,0:T(8,128)S(1)}, f32[12,512]{1,0:T(8,128)S(1)}, u32[]{:S(2)}, u32[]{:S(2)}) collective-permute-start(f32[12,512]{1,0:T(8,128)S(1)} %add.279), channel_id=1, source_target_pairs={{0,4},{2,6},{4,0},{6,2},{8,12},{10,14},{12,8},{14,10},{16,20},{18,... | collective-permute-start | bytes 73736 | tf_op jit(solution)/shard_map/ppermute | solution.py:1015
  219.0 19.0 %collective-permute-start.59 = (bf16[4,384,256]{2,1,0:T(8,128)(2,1)S(1)}, bf16[4,384,256]{2,1,0:T(8,128)(2,1)S(1)}, u32[]{:S(2)}, u32[]{:S(2)}) collective-permute-start(bf16[4,384,256]{2,1,0:T(8,128)(2,1)S(1)} %get-tuple-element.318), channel_id=1, source_target_pairs={{0,4},{2,6},{4,0},{6,2},{8,12},{10,14},{12,8},{14,10},{16,20},{18,... | collective-permute-start | bytes 2359304 | tf_op jit(solution)/shard_map/ppermute | solution.py:1015
  220.6 3.9 %collective-permute-start.57 = (f32[12,512]{1,0:T(8,128)S(1)}, f32[12,512]{1,0:T(8,128)S(1)}, u32[]{:S(2)}, u32[]{:S(2)}) collective-permute-start(f32[12,512]{1,0:T(8,128)S(1)} %add.280), channel_id=1, source_target_pairs={{0,8},{2,10},{4,12},{6,14},{8,0},{10,2},{12,4},{14,6},{16,24},{18,... | collective-permute-start | bytes 73736 | tf_op jit(solution)/shard_map/ppermute | solution.py:1015
  224.5 7.7 %collective-permute-start.58 = (f32[12,512]{1,0:T(8,128)S(1)}, f32[12,512]{1,0:T(8,128)S(1)}, u32[]{:S(2)}, u32[]{:S(2)}) collective-permute-start(f32[12,512]{1,0:T(8,128)S(1)} %add.283), channel_id=1, source_target_pairs={{0,16},{2,18},{4,20},{6,22},{8,24},{10,26},{12,28},{14,30},{16,0},... | collective-permute-start | bytes 73736 | tf_op jit(solution)/shard_map/ppermute | solution.py:1015
  239.2 11.6 %collective-permute-start.64 = (bf16[8,288,256]{2,1,0:T(8,128)(2,1)S(1)}, bf16[8,288,256]{2,1,0:T(8,128)(2,1)S(1)}, u32[]{:S(2)}, u32[]{:S(2)}) collective-permute-start(bf16[8,288,256]{2,1,0:T(8,128)(2,1)S(1)} %get-tuple-element.321), channel_id=1, source_target_pairs={{0,2},{2,0},{4,6},{6,4},{8,10},{10,8},{12,14},{14,12},{16,18},{18,... | collective-permute-start | bytes 3538952 | tf_op jit(solution)/shard_map/ppermute | solution.py:1015
  239.4 8.7 %collective-permute-start.72 = (bf16[2,256,256]{2,1,0:T(8,128)(2,1)S(1)}, bf16[2,256,256]{2,1,0:T(8,128)(2,1)S(1)}, u32[]{:S(2)}, u32[]{:S(2)}) collective-permute-start(bf16[2,256,256]{2,1,0:T(8,128)(2,1)S(1)} %get-tuple-element.379), channel_id=1, source_target_pairs={{0,8},{2,10},{4,12},{6,14},{8,0},{10,2},{12,4},{14,6},{16,24},{18,... | collective-permute-start | bytes 786440 | tf_op jit(solution)/shard_map/ppermute | solution.py:1015
  241.1 3.7 %collective-permute-start.61 = (f32[4,512]{1,0:T(4,128)S(1)}, f32[4,512]{1,0:T(4,128)S(1)}, u32[]{:S(2)}, u32[]{:S(2)}) collective-permute-start(f32[4,512]{1,0:T(4,128)S(1)} %add.285), channel_id=1, source_target_pairs={{0,4},{2,6},{4,0},{6,2},{8,12},{10,14},{12,8},{14,10},{16,20},{18,... | collective-permute-start | bytes 24584 | tf_op jit(solution)/shard_map/ppermute | solution.py:1015
  244.7 3.7 %collective-permute-start.62 = (f32[4,512]{1,0:T(4,128)S(1)}, f32[4,512]{1,0:T(4,128)S(1)}, u32[]{:S(2)}, u32[]{:S(2)}) collective-permute-start(f32[4,512]{1,0:T(4,128)S(1)} %add.286), channel_id=1, source_target_pairs={{0,8},{2,10},{4,12},{6,14},{8,0},{10,2},{12,4},{14,6},{16,24},{18,... | collective-permute-start | bytes 24584 | tf_op jit(solution)/shard_map/ppermute | solution.py:1015
  248.4 4.7 %collective-permute-start.63 = (f32[4,512]{1,0:T(4,128)S(1)}, f32[4,512]{1,0:T(4,128)S(1)}, u32[]{:S(2)}, u32[]{:S(2)}) collective-permute-start(f32[4,512]{1,0:T(4,128)S(1)} %add.287), channel_id=1, source_target_pairs={{0,16},{2,18},{4,20},{6,22},{8,24},{10,26},{12,28},{14,30},{16,0},... | collective-permute-start | bytes 24584 | tf_op jit(solution)/shard_map/ppermute | solution.py:1015
  250.9 16.0 %collective-permute-start.65 = (bf16[4,288,256]{2,1,0:T(8,128)(2,1)S(1)}, bf16[4,288,256]{2,1,0:T(8,128)(2,1)S(1)}, u32[]{:S(2)}, u32[]{:S(2)}) collective-permute-start(bf16[4,288,256]{2,1,0:T(8,128)(2,1)S(1)} %get-tuple-element.327), channel_id=1, source_target_pairs={{0,4},{2,6},{4,0},{6,2},{8,12},{10,14},{12,8},{14,10},{16,20},{18,... | collective-permute-start | bytes 1769480 | tf_op jit(solution)/shard_map/ppermute | solution.py:1015
  252.5 33.4 %collective-permute-start.73 = (bf16[1,672,256]{2,1,0:T(8,128)(2,1)S(1)}, bf16[1,672,256]{2,1,0:T(8,128)(2,1)S(1)}, u32[]{:S(2)}, u32[]{:S(2)}) collective-permute-start(bf16[1,672,256]{2,1,0:T(8,128)(2,1)S(1)} %pad_maximum_fusion.1), channel_id=1, source_target_pairs={{0,16},{2,18},{4,20},{6,22},{8,24},{10,26},{12,28},{14,30},{16,0},... | collective-permute-start | bytes 1032200 | tf_op jit(solution)/shard_map/ppermute | solution.py:1015
  255.1 3.7 %collective-permute-start.68 = (bf16[8,64,256]{2,1,0:T(8,128)(2,1)S(1)}, bf16[8,64,256]{2,1,0:T(8,128)(2,1)S(1)}, u32[]{:S(2)}, u32[]{:S(2)}) collective-permute-start(bf16[8,64,256]{2,1,0:T(8,128)(2,1)S(1)} %get-tuple-element.332), channel_id=1, source_target_pairs={{0,2},{2,0},{4,6},{6,4},{8,10},{10,8},{12,14},{14,12},{16,18},{18,... | collective-permute-start | bytes 786440 | tf_op jit(solution)/shard_map/ppermute | solution.py:1015
  255.2 18.4 %collective-permute-start.74 = (bf16[2,384,256]{2,1,0:T(8,128)(2,1)S(1)}, bf16[2,384,256]{2,1,0:T(8,128)(2,1)S(1)}, u32[]{:S(2)}, u32[]{:S(2)}) collective-permute-start(bf16[2,384,256]{2,1,0:T(8,128)(2,1)S(1)} %get-tuple-element.339), channel_id=1, source_target_pairs={{0,8},{2,10},{4,12},{6,14},{8,0},{10,2},{12,4},{14,6},{16,24},{18,... | collective-permute-start | bytes 1179656 | tf_op jit(solution)/shard_map/ppermute | solution.py:1015
  258.9 17.1 %collective-permute-start.69 = (bf16[4,64,256]{2,1,0:T(8,128)(2,1)S(1)}, bf16[4,64,256]{2,1,0:T(8,128)(2,1)S(1)}, u32[]{:S(2)}, u32[]{:S(2)}) collective-permute-start(bf16[4,64,256]{2,1,0:T(8,128)(2,1)S(1)} %get-tuple-element.389), channel_id=1, source_target_pairs={{0,4},{2,6},{4,0},{6,2},{8,12},{10,14},{12,8},{14,10},{16,20},{18,... | collective-permute-start | bytes 393224 | tf_op jit(solution)/shard_map/ppermute | solution.py:1015
  267.0 14.9 %collective-permute-start.66 = (bf16[2,288,256]{2,1,0:T(8,128)(2,1)S(1)}, bf16[2,288,256]{2,1,0:T(8,128)(2,1)S(1)}, u32[]{:S(2)}, u32[]{:S(2)}) collective-permute-start(bf16[2,288,256]{2,1,0:T(8,128)(2,1)S(1)} %get-tuple-element.330), channel_id=1, source_target_pairs={{0,8},{2,10},{4,12},{6,14},{8,0},{10,2},{12,4},{14,6},{16,24},{18,... | collective-permute-start | bytes 884744 | tf_op jit(solution)/shard_map/ppermute | solution.py:1015
  273.6 15.3 %collective-permute-start.75 = (bf16[1,384,256]{2,1,0:T(8,128)(2,1)S(1)}, bf16[1,384,256]{2,1,0:T(8,128)(2,1)S(1)}, u32[]{:S(2)}, u32[]{:S(2)}) collective-permute-start(bf16[1,384,256]{2,1,0:T(8,128)(2,1)S(1)} %get-tuple-element.382), channel_id=1, source_target_pairs={{0,16},{2,18},{4,20},{6,22},{8,24},{10,26},{12,28},{14,30},{16,0},... | collective-permute-start | bytes 589832 | tf_op jit(solution)/shard_map/ppermute | solution.py:1015
  276.0 9.5 %collective-permute-start.70 = (bf16[2,64,256]{2,1,0:T(8,128)(2,1)S(1)}, bf16[2,64,256]{2,1,0:T(8,128)(2,1)S(1)}, u32[]{:S(2)}, u32[]{:S(2)}) collective-permute-start(bf16[2,64,256]{2,1,0:T(8,128)(2,1)S(1)} %get-tuple-element.391), channel_id=1, source_target_pairs={{0,8},{2,10},{4,12},{6,14},{8,0},{10,2},{12,4},{14,6},{16,24},{18,... | collective-permute-start | bytes 196616 | tf_op jit(solution)/shard_map/ppermute | solution.py:1015
  281.9 10.9 %collective-permute-start.67 = (bf16[1,288,256]{2,1,0:T(8,128)(2,1)S(1)}, bf16[1,288,256]{2,1,0:T(8,128)(2,1)S(1)}, u32[]{:S(2)}, u32[]{:S(2)}) collective-permute-start(bf16[1,288,256]{2,1,0:T(8,128)(2,1)S(1)} %get-tuple-element.384), channel_id=1, source_target_pairs={{0,16},{2,18},{4,20},{6,22},{8,24},{10,26},{12,28},{14,30},{16,0},... | collective-permute-start | bytes 442376 | tf_op jit(solution)/shard_map/ppermute | solution.py:1015
  285.5 7.3 %collective-permute-start.71 = (bf16[1,64,256]{2,1,0:T(8,128)(2,1)S(1)}, bf16[1,64,256]{2,1,0:T(8,128)(2,1)S(1)}, u32[]{:S(2)}, u32[]{:S(2)}) collective-permute-start(bf16[1,64,256]{2,1,0:T(8,128)(2,1)S(1)} %get-tuple-element.392), channel_id=1, source_target_pairs={{0,16},{2,18},{4,20},{6,22},{8,24},{10,26},{12,28},{14,30},{16,0},... | collective-permute-start | bytes 98312 | tf_op jit(solution)/shard_map/ppermute | solution.py:1015
  (13 other events, 16.8 us)

commit v5 on v4

--- a/solution.py
+++ b/solution.py
@@ -52,25 +52,30 @@
     return a, low(v - f32(a))
 
 
-def split3(v):
-    a = low(v)
-    r = v - f32(a)
-    b = low(r)
-    return a, b, low(r - f32(b))
+def stack3(v):
+    a = f32(low(v))
+    r = v - a
+    b = f32(low(r))
+    return low(jnp.concatenate([a, b, r - b, jnp.zeros_like(v)], axis=0))
+
+
+def sum3(p):
+    return p[0:8] + p[8:16] + p[16:24]
 
 
 def dot3(v, w):
-    return sum(mm(p, w) for p in split3(v))
+    return sum3(mm(stack3(v), w))
 
 
 def dot3_nt(v, w):
-    return sum(mm_nt(p, w) for p in split3(v))
+    return sum3(mm_nt(stack3(v), w))
 
 
 def outer(a, b):
-    a1, a2 = split2(a)
-    b1, b2 = split2(b)
-    return mm_tn(a1, b1) + mm_tn(a1, b2) + mm_tn(a2, b1)
+    a1, b1 = f32(low(a)), f32(low(b))
+    zeros = jnp.zeros_like
+    left = low(jnp.concatenate([a1, a1, a - a1, zeros(a)], axis=0))
+    return mm_tn(left, low(jnp.concatenate([b1, b - b1, b1, zeros(b)], axis=0)))
 
 
 def sigmoid(v):
@@ -175,7 +180,10 @@
     return (p & 1) * 8 + (p & 2) * 2 + (p & 4) // 2 + (p & 8) // 8
 
 
-def setup_kernel(exact, crop, micro, fs, isc, keep, keep1, keep_half, sh, perm):
+def setup_kernel(
+    exact, crop, micro, px, w1_far, fs, isc, keep, keep1, keep_half, sh, perm, st, x, w1, flat, sems
+):
+    copies = copy_all([(px, x), (w1_far, w1)], sems)
     n = lax.axis_index("narrow").astype(jnp.int32)
     w = lax.axis_index("wide").astype(jnp.int32)
     isc[NARROW] = n
@@ -231,10 +239,6 @@
                 jnp.where(((r >> 3) == half) & (place == c * 8 + (r & 7)), 1.0, 0.0)
             )
         perm[half] = low(jnp.concatenate(planes, axis=0))
-
-
-def one_half_kernel(fs, px, keep, w1_far, st, x, w1, flat, sems):
-    copies = copy_all([(px, x), (w1_far, w1)], sems)
     copies[0].wait()
     for b in range(B):
         flat[b * HALF : (b + 1) * HALF, :] = x[b]
@@ -242,7 +246,7 @@
 
     def body(c):
         sl = cols(c)
-        v = mm(flat[...], w1[:, sl]) * keep[...]
+        v = mm(flat[...], w1[:, sl]) * keep_half[...]
         sums = [jnp.sum(v[b * HALF : (b + 1) * HALF], axis=0, keepdims=True) for b in range(B)]
         v2 = v * v
         sq = [jnp.sum(v2[b * HALF : (b + 1) * HALF], axis=0, keepdims=True) for b in range(B)]
@@ -255,10 +259,11 @@
 
 
 def stage_two_kernel(
-    fs, isc, own, other, part, part_other, perm, keep1, keep, w1, ws, gb, sh,
-    xp, strided, x1, col, pre2, st, tot1, tmp, hid, tot,
+    fs, isc, own, other, part, part_other, perm, keep1, keep, w1, ws_far, gb, sh,
+    xp, strided, x1, col, pre2, st, tot1, tmp, hid, tot, ws, sems,
 ):
     n = isc[NARROW]
+    copies = copy_all([(ws_far.at[3 * k : 3 * k + 3], ws.at[3 * k : 3 * k + 3]) for k in range(3)], sems)
     tot[...] = part[...] + part_other[...]
     tot1[...] = tot[...]
 
@@ -289,6 +294,7 @@
         if p == 0 or q == 0:
             h = low(mm(sh[3 * (0 if p == 0 else 1) + (0 if q == 0 else 1)], h))
         col[t] = h
+    wait_all(copies)
 
     def second(c):
         sl = cols(c)
@@ -948,10 +954,10 @@
 VECTORS = (512,) * 6 + (2048,) * 5 + (128,) * 2 + (256,) * 2 + (1024,) * 3
 
 
-def pack_kernel(isc, w5, w4, w6, ex, sq, ws_far, *refs):
+def pack_kernel(isc, w5, w4, w6, ex, sq, *refs):
     far, refs = refs[:18], refs[18:]
-    out, w5_half, w4_half, gb, vec1, sqb, vown, ws, w6v, exv, sqv, rows = refs[:12]
-    vecs, sems = refs[12:30], refs[30]
+    out, w5_half, w4_half, gb, vec1, sqb, vown, w6v, exv, sqv, rows = refs[:11]
+    vecs, sems = refs[11:29], refs[29]
     core = isc[CORE]
     pairs = [(f, v) for f, v in zip(far, vecs)] + [
         (w6.at[at_rows(core * 128, 128)], w6v),
@@ -959,7 +965,6 @@
         (sq.at[at_rows(core * 512, 512)], sqv),
         (w4.at[at_rows(core * 512, 512)], w4_half),
         (w5.at[at_rows(core * 2304, 2304)], w5_half),
-        (ws_far, ws),
     ]
     copies = copy_all(pairs, sems)
     wait_all(copies[:21])
@@ -1058,20 +1063,16 @@
     other_px = swap(own_px, "narrow", pair)
     ws_far = first_spatial.reshape(9, 512, 512)
 
-    fs_, isc_, keep, keep1, keep_half, sh, perm = call(
+    fs_, isc_, keep, keep1, keep_half, sh, perm, st1, xown, w1 = call(
         functools.partial(setup_kernel, exact),
         [
-            pltpu.SMEM((13,), F32), pltpu.SMEM((18,), jnp.int32), f(M, 1), f(4, M, 1), f(HROWS, 1),
-            h(9, M, M), h(2, M, HALF),
+            pltpu.SMEM((13,), F32), pltpu.SMEM((18,), jnp.int32), f(M, 1), f(4, M, 1), f(HROWS, 1), h(9, M, M), h(2, M, HALF),
+            f(4, 512), h(B, HALF, 1024), h(1024, 512),
         ],
-        [(SMEM, far(crop)[1]), (SMEM, far(micro)[1])], name="setup",
+        [(SMEM, far(crop)[1]), (SMEM, far(micro)[1]), far(own_px), far(first_reduce)],
+        [V((HROWS, 1024), BF), D((2,))], name="setup",
     )
     fs, isc = (SMEM, fs_), (SMEM, isc_)
-    st1, xown, w1 = call(
-        one_half_kernel, [f(4, 512), h(B, HALF, 1024), h(1024, 512)],
-        [fs, far(own_px), keep_half, far(first_reduce)],
-        [V((HROWS, 1024), BF), D((2,))], flops=5e8, name="one_half",
-    )
     part = steps(st1)[0][0]
 
     w5_own = second_spatial.reshape(9 * 512, 256)
@@ -1082,15 +1083,14 @@
         first_squeeze_bias, second_squeeze_bias,
         second_spatial_gain, second_spatial_bias, second_expand_gain, second_expand_bias, second_excite_bias,
     ]
-    pack, w5_half, w4_half, gb, vec1, sqb, vown, ws = call(
+    pack, w5_half, w4_half, gb, vec1, sqb, vown = call(
         pack_kernel,
         [
             ((PACK_ROWS, 256), BF), ((2304, 256), BF), ((512, 512), BF), f(8, 512), f(8, 2048), f(8, 128), h(16, 256),
-            h(9, 512, 512),
         ],
         [
             (SMEM, after(isc_, st1)), far(w5_own), far(second_reduce), far(second_expand), far(second_excite),
-            far(second_squeeze), far(ws_far),
+            far(second_squeeze),
         ] + [far(v) for v in vectors],
         [V((128, 2048), BF), V((64, 1024), BF), V((512, 128), BF), V((16, 256), F32)]
         + [V((size,), BF) for size in VECTORS] + [D((24,))],
@@ -1104,8 +1104,10 @@
     xp, strided, x1, col1, pre2, st2, tot1 = call(
         stage_two_kernel,
         [h(4, M, 1024), h(M, 1024), f(4, M, 512), h(9, M, 512), f(M, 512), f(4, 512), f(4, 512)],
-        [fs, isc, xown, other_px, part, part_other, perm, keep1, keep, w1, ws, gb, sh],
-        [V((4, M, 256), F32), V((4, M, 512), BF), V((4, 512), F32)],
+        [fs, isc, xown, other_px, part, part_other, perm, keep1, keep, w1, far(ws_far), gb, sh],
+        [
+            V((4, M, 256), F32), V((4, M, 512), BF), V((4, 512), F32), V((9, 512, 512), BF), D((3,)),
+        ],
         flops=4e9, size=2e7, name="stage_two",
     )
     parts2, sent2 = steps(st2, before={3: (w4_r1,)})

time: 294 us -> 293 us (level)
  Pallas kernels: 78.5 us -> 73 us
  waiting for transfers between devices: 124 us -> 127 us
    pallas_call x29 -> x28, Pallas kernels: 78.5 us -> 73 us  [call(): pl.pallas_call(body, out_shape=tuple((o if hasattr(o, 'memory_space') els...]
    ppermute x76, waiting for transfers between devices: 124 us -> 127 us  [swap(): return lax.ppermute(v, axis, pairs)]
  transfers between devices with their start and end apart: 76 -> 76, of which waited for: 57 -> 57; matrix products, arithmetic and copies ran while one was open for 0% -> 0% of each run, Pallas kernels for 21% -> 20%
where the time goes in v5:
time: 293 us; the launch traced here: 292 us
  waiting for transfers between devices  127 us (43%)
  starting transfers between devices  89.5 us (31%)
  Pallas kernels  73 us (25%)
    ppermute x76, waiting for transfers between devices, swap(): return lax.ppermute(v, axis, pairs)  127 us
    ppermute x76, starting transfers between devices, swap(): return lax.ppermute(v, axis, pairs)  89.5 us
    pallas_call x28, Pallas kernels, call(): pl.pallas_call(body, out_shape=tuple((o if hasattr(o, 'memory_space') els...  73 us
  transfers between devices with their start and end apart: 76, of which 57 were waited for; matrix products, arithmetic and copies ran while one was open for 0% of the time, Pallas kernels for 20%

profile of v5, /device:TPU:0, one launch (start us, length us, event | category | flops | bytes accessed | tf_op | source)
XLA Modules:
  0.0 292.2 jit_solution(3748899316941534621)
XLA Ops:
  0.7 3.0 %collective-permute-start = (bf16[4,112,1024]{2,1,0:T(8,128)(2,1)}, bf16[4,112,1024]{2,1,0:T(8,128)(2,1)S(1)}, u32[]{:S(2)}, u32[]{:S(2)}) collective-permute-start(bf16[4,112,1024]{2,1,0:T(8,128)(2,1)} %bitcast.46), channel_id=1, source_target_pairs={{0,1},{1,0},{2,3},{3,2},{4,5},{5,4},{6,7},{7,6},{8,9},{9,8},{10,11... | collective-permute-start | bytes 2752520 | tf_op jit(solution)/shard_map/ppermute | solution.py:1020
  3.7 2.9 setup.1
  9.3 2.2 collective-permute-done.2
  13.1 2.1 collective-permute-done.3
  15.2 2.6 collective-permute-start.4
  17.7 2.0 pack.1
  20.4 4.1 %collective-permute-done.5.part_other = f32[4,512]{1,0:T(4,128)S(1)} collective-permute-done((f32[4,512]{1,0:T(4,128)S(1)}, f32[4,512]{1,0:T(4,128)S(1)}, u32[]{:S(2)}, u32[]{:S(2)}) %collective-permute-start.5) | collective-permute-done | bytes 8224 | tf_op jit(solution)/shard_map/ppermute | solution.py:1020
  26.2 5.4 %stage_two.1 = (bf16[4,224,1024]{2,1,0:T(8,128)(2,1)S(1)}, bf16[224,1024]{1,0:T(8,128)(2,1)S(1)}, f32[4,224,512]{2,1,0:T(8,128)S(1)}, bf16[9,224,512]{2,1,0:T(8,...) custom-call(f32[13]{0:T(128)S(4)} %get-tuple-element.197.fs, ...), custom_call_target="tpu_custom_call" | custom-call | flops 40000000 | bytes 200000 | tf_op jit(solution)/shard_map/stage_two/pallas_call | solution.py:1005
  34.3 2.1 collective-permute-done.7
  40.6 2.1 collective-permute-done.8
  42.6 2.6 collective-permute-start.10
  45.2 3.1 %project.1 = (f32[224,2048]{1,0:T(8,128)S(1)}, f32[4,2048]{1,0:T(4,128)S(1)}, bf16[512,2048]{1,0:T(8,128)(2,1)S(1)}) custom-call(f32[13]{0:T(128)S(4)} %get-tuple-element.197.fs, bf16[224,1024]{1,0:T(8,128)(2,1)S(1)} %get-tuple-element.214.x.strided, f32[224,1]{1,0:T(8,128)S(1)} %get-tuple-element.206.keep, bf16[1024,2048]{1,0:T(8,128)(2,1)} %wp_far.3, ...), custom_call_target="tpu_custom_call" | custom-call | flops 10000000 | bytes 80000 | tf_op jit(solution)/shard_map/project/pallas_call | solution.py:1005
  53.0 2.8 collective-permute-done.12
  57.4 2.7 collective-permute-done.13
  61.6 3.8 %collective-permute-done.15 = f32[8,2048]{1,0:T(8,128)S(1)} collective-permute-done((f32[8,2048]{1,0:T(8,128)S(1)}, f32[8,2048]{1,0:T(8,128)S(1)}, u32[]{:S(2)}, u32[]{:S(2)}) %collective-permute-start.15) | collective-permute-done | bytes 65568 | tf_op jit(solution)/shard_map/ppermute | solution.py:1020
  67.3 3.7 %stage_four.1 = (bf16[224,2048]{1,0:T(8,128)(2,1)S(1)}, f32[224,512]{1,0:T(8,128)S(1)}, f32[4,512]{1,0:T(4,128)S(1)}, f32[8,2048]{1,0:T(8,128)S(1)}, f32[8,2048]...) custom-call(f32[13]{0:T(128)S(4)} %get-tuple-element.197.fs, ...), custom_call_target="tpu_custom_call" | custom-call | flops 10000000 | bytes 100000 | tf_op jit(solution)/shard_map/stage_four/pallas_call | solution.py:1005
  73.7 2.2 collective-permute-done.17
  77.5 2.1 collective-permute-done.18
  84.2 1.9 stage_five.1
  90.5 2.2 collective-permute-done.23
  94.2 2.1 collective-permute-done.24
  105.5 2.4 collective-permute-done.29
  109.6 2.3 collective-permute-done.30
  114.9 1.9 collective-permute-done.31
  116.8 5.2 %turn.1 = (bf16[224,1024]{1,0:T(8,128)(2,1)}, f32[224,2048]{1,0:T(8,128)S(1)}, f32[4,2048]{1,0:T(4,128)S(1)}, f32[8,512]{1,0:T(8,128)S(1)}, f32[4,2048]{1,0:T(4,...) custom-call(f32[13]{0:T(128)S(4)} %get-tuple-element.197.fs, ...), custom_call_target="tpu_custom_call" | custom-call | flops 10000000 | bytes 100000 | tf_op jit(solution)/shard_map/turn/pallas_call | solution.py:1005
  124.9 2.4 collective-permute-done.34
  128.9 2.3 collective-permute-done.35
  132.9 3.3 %collective-permute-done.36 = f32[4,2048]{1,0:T(4,128)S(1)} collective-permute-done((f32[4,2048]{1,0:T(4,128)S(1)}, f32[4,2048]{1,0:T(4,128)S(1)}, u32[]{:S(2)}, u32[]{:S(2)}) %collective-permute-start.36) | collective-permute-done | bytes 32800 | tf_op jit(solution)/shard_map/ppermute | solution.py:1020
  136.2 2.5 back_six.1
  141.4 2.4 collective-permute-done.38
  145.4 2.3 collective-permute-done.39
  149.3 3.3 %collective-permute-done.40 = f32[12,512]{1,0:T(8,128)S(1)} collective-permute-done((f32[12,512]{1,0:T(8,128)S(1)}, f32[12,512]{1,0:T(8,128)S(1)}, u32[]{:S(2)}, u32[]{:S(2)}) %collective-permute-start.40) | collective-permute-done | bytes 24608 | tf_op jit(solution)/shard_map/ppermute | solution.py:1020
  152.6 3.5 %back_five.1 = (bf16[224,512]{1,0:T(8,128)(2,1)S(1)}, f32[224,512]{1,0:T(8,128)S(1)}, f32[4,512]{1,0:T(4,128)S(1)}, f32[256]{0:T(256)}, f32[256]{0:T(256)}, /*index=5*/f32[1024]{0:T(1024)}, f32[128]{0:T(128)}, f32[5]{0:T(128)}) custom-call(f32[13]{0:T(128)S(4)} %get-tuple-element.197.fs, s32[18]{0:T(128)S(4)} %get-tuple-element.316.isc, ...), custom_call_target="tpu_custom_call" | custom-call | flops 20000000 | bytes 100000 | tf_op jit(solution)/shard_map/back_five/pallas_call | solution.py:1005
  156.1 3.2 %grads_a.1 = (bf16[8,416,256]{2,1,0:T(8,128)(2,1)S(1)}, bf16[8,416,256]{2,1,0:T(8,128)(2,1)S(1)}) custom-call(s32[18]{0:T(128)S(4)} %get-tuple-element.316.isc, bf16[224,512]{1,0:T(8,128)(2,1)S(1)} %get-tuple-element.264.h5, bf16[224,2048]{1,0:T(8,128)(2,1)S(1)} %get-tuple-element.265.d6, bf16[9,224,512]{2,1,0:T(8,128)(2,1)S(1)} %get-tuple-element.266.col4, ...), custom_call_target="tpu_custom_call" | custom-call | flops 20000000 | bytes 100000 | tf_op jit(solution)/shard_map/grads_a/pallas_call | solution.py:1005
  162.2 2.2 collective-permute-done.42
  167.7 2.1 collective-permute-done.44
  171.3 2.4 fetch_two.1.ws
  174.4 5.4 %back_four.1 = (bf16[224,512]{1,0:T(8,128)(2,1)S(1)}, f32[224,2048]{1,0:T(8,128)S(1)}, f32[8,2048]{1,0:T(8,128)S(1)}, f32[512]{0:T(512)}, f32[512]{0:T(512)}, /*...) custom-call(f32[13]{0:T(128)S(4)} %get-tuple-element.197.fs, ...), custom_call_target="tpu_custom_call" | custom-call | flops 10000000 | bytes 100000 | tf_op jit(solution)/shard_map/back_four/pallas_call | solution.py:1005
  180.9 4.5 %collective-permute-done.46 = bf16[4,416,256]{2,1,0:T(8,128)(2,1)S(1)} collective-permute-done((bf16[4,416,256]{2,1,0:T(8,128)(2,1)S(1)}, bf16[4,416,256]{2,1,0:T(8,128)(2,1)S(1)}, u32[]{:S(2)}, u32[]{:S(2)}) %collective-permute-start.46) | collective-permute-done | bytes 852000 | tf_op jit(solution)/shard_map/ppermute | solution.py:1020
  188.4 2.9 collective-permute-done.48
  192.9 2.7 collective-permute-done.49
  197.4 3.6 %collective-permute-done.51 = f32[8,2048]{1,0:T(8,128)S(1)} collective-permute-done((f32[8,2048]{1,0:T(8,128)S(1)}, f32[8,2048]{1,0:T(8,128)S(1)}, u32[]{:S(2)}, u32[]{:S(2)}) %collective-permute-start.51) | collective-permute-done | bytes 65568 | tf_op jit(solution)/shard_map/ppermute | solution.py:1020
  204.3 3.2 %back_three.1 = (bf16[224,2048]{1,0:T(8,128)(2,1)S(1)}, bf16[224,2048]{1,0:T(8,128)(2,1)S(1)}, f32[224,512]{1,0:T(8,128)S(1)}, f32[12,512]{1,0:T(8,128)S(1)}, f3...) custom-call(f32[13]{0:T(128)S(4)} %get-tuple-element.197.fs, f32[1,8,2048]{2,1,0:T(8,128)S(1)} %bitcast.39, ...), custom_call_target="tpu_custom_call" | custom-call | flops 10000000 | bytes 100000 | tf_op jit(solution)/shard_map/back_three/pallas_call | solution.py:1005
  207.5 1.9 grads_c.1
  209.4 2.0 collective-permute-done.52
  215.0 2.4 collective-permute-done.55
  220.8 2.3 collective-permute-done.57
  223.1 2.0 collective-permute-start.58
  225.1 5.7 %placed.1 = f32[448,1024]{1,0:T(8,128)S(1)} custom-call(s32[18]{0:T(128)S(4)} %get-tuple-element.316.isc, bf16[224,2048]{1,0:T(8,128)(2,1)S(1)} %get-tuple-element.300.dproj, bf16[1024,2048]{1,0:T(8,128)(2,1)} %wp_far.3), custom_call_target="tpu_custom_call" | custom-call | flops 10000000 | bytes 100000 | tf_op jit(solution)/shard_map/placed/pallas_call | solution.py:1005
  230.8 3.0 %back_two.1 = (bf16[224,512]{1,0:T(8,128)(2,1)S(1)}, f32[4,224,512]{2,1,0:T(8,128)S(1)}, f32[4,512]{1,0:T(4,128)S(1)}, f32[512]{0:T(512)}, f32[512]{0:T(512)}, /*index=5*/f32[2048]{0:T(1024)}, f32[128]{0:T(128)}) custom-call(f32[13]{0:T(128)S(4)} %get-tuple-element.197.fs, f32[1,12,512]{2,1,0:T(8,128)S(1)} %add_bitcast_fusion.1.parts, ...), custom_call_target="tpu_custom_call" | custom-call | flops 20000000 | bytes 100000 | tf_op jit(solution)/shard_map/back_two/pallas_call | solution.py:1005
  233.8 1.8 grads_d.1
  241.2 2.1 collective-permute-done.61
  243.8 3.0 %collective-permute-done.72 = bf16[2,256,256]{2,1,0:T(8,128)(2,1)S(1)} collective-permute-done((bf16[2,256,256]{2,1,0:T(8,128)(2,1)S(1)}, bf16[2,256,256]{2,1,0:T(8,128)(2,1)S(1)}, u32[]{:S(2)}, u32[]{:S(2)}) %collective-permute-start.72) | collective-permute-done | bytes 262176 | tf_op jit(solution)/shard_map/ppermute | solution.py:1020
  247.0 2.4 collective-permute-start.63
  251.7 2.0 back_one.1
  255.3 2.1 image.1
  258.9 6.6 %collective-permute-done.65 = bf16[4,288,256]{2,1,0:T(8,128)(2,1)S(1)} collective-permute-done((bf16[4,288,256]{2,1,0:T(8,128)(2,1)S(1)}, bf16[4,288,256]{2,1,0:T(8,128)(2,1)S(1)}, u32[]{:S(2)}, u32[]{:S(2)}) %collective-permute-start.65) | collective-permute-done | bytes 589856 | tf_op jit(solution)/shard_map/ppermute | solution.py:1020
  267.1 5.2 %collective-permute-done.74 = bf16[2,384,256]{2,1,0:T(8,128)(2,1)S(1)} collective-permute-done((bf16[2,384,256]{2,1,0:T(8,128)(2,1)S(1)}, bf16[2,384,256]{2,1,0:T(8,128)(2,1)S(1)}, u32[]{:S(2)}, u32[]{:S(2)}) %collective-permute-start.74) | collective-permute-done | bytes 393248 | tf_op jit(solution)/shard_map/ppermute | solution.py:1020
  272.3 2.3 collective-permute-start.75
  274.6 2.5 collective-permute-start.70
  277.1 3.4 %collective-permute-done.66 = bf16[2,288,256]{2,1,0:T(8,128)(2,1)S(1)} collective-permute-done((bf16[2,288,256]{2,1,0:T(8,128)(2,1)S(1)}, bf16[2,288,256]{2,1,0:T(8,128)(2,1)S(1)}, u32[]{:S(2)}, u32[]{:S(2)}) %collective-permute-start.66) | collective-permute-done | bytes 294944 | tf_op jit(solution)/shard_map/ppermute | solution.py:1020
  281.5 2.7 collective-permute-done.70
  284.6 3.0 %collective-permute-done.75.d = bf16[1,384,256]{2,1,0:T(8,128)(2,1)S(1)} collective-permute-done((bf16[1,384,256]{2,1,0:T(8,128)(2,1)S(1)}, bf16[1,384,256]{2,1,0:T(8,128)(2,1)S(1)}, u32[]{:S(2)}, u32[]{:S(2)}) %collective-permute-start.75) | collective-permute-done | bytes 196640 | tf_op jit(solution)/shard_map/ppermute | solution.py:1020
  288.6 2.8 collective-permute-done.71.d
  (183 shorter events, 106.2 us)
Async XLA Ops:
  0.7 23.8 %collective-permute-start = (bf16[4,112,1024]{2,1,0:T(8,128)(2,1)}, bf16[4,112,1024]{2,1,0:T(8,128)(2,1)S(1)}, u32[]{:S(2)}, u32[]{:S(2)}) collective-permute-start(bf16[4,112,1024]{2,1,0:T(8,128)(2,1)} %bitcast.46), channel_id=1, source_target_pairs={{0,1},{1,0},{2,3},{3,2},{4,5},{5,4},{6,7},{7,6},{8,9},{9,8},{10,11... | collective-permute-start | bytes 2752520 | tf_op jit(solution)/shard_map/ppermute | solution.py:1020
  7.8 3.7 %collective-permute-start.2 = (f32[4,512]{1,0:T(4,128)S(1)}, f32[4,512]{1,0:T(4,128)S(1)}, u32[]{:S(2)}, u32[]{:S(2)}) collective-permute-start(f32[4,512]{1,0:T(4,128)S(1)} %add.234), channel_id=1, source_target_pairs={{0,4},{2,6},{4,0},{6,2},{8,12},{10,14},{12,8},{14,10},{16,20},{18,... | collective-permute-start | bytes 24584 | tf_op jit(solution)/shard_map/ppermute | solution.py:1020
  11.5 3.7 %collective-permute-start.3 = (f32[4,512]{1,0:T(4,128)S(1)}, f32[4,512]{1,0:T(4,128)S(1)}, u32[]{:S(2)}, u32[]{:S(2)}) collective-permute-start(f32[4,512]{1,0:T(4,128)S(1)} %add.235), channel_id=1, source_target_pairs={{0,8},{2,10},{4,12},{6,14},{8,0},{10,2},{12,4},{14,6},{16,24},{18,... | collective-permute-start | bytes 24584 | tf_op jit(solution)/shard_map/ppermute | solution.py:1020
  15.2 4.6 %collective-permute-start.4 = (f32[4,512]{1,0:T(4,128)S(1)}, f32[4,512]{1,0:T(4,128)S(1)}, u32[]{:S(2)}, u32[]{:S(2)}) collective-permute-start(f32[4,512]{1,0:T(4,128)S(1)} %add.236), channel_id=1, source_target_pairs={{0,16},{2,18},{4,20},{6,22},{8,24},{10,26},{12,28},{14,30},{16,0},... | collective-permute-start | bytes 24584 | tf_op jit(solution)/shard_map/ppermute | solution.py:1020
  19.8 4.6 %collective-permute-start.5 = (f32[4,512]{1,0:T(4,128)S(1)}, f32[4,512]{1,0:T(4,128)S(1)}, u32[]{:S(2)}, u32[]{:S(2)}) collective-permute-start(f32[4,512]{1,0:T(4,128)S(1)} %add.237.part), channel_id=1, source_target_pairs={{0,1},{1,0},{2,3},{3,2},{4,5},{5,4},{6,7},{7,6},{8,9},{9,8},{10,11... | collective-permute-start | bytes 24584 | tf_op jit(solution)/shard_map/ppermute | solution.py:1020
  24.4 13.1 %collective-permute-start.9 = (bf16[512,512]{1,0:T(8,128)(2,1)S(1)}, bf16[512,512]{1,0:T(8,128)(2,1)S(1)}, u32[]{:S(2)}, u32[]{:S(2)}) collective-permute-start(bf16[512,512]{1,0:T(8,128)(2,1)S(1)} %get-tuple-element.211), channel_id=1, source_target_pairs={{0,1},{1,0},{2,3},{3,2},{4,5},{5,4},{6,7},{7,6},{8,9},{9,8},{10,11... | collective-permute-start | bytes 1572872 | tf_op jit(solution)/shard_map/ppermute | solution.py:1020
  32.8 3.7 %collective-permute-start.7 = (f32[4,512]{1,0:T(4,128)S(1)}, f32[4,512]{1,0:T(4,128)S(1)}, u32[]{:S(2)}, u32[]{:S(2)}) collective-permute-start(f32[4,512]{1,0:T(4,128)S(1)} %add.238), channel_id=1, source_target_pairs={{0,4},{2,6},{4,0},{6,2},{8,12},{10,14},{12,8},{14,10},{16,20},{18,... | collective-permute-start | bytes 24584 | tf_op jit(solution)/shard_map/ppermute | solution.py:1020
  37.6 27.8 %collective-permute-start.19 = (bf16[2304,256]{1,0:T(8,128)(2,1)S(1)}, bf16[2304,256]{1,0:T(8,128)(2,1)S(1)}, u32[]{:S(2)}, u32[]{:S(2)}) collective-permute-start(bf16[2304,256]{1,0:T(8,128)(2,1)S(1)} %get-tuple-element.227), channel_id=1, source_target_pairs={{0,1},{1,0},{2,3},{3,2},{4,5},{5,4},{6,7},{7,6},{8,9},{9,8},{10,11... | collective-permute-start | bytes 3538952 | tf_op jit(solution)/shard_map/ppermute | solution.py:1020
  39.0 21.1 %collective-permute-start.14 = (bf16[512,512]{1,0:T(8,128)(2,1)S(1)}, bf16[512,512]{1,0:T(8,128)(2,1)S(1)}, u32[]{:S(2)}, u32[]{:S(2)}) collective-permute-start(bf16[512,512]{1,0:T(8,128)(2,1)S(1)} %collective-permute-done.9.r1), channel_id=1, source_target_pairs={{0,2},{2,0},{4,6},{6,4},{8,10},{10,8},{12,14},{14,12},{16,18},{18,... | collective-permute-start | bytes 1572872 | tf_op jit(solution)/shard_map/ppermute | solution.py:1020
  39.0 3.7 %collective-permute-start.8 = (f32[4,512]{1,0:T(4,128)S(1)}, f32[4,512]{1,0:T(4,128)S(1)}, u32[]{:S(2)}, u32[]{:S(2)}) collective-permute-start(f32[4,512]{1,0:T(4,128)S(1)} %add.239), channel_id=1, source_target_pairs={{0,8},{2,10},{4,12},{6,14},{8,0},{10,2},{12,4},{14,6},{16,24},{18,... | collective-permute-start | bytes 24584 | tf_op jit(solution)/shard_map/ppermute | solution.py:1020
  42.6 5.7 %collective-permute-start.10 = (f32[4,512]{1,0:T(4,128)S(1)}, f32[4,512]{1,0:T(4,128)S(1)}, u32[]{:S(2)}, u32[]{:S(2)}) collective-permute-start(f32[4,512]{1,0:T(4,128)S(1)} %add.240), channel_id=1, source_target_pairs={{0,16},{2,18},{4,20},{6,22},{8,24},{10,26},{12,28},{14,30},{16,0},... | collective-permute-start | bytes 24584 | tf_op jit(solution)/shard_map/ppermute | solution.py:1020
  51.4 4.3 %collective-permute-start.12 = (f32[8,2048]{1,0:T(8,128)S(1)}, f32[8,2048]{1,0:T(8,128)S(1)}, u32[]{:S(2)}, u32[]{:S(2)}) collective-permute-start(f32[8,2048]{1,0:T(8,128)S(1)} %add.242), channel_id=1, source_target_pairs={{0,4},{2,6},{4,0},{6,2},{8,12},{10,14},{12,8},{14,10},{16,20},{18,... | collective-permute-start | bytes 196616 | tf_op jit(solution)/shard_map/ppermute | solution.py:1020
  55.8 4.3 %collective-permute-start.13 = (f32[8,2048]{1,0:T(8,128)S(1)}, f32[8,2048]{1,0:T(8,128)S(1)}, u32[]{:S(2)}, u32[]{:S(2)}) collective-permute-start(f32[8,2048]{1,0:T(8,128)S(1)} %add.243), channel_id=1, source_target_pairs={{0,8},{2,10},{4,12},{6,14},{8,0},{10,2},{12,4},{14,6},{16,24},{18,... | collective-permute-start | bytes 196616 | tf_op jit(solution)/shard_map/ppermute | solution.py:1020
  60.1 5.2 %collective-permute-start.15 = (f32[8,2048]{1,0:T(8,128)S(1)}, f32[8,2048]{1,0:T(8,128)S(1)}, u32[]{:S(2)}, u32[]{:S(2)}) collective-permute-start(f32[8,2048]{1,0:T(8,128)S(1)} %add.244), channel_id=1, source_target_pairs={{0,16},{2,18},{4,20},{6,22},{8,24},{10,26},{12,28},{14,30},{16,0},... | collective-permute-start | bytes 196616 | tf_op jit(solution)/shard_map/ppermute | solution.py:1020
  65.4 14.2 %collective-permute-start.20 = (bf16[2304,256]{1,0:T(8,128)(2,1)S(1)}, bf16[2304,256]{1,0:T(8,128)(2,1)S(1)}, u32[]{:S(2)}, u32[]{:S(2)}) collective-permute-start(bf16[2304,256]{1,0:T(8,128)(2,1)S(1)} %collective-permute-done.19.r1), channel_id=1, source_target_pairs={{0,2},{2,0},{4,6},{6,4},{8,10},{10,8},{12,14},{14,12},{16,18},{18,... | collective-permute-start | bytes 3538952 | tf_op jit(solution)/shard_map/ppermute | solution.py:1020
  65.5 20.7 %collective-permute-start.25 = (bf16[1552,256]{1,0:T(8,128)(2,1)S(1)}, bf16[1552,256]{1,0:T(8,128)(2,1)S(1)}, u32[]{:S(2)}, u32[]{:S(2)}) collective-permute-start(bf16[1552,256]{1,0:T(8,128)(2,1)S(1)} %get-tuple-element.234), channel_id=1, source_target_pairs={{0,1},{1,0},{2,3},{3,2},{4,5},{5,4},{6,7},{7,6},{8,9},{9,8},{10,11... | collective-permute-start | bytes 2383880 | tf_op jit(solution)/shard_map/ppermute | solution.py:1020
  72.2 3.7 %collective-permute-start.17 = (f32[4,512]{1,0:T(4,128)S(1)}, f32[4,512]{1,0:T(4,128)S(1)}, u32[]{:S(2)}, u32[]{:S(2)}) collective-permute-start(f32[4,512]{1,0:T(4,128)S(1)} %add.246), channel_id=1, source_target_pairs={{0,4},{2,6},{4,0},{6,2},{8,12},{10,14},{12,8},{14,10},{16,20},{18,... | collective-permute-start | bytes 24584 | tf_op jit(solution)/shard_map/ppermute | solution.py:1020
  75.9 3.7 %collective-permute-start.18 = (f32[4,512]{1,0:T(4,128)S(1)}, f32[4,512]{1,0:T(4,128)S(1)}, u32[]{:S(2)}, u32[]{:S(2)}) collective-permute-start(f32[4,512]{1,0:T(4,128)S(1)} %add.247), channel_id=1, source_target_pairs={{0,8},{2,10},{4,12},{6,14},{8,0},{10,2},{12,4},{14,6},{16,24},{18,... | collective-permute-start | bytes 24584 | tf_op jit(solution)/shard_map/ppermute | solution.py:1020
  79.6 4.6 %collective-permute-start.21 = (f32[4,512]{1,0:T(4,128)S(1)}, f32[4,512]{1,0:T(4,128)S(1)}, u32[]{:S(2)}, u32[]{:S(2)}) collective-permute-start(f32[4,512]{1,0:T(4,128)S(1)} %add.248), channel_id=1, source_target_pairs={{0,16},{2,18},{4,20},{6,22},{8,24},{10,26},{12,28},{14,30},{16,0},... | collective-permute-start | bytes 24584 | tf_op jit(solution)/shard_map/ppermute | solution.py:1020
  86.2 10.2 %collective-permute-start.26 = (bf16[1552,256]{1,0:T(8,128)(2,1)S(1)}, bf16[1552,256]{1,0:T(8,128)(2,1)S(1)}, u32[]{:S(2)}, u32[]{:S(2)}) collective-permute-start(bf16[1552,256]{1,0:T(8,128)(2,1)S(1)} %collective-permute-done.25.r1), channel_id=1, source_target_pairs={{0,2},{2,0},{4,6},{6,4},{8,10},{10,8},{12,14},{14,12},{16,18},{18,... | collective-permute-start | bytes 2383880 | tf_op jit(solution)/shard_map/ppermute | solution.py:1020
  86.2 27.3 %collective-permute-start.32 = (bf16[224,1024]{1,0:T(8,128)(2,1)S(1)}, bf16[224,1024]{1,0:T(8,128)(2,1)S(1)}, u32[]{:S(2)}, u32[]{:S(2)}) collective-permute-start(bf16[224,1024]{1,0:T(8,128)(2,1)S(1)} %bitcast.49), channel_id=1, source_target_pairs={{0,1},{1,0},{2,3},{3,2},{4,5},{5,4},{6,7},{7,6},{8,9},{9,8},{10,11... | collective-permute-start | bytes 1376264 | tf_op jit(solution)/shard_map/ppermute | solution.py:1020
  89.0 3.7 %collective-permute-start.23 = (f32[4,512]{1,0:T(4,128)S(1)}, f32[4,512]{1,0:T(4,128)S(1)}, u32[]{:S(2)}, u32[]{:S(2)}) collective-permute-start(f32[4,512]{1,0:T(4,128)S(1)} %add.250), channel_id=1, source_target_pairs={{0,4},{2,6},{4,0},{6,2},{8,12},{10,14},{12,8},{14,10},{16,20},{18,... | collective-permute-start | bytes 24584 | tf_op jit(solution)/shard_map/ppermute | solution.py:1020
  92.7 3.7 %collective-permute-start.24 = (f32[4,512]{1,0:T(4,128)S(1)}, f32[4,512]{1,0:T(4,128)S(1)}, u32[]{:S(2)}, u32[]{:S(2)}) collective-permute-start(f32[4,512]{1,0:T(4,128)S(1)} %add.251), channel_id=1, source_target_pairs={{0,8},{2,10},{4,12},{6,14},{8,0},{10,2},{12,4},{14,6},{16,24},{18,... | collective-permute-start | bytes 24584 | tf_op jit(solution)/shard_map/ppermute | solution.py:1020
  96.3 4.6 %collective-permute-start.27 = (f32[4,512]{1,0:T(4,128)S(1)}, f32[4,512]{1,0:T(4,128)S(1)}, u32[]{:S(2)}, u32[]{:S(2)}) collective-permute-start(f32[4,512]{1,0:T(4,128)S(1)} %add.252), channel_id=1, source_target_pairs={{0,16},{2,18},{4,20},{6,22},{8,24},{10,26},{12,28},{14,30},{16,0},... | collective-permute-start | bytes 24584 | tf_op jit(solution)/shard_map/ppermute | solution.py:1020
  104.0 4.0 %collective-permute-start.29 = (f32[4,2048]{1,0:T(4,128)S(1)}, f32[4,2048]{1,0:T(4,128)S(1)}, u32[]{:S(2)}, u32[]{:S(2)}) collective-permute-start(f32[4,2048]{1,0:T(4,128)S(1)} %add.254), channel_id=1, source_target_pairs={{0,4},{2,6},{4,0},{6,2},{8,12},{10,14},{12,8},{14,10},{16,20},{18,... | collective-permute-start | bytes 98312 | tf_op jit(solution)/shard_map/ppermute | solution.py:1020
  107.9 4.0 %collective-permute-start.30 = (f32[4,2048]{1,0:T(4,128)S(1)}, f32[4,2048]{1,0:T(4,128)S(1)}, u32[]{:S(2)}, u32[]{:S(2)}) collective-permute-start(f32[4,2048]{1,0:T(4,128)S(1)} %add.255), channel_id=1, source_target_pairs={{0,8},{2,10},{4,12},{6,14},{8,0},{10,2},{12,4},{14,6},{16,24},{18,... | collective-permute-start | bytes 98312 | tf_op jit(solution)/shard_map/ppermute | solution.py:1020
  111.9 4.9 %collective-permute-start.31 = (f32[4,2048]{1,0:T(4,128)S(1)}, f32[4,2048]{1,0:T(4,128)S(1)}, u32[]{:S(2)}, u32[]{:S(2)}) collective-permute-start(f32[4,2048]{1,0:T(4,128)S(1)} %add.256), channel_id=1, source_target_pairs={{0,16},{2,18},{4,20},{6,22},{8,24},{10,26},{12,28},{14,30},{16,0},... | collective-permute-start | bytes 98312 | tf_op jit(solution)/shard_map/ppermute | solution.py:1020
  123.3 4.0 %collective-permute-start.34 = (f32[4,2048]{1,0:T(4,128)S(1)}, f32[4,2048]{1,0:T(4,128)S(1)}, u32[]{:S(2)}, u32[]{:S(2)}) collective-permute-start(f32[4,2048]{1,0:T(4,128)S(1)} %add.258), channel_id=1, source_target_pairs={{0,4},{2,6},{4,0},{6,2},{8,12},{10,14},{12,8},{14,10},{16,20},{18,... | collective-permute-start | bytes 98312 | tf_op jit(solution)/shard_map/ppermute | solution.py:1020
  127.3 4.0 %collective-permute-start.35 = (f32[4,2048]{1,0:T(4,128)S(1)}, f32[4,2048]{1,0:T(4,128)S(1)}, u32[]{:S(2)}, u32[]{:S(2)}) collective-permute-start(f32[4,2048]{1,0:T(4,128)S(1)} %add.259), channel_id=1, source_target_pairs={{0,8},{2,10},{4,12},{6,14},{8,0},{10,2},{12,4},{14,6},{16,24},{18,... | collective-permute-start | bytes 98312 | tf_op jit(solution)/shard_map/ppermute | solution.py:1020
  131.3 4.9 %collective-permute-start.36 = (f32[4,2048]{1,0:T(4,128)S(1)}, f32[4,2048]{1,0:T(4,128)S(1)}, u32[]{:S(2)}, u32[]{:S(2)}) collective-permute-start(f32[4,2048]{1,0:T(4,128)S(1)} %add.260), channel_id=1, source_target_pairs={{0,16},{2,18},{4,20},{6,22},{8,24},{10,26},{12,28},{14,30},{16,0},... | collective-permute-start | bytes 98312 | tf_op jit(solution)/shard_map/ppermute | solution.py:1020
  139.9 3.9 %collective-permute-start.38 = (f32[12,512]{1,0:T(8,128)S(1)}, f32[12,512]{1,0:T(8,128)S(1)}, u32[]{:S(2)}, u32[]{:S(2)}) collective-permute-start(f32[12,512]{1,0:T(8,128)S(1)} %add.262), channel_id=1, source_target_pairs={{0,4},{2,6},{4,0},{6,2},{8,12},{10,14},{12,8},{14,10},{16,20},{18,... | collective-permute-start | bytes 73736 | tf_op jit(solution)/shard_map/ppermute | solution.py:1020
  143.8 3.9 %collective-permute-start.39 = (f32[12,512]{1,0:T(8,128)S(1)}, f32[12,512]{1,0:T(8,128)S(1)}, u32[]{:S(2)}, u32[]{:S(2)}) collective-permute-start(f32[12,512]{1,0:T(8,128)S(1)} %add.263), channel_id=1, source_target_pairs={{0,8},{2,10},{4,12},{6,14},{8,0},{10,2},{12,4},{14,6},{16,24},{18,... | collective-permute-start | bytes 73736 | tf_op jit(solution)/shard_map/ppermute | solution.py:1020
  147.8 4.8 %collective-permute-start.40 = (f32[12,512]{1,0:T(8,128)S(1)}, f32[12,512]{1,0:T(8,128)S(1)}, u32[]{:S(2)}, u32[]{:S(2)}) collective-permute-start(f32[12,512]{1,0:T(8,128)S(1)} %add.264), channel_id=1, source_target_pairs={{0,16},{2,18},{4,20},{6,22},{8,24},{10,26},{12,28},{14,30},{16,0},... | collective-permute-start | bytes 73736 | tf_op jit(solution)/shard_map/ppermute | solution.py:1020
  160.5 3.8 %collective-permute-start.43 = (bf16[8,416,256]{2,1,0:T(8,128)(2,1)S(1)}, bf16[8,416,256]{2,1,0:T(8,128)(2,1)S(1)}, u32[]{:S(2)}, u32[]{:S(2)}) collective-permute-start(bf16[8,416,256]{2,1,0:T(8,128)(2,1)S(1)} %get-tuple-element.271), channel_id=1, source_target_pairs={{0,2},{2,0},{4,6},{6,4},{8,10},{10,8},{12,14},{14,12},{16,18},{18,... | collective-permute-start | bytes 5111816 | tf_op jit(solution)/shard_map/ppermute | solution.py:1020
  160.7 3.7 %collective-permute-start.42 = (f32[4,512]{1,0:T(4,128)S(1)}, f32[4,512]{1,0:T(4,128)S(1)}, u32[]{:S(2)}, u32[]{:S(2)}) collective-permute-start(f32[4,512]{1,0:T(4,128)S(1)} %add.266), channel_id=1, source_target_pairs={{0,4},{2,6},{4,0},{6,2},{8,12},{10,14},{12,8},{14,10},{16,20},{18,... | collective-permute-start | bytes 24584 | tf_op jit(solution)/shard_map/ppermute | solution.py:1020
  164.6 20.9 %collective-permute-start.46 = (bf16[4,416,256]{2,1,0:T(8,128)(2,1)S(1)}, bf16[4,416,256]{2,1,0:T(8,128)(2,1)S(1)}, u32[]{:S(2)}, u32[]{:S(2)}) collective-permute-start(bf16[4,416,256]{2,1,0:T(8,128)(2,1)S(1)} %get-tuple-element.288), channel_id=1, source_target_pairs={{0,4},{2,6},{4,0},{6,2},{8,12},{10,14},{12,8},{14,10},{16,20},{18,... | collective-permute-start | bytes 2555912 | tf_op jit(solution)/shard_map/ppermute | solution.py:1020
  166.1 3.7 %collective-permute-start.44 = (f32[4,512]{1,0:T(4,128)S(1)}, f32[4,512]{1,0:T(4,128)S(1)}, u32[]{:S(2)}, u32[]{:S(2)}) collective-permute-start(f32[4,512]{1,0:T(4,128)S(1)} %add.267), channel_id=1, source_target_pairs={{0,8},{2,10},{4,12},{6,14},{8,0},{10,2},{12,4},{14,6},{16,24},{18,... | collective-permute-start | bytes 24584 | tf_op jit(solution)/shard_map/ppermute | solution.py:1020
  169.8 4.5 %collective-permute-start.45 = (f32[4,512]{1,0:T(4,128)S(1)}, f32[4,512]{1,0:T(4,128)S(1)}, u32[]{:S(2)}, u32[]{:S(2)}) collective-permute-start(f32[4,512]{1,0:T(4,128)S(1)} %add.270), channel_id=1, source_target_pairs={{0,16},{2,18},{4,20},{6,22},{8,24},{10,26},{12,28},{14,30},{16,0},... | collective-permute-start | bytes 24584 | tf_op jit(solution)/shard_map/ppermute | solution.py:1020
  186.7 8.9 %collective-permute-start.50 = (bf16[8,256,256]{2,1,0:T(8,128)(2,1)S(1)}, bf16[8,256,256]{2,1,0:T(8,128)(2,1)S(1)}, u32[]{:S(2)}, u32[]{:S(2)}) collective-permute-start(bf16[8,256,256]{2,1,0:T(8,128)(2,1)S(1)} %get-tuple-element.291), channel_id=1, source_target_pairs={{0,2},{2,0},{4,6},{6,4},{8,10},{10,8},{12,14},{14,12},{16,18},{18,... | collective-permute-start | bytes 3145736 | tf_op jit(solution)/shard_map/ppermute | solution.py:1020
  186.9 4.4 %collective-permute-start.48 = (f32[8,2048]{1,0:T(8,128)S(1)}, f32[8,2048]{1,0:T(8,128)S(1)}, u32[]{:S(2)}, u32[]{:S(2)}) collective-permute-start(f32[8,2048]{1,0:T(8,128)S(1)} %add.272), channel_id=1, source_target_pairs={{0,4},{2,6},{4,0},{6,2},{8,12},{10,14},{12,8},{14,10},{16,20},{18,... | collective-permute-start | bytes 196616 | tf_op jit(solution)/shard_map/ppermute | solution.py:1020
  191.3 4.3 %collective-permute-start.49 = (f32[8,2048]{1,0:T(8,128)S(1)}, f32[8,2048]{1,0:T(8,128)S(1)}, u32[]{:S(2)}, u32[]{:S(2)}) collective-permute-start(f32[8,2048]{1,0:T(8,128)S(1)} %add.273), channel_id=1, source_target_pairs={{0,8},{2,10},{4,12},{6,14},{8,0},{10,2},{12,4},{14,6},{16,24},{18,... | collective-permute-start | bytes 196616 | tf_op jit(solution)/shard_map/ppermute | solution.py:1020
  195.8 5.2 %collective-permute-start.51 = (f32[8,2048]{1,0:T(8,128)S(1)}, f32[8,2048]{1,0:T(8,128)S(1)}, u32[]{:S(2)}, u32[]{:S(2)}) collective-permute-start(f32[8,2048]{1,0:T(8,128)S(1)} %add.274), channel_id=1, source_target_pairs={{0,16},{2,18},{4,20},{6,22},{8,24},{10,26},{12,28},{14,30},{16,0},... | collective-permute-start | bytes 196616 | tf_op jit(solution)/shard_map/ppermute | solution.py:1020
  201.0 11.1 %collective-permute-start.53 = (bf16[4,256,256]{2,1,0:T(8,128)(2,1)S(1)}, bf16[4,256,256]{2,1,0:T(8,128)(2,1)S(1)}, u32[]{:S(2)}, u32[]{:S(2)}) collective-permute-start(bf16[4,256,256]{2,1,0:T(8,128)(2,1)S(1)} %get-tuple-element.304), channel_id=1, source_target_pairs={{0,4},{2,6},{4,0},{6,2},{8,12},{10,14},{12,8},{14,10},{16,20},{18,... | collective-permute-start | bytes 1572872 | tf_op jit(solution)/shard_map/ppermute | solution.py:1020
  202.7 8.8 %collective-permute-start.52 = (bf16[2,416,256]{2,1,0:T(8,128)(2,1)S(1)}, bf16[2,416,256]{2,1,0:T(8,128)(2,1)S(1)}, u32[]{:S(2)}, u32[]{:S(2)}) collective-permute-start(bf16[2,416,256]{2,1,0:T(8,128)(2,1)S(1)} %get-tuple-element.303), channel_id=1, source_target_pairs={{0,8},{2,10},{4,12},{6,14},{8,0},{10,2},{12,4},{14,6},{16,24},{18,... | collective-permute-start | bytes 1277960 | tf_op jit(solution)/shard_map/ppermute | solution.py:1020
  213.4 4.1 %collective-permute-start.56 = (bf16[8,384,256]{2,1,0:T(8,128)(2,1)S(1)}, bf16[8,384,256]{2,1,0:T(8,128)(2,1)S(1)}, u32[]{:S(2)}, u32[]{:S(2)}) collective-permute-start(bf16[8,384,256]{2,1,0:T(8,128)(2,1)S(1)} %get-tuple-element.306), channel_id=1, source_target_pairs={{0,2},{2,0},{4,6},{6,4},{8,10},{10,8},{12,14},{14,12},{16,18},{18,... | collective-permute-start | bytes 4718600 | tf_op jit(solution)/shard_map/ppermute | solution.py:1020
  213.5 3.9 %collective-permute-start.55 = (f32[12,512]{1,0:T(8,128)S(1)}, f32[12,512]{1,0:T(8,128)S(1)}, u32[]{:S(2)}, u32[]{:S(2)}) collective-permute-start(f32[12,512]{1,0:T(8,128)S(1)} %add.279), channel_id=1, source_target_pairs={{0,4},{2,6},{4,0},{6,2},{8,12},{10,14},{12,8},{14,10},{16,20},{18,... | collective-permute-start | bytes 73736 | tf_op jit(solution)/shard_map/ppermute | solution.py:1020
  217.6 19.0 %collective-permute-start.59 = (bf16[4,384,256]{2,1,0:T(8,128)(2,1)S(1)}, bf16[4,384,256]{2,1,0:T(8,128)(2,1)S(1)}, u32[]{:S(2)}, u32[]{:S(2)}) collective-permute-start(bf16[4,384,256]{2,1,0:T(8,128)(2,1)S(1)} %get-tuple-element.315), channel_id=1, source_target_pairs={{0,4},{2,6},{4,0},{6,2},{8,12},{10,14},{12,8},{14,10},{16,20},{18,... | collective-permute-start | bytes 2359304 | tf_op jit(solution)/shard_map/ppermute | solution.py:1020
  219.2 3.9 %collective-permute-start.57 = (f32[12,512]{1,0:T(8,128)S(1)}, f32[12,512]{1,0:T(8,128)S(1)}, u32[]{:S(2)}, u32[]{:S(2)}) collective-permute-start(f32[12,512]{1,0:T(8,128)S(1)} %add.280), channel_id=1, source_target_pairs={{0,8},{2,10},{4,12},{6,14},{8,0},{10,2},{12,4},{14,6},{16,24},{18,... | collective-permute-start | bytes 73736 | tf_op jit(solution)/shard_map/ppermute | solution.py:1020
  223.1 7.7 %collective-permute-start.58 = (f32[12,512]{1,0:T(8,128)S(1)}, f32[12,512]{1,0:T(8,128)S(1)}, u32[]{:S(2)}, u32[]{:S(2)}) collective-permute-start(f32[12,512]{1,0:T(8,128)S(1)} %add.283), channel_id=1, source_target_pairs={{0,16},{2,18},{4,20},{6,22},{8,24},{10,26},{12,28},{14,30},{16,0},... | collective-permute-start | bytes 73736 | tf_op jit(solution)/shard_map/ppermute | solution.py:1020
  237.8 11.6 %collective-permute-start.64 = (bf16[8,288,256]{2,1,0:T(8,128)(2,1)S(1)}, bf16[8,288,256]{2,1,0:T(8,128)(2,1)S(1)}, u32[]{:S(2)}, u32[]{:S(2)}) collective-permute-start(bf16[8,288,256]{2,1,0:T(8,128)(2,1)S(1)} %get-tuple-element.318), channel_id=1, source_target_pairs={{0,2},{2,0},{4,6},{6,4},{8,10},{10,8},{12,14},{14,12},{16,18},{18,... | collective-permute-start | bytes 3538952 | tf_op jit(solution)/shard_map/ppermute | solution.py:1020
  238.0 8.7 %collective-permute-start.72 = (bf16[2,256,256]{2,1,0:T(8,128)(2,1)S(1)}, bf16[2,256,256]{2,1,0:T(8,128)(2,1)S(1)}, u32[]{:S(2)}, u32[]{:S(2)}) collective-permute-start(bf16[2,256,256]{2,1,0:T(8,128)(2,1)S(1)} %get-tuple-element.377), channel_id=1, source_target_pairs={{0,8},{2,10},{4,12},{6,14},{8,0},{10,2},{12,4},{14,6},{16,24},{18,... | collective-permute-start | bytes 786440 | tf_op jit(solution)/shard_map/ppermute | solution.py:1020
  239.7 3.7 %collective-permute-start.61 = (f32[4,512]{1,0:T(4,128)S(1)}, f32[4,512]{1,0:T(4,128)S(1)}, u32[]{:S(2)}, u32[]{:S(2)}) collective-permute-start(f32[4,512]{1,0:T(4,128)S(1)} %add.285), channel_id=1, source_target_pairs={{0,4},{2,6},{4,0},{6,2},{8,12},{10,14},{12,8},{14,10},{16,20},{18,... | collective-permute-start | bytes 24584 | tf_op jit(solution)/shard_map/ppermute | solution.py:1020
  243.3 3.7 %collective-permute-start.62 = (f32[4,512]{1,0:T(4,128)S(1)}, f32[4,512]{1,0:T(4,128)S(1)}, u32[]{:S(2)}, u32[]{:S(2)}) collective-permute-start(f32[4,512]{1,0:T(4,128)S(1)} %add.286), channel_id=1, source_target_pairs={{0,8},{2,10},{4,12},{6,14},{8,0},{10,2},{12,4},{14,6},{16,24},{18,... | collective-permute-start | bytes 24584 | tf_op jit(solution)/shard_map/ppermute | solution.py:1020
  247.0 4.7 %collective-permute-start.63 = (f32[4,512]{1,0:T(4,128)S(1)}, f32[4,512]{1,0:T(4,128)S(1)}, u32[]{:S(2)}, u32[]{:S(2)}) collective-permute-start(f32[4,512]{1,0:T(4,128)S(1)} %add.287), channel_id=1, source_target_pairs={{0,16},{2,18},{4,20},{6,22},{8,24},{10,26},{12,28},{14,30},{16,0},... | collective-permute-start | bytes 24584 | tf_op jit(solution)/shard_map/ppermute | solution.py:1020
  249.5 16.0 %collective-permute-start.65 = (bf16[4,288,256]{2,1,0:T(8,128)(2,1)S(1)}, bf16[4,288,256]{2,1,0:T(8,128)(2,1)S(1)}, u32[]{:S(2)}, u32[]{:S(2)}) collective-permute-start(bf16[4,288,256]{2,1,0:T(8,128)(2,1)S(1)} %get-tuple-element.325), channel_id=1, source_target_pairs={{0,4},{2,6},{4,0},{6,2},{8,12},{10,14},{12,8},{14,10},{16,20},{18,... | collective-permute-start | bytes 1769480 | tf_op jit(solution)/shard_map/ppermute | solution.py:1020
  251.1 33.4 %collective-permute-start.73 = (bf16[1,672,256]{2,1,0:T(8,128)(2,1)S(1)}, bf16[1,672,256]{2,1,0:T(8,128)(2,1)S(1)}, u32[]{:S(2)}, u32[]{:S(2)}) collective-permute-start(bf16[1,672,256]{2,1,0:T(8,128)(2,1)S(1)} %pad_maximum_fusion.1), channel_id=1, source_target_pairs={{0,16},{2,18},{4,20},{6,22},{8,24},{10,26},{12,28},{14,30},{16,0},... | collective-permute-start | bytes 1032200 | tf_op jit(solution)/shard_map/ppermute | solution.py:1020
  253.7 3.7 %collective-permute-start.68 = (bf16[8,64,256]{2,1,0:T(8,128)(2,1)S(1)}, bf16[8,64,256]{2,1,0:T(8,128)(2,1)S(1)}, u32[]{:S(2)}, u32[]{:S(2)}) collective-permute-start(bf16[8,64,256]{2,1,0:T(8,128)(2,1)S(1)} %get-tuple-element.330), channel_id=1, source_target_pairs={{0,2},{2,0},{4,6},{6,4},{8,10},{10,8},{12,14},{14,12},{16,18},{18,... | collective-permute-start | bytes 786440 | tf_op jit(solution)/shard_map/ppermute | solution.py:1020
  253.8 18.4 %collective-permute-start.74 = (bf16[2,384,256]{2,1,0:T(8,128)(2,1)S(1)}, bf16[2,384,256]{2,1,0:T(8,128)(2,1)S(1)}, u32[]{:S(2)}, u32[]{:S(2)}) collective-permute-start(bf16[2,384,256]{2,1,0:T(8,128)(2,1)S(1)} %get-tuple-element.337), channel_id=1, source_target_pairs={{0,8},{2,10},{4,12},{6,14},{8,0},{10,2},{12,4},{14,6},{16,24},{18,... | collective-permute-start | bytes 1179656 | tf_op jit(solution)/shard_map/ppermute | solution.py:1020
  257.5 17.1 %collective-permute-start.69 = (bf16[4,64,256]{2,1,0:T(8,128)(2,1)S(1)}, bf16[4,64,256]{2,1,0:T(8,128)(2,1)S(1)}, u32[]{:S(2)}, u32[]{:S(2)}) collective-permute-start(bf16[4,64,256]{2,1,0:T(8,128)(2,1)S(1)} %get-tuple-element.387), channel_id=1, source_target_pairs={{0,4},{2,6},{4,0},{6,2},{8,12},{10,14},{12,8},{14,10},{16,20},{18,... | collective-permute-start | bytes 393224 | tf_op jit(solution)/shard_map/ppermute | solution.py:1020
  265.6 14.9 %collective-permute-start.66 = (bf16[2,288,256]{2,1,0:T(8,128)(2,1)S(1)}, bf16[2,288,256]{2,1,0:T(8,128)(2,1)S(1)}, u32[]{:S(2)}, u32[]{:S(2)}) collective-permute-start(bf16[2,288,256]{2,1,0:T(8,128)(2,1)S(1)} %get-tuple-element.328), channel_id=1, source_target_pairs={{0,8},{2,10},{4,12},{6,14},{8,0},{10,2},{12,4},{14,6},{16,24},{18,... | collective-permute-start | bytes 884744 | tf_op jit(solution)/shard_map/ppermute | solution.py:1020
  272.3 15.3 %collective-permute-start.75 = (bf16[1,384,256]{2,1,0:T(8,128)(2,1)S(1)}, bf16[1,384,256]{2,1,0:T(8,128)(2,1)S(1)}, u32[]{:S(2)}, u32[]{:S(2)}) collective-permute-start(bf16[1,384,256]{2,1,0:T(8,128)(2,1)S(1)} %get-tuple-element.380), channel_id=1, source_target_pairs={{0,16},{2,18},{4,20},{6,22},{8,24},{10,26},{12,28},{14,30},{16,0},... | collective-permute-start | bytes 589832 | tf_op jit(solution)/shard_map/ppermute | solution.py:1020
  274.6 9.6 %collective-permute-start.70 = (bf16[2,64,256]{2,1,0:T(8,128)(2,1)S(1)}, bf16[2,64,256]{2,1,0:T(8,128)(2,1)S(1)}, u32[]{:S(2)}, u32[]{:S(2)}) collective-permute-start(bf16[2,64,256]{2,1,0:T(8,128)(2,1)S(1)} %get-tuple-element.389), channel_id=1, source_target_pairs={{0,8},{2,10},{4,12},{6,14},{8,0},{10,2},{12,4},{14,6},{16,24},{18,... | collective-permute-start | bytes 196616 | tf_op jit(solution)/shard_map/ppermute | solution.py:1020
  280.5 10.9 %collective-permute-start.67 = (bf16[1,288,256]{2,1,0:T(8,128)(2,1)S(1)}, bf16[1,288,256]{2,1,0:T(8,128)(2,1)S(1)}, u32[]{:S(2)}, u32[]{:S(2)}) collective-permute-start(bf16[1,288,256]{2,1,0:T(8,128)(2,1)S(1)} %get-tuple-element.382), channel_id=1, source_target_pairs={{0,16},{2,18},{4,20},{6,22},{8,24},{10,26},{12,28},{14,30},{16,0},... | collective-permute-start | bytes 442376 | tf_op jit(solution)/shard_map/ppermute | solution.py:1020
  284.1 7.3 %collective-permute-start.71 = (bf16[1,64,256]{2,1,0:T(8,128)(2,1)S(1)}, bf16[1,64,256]{2,1,0:T(8,128)(2,1)S(1)}, u32[]{:S(2)}, u32[]{:S(2)}) collective-permute-start(bf16[1,64,256]{2,1,0:T(8,128)(2,1)S(1)} %get-tuple-element.390), channel_id=1, source_target_pairs={{0,16},{2,18},{4,20},{6,22},{8,24},{10,26},{12,28},{14,30},{16,0},... | collective-permute-start | bytes 98312 | tf_op jit(solution)/shard_map/ppermute | solution.py:1020
  (13 other events, 16.8 us)

commit v6 on v5

--- a/solution.py
+++ b/solution.py
@@ -151,13 +151,8 @@
     return group_sums(d, fs) + group_sums(d * x, fs)
 
 
-def loop(count, body):
-    lax.fori_loop(0, count, lambda c, _: (body(c), 0)[1], 0, unroll=UNROLL)
-
-
-def loop_from(first, last, body):
-    for c in range(first, last):
-        body(c)
+def loop(count, body, unroll=UNROLL):
+    lax.fori_loop(0, count, lambda c, _: (body(c), 0)[1], 0, unroll=unroll)
 
 
 def copy_all(pairs, sems):
@@ -308,13 +303,14 @@
 
 
 def project_kernel(fs, x, keep, wp_far, w3_far, prep, st, w3, wp, sems):
-    copies = []
-    for c in range(4):
-        sl = slice(c * 512, (c + 1) * 512)
-        copies.append(pltpu.make_async_copy(wp_far.at[:, sl], wp.at[:, sl], sems.at[c]))
-    copies.append(pltpu.make_async_copy(w3_far, w3, sems.at[4]))
-    for c in copies:
-        c.start()
+    def part(k):
+        sl = cols(k, 512)
+        return pltpu.make_async_copy(wp_far.at[:, sl], wp.at[:, sl], sems.at[k])
+
+    for k in range(4):
+        part(k).start()
+    w3_copy = pltpu.make_async_copy(w3_far, w3, sems.at[4])
+    w3_copy.start()
 
     def body(c):
         sl = cols(c)
@@ -322,10 +318,13 @@
         prep[:, sl] = v
         put(st, 0, stat_rows(v, keep[...], fs), sl)
 
-    for c in range(4):
-        copies[c].wait()
-        loop_from(2 * c, 2 * c + 2, body)
-    copies[4].wait()
+    def pair(k):
+        part(k).wait()
+        body(2 * k)
+        body(2 * k + 1)
+
+    loop(4, pair, 1)
+    w3_copy.wait()
 
 
 def stage_three_kernel(fs, parts, pre2, stp, keep, w3, gb, h2, pre3, st, tot2, tot):
@@ -343,7 +342,7 @@
         pre3[:, sl] = v
         put(st, 0, stat_rows(v, keep[...], fs), sl)
 
-    loop(8, body)
+    loop(8, body, 4)
 
 
 def fetch_four_kernel(isc, own, r1, r2, w4, sems):
@@ -379,7 +378,7 @@
         s = ((prep[:, sl] - mean) * scale * vec[2:3, sl] + vec[3:4, sl]) * keep[...]
         short[:, sl] = s
 
-    loop(8, units)
+    loop(8, units, 4)
     wait_all(copies)
     sp[...] = dot3(pooled[...], sq[...]) + sqb[0:1, :]
     squeezed = sp[...] * sigmoid(sp[...])
@@ -399,7 +398,7 @@
         lows[:, sl] = lo
         acc[...] += mm(lo, w4[cols(c), :])
 
-    loop(8, streams)
+    loop(8, streams, 4)
     pre4[...] = acc[...]
     put(st, 0, stat_rows(acc[...], keep[...], fs), slice(0, 512))
 
@@ -518,7 +517,7 @@
         for b, r in enumerate(image_sums(u)):
             pooled[b : b + 1, sl] = r * fs[CELLS + b]
 
-    loop(8, units)
+    loop(8, units, 4)
     sp[...] = dot3(pooled[...], sq[...]) + sqb[1:2, :]
     squeezed[...] = sp[...] * sigmoid(sp[...])
     for h in range(2):
@@ -544,7 +543,7 @@
         extra[6:7, 256:512] += jnp.sum(branch * branch, axis=0, keepdims=True)
         extra[7:8, 0:256] += jnp.sum(stream * stream, axis=0, keepdims=True)
 
-    loop(8, streams)
+    loop(8, streams, 4)
     result[...] = res[n]
     de[...] = de[...] * gate[...] * (1.0 - gate[...])
     back = 0.0
@@ -569,7 +568,7 @@
         ) * keep[...]
         put(pay, 0, back_rows(du, x, fs), sl)
 
-    loop(8, tops)
+    loop(8, tops, 4)
 
 
 def whole_gain(tot, at, gain, bias):
@@ -604,7 +603,7 @@
         d6[:, sl] = d
         acc[...] += mm_nt(d, w6[:, sl])
 
-    loop(8, body)
+    loop(8, body, 4)
     mean, scale = coefs(tot5, 0, slice(0, 512), fs, INV_OUT)
     x = (pre5[...] - mean) * scale
     o = x * gain5[0:1, :] + gain5[1:2, :]
@@ -810,18 +809,18 @@
             g = g + mm_tn(xp[k, :, cols(c)], dn[k, :, cols(n)])
         full[cols(c), :] = low(g)
 
-    loop(4, body)
+    loop(4, body, 4)
     deal(isc, full, 64, gkeep, gsend, 0)
 
 
 def placed_kernel(isc, dproj, wp_far, out, cc, pick_own, spread, wp, sems):
     n = isc[NARROW]
-    copies = [
-        pltpu.make_async_copy(wp_far.at[cut], wp.at[cut], sems.at[k])
-        for k, cut in enumerate(slice(256 * k, 256 * (k + 1)) for k in range(4))
-    ]
-    for c in copies:
-        c.start()
+
+    def part(k):
+        return pltpu.make_async_copy(wp_far.at[cols(k), :], wp.at[cols(k), :], sems.at[k])
+
+    for k in range(4):
+        part(k).start()
     for b in range(B):
         place = lax.broadcasted_iota(jnp.int32, (32, M), 1)
         it = lax.broadcasted_iota(jnp.int32, (32, M), 0)
@@ -834,11 +833,14 @@
             ((it & 9) == 0) & (place == b * 32 + (it >> 4) * 4 + ((it & 7) >> 1)), 1.0, 0.0
         ))
     cc[...] = low(mm(pick_own[...], dproj[...]))
-    for c in range(4):
-        sl = cols(c)
-        copies[c].wait()
+
+    def body(c):
+        sl = cols(c)
+        part(c).wait()
         hi, lo = split2(mm_nt(cc[...], wp[sl, :]))
         out[:, sl] = mm(spread[...], hi) + mm(spread[...], lo)
+
+    loop(4, body, 1)
 
 
 def image_kernel(isc, perm, d1, placed, keep, w1, out, dc):
@@ -856,7 +858,7 @@
     def expand2(c):
         wider[:, cols(c)] = low(mm_tn(h5[:, cols(n)], d6[:, cols(c)]))
 
-    loop(8, expand2)
+    loop(8, expand2, 4)
     for p in range(16):
         sl = cols(isc[DEST + p], 128)
         for k in range(2):
@@ -868,7 +870,7 @@
         full[...] = low(mm_tn(col4[t], d5[:, cols(n)]))
         deal(isc, full, 32, gkeep, gsend, 128 + t * 32)
 
-    loop(9, spatial)
+    loop(9, spatial, 3)
 
 
 def gate_grads(isc, n, c, at, squeezed, pooled, de, ds, gkeep, gsend, q, e):
@@ -893,7 +895,7 @@
         gate_grads(isc, n, c, 128, sq2, pooled2, de2, ds2, gkeep, gsend, q, e)
         gate_grads(isc, n, c, 192, sq1, pooled1, de1, ds1, gkeep, gsend, q, e)
 
-    loop(4, body)
+    loop(4, body, 4)
 
 
 def grads_c_kernel(isc, h2, d3, strided, dproj, gkeep, gsend, full, taller):
@@ -906,7 +908,7 @@
         taller[...] = low(mm_tn(strided[...], dproj[:, sl]))
         deal(isc, taller, 64, gkeep, gsend, 128 + c * 64)
 
-    loop(4, body)
+    loop(4, body, 4)
 
 
 def grads_d_kernel(isc, col1, d2, gkeep, gsend, full):

time: 293 us -> 290 us (0.990)
  Pallas kernels: 73 us -> 69.7 us
    pallas_call x28, Pallas kernels: 73 us -> 69.7 us  [call(): pl.pallas_call(body, out_shape=tuple((o if hasattr(o, 'memory_space') els...]
  transfers between devices with their start and end apart: 76 -> 76, of which waited for: 57 -> 57; matrix products, arithmetic and copies ran while one was open for 0% -> 0% of each run, Pallas kernels for 20% -> 19%
where the time goes in v6:
time: 290 us
  waiting for transfers between devices  129 us (44%)
  starting transfers between devices  88.9 us (31%)
  Pallas kernels  69.7 us (24%)
    ppermute x76, waiting for transfers between devices, swap(): return lax.ppermute(v, axis, pairs)  129 us
    ppermute x76, starting transfers between devices, swap(): return lax.ppermute(v, axis, pairs)  88.9 us
    pallas_call x28, Pallas kernels, call(): pl.pallas_call(body, out_shape=tuple((o if hasattr(o, 'memory_space') els...  69.7 us
  transfers between devices with their start and end apart: 76, of which 57 were waited for; matrix products, arithmetic and copies ran while one was open for 0% of the time, Pallas kernels for 19%

profile of v6, /device:TPU:0, one launch (start us, length us, event | category | flops | bytes accessed | tf_op | source)
XLA Modules:
  0.0 289.9 jit_solution(3623888945080768330)
XLA Ops:
  0.7 3.0 %collective-permute-start = (bf16[4,112,1024]{2,1,0:T(8,128)(2,1)}, bf16[4,112,1024]{2,1,0:T(8,128)(2,1)S(1)}, u32[]{:S(2)}, u32[]{:S(2)}) collective-permute-start(bf16[4,112,1024]{2,1,0:T(8,128)(2,1)} %bitcast.46), channel_id=1, source_target_pairs={{0,1},{1,0},{2,3},{3,2},{4,5},{5,4},{6,7},{7,6},{8,9},{9,8},{10,11... | collective-permute-start | bytes 2752520 | tf_op jit(solution)/shard_map/ppermute | solution.py:1022
  3.7 2.9 setup.1
  9.3 2.2 collective-permute-done.2
  13.1 2.1 collective-permute-done.3
  15.2 2.6 collective-permute-start.4
  17.7 2.0 pack.1
  20.4 4.1 %collective-permute-done.5.part_other = f32[4,512]{1,0:T(4,128)S(1)} collective-permute-done((f32[4,512]{1,0:T(4,128)S(1)}, f32[4,512]{1,0:T(4,128)S(1)}, u32[]{:S(2)}, u32[]{:S(2)}) %collective-permute-start.5) | collective-permute-done | bytes 8224 | tf_op jit(solution)/shard_map/ppermute | solution.py:1022
  24.4 1.7 collective-permute-start.9
  26.2 5.4 %stage_two.1 = (bf16[4,224,1024]{2,1,0:T(8,128)(2,1)S(1)}, bf16[224,1024]{1,0:T(8,128)(2,1)S(1)}, f32[4,224,512]{2,1,0:T(8,128)S(1)}, bf16[9,224,512]{2,1,0:T(8,...) custom-call(f32[13]{0:T(128)S(4)} %get-tuple-element.197.fs, ...), custom_call_target="tpu_custom_call" | custom-call | flops 40000000 | bytes 200000 | tf_op jit(solution)/shard_map/stage_two/pallas_call | solution.py:1007
  34.3 2.1 collective-permute-done.7
  40.6 2.1 collective-permute-done.8
  42.6 2.6 collective-permute-start.10
  45.2 3.3 %project.1 = (f32[224,2048]{1,0:T(8,128)S(1)}, f32[4,2048]{1,0:T(4,128)S(1)}, bf16[512,2048]{1,0:T(8,128)(2,1)S(1)}) custom-call(f32[13]{0:T(128)S(4)} %get-tuple-element.197.fs, bf16[224,1024]{1,0:T(8,128)(2,1)S(1)} %get-tuple-element.214.x.strided, f32[224,1]{1,0:T(8,128)S(1)} %get-tuple-element.206.keep, bf16[1024,2048]{1,0:T(8,128)(2,1)} %wp_far.3, ...), custom_call_target="tpu_custom_call" | custom-call | flops 10000000 | bytes 80000 | tf_op jit(solution)/shard_map/project/pallas_call | solution.py:1007
  52.6 2.8 collective-permute-done.12
  57.1 2.7 collective-permute-done.13
  61.1 3.9 %collective-permute-done.15 = f32[8,2048]{1,0:T(8,128)S(1)} collective-permute-done((f32[8,2048]{1,0:T(8,128)S(1)}, f32[8,2048]{1,0:T(8,128)S(1)}, u32[]{:S(2)}, u32[]{:S(2)}) %collective-permute-start.15) | collective-permute-done | bytes 65568 | tf_op jit(solution)/shard_map/ppermute | solution.py:1022
  67.0 3.4 %stage_four.1 = (bf16[224,2048]{1,0:T(8,128)(2,1)S(1)}, f32[224,512]{1,0:T(8,128)S(1)}, f32[4,512]{1,0:T(4,128)S(1)}, f32[8,2048]{1,0:T(8,128)S(1)}, f32[8,2048]...) custom-call(f32[13]{0:T(128)S(4)} %get-tuple-element.197.fs, ...), custom_call_target="tpu_custom_call" | custom-call | flops 10000000 | bytes 100000 | tf_op jit(solution)/shard_map/stage_four/pallas_call | solution.py:1007
  73.1 2.2 collective-permute-done.17
  76.8 2.1 collective-permute-done.18
  78.9 1.8 collective-permute-start.21
  83.6 1.9 stage_five.1
  89.9 2.2 collective-permute-done.23
  93.6 2.1 collective-permute-done.24
  104.9 2.4 collective-permute-done.29
  109.0 2.3 collective-permute-done.30
  114.1 2.1 collective-permute-done.31
  116.2 5.0 %turn.1 = (bf16[224,1024]{1,0:T(8,128)(2,1)}, f32[224,2048]{1,0:T(8,128)S(1)}, f32[4,2048]{1,0:T(4,128)S(1)}, f32[8,512]{1,0:T(8,128)S(1)}, f32[4,2048]{1,0:T(4,...) custom-call(f32[13]{0:T(128)S(4)} %get-tuple-element.197.fs, ...), custom_call_target="tpu_custom_call" | custom-call | flops 10000000 | bytes 100000 | tf_op jit(solution)/shard_map/turn/pallas_call | solution.py:1007
  124.0 2.4 collective-permute-done.34
  128.1 2.3 collective-permute-done.35
  131.9 3.4 %collective-permute-done.36 = f32[4,2048]{1,0:T(4,128)S(1)} collective-permute-done((f32[4,2048]{1,0:T(4,128)S(1)}, f32[4,2048]{1,0:T(4,128)S(1)}, u32[]{:S(2)}, u32[]{:S(2)}) %collective-permute-start.36) | collective-permute-done | bytes 32800 | tf_op jit(solution)/shard_map/ppermute | solution.py:1022
  135.3 2.2 back_six.1
  140.3 2.4 collective-permute-done.38
  144.3 2.3 collective-permute-done.39
  148.0 3.4 %collective-permute-done.40 = f32[12,512]{1,0:T(8,128)S(1)} collective-permute-done((f32[12,512]{1,0:T(8,128)S(1)}, f32[12,512]{1,0:T(8,128)S(1)}, u32[]{:S(2)}, u32[]{:S(2)}) %collective-permute-start.40) | collective-permute-done | bytes 24608 | tf_op jit(solution)/shard_map/ppermute | solution.py:1022
  151.4 3.5 %back_five.1 = (bf16[224,512]{1,0:T(8,128)(2,1)S(1)}, f32[224,512]{1,0:T(8,128)S(1)}, f32[4,512]{1,0:T(4,128)S(1)}, f32[256]{0:T(256)}, f32[256]{0:T(256)}, /*index=5*/f32[1024]{0:T(1024)}, f32[128]{0:T(128)}, f32[5]{0:T(128)}) custom-call(f32[13]{0:T(128)S(4)} %get-tuple-element.197.fs, s32[18]{0:T(128)S(4)} %get-tuple-element.316.isc, ...), custom_call_target="tpu_custom_call" | custom-call | flops 20000000 | bytes 100000 | tf_op jit(solution)/shard_map/back_five/pallas_call | solution.py:1007
  154.9 2.4 grads_a.1
  160.2 2.2 collective-permute-done.42
  165.8 2.1 collective-permute-done.44
  169.3 2.4 fetch_two.1.ws
  172.4 5.4 %back_four.1 = (bf16[224,512]{1,0:T(8,128)(2,1)S(1)}, f32[224,2048]{1,0:T(8,128)S(1)}, f32[8,2048]{1,0:T(8,128)S(1)}, f32[512]{0:T(512)}, f32[512]{0:T(512)}, /*...) custom-call(f32[13]{0:T(128)S(4)} %get-tuple-element.197.fs, ...), custom_call_target="tpu_custom_call" | custom-call | flops 10000000 | bytes 100000 | tf_op jit(solution)/shard_map/back_four/pallas_call | solution.py:1007
  178.7 4.7 %collective-permute-done.46 = bf16[4,416,256]{2,1,0:T(8,128)(2,1)S(1)} collective-permute-done((bf16[4,416,256]{2,1,0:T(8,128)(2,1)S(1)}, bf16[4,416,256]{2,1,0:T(8,128)(2,1)S(1)}, u32[]{:S(2)}, u32[]{:S(2)}) %collective-permute-start.46) | collective-permute-done | bytes 852000 | tf_op jit(solution)/shard_map/ppermute | solution.py:1022
  186.5 2.9 collective-permute-done.48
  191.0 2.7 collective-permute-done.49
  195.3 3.8 %collective-permute-done.51 = f32[8,2048]{1,0:T(8,128)S(1)} collective-permute-done((f32[8,2048]{1,0:T(8,128)S(1)}, f32[8,2048]{1,0:T(8,128)S(1)}, u32[]{:S(2)}, u32[]{:S(2)}) %collective-permute-start.51) | collective-permute-done | bytes 65568 | tf_op jit(solution)/shard_map/ppermute | solution.py:1022
  202.4 3.5 %back_three.1 = (bf16[224,2048]{1,0:T(8,128)(2,1)S(1)}, bf16[224,2048]{1,0:T(8,128)(2,1)S(1)}, f32[224,512]{1,0:T(8,128)S(1)}, f32[12,512]{1,0:T(8,128)S(1)}, f3...) custom-call(f32[13]{0:T(128)S(4)} %get-tuple-element.197.fs, f32[1,8,2048]{2,1,0:T(8,128)S(1)} %bitcast.39, ...), custom_call_target="tpu_custom_call" | custom-call | flops 10000000 | bytes 100000 | tf_op jit(solution)/shard_map/back_three/pallas_call | solution.py:1007
  207.1 2.3 collective-permute-done.52
  213.1 2.4 collective-permute-done.55
  218.9 2.3 collective-permute-done.57
  221.2 1.8 collective-permute-start.58
  223.0 5.2 %placed.1 = f32[448,1024]{1,0:T(8,128)S(1)} custom-call(s32[18]{0:T(128)S(4)} %get-tuple-element.316.isc, bf16[224,2048]{1,0:T(8,128)(2,1)S(1)} %get-tuple-element.300.dproj, bf16[1024,2048]{1,0:T(8,128)(2,1)} %wp_far.3), custom_call_target="tpu_custom_call" | custom-call | flops 10000000 | bytes 100000 | tf_op jit(solution)/shard_map/placed/pallas_call | solution.py:1007
  228.2 3.0 %back_two.1 = (bf16[224,512]{1,0:T(8,128)(2,1)S(1)}, f32[4,224,512]{2,1,0:T(8,128)S(1)}, f32[4,512]{1,0:T(4,128)S(1)}, f32[512]{0:T(512)}, f32[512]{0:T(512)}, /*index=5*/f32[2048]{0:T(1024)}, f32[128]{0:T(128)}) custom-call(f32[13]{0:T(128)S(4)} %get-tuple-element.197.fs, f32[1,12,512]{2,1,0:T(8,128)S(1)} %add_bitcast_fusion.1.parts, ...), custom_call_target="tpu_custom_call" | custom-call | flops 20000000 | bytes 100000 | tf_op jit(solution)/shard_map/back_two/pallas_call | solution.py:1007
  231.3 1.8 grads_d.1
  239.3 2.1 collective-permute-done.61
  241.8 3.0 %collective-permute-done.72 = bf16[2,256,256]{2,1,0:T(8,128)(2,1)S(1)} collective-permute-done((bf16[2,256,256]{2,1,0:T(8,128)(2,1)S(1)}, bf16[2,256,256]{2,1,0:T(8,128)(2,1)S(1)}, u32[]{:S(2)}, u32[]{:S(2)}) %collective-permute-start.72) | collective-permute-done | bytes 262176 | tf_op jit(solution)/shard_map/ppermute | solution.py:1022
  245.1 2.3 collective-permute-start.63
  253.1 2.1 image.1
  256.6 6.8 %collective-permute-done.65 = bf16[4,288,256]{2,1,0:T(8,128)(2,1)S(1)} collective-permute-done((bf16[4,288,256]{2,1,0:T(8,128)(2,1)S(1)}, bf16[4,288,256]{2,1,0:T(8,128)(2,1)S(1)}, u32[]{:S(2)}, u32[]{:S(2)}) %collective-permute-start.65) | collective-permute-done | bytes 589856 | tf_op jit(solution)/shard_map/ppermute | solution.py:1022
  265.0 5.0 %collective-permute-done.74 = bf16[2,384,256]{2,1,0:T(8,128)(2,1)S(1)} collective-permute-done((bf16[2,384,256]{2,1,0:T(8,128)(2,1)S(1)}, bf16[2,384,256]{2,1,0:T(8,128)(2,1)S(1)}, u32[]{:S(2)}, u32[]{:S(2)}) %collective-permute-start.74) | collective-permute-done | bytes 393248 | tf_op jit(solution)/shard_map/ppermute | solution.py:1022
  270.0 2.1 collective-permute-start.75
  272.2 2.5 collective-permute-start.70
  274.7 3.4 %collective-permute-done.66 = bf16[2,288,256]{2,1,0:T(8,128)(2,1)S(1)} collective-permute-done((bf16[2,288,256]{2,1,0:T(8,128)(2,1)S(1)}, bf16[2,288,256]{2,1,0:T(8,128)(2,1)S(1)}, u32[]{:S(2)}, u32[]{:S(2)}) %collective-permute-start.66) | collective-permute-done | bytes 294944 | tf_op jit(solution)/shard_map/ppermute | solution.py:1022
  279.2 2.5 collective-permute-done.70
  282.2 3.1 %collective-permute-done.75.d = bf16[1,384,256]{2,1,0:T(8,128)(2,1)S(1)} collective-permute-done((bf16[1,384,256]{2,1,0:T(8,128)(2,1)S(1)}, bf16[1,384,256]{2,1,0:T(8,128)(2,1)S(1)}, u32[]{:S(2)}, u32[]{:S(2)}) %collective-permute-start.75) | collective-permute-done | bytes 196640 | tf_op jit(solution)/shard_map/ppermute | solution.py:1022
  286.3 2.8 collective-permute-done.71.d
  (183 shorter events, 105.4 us)
Async XLA Ops:
  0.7 23.8 %collective-permute-start = (bf16[4,112,1024]{2,1,0:T(8,128)(2,1)}, bf16[4,112,1024]{2,1,0:T(8,128)(2,1)S(1)}, u32[]{:S(2)}, u32[]{:S(2)}) collective-permute-start(bf16[4,112,1024]{2,1,0:T(8,128)(2,1)} %bitcast.46), channel_id=1, source_target_pairs={{0,1},{1,0},{2,3},{3,2},{4,5},{5,4},{6,7},{7,6},{8,9},{9,8},{10,11... | collective-permute-start | bytes 2752520 | tf_op jit(solution)/shard_map/ppermute | solution.py:1022
  7.8 3.7 %collective-permute-start.2 = (f32[4,512]{1,0:T(4,128)S(1)}, f32[4,512]{1,0:T(4,128)S(1)}, u32[]{:S(2)}, u32[]{:S(2)}) collective-permute-start(f32[4,512]{1,0:T(4,128)S(1)} %add.234), channel_id=1, source_target_pairs={{0,4},{2,6},{4,0},{6,2},{8,12},{10,14},{12,8},{14,10},{16,20},{18,... | collective-permute-start | bytes 24584 | tf_op jit(solution)/shard_map/ppermute | solution.py:1022
  11.5 3.7 %collective-permute-start.3 = (f32[4,512]{1,0:T(4,128)S(1)}, f32[4,512]{1,0:T(4,128)S(1)}, u32[]{:S(2)}, u32[]{:S(2)}) collective-permute-start(f32[4,512]{1,0:T(4,128)S(1)} %add.235), channel_id=1, source_target_pairs={{0,8},{2,10},{4,12},{6,14},{8,0},{10,2},{12,4},{14,6},{16,24},{18,... | collective-permute-start | bytes 24584 | tf_op jit(solution)/shard_map/ppermute | solution.py:1022
  15.2 4.6 %collective-permute-start.4 = (f32[4,512]{1,0:T(4,128)S(1)}, f32[4,512]{1,0:T(4,128)S(1)}, u32[]{:S(2)}, u32[]{:S(2)}) collective-permute-start(f32[4,512]{1,0:T(4,128)S(1)} %add.236), channel_id=1, source_target_pairs={{0,16},{2,18},{4,20},{6,22},{8,24},{10,26},{12,28},{14,30},{16,0},... | collective-permute-start | bytes 24584 | tf_op jit(solution)/shard_map/ppermute | solution.py:1022
  19.8 4.6 %collective-permute-start.5 = (f32[4,512]{1,0:T(4,128)S(1)}, f32[4,512]{1,0:T(4,128)S(1)}, u32[]{:S(2)}, u32[]{:S(2)}) collective-permute-start(f32[4,512]{1,0:T(4,128)S(1)} %add.237.part), channel_id=1, source_target_pairs={{0,1},{1,0},{2,3},{3,2},{4,5},{5,4},{6,7},{7,6},{8,9},{9,8},{10,11... | collective-permute-start | bytes 24584 | tf_op jit(solution)/shard_map/ppermute | solution.py:1022
  24.4 13.1 %collective-permute-start.9 = (bf16[512,512]{1,0:T(8,128)(2,1)S(1)}, bf16[512,512]{1,0:T(8,128)(2,1)S(1)}, u32[]{:S(2)}, u32[]{:S(2)}) collective-permute-start(bf16[512,512]{1,0:T(8,128)(2,1)S(1)} %get-tuple-element.211), channel_id=1, source_target_pairs={{0,1},{1,0},{2,3},{3,2},{4,5},{5,4},{6,7},{7,6},{8,9},{9,8},{10,11... | collective-permute-start | bytes 1572872 | tf_op jit(solution)/shard_map/ppermute | solution.py:1022
  32.8 3.7 %collective-permute-start.7 = (f32[4,512]{1,0:T(4,128)S(1)}, f32[4,512]{1,0:T(4,128)S(1)}, u32[]{:S(2)}, u32[]{:S(2)}) collective-permute-start(f32[4,512]{1,0:T(4,128)S(1)} %add.238), channel_id=1, source_target_pairs={{0,4},{2,6},{4,0},{6,2},{8,12},{10,14},{12,8},{14,10},{16,20},{18,... | collective-permute-start | bytes 24584 | tf_op jit(solution)/shard_map/ppermute | solution.py:1022
  37.6 27.5 %collective-permute-start.19 = (bf16[2304,256]{1,0:T(8,128)(2,1)S(1)}, bf16[2304,256]{1,0:T(8,128)(2,1)S(1)}, u32[]{:S(2)}, u32[]{:S(2)}) collective-permute-start(bf16[2304,256]{1,0:T(8,128)(2,1)S(1)} %get-tuple-element.227), channel_id=1, source_target_pairs={{0,1},{1,0},{2,3},{3,2},{4,5},{5,4},{6,7},{7,6},{8,9},{9,8},{10,11... | collective-permute-start | bytes 3538952 | tf_op jit(solution)/shard_map/ppermute | solution.py:1022
  39.0 20.8 %collective-permute-start.14 = (bf16[512,512]{1,0:T(8,128)(2,1)S(1)}, bf16[512,512]{1,0:T(8,128)(2,1)S(1)}, u32[]{:S(2)}, u32[]{:S(2)}) collective-permute-start(bf16[512,512]{1,0:T(8,128)(2,1)S(1)} %collective-permute-done.9.r1), channel_id=1, source_target_pairs={{0,2},{2,0},{4,6},{6,4},{8,10},{10,8},{12,14},{14,12},{16,18},{18,... | collective-permute-start | bytes 1572872 | tf_op jit(solution)/shard_map/ppermute | solution.py:1022
  39.0 3.7 %collective-permute-start.8 = (f32[4,512]{1,0:T(4,128)S(1)}, f32[4,512]{1,0:T(4,128)S(1)}, u32[]{:S(2)}, u32[]{:S(2)}) collective-permute-start(f32[4,512]{1,0:T(4,128)S(1)} %add.239), channel_id=1, source_target_pairs={{0,8},{2,10},{4,12},{6,14},{8,0},{10,2},{12,4},{14,6},{16,24},{18,... | collective-permute-start | bytes 24584 | tf_op jit(solution)/shard_map/ppermute | solution.py:1022
  42.6 5.9 %collective-permute-start.10 = (f32[4,512]{1,0:T(4,128)S(1)}, f32[4,512]{1,0:T(4,128)S(1)}, u32[]{:S(2)}, u32[]{:S(2)}) collective-permute-start(f32[4,512]{1,0:T(4,128)S(1)} %add.240), channel_id=1, source_target_pairs={{0,16},{2,18},{4,20},{6,22},{8,24},{10,26},{12,28},{14,30},{16,0},... | collective-permute-start | bytes 24584 | tf_op jit(solution)/shard_map/ppermute | solution.py:1022
  51.1 4.3 %collective-permute-start.12 = (f32[8,2048]{1,0:T(8,128)S(1)}, f32[8,2048]{1,0:T(8,128)S(1)}, u32[]{:S(2)}, u32[]{:S(2)}) collective-permute-start(f32[8,2048]{1,0:T(8,128)S(1)} %add.242), channel_id=1, source_target_pairs={{0,4},{2,6},{4,0},{6,2},{8,12},{10,14},{12,8},{14,10},{16,20},{18,... | collective-permute-start | bytes 196616 | tf_op jit(solution)/shard_map/ppermute | solution.py:1022
  55.4 4.3 %collective-permute-start.13 = (f32[8,2048]{1,0:T(8,128)S(1)}, f32[8,2048]{1,0:T(8,128)S(1)}, u32[]{:S(2)}, u32[]{:S(2)}) collective-permute-start(f32[8,2048]{1,0:T(8,128)S(1)} %add.243), channel_id=1, source_target_pairs={{0,8},{2,10},{4,12},{6,14},{8,0},{10,2},{12,4},{14,6},{16,24},{18,... | collective-permute-start | bytes 196616 | tf_op jit(solution)/shard_map/ppermute | solution.py:1022
  59.8 5.2 %collective-permute-start.15 = (f32[8,2048]{1,0:T(8,128)S(1)}, f32[8,2048]{1,0:T(8,128)S(1)}, u32[]{:S(2)}, u32[]{:S(2)}) collective-permute-start(f32[8,2048]{1,0:T(8,128)S(1)} %add.244), channel_id=1, source_target_pairs={{0,16},{2,18},{4,20},{6,22},{8,24},{10,26},{12,28},{14,30},{16,0},... | collective-permute-start | bytes 196616 | tf_op jit(solution)/shard_map/ppermute | solution.py:1022
  65.0 13.9 %collective-permute-start.20 = (bf16[2304,256]{1,0:T(8,128)(2,1)S(1)}, bf16[2304,256]{1,0:T(8,128)(2,1)S(1)}, u32[]{:S(2)}, u32[]{:S(2)}) collective-permute-start(bf16[2304,256]{1,0:T(8,128)(2,1)S(1)} %collective-permute-done.19.r1), channel_id=1, source_target_pairs={{0,2},{2,0},{4,6},{6,4},{8,10},{10,8},{12,14},{14,12},{16,18},{18,... | collective-permute-start | bytes 3538952 | tf_op jit(solution)/shard_map/ppermute | solution.py:1022
  65.1 20.4 %collective-permute-start.25 = (bf16[1552,256]{1,0:T(8,128)(2,1)S(1)}, bf16[1552,256]{1,0:T(8,128)(2,1)S(1)}, u32[]{:S(2)}, u32[]{:S(2)}) collective-permute-start(bf16[1552,256]{1,0:T(8,128)(2,1)S(1)} %get-tuple-element.234), channel_id=1, source_target_pairs={{0,1},{1,0},{2,3},{3,2},{4,5},{5,4},{6,7},{7,6},{8,9},{9,8},{10,11... | collective-permute-start | bytes 2383880 | tf_op jit(solution)/shard_map/ppermute | solution.py:1022
  71.6 3.7 %collective-permute-start.17 = (f32[4,512]{1,0:T(4,128)S(1)}, f32[4,512]{1,0:T(4,128)S(1)}, u32[]{:S(2)}, u32[]{:S(2)}) collective-permute-start(f32[4,512]{1,0:T(4,128)S(1)} %add.246), channel_id=1, source_target_pairs={{0,4},{2,6},{4,0},{6,2},{8,12},{10,14},{12,8},{14,10},{16,20},{18,... | collective-permute-start | bytes 24584 | tf_op jit(solution)/shard_map/ppermute | solution.py:1022
  75.3 3.7 %collective-permute-start.18 = (f32[4,512]{1,0:T(4,128)S(1)}, f32[4,512]{1,0:T(4,128)S(1)}, u32[]{:S(2)}, u32[]{:S(2)}) collective-permute-start(f32[4,512]{1,0:T(4,128)S(1)} %add.247), channel_id=1, source_target_pairs={{0,8},{2,10},{4,12},{6,14},{8,0},{10,2},{12,4},{14,6},{16,24},{18,... | collective-permute-start | bytes 24584 | tf_op jit(solution)/shard_map/ppermute | solution.py:1022
  78.9 4.6 %collective-permute-start.21 = (f32[4,512]{1,0:T(4,128)S(1)}, f32[4,512]{1,0:T(4,128)S(1)}, u32[]{:S(2)}, u32[]{:S(2)}) collective-permute-start(f32[4,512]{1,0:T(4,128)S(1)} %add.248), channel_id=1, source_target_pairs={{0,16},{2,18},{4,20},{6,22},{8,24},{10,26},{12,28},{14,30},{16,0},... | collective-permute-start | bytes 24584 | tf_op jit(solution)/shard_map/ppermute | solution.py:1022
  85.5 10.2 %collective-permute-start.26 = (bf16[1552,256]{1,0:T(8,128)(2,1)S(1)}, bf16[1552,256]{1,0:T(8,128)(2,1)S(1)}, u32[]{:S(2)}, u32[]{:S(2)}) collective-permute-start(bf16[1552,256]{1,0:T(8,128)(2,1)S(1)} %collective-permute-done.25.r1), channel_id=1, source_target_pairs={{0,2},{2,0},{4,6},{6,4},{8,10},{10,8},{12,14},{14,12},{16,18},{18,... | collective-permute-start | bytes 2383880 | tf_op jit(solution)/shard_map/ppermute | solution.py:1022
  85.6 27.2 %collective-permute-start.32 = (bf16[224,1024]{1,0:T(8,128)(2,1)S(1)}, bf16[224,1024]{1,0:T(8,128)(2,1)S(1)}, u32[]{:S(2)}, u32[]{:S(2)}) collective-permute-start(bf16[224,1024]{1,0:T(8,128)(2,1)S(1)} %bitcast.49), channel_id=1, source_target_pairs={{0,1},{1,0},{2,3},{3,2},{4,5},{5,4},{6,7},{7,6},{8,9},{9,8},{10,11... | collective-permute-start | bytes 1376264 | tf_op jit(solution)/shard_map/ppermute | solution.py:1022
  88.4 3.7 %collective-permute-start.23 = (f32[4,512]{1,0:T(4,128)S(1)}, f32[4,512]{1,0:T(4,128)S(1)}, u32[]{:S(2)}, u32[]{:S(2)}) collective-permute-start(f32[4,512]{1,0:T(4,128)S(1)} %add.250), channel_id=1, source_target_pairs={{0,4},{2,6},{4,0},{6,2},{8,12},{10,14},{12,8},{14,10},{16,20},{18,... | collective-permute-start | bytes 24584 | tf_op jit(solution)/shard_map/ppermute | solution.py:1022
  92.0 3.7 %collective-permute-start.24 = (f32[4,512]{1,0:T(4,128)S(1)}, f32[4,512]{1,0:T(4,128)S(1)}, u32[]{:S(2)}, u32[]{:S(2)}) collective-permute-start(f32[4,512]{1,0:T(4,128)S(1)} %add.251), channel_id=1, source_target_pairs={{0,8},{2,10},{4,12},{6,14},{8,0},{10,2},{12,4},{14,6},{16,24},{18,... | collective-permute-start | bytes 24584 | tf_op jit(solution)/shard_map/ppermute | solution.py:1022
  95.7 4.6 %collective-permute-start.27 = (f32[4,512]{1,0:T(4,128)S(1)}, f32[4,512]{1,0:T(4,128)S(1)}, u32[]{:S(2)}, u32[]{:S(2)}) collective-permute-start(f32[4,512]{1,0:T(4,128)S(1)} %add.252), channel_id=1, source_target_pairs={{0,16},{2,18},{4,20},{6,22},{8,24},{10,26},{12,28},{14,30},{16,0},... | collective-permute-start | bytes 24584 | tf_op jit(solution)/shard_map/ppermute | solution.py:1022
  103.3 4.0 %collective-permute-start.29 = (f32[4,2048]{1,0:T(4,128)S(1)}, f32[4,2048]{1,0:T(4,128)S(1)}, u32[]{:S(2)}, u32[]{:S(2)}) collective-permute-start(f32[4,2048]{1,0:T(4,128)S(1)} %add.254), channel_id=1, source_target_pairs={{0,4},{2,6},{4,0},{6,2},{8,12},{10,14},{12,8},{14,10},{16,20},{18,... | collective-permute-start | bytes 98312 | tf_op jit(solution)/shard_map/ppermute | solution.py:1022
  107.3 4.0 %collective-permute-start.30 = (f32[4,2048]{1,0:T(4,128)S(1)}, f32[4,2048]{1,0:T(4,128)S(1)}, u32[]{:S(2)}, u32[]{:S(2)}) collective-permute-start(f32[4,2048]{1,0:T(4,128)S(1)} %add.255), channel_id=1, source_target_pairs={{0,8},{2,10},{4,12},{6,14},{8,0},{10,2},{12,4},{14,6},{16,24},{18,... | collective-permute-start | bytes 98312 | tf_op jit(solution)/shard_map/ppermute | solution.py:1022
  111.3 4.9 %collective-permute-start.31 = (f32[4,2048]{1,0:T(4,128)S(1)}, f32[4,2048]{1,0:T(4,128)S(1)}, u32[]{:S(2)}, u32[]{:S(2)}) collective-permute-start(f32[4,2048]{1,0:T(4,128)S(1)} %add.256), channel_id=1, source_target_pairs={{0,16},{2,18},{4,20},{6,22},{8,24},{10,26},{12,28},{14,30},{16,0},... | collective-permute-start | bytes 98312 | tf_op jit(solution)/shard_map/ppermute | solution.py:1022
  122.4 4.0 %collective-permute-start.34 = (f32[4,2048]{1,0:T(4,128)S(1)}, f32[4,2048]{1,0:T(4,128)S(1)}, u32[]{:S(2)}, u32[]{:S(2)}) collective-permute-start(f32[4,2048]{1,0:T(4,128)S(1)} %add.258), channel_id=1, source_target_pairs={{0,4},{2,6},{4,0},{6,2},{8,12},{10,14},{12,8},{14,10},{16,20},{18,... | collective-permute-start | bytes 98312 | tf_op jit(solution)/shard_map/ppermute | solution.py:1022
  126.4 4.0 %collective-permute-start.35 = (f32[4,2048]{1,0:T(4,128)S(1)}, f32[4,2048]{1,0:T(4,128)S(1)}, u32[]{:S(2)}, u32[]{:S(2)}) collective-permute-start(f32[4,2048]{1,0:T(4,128)S(1)} %add.259), channel_id=1, source_target_pairs={{0,8},{2,10},{4,12},{6,14},{8,0},{10,2},{12,4},{14,6},{16,24},{18,... | collective-permute-start | bytes 98312 | tf_op jit(solution)/shard_map/ppermute | solution.py:1022
  130.4 4.9 %collective-permute-start.36 = (f32[4,2048]{1,0:T(4,128)S(1)}, f32[4,2048]{1,0:T(4,128)S(1)}, u32[]{:S(2)}, u32[]{:S(2)}) collective-permute-start(f32[4,2048]{1,0:T(4,128)S(1)} %add.260), channel_id=1, source_target_pairs={{0,16},{2,18},{4,20},{6,22},{8,24},{10,26},{12,28},{14,30},{16,0},... | collective-permute-start | bytes 98312 | tf_op jit(solution)/shard_map/ppermute | solution.py:1022
  138.8 3.9 %collective-permute-start.38 = (f32[12,512]{1,0:T(8,128)S(1)}, f32[12,512]{1,0:T(8,128)S(1)}, u32[]{:S(2)}, u32[]{:S(2)}) collective-permute-start(f32[12,512]{1,0:T(8,128)S(1)} %add.262), channel_id=1, source_target_pairs={{0,4},{2,6},{4,0},{6,2},{8,12},{10,14},{12,8},{14,10},{16,20},{18,... | collective-permute-start | bytes 73736 | tf_op jit(solution)/shard_map/ppermute | solution.py:1022
  142.7 3.9 %collective-permute-start.39 = (f32[12,512]{1,0:T(8,128)S(1)}, f32[12,512]{1,0:T(8,128)S(1)}, u32[]{:S(2)}, u32[]{:S(2)}) collective-permute-start(f32[12,512]{1,0:T(8,128)S(1)} %add.263), channel_id=1, source_target_pairs={{0,8},{2,10},{4,12},{6,14},{8,0},{10,2},{12,4},{14,6},{16,24},{18,... | collective-permute-start | bytes 73736 | tf_op jit(solution)/shard_map/ppermute | solution.py:1022
  146.6 4.8 %collective-permute-start.40 = (f32[12,512]{1,0:T(8,128)S(1)}, f32[12,512]{1,0:T(8,128)S(1)}, u32[]{:S(2)}, u32[]{:S(2)}) collective-permute-start(f32[12,512]{1,0:T(8,128)S(1)} %add.264), channel_id=1, source_target_pairs={{0,16},{2,18},{4,20},{6,22},{8,24},{10,26},{12,28},{14,30},{16,0},... | collective-permute-start | bytes 73736 | tf_op jit(solution)/shard_map/ppermute | solution.py:1022
  158.6 3.8 %collective-permute-start.43 = (bf16[8,416,256]{2,1,0:T(8,128)(2,1)S(1)}, bf16[8,416,256]{2,1,0:T(8,128)(2,1)S(1)}, u32[]{:S(2)}, u32[]{:S(2)}) collective-permute-start(bf16[8,416,256]{2,1,0:T(8,128)(2,1)S(1)} %get-tuple-element.271), channel_id=1, source_target_pairs={{0,2},{2,0},{4,6},{6,4},{8,10},{10,8},{12,14},{14,12},{16,18},{18,... | collective-permute-start | bytes 5111816 | tf_op jit(solution)/shard_map/ppermute | solution.py:1022
  158.8 3.7 %collective-permute-start.42 = (f32[4,512]{1,0:T(4,128)S(1)}, f32[4,512]{1,0:T(4,128)S(1)}, u32[]{:S(2)}, u32[]{:S(2)}) collective-permute-start(f32[4,512]{1,0:T(4,128)S(1)} %add.266), channel_id=1, source_target_pairs={{0,4},{2,6},{4,0},{6,2},{8,12},{10,14},{12,8},{14,10},{16,20},{18,... | collective-permute-start | bytes 24584 | tf_op jit(solution)/shard_map/ppermute | solution.py:1022
  162.6 20.9 %collective-permute-start.46 = (bf16[4,416,256]{2,1,0:T(8,128)(2,1)S(1)}, bf16[4,416,256]{2,1,0:T(8,128)(2,1)S(1)}, u32[]{:S(2)}, u32[]{:S(2)}) collective-permute-start(bf16[4,416,256]{2,1,0:T(8,128)(2,1)S(1)} %get-tuple-element.288), channel_id=1, source_target_pairs={{0,4},{2,6},{4,0},{6,2},{8,12},{10,14},{12,8},{14,10},{16,20},{18,... | collective-permute-start | bytes 2555912 | tf_op jit(solution)/shard_map/ppermute | solution.py:1022
  164.2 3.7 %collective-permute-start.44 = (f32[4,512]{1,0:T(4,128)S(1)}, f32[4,512]{1,0:T(4,128)S(1)}, u32[]{:S(2)}, u32[]{:S(2)}) collective-permute-start(f32[4,512]{1,0:T(4,128)S(1)} %add.267), channel_id=1, source_target_pairs={{0,8},{2,10},{4,12},{6,14},{8,0},{10,2},{12,4},{14,6},{16,24},{18,... | collective-permute-start | bytes 24584 | tf_op jit(solution)/shard_map/ppermute | solution.py:1022
  167.8 4.5 %collective-permute-start.45 = (f32[4,512]{1,0:T(4,128)S(1)}, f32[4,512]{1,0:T(4,128)S(1)}, u32[]{:S(2)}, u32[]{:S(2)}) collective-permute-start(f32[4,512]{1,0:T(4,128)S(1)} %add.270), channel_id=1, source_target_pairs={{0,16},{2,18},{4,20},{6,22},{8,24},{10,26},{12,28},{14,30},{16,0},... | collective-permute-start | bytes 24584 | tf_op jit(solution)/shard_map/ppermute | solution.py:1022
  184.7 8.9 %collective-permute-start.50 = (bf16[8,256,256]{2,1,0:T(8,128)(2,1)S(1)}, bf16[8,256,256]{2,1,0:T(8,128)(2,1)S(1)}, u32[]{:S(2)}, u32[]{:S(2)}) collective-permute-start(bf16[8,256,256]{2,1,0:T(8,128)(2,1)S(1)} %get-tuple-element.291), channel_id=1, source_target_pairs={{0,2},{2,0},{4,6},{6,4},{8,10},{10,8},{12,14},{14,12},{16,18},{18,... | collective-permute-start | bytes 3145736 | tf_op jit(solution)/shard_map/ppermute | solution.py:1022
  185.0 4.4 %collective-permute-start.48 = (f32[8,2048]{1,0:T(8,128)S(1)}, f32[8,2048]{1,0:T(8,128)S(1)}, u32[]{:S(2)}, u32[]{:S(2)}) collective-permute-start(f32[8,2048]{1,0:T(8,128)S(1)} %add.272), channel_id=1, source_target_pairs={{0,4},{2,6},{4,0},{6,2},{8,12},{10,14},{12,8},{14,10},{16,20},{18,... | collective-permute-start | bytes 196616 | tf_op jit(solution)/shard_map/ppermute | solution.py:1022
  189.3 4.3 %collective-permute-start.49 = (f32[8,2048]{1,0:T(8,128)S(1)}, f32[8,2048]{1,0:T(8,128)S(1)}, u32[]{:S(2)}, u32[]{:S(2)}) collective-permute-start(f32[8,2048]{1,0:T(8,128)S(1)} %add.273), channel_id=1, source_target_pairs={{0,8},{2,10},{4,12},{6,14},{8,0},{10,2},{12,4},{14,6},{16,24},{18,... | collective-permute-start | bytes 196616 | tf_op jit(solution)/shard_map/ppermute | solution.py:1022
  193.8 5.2 %collective-permute-start.51 = (f32[8,2048]{1,0:T(8,128)S(1)}, f32[8,2048]{1,0:T(8,128)S(1)}, u32[]{:S(2)}, u32[]{:S(2)}) collective-permute-start(f32[8,2048]{1,0:T(8,128)S(1)} %add.274), channel_id=1, source_target_pairs={{0,16},{2,18},{4,20},{6,22},{8,24},{10,26},{12,28},{14,30},{16,0},... | collective-permute-start | bytes 196616 | tf_op jit(solution)/shard_map/ppermute | solution.py:1022
  199.0 11.1 %collective-permute-start.53 = (bf16[4,256,256]{2,1,0:T(8,128)(2,1)S(1)}, bf16[4,256,256]{2,1,0:T(8,128)(2,1)S(1)}, u32[]{:S(2)}, u32[]{:S(2)}) collective-permute-start(bf16[4,256,256]{2,1,0:T(8,128)(2,1)S(1)} %get-tuple-element.304), channel_id=1, source_target_pairs={{0,4},{2,6},{4,0},{6,2},{8,12},{10,14},{12,8},{14,10},{16,20},{18,... | collective-permute-start | bytes 1572872 | tf_op jit(solution)/shard_map/ppermute | solution.py:1022
  200.7 8.8 %collective-permute-start.52 = (bf16[2,416,256]{2,1,0:T(8,128)(2,1)S(1)}, bf16[2,416,256]{2,1,0:T(8,128)(2,1)S(1)}, u32[]{:S(2)}, u32[]{:S(2)}) collective-permute-start(bf16[2,416,256]{2,1,0:T(8,128)(2,1)S(1)} %get-tuple-element.303), channel_id=1, source_target_pairs={{0,8},{2,10},{4,12},{6,14},{8,0},{10,2},{12,4},{14,6},{16,24},{18,... | collective-permute-start | bytes 1277960 | tf_op jit(solution)/shard_map/ppermute | solution.py:1022
  211.4 4.1 %collective-permute-start.56 = (bf16[8,384,256]{2,1,0:T(8,128)(2,1)S(1)}, bf16[8,384,256]{2,1,0:T(8,128)(2,1)S(1)}, u32[]{:S(2)}, u32[]{:S(2)}) collective-permute-start(bf16[8,384,256]{2,1,0:T(8,128)(2,1)S(1)} %get-tuple-element.306), channel_id=1, source_target_pairs={{0,2},{2,0},{4,6},{6,4},{8,10},{10,8},{12,14},{14,12},{16,18},{18,... | collective-permute-start | bytes 4718600 | tf_op jit(solution)/shard_map/ppermute | solution.py:1022
  211.6 3.9 %collective-permute-start.55 = (f32[12,512]{1,0:T(8,128)S(1)}, f32[12,512]{1,0:T(8,128)S(1)}, u32[]{:S(2)}, u32[]{:S(2)}) collective-permute-start(f32[12,512]{1,0:T(8,128)S(1)} %add.279), channel_id=1, source_target_pairs={{0,4},{2,6},{4,0},{6,2},{8,12},{10,14},{12,8},{14,10},{16,20},{18,... | collective-permute-start | bytes 73736 | tf_op jit(solution)/shard_map/ppermute | solution.py:1022
  215.7 19.0 %collective-permute-start.59 = (bf16[4,384,256]{2,1,0:T(8,128)(2,1)S(1)}, bf16[4,384,256]{2,1,0:T(8,128)(2,1)S(1)}, u32[]{:S(2)}, u32[]{:S(2)}) collective-permute-start(bf16[4,384,256]{2,1,0:T(8,128)(2,1)S(1)} %get-tuple-element.315), channel_id=1, source_target_pairs={{0,4},{2,6},{4,0},{6,2},{8,12},{10,14},{12,8},{14,10},{16,20},{18,... | collective-permute-start | bytes 2359304 | tf_op jit(solution)/shard_map/ppermute | solution.py:1022
  217.3 3.9 %collective-permute-start.57 = (f32[12,512]{1,0:T(8,128)S(1)}, f32[12,512]{1,0:T(8,128)S(1)}, u32[]{:S(2)}, u32[]{:S(2)}) collective-permute-start(f32[12,512]{1,0:T(8,128)S(1)} %add.280), channel_id=1, source_target_pairs={{0,8},{2,10},{4,12},{6,14},{8,0},{10,2},{12,4},{14,6},{16,24},{18,... | collective-permute-start | bytes 73736 | tf_op jit(solution)/shard_map/ppermute | solution.py:1022
  221.2 7.0 %collective-permute-start.58 = (f32[12,512]{1,0:T(8,128)S(1)}, f32[12,512]{1,0:T(8,128)S(1)}, u32[]{:S(2)}, u32[]{:S(2)}) collective-permute-start(f32[12,512]{1,0:T(8,128)S(1)} %add.283), channel_id=1, source_target_pairs={{0,16},{2,18},{4,20},{6,22},{8,24},{10,26},{12,28},{14,30},{16,0},... | collective-permute-start | bytes 73736 | tf_op jit(solution)/shard_map/ppermute | solution.py:1022
  235.9 11.5 %collective-permute-start.64 = (bf16[8,288,256]{2,1,0:T(8,128)(2,1)S(1)}, bf16[8,288,256]{2,1,0:T(8,128)(2,1)S(1)}, u32[]{:S(2)}, u32[]{:S(2)}) collective-permute-start(bf16[8,288,256]{2,1,0:T(8,128)(2,1)S(1)} %get-tuple-element.318), channel_id=1, source_target_pairs={{0,2},{2,0},{4,6},{6,4},{8,10},{10,8},{12,14},{14,12},{16,18},{18,... | collective-permute-start | bytes 3538952 | tf_op jit(solution)/shard_map/ppermute | solution.py:1022
  236.1 8.7 %collective-permute-start.72 = (bf16[2,256,256]{2,1,0:T(8,128)(2,1)S(1)}, bf16[2,256,256]{2,1,0:T(8,128)(2,1)S(1)}, u32[]{:S(2)}, u32[]{:S(2)}) collective-permute-start(bf16[2,256,256]{2,1,0:T(8,128)(2,1)S(1)} %get-tuple-element.377), channel_id=1, source_target_pairs={{0,8},{2,10},{4,12},{6,14},{8,0},{10,2},{12,4},{14,6},{16,24},{18,... | collective-permute-start | bytes 786440 | tf_op jit(solution)/shard_map/ppermute | solution.py:1022
  237.8 3.7 %collective-permute-start.61 = (f32[4,512]{1,0:T(4,128)S(1)}, f32[4,512]{1,0:T(4,128)S(1)}, u32[]{:S(2)}, u32[]{:S(2)}) collective-permute-start(f32[4,512]{1,0:T(4,128)S(1)} %add.285), channel_id=1, source_target_pairs={{0,4},{2,6},{4,0},{6,2},{8,12},{10,14},{12,8},{14,10},{16,20},{18,... | collective-permute-start | bytes 24584 | tf_op jit(solution)/shard_map/ppermute | solution.py:1022
  241.4 3.7 %collective-permute-start.62 = (f32[4,512]{1,0:T(4,128)S(1)}, f32[4,512]{1,0:T(4,128)S(1)}, u32[]{:S(2)}, u32[]{:S(2)}) collective-permute-start(f32[4,512]{1,0:T(4,128)S(1)} %add.286), channel_id=1, source_target_pairs={{0,8},{2,10},{4,12},{6,14},{8,0},{10,2},{12,4},{14,6},{16,24},{18,... | collective-permute-start | bytes 24584 | tf_op jit(solution)/shard_map/ppermute | solution.py:1022
  245.1 4.7 %collective-permute-start.63 = (f32[4,512]{1,0:T(4,128)S(1)}, f32[4,512]{1,0:T(4,128)S(1)}, u32[]{:S(2)}, u32[]{:S(2)}) collective-permute-start(f32[4,512]{1,0:T(4,128)S(1)} %add.287), channel_id=1, source_target_pairs={{0,16},{2,18},{4,20},{6,22},{8,24},{10,26},{12,28},{14,30},{16,0},... | collective-permute-start | bytes 24584 | tf_op jit(solution)/shard_map/ppermute | solution.py:1022
  247.5 16.0 %collective-permute-start.65 = (bf16[4,288,256]{2,1,0:T(8,128)(2,1)S(1)}, bf16[4,288,256]{2,1,0:T(8,128)(2,1)S(1)}, u32[]{:S(2)}, u32[]{:S(2)}) collective-permute-start(bf16[4,288,256]{2,1,0:T(8,128)(2,1)S(1)} %get-tuple-element.325), channel_id=1, source_target_pairs={{0,4},{2,6},{4,0},{6,2},{8,12},{10,14},{12,8},{14,10},{16,20},{18,... | collective-permute-start | bytes 1769480 | tf_op jit(solution)/shard_map/ppermute | solution.py:1022
  249.0 33.1 %collective-permute-start.73 = (bf16[1,672,256]{2,1,0:T(8,128)(2,1)S(1)}, bf16[1,672,256]{2,1,0:T(8,128)(2,1)S(1)}, u32[]{:S(2)}, u32[]{:S(2)}) collective-permute-start(bf16[1,672,256]{2,1,0:T(8,128)(2,1)S(1)} %pad_maximum_fusion.1), channel_id=1, source_target_pairs={{0,16},{2,18},{4,20},{6,22},{8,24},{10,26},{12,28},{14,30},{16,0},... | collective-permute-start | bytes 1032200 | tf_op jit(solution)/shard_map/ppermute | solution.py:1022
  251.5 3.7 %collective-permute-start.68 = (bf16[8,64,256]{2,1,0:T(8,128)(2,1)S(1)}, bf16[8,64,256]{2,1,0:T(8,128)(2,1)S(1)}, u32[]{:S(2)}, u32[]{:S(2)}) collective-permute-start(bf16[8,64,256]{2,1,0:T(8,128)(2,1)S(1)} %get-tuple-element.330), channel_id=1, source_target_pairs={{0,2},{2,0},{4,6},{6,4},{8,10},{10,8},{12,14},{14,12},{16,18},{18,... | collective-permute-start | bytes 786440 | tf_op jit(solution)/shard_map/ppermute | solution.py:1022
  251.6 18.4 %collective-permute-start.74 = (bf16[2,384,256]{2,1,0:T(8,128)(2,1)S(1)}, bf16[2,384,256]{2,1,0:T(8,128)(2,1)S(1)}, u32[]{:S(2)}, u32[]{:S(2)}) collective-permute-start(bf16[2,384,256]{2,1,0:T(8,128)(2,1)S(1)} %get-tuple-element.337), channel_id=1, source_target_pairs={{0,8},{2,10},{4,12},{6,14},{8,0},{10,2},{12,4},{14,6},{16,24},{18,... | collective-permute-start | bytes 1179656 | tf_op jit(solution)/shard_map/ppermute | solution.py:1022
  255.2 16.9 %collective-permute-start.69 = (bf16[4,64,256]{2,1,0:T(8,128)(2,1)S(1)}, bf16[4,64,256]{2,1,0:T(8,128)(2,1)S(1)}, u32[]{:S(2)}, u32[]{:S(2)}) collective-permute-start(bf16[4,64,256]{2,1,0:T(8,128)(2,1)S(1)} %get-tuple-element.387), channel_id=1, source_target_pairs={{0,4},{2,6},{4,0},{6,2},{8,12},{10,14},{12,8},{14,10},{16,20},{18,... | collective-permute-start | bytes 393224 | tf_op jit(solution)/shard_map/ppermute | solution.py:1022
  263.5 14.6 %collective-permute-start.66 = (bf16[2,288,256]{2,1,0:T(8,128)(2,1)S(1)}, bf16[2,288,256]{2,1,0:T(8,128)(2,1)S(1)}, u32[]{:S(2)}, u32[]{:S(2)}) collective-permute-start(bf16[2,288,256]{2,1,0:T(8,128)(2,1)S(1)} %get-tuple-element.328), channel_id=1, source_target_pairs={{0,8},{2,10},{4,12},{6,14},{8,0},{10,2},{12,4},{14,6},{16,24},{18,... | collective-permute-start | bytes 884744 | tf_op jit(solution)/shard_map/ppermute | solution.py:1022
  270.0 15.3 %collective-permute-start.75 = (bf16[1,384,256]{2,1,0:T(8,128)(2,1)S(1)}, bf16[1,384,256]{2,1,0:T(8,128)(2,1)S(1)}, u32[]{:S(2)}, u32[]{:S(2)}) collective-permute-start(bf16[1,384,256]{2,1,0:T(8,128)(2,1)S(1)} %get-tuple-element.380), channel_id=1, source_target_pairs={{0,16},{2,18},{4,20},{6,22},{8,24},{10,26},{12,28},{14,30},{16,0},... | collective-permute-start | bytes 589832 | tf_op jit(solution)/shard_map/ppermute | solution.py:1022
  272.2 9.5 %collective-permute-start.70 = (bf16[2,64,256]{2,1,0:T(8,128)(2,1)S(1)}, bf16[2,64,256]{2,1,0:T(8,128)(2,1)S(1)}, u32[]{:S(2)}, u32[]{:S(2)}) collective-permute-start(bf16[2,64,256]{2,1,0:T(8,128)(2,1)S(1)} %get-tuple-element.389), channel_id=1, source_target_pairs={{0,8},{2,10},{4,12},{6,14},{8,0},{10,2},{12,4},{14,6},{16,24},{18,... | collective-permute-start | bytes 196616 | tf_op jit(solution)/shard_map/ppermute | solution.py:1022
  278.2 11.0 %collective-permute-start.67 = (bf16[1,288,256]{2,1,0:T(8,128)(2,1)S(1)}, bf16[1,288,256]{2,1,0:T(8,128)(2,1)S(1)}, u32[]{:S(2)}, u32[]{:S(2)}) collective-permute-start(bf16[1,288,256]{2,1,0:T(8,128)(2,1)S(1)} %get-tuple-element.382), channel_id=1, source_target_pairs={{0,16},{2,18},{4,20},{6,22},{8,24},{10,26},{12,28},{14,30},{16,0},... | collective-permute-start | bytes 442376 | tf_op jit(solution)/shard_map/ppermute | solution.py:1022
  281.7 7.5 %collective-permute-start.71 = (bf16[1,64,256]{2,1,0:T(8,128)(2,1)S(1)}, bf16[1,64,256]{2,1,0:T(8,128)(2,1)S(1)}, u32[]{:S(2)}, u32[]{:S(2)}) collective-permute-start(bf16[1,64,256]{2,1,0:T(8,128)(2,1)S(1)} %get-tuple-element.390), channel_id=1, source_target_pairs={{0,16},{2,18},{4,20},{6,22},{8,24},{10,26},{12,28},{14,30},{16,0},... | collective-permute-start | bytes 98312 | tf_op jit(solution)/shard_map/ppermute | solution.py:1022
  (13 other events, 16.8 us)

commit v7 on v6

--- a/solution.py
+++ b/solution.py
@@ -1126,8 +1126,6 @@
         flops=1e9, size=6e6, name="stage_three",
     )
     parts3, _ = steps(st3, before={3: (w4_r2,)})
-    w5_r2 = swap(after(w5_r1, parts3), "wide", near)
-    pk1 = swap(after(pack, w5_r1, parts3), "narrow", pair)
     w4 = call(
         fetch_four_kernel, [h(2048, 512)],
         [(SMEM, after(isc_, st3)), far(second_reduce), (ANY, w4_r1), (ANY, w4_r2)], [D((3,))],
@@ -1145,7 +1143,15 @@
         ],
         flops=1e9, size=1e7, name="stage_four",
     )
-    parts4, _ = steps(st4, before={3: (w5_r2,)})
+    held = {}
+
+    def core_half(results):
+        held["w5"] = swap(after(w5_r1, results[0]), "wide", near)
+        return (held["w5"],)
+
+    parts4, _ = steps(st4, before={3: core_half})
+    w5_r2 = held["w5"]
+    pk1 = swap(after(pack, w5_r1, st4), "narrow", pair)
     w5 = call(
         fetch_five_kernel, [h(2, 4608, 256)],
         [(SMEM, after(isc_, st4)), far(w5_own), (ANY, w5_r1), (ANY, w5_r2)], [D((3,))],
@@ -1156,8 +1162,13 @@
         [fs, parts4, pre4, keep, gb, sh, w5], [V((4, 512), F32)],
         flops=2e9, size=1e7, name="stage_five",
     )
-    pk2 = swap(after(pk1, st5), "wide", near)
-    parts5, _ = steps(st5, before={3: (pk2,)})
+
+    def core_rest(results):
+        held["rest"] = swap(after(pk1, results[1]), "wide", near)
+        return (held["rest"],)
+
+    parts5, _ = steps(st5, before={3: core_rest})
+    pk2 = held["rest"]
     og_other = swap(after(og_own, pk1, st5), "narrow", pair)
     pk1, pk2 = (ANY, pk1), (ANY, pk2)
     w6, gain5, vec2 = call(
@@ -1219,8 +1230,6 @@
         grads_a_kernel, [h(8, 416, 256)] * 2, [isc, h5, d6, col4, d5],
         [V((256, 2048), BF), V((512, 256), BF)], flops=2e9, size=1e7, name="grads_a",
     )
-    held = {}
-
     def core_step(name, g, tied=True):
         def due(results):
             held[name], _ = step(g, 0, *(results[:1] if tied else ()))

time: 290 us -> 289 us (level)
  transfers between devices with their start and end apart: 76 -> 76, of which waited for: 57 -> 58; matrix products, arithmetic and copies ran while one was open for 0% -> 0% of each run, Pallas kernels for 19% -> 19%
where the time goes in v7:
time: 289 us
  waiting for transfers between devices  129 us (45%)
  starting transfers between devices  87.6 us (30%)
  Pallas kernels  69.8 us (24%)
    ppermute x76, waiting for transfers between devices, swap(): return lax.ppermute(v, axis, pairs)  129 us
    ppermute x76, starting transfers between devices, swap(): return lax.ppermute(v, axis, pairs)  87.6 us
    pallas_call x28, Pallas kernels, call(): pl.pallas_call(body, out_shape=tuple((o if hasattr(o, 'memory_space') els...  69.8 us
  transfers between devices with their start and end apart: 76, of which 58 were waited for; matrix products, arithmetic and copies ran while one was open for 0% of the time, Pallas kernels for 19%

profile of v7, /device:TPU:0, one launch (start us, length us, event | category | flops | bytes accessed | tf_op | source)
XLA Modules:
  0.0 288.8 jit_solution(15855362411154714108)
XLA Ops:
  0.7 3.0 %collective-permute-start = (bf16[4,112,1024]{2,1,0:T(8,128)(2,1)}, bf16[4,112,1024]{2,1,0:T(8,128)(2,1)S(1)}, u32[]{:S(2)}, u32[]{:S(2)}) collective-permute-start(bf16[4,112,1024]{2,1,0:T(8,128)(2,1)} %bitcast.46), channel_id=1, source_target_pairs={{0,1},{1,0},{2,3},{3,2},{4,5},{5,4},{6,7},{7,6},{8,9},{9,8},{10,11... | collective-permute-start | bytes 2752520 | tf_op jit(solution)/shard_map/ppermute | solution.py:1022
  3.7 2.9 setup.1
  9.3 2.2 collective-permute-done.2
  13.1 2.1 collective-permute-done.3
  15.2 2.6 collective-permute-start.4
  17.7 2.0 pack.1
  20.4 4.1 %collective-permute-done.5.part_other = f32[4,512]{1,0:T(4,128)S(1)} collective-permute-done((f32[4,512]{1,0:T(4,128)S(1)}, f32[4,512]{1,0:T(4,128)S(1)}, u32[]{:S(2)}, u32[]{:S(2)}) %collective-permute-start.5) | collective-permute-done | bytes 8224 | tf_op jit(solution)/shard_map/ppermute | solution.py:1022
  24.4 1.7 collective-permute-start.9
  26.2 5.4 %stage_two.1 = (bf16[4,224,1024]{2,1,0:T(8,128)(2,1)S(1)}, bf16[224,1024]{1,0:T(8,128)(2,1)S(1)}, f32[4,224,512]{2,1,0:T(8,128)S(1)}, bf16[9,224,512]{2,1,0:T(8,...) custom-call(f32[13]{0:T(128)S(4)} %get-tuple-element.197.fs, ...), custom_call_target="tpu_custom_call" | custom-call | flops 40000000 | bytes 200000 | tf_op jit(solution)/shard_map/stage_two/pallas_call | solution.py:1007
  34.3 2.1 collective-permute-done.7
  40.6 2.1 collective-permute-done.8
  42.6 2.6 collective-permute-start.10
  45.2 3.3 %project.1 = (f32[224,2048]{1,0:T(8,128)S(1)}, f32[4,2048]{1,0:T(4,128)S(1)}, bf16[512,2048]{1,0:T(8,128)(2,1)S(1)}) custom-call(f32[13]{0:T(128)S(4)} %get-tuple-element.197.fs, bf16[224,1024]{1,0:T(8,128)(2,1)S(1)} %get-tuple-element.214.x.strided, f32[224,1]{1,0:T(8,128)S(1)} %get-tuple-element.206.keep, bf16[1024,2048]{1,0:T(8,128)(2,1)} %wp_far.3, ...), custom_call_target="tpu_custom_call" | custom-call | flops 10000000 | bytes 80000 | tf_op jit(solution)/shard_map/project/pallas_call | solution.py:1007
  52.6 2.8 collective-permute-done.12
  57.1 2.7 collective-permute-done.13
  62.4 2.6 collective-permute-done.15
  65.0 3.4 %stage_four.1 = (bf16[224,2048]{1,0:T(8,128)(2,1)S(1)}, f32[224,512]{1,0:T(8,128)S(1)}, f32[4,512]{1,0:T(4,128)S(1)}, f32[8,2048]{1,0:T(8,128)S(1)}, f32[8,2048]...) custom-call(f32[13]{0:T(128)S(4)} %get-tuple-element.197.fs, ...), custom_call_target="tpu_custom_call" | custom-call | flops 10000000 | bytes 100000 | tf_op jit(solution)/shard_map/stage_four/pallas_call | solution.py:1007
  71.9 2.2 collective-permute-done.17
  75.7 2.1 collective-permute-done.18
  82.4 1.9 stage_five.1
  87.0 2.2 collective-permute-done.23
  92.5 2.1 collective-permute-done.24
  97.4 1.7 collective-permute-done.27
  103.7 2.4 collective-permute-done.29
  107.8 2.3 collective-permute-done.30
  113.0 2.1 collective-permute-done.31
  115.0 5.0 %turn.1 = (bf16[224,1024]{1,0:T(8,128)(2,1)}, f32[224,2048]{1,0:T(8,128)S(1)}, f32[4,2048]{1,0:T(4,128)S(1)}, f32[8,512]{1,0:T(8,128)S(1)}, f32[4,2048]{1,0:T(4,...) custom-call(f32[13]{0:T(128)S(4)} %get-tuple-element.197.fs, ...), custom_call_target="tpu_custom_call" | custom-call | flops 10000000 | bytes 100000 | tf_op jit(solution)/shard_map/turn/pallas_call | solution.py:1007
  122.9 2.4 collective-permute-done.34
  127.0 2.3 collective-permute-done.35
  130.8 3.4 %collective-permute-done.36 = f32[4,2048]{1,0:T(4,128)S(1)} collective-permute-done((f32[4,2048]{1,0:T(4,128)S(1)}, f32[4,2048]{1,0:T(4,128)S(1)}, u32[]{:S(2)}, u32[]{:S(2)}) %collective-permute-start.36) | collective-permute-done | bytes 32800 | tf_op jit(solution)/shard_map/ppermute | solution.py:1022
  134.2 2.2 back_six.1
  139.2 2.4 collective-permute-done.38
  143.2 2.3 collective-permute-done.39
  146.9 3.4 %collective-permute-done.40 = f32[12,512]{1,0:T(8,128)S(1)} collective-permute-done((f32[12,512]{1,0:T(8,128)S(1)}, f32[12,512]{1,0:T(8,128)S(1)}, u32[]{:S(2)}, u32[]{:S(2)}) %collective-permute-start.40) | collective-permute-done | bytes 24608 | tf_op jit(solution)/shard_map/ppermute | solution.py:1022
  150.3 3.5 %back_five.1 = (bf16[224,512]{1,0:T(8,128)(2,1)S(1)}, f32[224,512]{1,0:T(8,128)S(1)}, f32[4,512]{1,0:T(4,128)S(1)}, f32[256]{0:T(256)}, f32[256]{0:T(256)}, /*index=5*/f32[1024]{0:T(1024)}, f32[128]{0:T(128)}, f32[5]{0:T(128)}) custom-call(f32[13]{0:T(128)S(4)} %get-tuple-element.197.fs, s32[18]{0:T(128)S(4)} %get-tuple-element.316.isc, ...), custom_call_target="tpu_custom_call" | custom-call | flops 20000000 | bytes 100000 | tf_op jit(solution)/shard_map/back_five/pallas_call | solution.py:1007
  153.8 2.4 grads_a.1
  159.1 2.2 collective-permute-done.42
  164.7 2.1 collective-permute-done.44
  168.1 2.4 fetch_two.1.ws
  171.3 5.4 %back_four.1 = (bf16[224,512]{1,0:T(8,128)(2,1)S(1)}, f32[224,2048]{1,0:T(8,128)S(1)}, f32[8,2048]{1,0:T(8,128)S(1)}, f32[512]{0:T(512)}, f32[512]{0:T(512)}, /*...) custom-call(f32[13]{0:T(128)S(4)} %get-tuple-element.197.fs, ...), custom_call_target="tpu_custom_call" | custom-call | flops 10000000 | bytes 100000 | tf_op jit(solution)/shard_map/back_four/pallas_call | solution.py:1007
  177.6 4.7 %collective-permute-done.46 = bf16[4,416,256]{2,1,0:T(8,128)(2,1)S(1)} collective-permute-done((bf16[4,416,256]{2,1,0:T(8,128)(2,1)S(1)}, bf16[4,416,256]{2,1,0:T(8,128)(2,1)S(1)}, u32[]{:S(2)}, u32[]{:S(2)}) %collective-permute-start.46) | collective-permute-done | bytes 852000 | tf_op jit(solution)/shard_map/ppermute | solution.py:1022
  185.3 2.9 collective-permute-done.48
  189.9 2.7 collective-permute-done.49
  194.1 3.8 %collective-permute-done.51 = f32[8,2048]{1,0:T(8,128)S(1)} collective-permute-done((f32[8,2048]{1,0:T(8,128)S(1)}, f32[8,2048]{1,0:T(8,128)S(1)}, u32[]{:S(2)}, u32[]{:S(2)}) %collective-permute-start.51) | collective-permute-done | bytes 65568 | tf_op jit(solution)/shard_map/ppermute | solution.py:1022
  201.3 3.5 %back_three.1 = (bf16[224,2048]{1,0:T(8,128)(2,1)S(1)}, bf16[224,2048]{1,0:T(8,128)(2,1)S(1)}, f32[224,512]{1,0:T(8,128)S(1)}, f32[12,512]{1,0:T(8,128)S(1)}, f3...) custom-call(f32[13]{0:T(128)S(4)} %get-tuple-element.197.fs, f32[1,8,2048]{2,1,0:T(8,128)S(1)} %bitcast.39, ...), custom_call_target="tpu_custom_call" | custom-call | flops 10000000 | bytes 100000 | tf_op jit(solution)/shard_map/back_three/pallas_call | solution.py:1007
  206.0 2.3 collective-permute-done.52
  211.9 2.4 collective-permute-done.55
  217.7 2.3 collective-permute-done.57
  220.1 1.8 collective-permute-start.58
  221.9 5.2 %placed.1 = f32[448,1024]{1,0:T(8,128)S(1)} custom-call(s32[18]{0:T(128)S(4)} %get-tuple-element.316.isc, bf16[224,2048]{1,0:T(8,128)(2,1)S(1)} %get-tuple-element.300.dproj, bf16[1024,2048]{1,0:T(8,128)(2,1)} %wp_far.3), custom_call_target="tpu_custom_call" | custom-call | flops 10000000 | bytes 100000 | tf_op jit(solution)/shard_map/placed/pallas_call | solution.py:1007
  227.1 3.0 %back_two.1 = (bf16[224,512]{1,0:T(8,128)(2,1)S(1)}, f32[4,224,512]{2,1,0:T(8,128)S(1)}, f32[4,512]{1,0:T(4,128)S(1)}, f32[512]{0:T(512)}, f32[512]{0:T(512)}, /*index=5*/f32[2048]{0:T(1024)}, f32[128]{0:T(128)}) custom-call(f32[13]{0:T(128)S(4)} %get-tuple-element.197.fs, f32[1,12,512]{2,1,0:T(8,128)S(1)} %add_bitcast_fusion.1.parts, ...), custom_call_target="tpu_custom_call" | custom-call | flops 20000000 | bytes 100000 | tf_op jit(solution)/shard_map/back_two/pallas_call | solution.py:1007
  230.1 1.8 grads_d.1
  238.2 2.1 collective-permute-done.61
  240.7 3.0 %collective-permute-done.72 = bf16[2,256,256]{2,1,0:T(8,128)(2,1)S(1)} collective-permute-done((bf16[2,256,256]{2,1,0:T(8,128)(2,1)S(1)}, bf16[2,256,256]{2,1,0:T(8,128)(2,1)S(1)}, u32[]{:S(2)}, u32[]{:S(2)}) %collective-permute-start.72) | collective-permute-done | bytes 262176 | tf_op jit(solution)/shard_map/ppermute | solution.py:1022
  243.9 2.2 collective-permute-start.63
  252.0 2.1 image.1
  255.5 6.8 %collective-permute-done.65 = bf16[4,288,256]{2,1,0:T(8,128)(2,1)S(1)} collective-permute-done((bf16[4,288,256]{2,1,0:T(8,128)(2,1)S(1)}, bf16[4,288,256]{2,1,0:T(8,128)(2,1)S(1)}, u32[]{:S(2)}, u32[]{:S(2)}) %collective-permute-start.65) | collective-permute-done | bytes 589856 | tf_op jit(solution)/shard_map/ppermute | solution.py:1022
  263.8 5.0 %collective-permute-done.74 = bf16[2,384,256]{2,1,0:T(8,128)(2,1)S(1)} collective-permute-done((bf16[2,384,256]{2,1,0:T(8,128)(2,1)S(1)}, bf16[2,384,256]{2,1,0:T(8,128)(2,1)S(1)}, u32[]{:S(2)}, u32[]{:S(2)}) %collective-permute-start.74) | collective-permute-done | bytes 393248 | tf_op jit(solution)/shard_map/ppermute | solution.py:1022
  268.9 2.1 collective-permute-start.75
  271.0 2.5 collective-permute-start.70
  273.6 3.4 %collective-permute-done.66 = bf16[2,288,256]{2,1,0:T(8,128)(2,1)S(1)} collective-permute-done((bf16[2,288,256]{2,1,0:T(8,128)(2,1)S(1)}, bf16[2,288,256]{2,1,0:T(8,128)(2,1)S(1)}, u32[]{:S(2)}, u32[]{:S(2)}) %collective-permute-start.66) | collective-permute-done | bytes 294944 | tf_op jit(solution)/shard_map/ppermute | solution.py:1022
  278.0 2.5 collective-permute-done.70
  281.1 3.1 %collective-permute-done.75.d = bf16[1,384,256]{2,1,0:T(8,128)(2,1)S(1)} collective-permute-done((bf16[1,384,256]{2,1,0:T(8,128)(2,1)S(1)}, bf16[1,384,256]{2,1,0:T(8,128)(2,1)S(1)}, u32[]{:S(2)}, u32[]{:S(2)}) %collective-permute-start.75) | collective-permute-done | bytes 196640 | tf_op jit(solution)/shard_map/ppermute | solution.py:1022
  285.2 2.8 collective-permute-done.71.d
  (183 shorter events, 105.6 us)
Async XLA Ops:
  0.7 23.8 %collective-permute-start = (bf16[4,112,1024]{2,1,0:T(8,128)(2,1)}, bf16[4,112,1024]{2,1,0:T(8,128)(2,1)S(1)}, u32[]{:S(2)}, u32[]{:S(2)}) collective-permute-start(bf16[4,112,1024]{2,1,0:T(8,128)(2,1)} %bitcast.46), channel_id=1, source_target_pairs={{0,1},{1,0},{2,3},{3,2},{4,5},{5,4},{6,7},{7,6},{8,9},{9,8},{10,11... | collective-permute-start | bytes 2752520 | tf_op jit(solution)/shard_map/ppermute | solution.py:1022
  7.8 3.7 %collective-permute-start.2 = (f32[4,512]{1,0:T(4,128)S(1)}, f32[4,512]{1,0:T(4,128)S(1)}, u32[]{:S(2)}, u32[]{:S(2)}) collective-permute-start(f32[4,512]{1,0:T(4,128)S(1)} %add.234), channel_id=1, source_target_pairs={{0,4},{2,6},{4,0},{6,2},{8,12},{10,14},{12,8},{14,10},{16,20},{18,... | collective-permute-start | bytes 24584 | tf_op jit(solution)/shard_map/ppermute | solution.py:1022
  11.5 3.7 %collective-permute-start.3 = (f32[4,512]{1,0:T(4,128)S(1)}, f32[4,512]{1,0:T(4,128)S(1)}, u32[]{:S(2)}, u32[]{:S(2)}) collective-permute-start(f32[4,512]{1,0:T(4,128)S(1)} %add.235), channel_id=1, source_target_pairs={{0,8},{2,10},{4,12},{6,14},{8,0},{10,2},{12,4},{14,6},{16,24},{18,... | collective-permute-start | bytes 24584 | tf_op jit(solution)/shard_map/ppermute | solution.py:1022
  15.2 4.6 %collective-permute-start.4 = (f32[4,512]{1,0:T(4,128)S(1)}, f32[4,512]{1,0:T(4,128)S(1)}, u32[]{:S(2)}, u32[]{:S(2)}) collective-permute-start(f32[4,512]{1,0:T(4,128)S(1)} %add.236), channel_id=1, source_target_pairs={{0,16},{2,18},{4,20},{6,22},{8,24},{10,26},{12,28},{14,30},{16,0},... | collective-permute-start | bytes 24584 | tf_op jit(solution)/shard_map/ppermute | solution.py:1022
  19.8 4.6 %collective-permute-start.5 = (f32[4,512]{1,0:T(4,128)S(1)}, f32[4,512]{1,0:T(4,128)S(1)}, u32[]{:S(2)}, u32[]{:S(2)}) collective-permute-start(f32[4,512]{1,0:T(4,128)S(1)} %add.237.part), channel_id=1, source_target_pairs={{0,1},{1,0},{2,3},{3,2},{4,5},{5,4},{6,7},{7,6},{8,9},{9,8},{10,11... | collective-permute-start | bytes 24584 | tf_op jit(solution)/shard_map/ppermute | solution.py:1022
  24.4 13.1 %collective-permute-start.9 = (bf16[512,512]{1,0:T(8,128)(2,1)S(1)}, bf16[512,512]{1,0:T(8,128)(2,1)S(1)}, u32[]{:S(2)}, u32[]{:S(2)}) collective-permute-start(bf16[512,512]{1,0:T(8,128)(2,1)S(1)} %get-tuple-element.211), channel_id=1, source_target_pairs={{0,1},{1,0},{2,3},{3,2},{4,5},{5,4},{6,7},{7,6},{8,9},{9,8},{10,11... | collective-permute-start | bytes 1572872 | tf_op jit(solution)/shard_map/ppermute | solution.py:1022
  32.8 3.7 %collective-permute-start.7 = (f32[4,512]{1,0:T(4,128)S(1)}, f32[4,512]{1,0:T(4,128)S(1)}, u32[]{:S(2)}, u32[]{:S(2)}) collective-permute-start(f32[4,512]{1,0:T(4,128)S(1)} %add.238), channel_id=1, source_target_pairs={{0,4},{2,6},{4,0},{6,2},{8,12},{10,14},{12,8},{14,10},{16,20},{18,... | collective-permute-start | bytes 24584 | tf_op jit(solution)/shard_map/ppermute | solution.py:1022
  37.6 32.1 %collective-permute-start.19 = (bf16[2304,256]{1,0:T(8,128)(2,1)S(1)}, bf16[2304,256]{1,0:T(8,128)(2,1)S(1)}, u32[]{:S(2)}, u32[]{:S(2)}) collective-permute-start(bf16[2304,256]{1,0:T(8,128)(2,1)S(1)} %get-tuple-element.227), channel_id=1, source_target_pairs={{0,1},{1,0},{2,3},{3,2},{4,5},{5,4},{6,7},{7,6},{8,9},{9,8},{10,11... | collective-permute-start | bytes 3538952 | tf_op jit(solution)/shard_map/ppermute | solution.py:1022
  39.0 20.8 %collective-permute-start.14 = (bf16[512,512]{1,0:T(8,128)(2,1)S(1)}, bf16[512,512]{1,0:T(8,128)(2,1)S(1)}, u32[]{:S(2)}, u32[]{:S(2)}) collective-permute-start(bf16[512,512]{1,0:T(8,128)(2,1)S(1)} %collective-permute-done.9.r1), channel_id=1, source_target_pairs={{0,2},{2,0},{4,6},{6,4},{8,10},{10,8},{12,14},{14,12},{16,18},{18,... | collective-permute-start | bytes 1572872 | tf_op jit(solution)/shard_map/ppermute | solution.py:1022
  39.0 3.7 %collective-permute-start.8 = (f32[4,512]{1,0:T(4,128)S(1)}, f32[4,512]{1,0:T(4,128)S(1)}, u32[]{:S(2)}, u32[]{:S(2)}) collective-permute-start(f32[4,512]{1,0:T(4,128)S(1)} %add.239), channel_id=1, source_target_pairs={{0,8},{2,10},{4,12},{6,14},{8,0},{10,2},{12,4},{14,6},{16,24},{18,... | collective-permute-start | bytes 24584 | tf_op jit(solution)/shard_map/ppermute | solution.py:1022
  42.6 5.9 %collective-permute-start.10 = (f32[4,512]{1,0:T(4,128)S(1)}, f32[4,512]{1,0:T(4,128)S(1)}, u32[]{:S(2)}, u32[]{:S(2)}) collective-permute-start(f32[4,512]{1,0:T(4,128)S(1)} %add.240), channel_id=1, source_target_pairs={{0,16},{2,18},{4,20},{6,22},{8,24},{10,26},{12,28},{14,30},{16,0},... | collective-permute-start | bytes 24584 | tf_op jit(solution)/shard_map/ppermute | solution.py:1022
  51.1 4.3 %collective-permute-start.12 = (f32[8,2048]{1,0:T(8,128)S(1)}, f32[8,2048]{1,0:T(8,128)S(1)}, u32[]{:S(2)}, u32[]{:S(2)}) collective-permute-start(f32[8,2048]{1,0:T(8,128)S(1)} %add.242), channel_id=1, source_target_pairs={{0,4},{2,6},{4,0},{6,2},{8,12},{10,14},{12,8},{14,10},{16,20},{18,... | collective-permute-start | bytes 196616 | tf_op jit(solution)/shard_map/ppermute | solution.py:1022
  55.4 4.3 %collective-permute-start.13 = (f32[8,2048]{1,0:T(8,128)S(1)}, f32[8,2048]{1,0:T(8,128)S(1)}, u32[]{:S(2)}, u32[]{:S(2)}) collective-permute-start(f32[8,2048]{1,0:T(8,128)S(1)} %add.243), channel_id=1, source_target_pairs={{0,8},{2,10},{4,12},{6,14},{8,0},{10,2},{12,4},{14,6},{16,24},{18,... | collective-permute-start | bytes 196616 | tf_op jit(solution)/shard_map/ppermute | solution.py:1022
  59.8 5.2 %collective-permute-start.15 = (f32[8,2048]{1,0:T(8,128)S(1)}, f32[8,2048]{1,0:T(8,128)S(1)}, u32[]{:S(2)}, u32[]{:S(2)}) collective-permute-start(f32[8,2048]{1,0:T(8,128)S(1)} %add.244), channel_id=1, source_target_pairs={{0,16},{2,18},{4,20},{6,22},{8,24},{10,26},{12,28},{14,30},{16,0},... | collective-permute-start | bytes 196616 | tf_op jit(solution)/shard_map/ppermute | solution.py:1022
  69.7 8.1 %collective-permute-start.20 = (bf16[2304,256]{1,0:T(8,128)(2,1)S(1)}, bf16[2304,256]{1,0:T(8,128)(2,1)S(1)}, u32[]{:S(2)}, u32[]{:S(2)}) collective-permute-start(bf16[2304,256]{1,0:T(8,128)(2,1)S(1)} %collective-permute-done.19.r1), channel_id=1, source_target_pairs={{0,2},{2,0},{4,6},{6,4},{8,10},{10,8},{12,14},{14,12},{16,18},{18,... | collective-permute-start | bytes 3538952 | tf_op jit(solution)/shard_map/ppermute | solution.py:1022
  69.9 20.0 %collective-permute-start.25 = (bf16[1552,256]{1,0:T(8,128)(2,1)S(1)}, bf16[1552,256]{1,0:T(8,128)(2,1)S(1)}, u32[]{:S(2)}, u32[]{:S(2)}) collective-permute-start(bf16[1552,256]{1,0:T(8,128)(2,1)S(1)} %get-tuple-element.234), channel_id=1, source_target_pairs={{0,1},{1,0},{2,3},{3,2},{4,5},{5,4},{6,7},{7,6},{8,9},{9,8},{10,11... | collective-permute-start | bytes 2383880 | tf_op jit(solution)/shard_map/ppermute | solution.py:1022
  70.4 3.7 %collective-permute-start.17 = (f32[4,512]{1,0:T(4,128)S(1)}, f32[4,512]{1,0:T(4,128)S(1)}, u32[]{:S(2)}, u32[]{:S(2)}) collective-permute-start(f32[4,512]{1,0:T(4,128)S(1)} %add.246), channel_id=1, source_target_pairs={{0,4},{2,6},{4,0},{6,2},{8,12},{10,14},{12,8},{14,10},{16,20},{18,... | collective-permute-start | bytes 24584 | tf_op jit(solution)/shard_map/ppermute | solution.py:1022
  74.1 3.7 %collective-permute-start.18 = (f32[4,512]{1,0:T(4,128)S(1)}, f32[4,512]{1,0:T(4,128)S(1)}, u32[]{:S(2)}, u32[]{:S(2)}) collective-permute-start(f32[4,512]{1,0:T(4,128)S(1)} %add.247), channel_id=1, source_target_pairs={{0,8},{2,10},{4,12},{6,14},{8,0},{10,2},{12,4},{14,6},{16,24},{18,... | collective-permute-start | bytes 24584 | tf_op jit(solution)/shard_map/ppermute | solution.py:1022
  77.7 4.6 %collective-permute-start.21 = (f32[4,512]{1,0:T(4,128)S(1)}, f32[4,512]{1,0:T(4,128)S(1)}, u32[]{:S(2)}, u32[]{:S(2)}) collective-permute-start(f32[4,512]{1,0:T(4,128)S(1)} %add.248), channel_id=1, source_target_pairs={{0,16},{2,18},{4,20},{6,22},{8,24},{10,26},{12,28},{14,30},{16,0},... | collective-permute-start | bytes 24584 | tf_op jit(solution)/shard_map/ppermute | solution.py:1022
  85.6 3.7 %collective-permute-start.23 = (f32[4,512]{1,0:T(4,128)S(1)}, f32[4,512]{1,0:T(4,128)S(1)}, u32[]{:S(2)}, u32[]{:S(2)}) collective-permute-start(f32[4,512]{1,0:T(4,128)S(1)} %add.250), channel_id=1, source_target_pairs={{0,4},{2,6},{4,0},{6,2},{8,12},{10,14},{12,8},{14,10},{16,20},{18,... | collective-permute-start | bytes 24584 | tf_op jit(solution)/shard_map/ppermute | solution.py:1022
  89.9 4.7 %collective-permute-start.26 = (bf16[1552,256]{1,0:T(8,128)(2,1)S(1)}, bf16[1552,256]{1,0:T(8,128)(2,1)S(1)}, u32[]{:S(2)}, u32[]{:S(2)}) collective-permute-start(bf16[1552,256]{1,0:T(8,128)(2,1)S(1)} %collective-permute-done.25.r1), channel_id=1, source_target_pairs={{0,2},{2,0},{4,6},{6,4},{8,10},{10,8},{12,14},{14,12},{16,18},{18,... | collective-permute-start | bytes 2383880 | tf_op jit(solution)/shard_map/ppermute | solution.py:1022
  89.9 21.7 %collective-permute-start.32 = (bf16[224,1024]{1,0:T(8,128)(2,1)S(1)}, bf16[224,1024]{1,0:T(8,128)(2,1)S(1)}, u32[]{:S(2)}, u32[]{:S(2)}) collective-permute-start(bf16[224,1024]{1,0:T(8,128)(2,1)S(1)} %bitcast.49), channel_id=1, source_target_pairs={{0,1},{1,0},{2,3},{3,2},{4,5},{5,4},{6,7},{7,6},{8,9},{9,8},{10,11... | collective-permute-start | bytes 1376264 | tf_op jit(solution)/shard_map/ppermute | solution.py:1022
  90.9 3.7 %collective-permute-start.24 = (f32[4,512]{1,0:T(4,128)S(1)}, f32[4,512]{1,0:T(4,128)S(1)}, u32[]{:S(2)}, u32[]{:S(2)}) collective-permute-start(f32[4,512]{1,0:T(4,128)S(1)} %add.251), channel_id=1, source_target_pairs={{0,8},{2,10},{4,12},{6,14},{8,0},{10,2},{12,4},{14,6},{16,24},{18,... | collective-permute-start | bytes 24584 | tf_op jit(solution)/shard_map/ppermute | solution.py:1022
  94.5 4.6 %collective-permute-start.27 = (f32[4,512]{1,0:T(4,128)S(1)}, f32[4,512]{1,0:T(4,128)S(1)}, u32[]{:S(2)}, u32[]{:S(2)}) collective-permute-start(f32[4,512]{1,0:T(4,128)S(1)} %add.252), channel_id=1, source_target_pairs={{0,16},{2,18},{4,20},{6,22},{8,24},{10,26},{12,28},{14,30},{16,0},... | collective-permute-start | bytes 24584 | tf_op jit(solution)/shard_map/ppermute | solution.py:1022
  102.2 4.0 %collective-permute-start.29 = (f32[4,2048]{1,0:T(4,128)S(1)}, f32[4,2048]{1,0:T(4,128)S(1)}, u32[]{:S(2)}, u32[]{:S(2)}) collective-permute-start(f32[4,2048]{1,0:T(4,128)S(1)} %add.254), channel_id=1, source_target_pairs={{0,4},{2,6},{4,0},{6,2},{8,12},{10,14},{12,8},{14,10},{16,20},{18,... | collective-permute-start | bytes 98312 | tf_op jit(solution)/shard_map/ppermute | solution.py:1022
  106.2 4.0 %collective-permute-start.30 = (f32[4,2048]{1,0:T(4,128)S(1)}, f32[4,2048]{1,0:T(4,128)S(1)}, u32[]{:S(2)}, u32[]{:S(2)}) collective-permute-start(f32[4,2048]{1,0:T(4,128)S(1)} %add.255), channel_id=1, source_target_pairs={{0,8},{2,10},{4,12},{6,14},{8,0},{10,2},{12,4},{14,6},{16,24},{18,... | collective-permute-start | bytes 98312 | tf_op jit(solution)/shard_map/ppermute | solution.py:1022
  110.2 4.9 %collective-permute-start.31 = (f32[4,2048]{1,0:T(4,128)S(1)}, f32[4,2048]{1,0:T(4,128)S(1)}, u32[]{:S(2)}, u32[]{:S(2)}) collective-permute-start(f32[4,2048]{1,0:T(4,128)S(1)} %add.256), channel_id=1, source_target_pairs={{0,16},{2,18},{4,20},{6,22},{8,24},{10,26},{12,28},{14,30},{16,0},... | collective-permute-start | bytes 98312 | tf_op jit(solution)/shard_map/ppermute | solution.py:1022
  121.3 4.0 %collective-permute-start.34 = (f32[4,2048]{1,0:T(4,128)S(1)}, f32[4,2048]{1,0:T(4,128)S(1)}, u32[]{:S(2)}, u32[]{:S(2)}) collective-permute-start(f32[4,2048]{1,0:T(4,128)S(1)} %add.258), channel_id=1, source_target_pairs={{0,4},{2,6},{4,0},{6,2},{8,12},{10,14},{12,8},{14,10},{16,20},{18,... | collective-permute-start | bytes 98312 | tf_op jit(solution)/shard_map/ppermute | solution.py:1022
  125.3 4.0 %collective-permute-start.35 = (f32[4,2048]{1,0:T(4,128)S(1)}, f32[4,2048]{1,0:T(4,128)S(1)}, u32[]{:S(2)}, u32[]{:S(2)}) collective-permute-start(f32[4,2048]{1,0:T(4,128)S(1)} %add.259), channel_id=1, source_target_pairs={{0,8},{2,10},{4,12},{6,14},{8,0},{10,2},{12,4},{14,6},{16,24},{18,... | collective-permute-start | bytes 98312 | tf_op jit(solution)/shard_map/ppermute | solution.py:1022
  129.3 4.9 %collective-permute-start.36 = (f32[4,2048]{1,0:T(4,128)S(1)}, f32[4,2048]{1,0:T(4,128)S(1)}, u32[]{:S(2)}, u32[]{:S(2)}) collective-permute-start(f32[4,2048]{1,0:T(4,128)S(1)} %add.260), channel_id=1, source_target_pairs={{0,16},{2,18},{4,20},{6,22},{8,24},{10,26},{12,28},{14,30},{16,0},... | collective-permute-start | bytes 98312 | tf_op jit(solution)/shard_map/ppermute | solution.py:1022
  137.7 3.9 %collective-permute-start.38 = (f32[12,512]{1,0:T(8,128)S(1)}, f32[12,512]{1,0:T(8,128)S(1)}, u32[]{:S(2)}, u32[]{:S(2)}) collective-permute-start(f32[12,512]{1,0:T(8,128)S(1)} %add.262), channel_id=1, source_target_pairs={{0,4},{2,6},{4,0},{6,2},{8,12},{10,14},{12,8},{14,10},{16,20},{18,... | collective-permute-start | bytes 73736 | tf_op jit(solution)/shard_map/ppermute | solution.py:1022
  141.6 3.9 %collective-permute-start.39 = (f32[12,512]{1,0:T(8,128)S(1)}, f32[12,512]{1,0:T(8,128)S(1)}, u32[]{:S(2)}, u32[]{:S(2)}) collective-permute-start(f32[12,512]{1,0:T(8,128)S(1)} %add.263), channel_id=1, source_target_pairs={{0,8},{2,10},{4,12},{6,14},{8,0},{10,2},{12,4},{14,6},{16,24},{18,... | collective-permute-start | bytes 73736 | tf_op jit(solution)/shard_map/ppermute | solution.py:1022
  145.5 4.8 %collective-permute-start.40 = (f32[12,512]{1,0:T(8,128)S(1)}, f32[12,512]{1,0:T(8,128)S(1)}, u32[]{:S(2)}, u32[]{:S(2)}) collective-permute-start(f32[12,512]{1,0:T(8,128)S(1)} %add.264), channel_id=1, source_target_pairs={{0,16},{2,18},{4,20},{6,22},{8,24},{10,26},{12,28},{14,30},{16,0},... | collective-permute-start | bytes 73736 | tf_op jit(solution)/shard_map/ppermute | solution.py:1022
  157.5 3.8 %collective-permute-start.43 = (bf16[8,416,256]{2,1,0:T(8,128)(2,1)S(1)}, bf16[8,416,256]{2,1,0:T(8,128)(2,1)S(1)}, u32[]{:S(2)}, u32[]{:S(2)}) collective-permute-start(bf16[8,416,256]{2,1,0:T(8,128)(2,1)S(1)} %get-tuple-element.271), channel_id=1, source_target_pairs={{0,2},{2,0},{4,6},{6,4},{8,10},{10,8},{12,14},{14,12},{16,18},{18,... | collective-permute-start | bytes 5111816 | tf_op jit(solution)/shard_map/ppermute | solution.py:1022
  157.6 3.7 %collective-permute-start.42 = (f32[4,512]{1,0:T(4,128)S(1)}, f32[4,512]{1,0:T(4,128)S(1)}, u32[]{:S(2)}, u32[]{:S(2)}) collective-permute-start(f32[4,512]{1,0:T(4,128)S(1)} %add.266), channel_id=1, source_target_pairs={{0,4},{2,6},{4,0},{6,2},{8,12},{10,14},{12,8},{14,10},{16,20},{18,... | collective-permute-start | bytes 24584 | tf_op jit(solution)/shard_map/ppermute | solution.py:1022
  161.5 20.9 %collective-permute-start.46 = (bf16[4,416,256]{2,1,0:T(8,128)(2,1)S(1)}, bf16[4,416,256]{2,1,0:T(8,128)(2,1)S(1)}, u32[]{:S(2)}, u32[]{:S(2)}) collective-permute-start(bf16[4,416,256]{2,1,0:T(8,128)(2,1)S(1)} %get-tuple-element.288), channel_id=1, source_target_pairs={{0,4},{2,6},{4,0},{6,2},{8,12},{10,14},{12,8},{14,10},{16,20},{18,... | collective-permute-start | bytes 2555912 | tf_op jit(solution)/shard_map/ppermute | solution.py:1022
  163.1 3.7 %collective-permute-start.44 = (f32[4,512]{1,0:T(4,128)S(1)}, f32[4,512]{1,0:T(4,128)S(1)}, u32[]{:S(2)}, u32[]{:S(2)}) collective-permute-start(f32[4,512]{1,0:T(4,128)S(1)} %add.267), channel_id=1, source_target_pairs={{0,8},{2,10},{4,12},{6,14},{8,0},{10,2},{12,4},{14,6},{16,24},{18,... | collective-permute-start | bytes 24584 | tf_op jit(solution)/shard_map/ppermute | solution.py:1022
  166.7 4.5 %collective-permute-start.45 = (f32[4,512]{1,0:T(4,128)S(1)}, f32[4,512]{1,0:T(4,128)S(1)}, u32[]{:S(2)}, u32[]{:S(2)}) collective-permute-start(f32[4,512]{1,0:T(4,128)S(1)} %add.270), channel_id=1, source_target_pairs={{0,16},{2,18},{4,20},{6,22},{8,24},{10,26},{12,28},{14,30},{16,0},... | collective-permute-start | bytes 24584 | tf_op jit(solution)/shard_map/ppermute | solution.py:1022
  183.6 8.9 %collective-permute-start.50 = (bf16[8,256,256]{2,1,0:T(8,128)(2,1)S(1)}, bf16[8,256,256]{2,1,0:T(8,128)(2,1)S(1)}, u32[]{:S(2)}, u32[]{:S(2)}) collective-permute-start(bf16[8,256,256]{2,1,0:T(8,128)(2,1)S(1)} %get-tuple-element.291), channel_id=1, source_target_pairs={{0,2},{2,0},{4,6},{6,4},{8,10},{10,8},{12,14},{14,12},{16,18},{18,... | collective-permute-start | bytes 3145736 | tf_op jit(solution)/shard_map/ppermute | solution.py:1022
  183.8 4.4 %collective-permute-start.48 = (f32[8,2048]{1,0:T(8,128)S(1)}, f32[8,2048]{1,0:T(8,128)S(1)}, u32[]{:S(2)}, u32[]{:S(2)}) collective-permute-start(f32[8,2048]{1,0:T(8,128)S(1)} %add.272), channel_id=1, source_target_pairs={{0,4},{2,6},{4,0},{6,2},{8,12},{10,14},{12,8},{14,10},{16,20},{18,... | collective-permute-start | bytes 196616 | tf_op jit(solution)/shard_map/ppermute | solution.py:1022
  188.2 4.3 %collective-permute-start.49 = (f32[8,2048]{1,0:T(8,128)S(1)}, f32[8,2048]{1,0:T(8,128)S(1)}, u32[]{:S(2)}, u32[]{:S(2)}) collective-permute-start(f32[8,2048]{1,0:T(8,128)S(1)} %add.273), channel_id=1, source_target_pairs={{0,8},{2,10},{4,12},{6,14},{8,0},{10,2},{12,4},{14,6},{16,24},{18,... | collective-permute-start | bytes 196616 | tf_op jit(solution)/shard_map/ppermute | solution.py:1022
  192.7 5.2 %collective-permute-start.51 = (f32[8,2048]{1,0:T(8,128)S(1)}, f32[8,2048]{1,0:T(8,128)S(1)}, u32[]{:S(2)}, u32[]{:S(2)}) collective-permute-start(f32[8,2048]{1,0:T(8,128)S(1)} %add.274), channel_id=1, source_target_pairs={{0,16},{2,18},{4,20},{6,22},{8,24},{10,26},{12,28},{14,30},{16,0},... | collective-permute-start | bytes 196616 | tf_op jit(solution)/shard_map/ppermute | solution.py:1022
  197.9 11.1 %collective-permute-start.53 = (bf16[4,256,256]{2,1,0:T(8,128)(2,1)S(1)}, bf16[4,256,256]{2,1,0:T(8,128)(2,1)S(1)}, u32[]{:S(2)}, u32[]{:S(2)}) collective-permute-start(bf16[4,256,256]{2,1,0:T(8,128)(2,1)S(1)} %get-tuple-element.304), channel_id=1, source_target_pairs={{0,4},{2,6},{4,0},{6,2},{8,12},{10,14},{12,8},{14,10},{16,20},{18,... | collective-permute-start | bytes 1572872 | tf_op jit(solution)/shard_map/ppermute | solution.py:1022
  199.6 8.8 %collective-permute-start.52 = (bf16[2,416,256]{2,1,0:T(8,128)(2,1)S(1)}, bf16[2,416,256]{2,1,0:T(8,128)(2,1)S(1)}, u32[]{:S(2)}, u32[]{:S(2)}) collective-permute-start(bf16[2,416,256]{2,1,0:T(8,128)(2,1)S(1)} %get-tuple-element.303), channel_id=1, source_target_pairs={{0,8},{2,10},{4,12},{6,14},{8,0},{10,2},{12,4},{14,6},{16,24},{18,... | collective-permute-start | bytes 1277960 | tf_op jit(solution)/shard_map/ppermute | solution.py:1022
  210.3 4.1 %collective-permute-start.56 = (bf16[8,384,256]{2,1,0:T(8,128)(2,1)S(1)}, bf16[8,384,256]{2,1,0:T(8,128)(2,1)S(1)}, u32[]{:S(2)}, u32[]{:S(2)}) collective-permute-start(bf16[8,384,256]{2,1,0:T(8,128)(2,1)S(1)} %get-tuple-element.306), channel_id=1, source_target_pairs={{0,2},{2,0},{4,6},{6,4},{8,10},{10,8},{12,14},{14,12},{16,18},{18,... | collective-permute-start | bytes 4718600 | tf_op jit(solution)/shard_map/ppermute | solution.py:1022
  210.4 3.9 %collective-permute-start.55 = (f32[12,512]{1,0:T(8,128)S(1)}, f32[12,512]{1,0:T(8,128)S(1)}, u32[]{:S(2)}, u32[]{:S(2)}) collective-permute-start(f32[12,512]{1,0:T(8,128)S(1)} %add.279), channel_id=1, source_target_pairs={{0,4},{2,6},{4,0},{6,2},{8,12},{10,14},{12,8},{14,10},{16,20},{18,... | collective-permute-start | bytes 73736 | tf_op jit(solution)/shard_map/ppermute | solution.py:1022
  214.6 19.0 %collective-permute-start.59 = (bf16[4,384,256]{2,1,0:T(8,128)(2,1)S(1)}, bf16[4,384,256]{2,1,0:T(8,128)(2,1)S(1)}, u32[]{:S(2)}, u32[]{:S(2)}) collective-permute-start(bf16[4,384,256]{2,1,0:T(8,128)(2,1)S(1)} %get-tuple-element.315), channel_id=1, source_target_pairs={{0,4},{2,6},{4,0},{6,2},{8,12},{10,14},{12,8},{14,10},{16,20},{18,... | collective-permute-start | bytes 2359304 | tf_op jit(solution)/shard_map/ppermute | solution.py:1022
  216.1 3.9 %collective-permute-start.57 = (f32[12,512]{1,0:T(8,128)S(1)}, f32[12,512]{1,0:T(8,128)S(1)}, u32[]{:S(2)}, u32[]{:S(2)}) collective-permute-start(f32[12,512]{1,0:T(8,128)S(1)} %add.280), channel_id=1, source_target_pairs={{0,8},{2,10},{4,12},{6,14},{8,0},{10,2},{12,4},{14,6},{16,24},{18,... | collective-permute-start | bytes 73736 | tf_op jit(solution)/shard_map/ppermute | solution.py:1022
  220.1 7.0 %collective-permute-start.58 = (f32[12,512]{1,0:T(8,128)S(1)}, f32[12,512]{1,0:T(8,128)S(1)}, u32[]{:S(2)}, u32[]{:S(2)}) collective-permute-start(f32[12,512]{1,0:T(8,128)S(1)} %add.283), channel_id=1, source_target_pairs={{0,16},{2,18},{4,20},{6,22},{8,24},{10,26},{12,28},{14,30},{16,0},... | collective-permute-start | bytes 73736 | tf_op jit(solution)/shard_map/ppermute | solution.py:1022
  234.7 11.4 %collective-permute-start.64 = (bf16[8,288,256]{2,1,0:T(8,128)(2,1)S(1)}, bf16[8,288,256]{2,1,0:T(8,128)(2,1)S(1)}, u32[]{:S(2)}, u32[]{:S(2)}) collective-permute-start(bf16[8,288,256]{2,1,0:T(8,128)(2,1)S(1)} %get-tuple-element.318), channel_id=1, source_target_pairs={{0,2},{2,0},{4,6},{6,4},{8,10},{10,8},{12,14},{14,12},{16,18},{18,... | collective-permute-start | bytes 3538952 | tf_op jit(solution)/shard_map/ppermute | solution.py:1022
  235.0 8.7 %collective-permute-start.72 = (bf16[2,256,256]{2,1,0:T(8,128)(2,1)S(1)}, bf16[2,256,256]{2,1,0:T(8,128)(2,1)S(1)}, u32[]{:S(2)}, u32[]{:S(2)}) collective-permute-start(bf16[2,256,256]{2,1,0:T(8,128)(2,1)S(1)} %get-tuple-element.377), channel_id=1, source_target_pairs={{0,8},{2,10},{4,12},{6,14},{8,0},{10,2},{12,4},{14,6},{16,24},{18,... | collective-permute-start | bytes 786440 | tf_op jit(solution)/shard_map/ppermute | solution.py:1022
  236.6 3.7 %collective-permute-start.61 = (f32[4,512]{1,0:T(4,128)S(1)}, f32[4,512]{1,0:T(4,128)S(1)}, u32[]{:S(2)}, u32[]{:S(2)}) collective-permute-start(f32[4,512]{1,0:T(4,128)S(1)} %add.285), channel_id=1, source_target_pairs={{0,4},{2,6},{4,0},{6,2},{8,12},{10,14},{12,8},{14,10},{16,20},{18,... | collective-permute-start | bytes 24584 | tf_op jit(solution)/shard_map/ppermute | solution.py:1022
  240.3 3.7 %collective-permute-start.62 = (f32[4,512]{1,0:T(4,128)S(1)}, f32[4,512]{1,0:T(4,128)S(1)}, u32[]{:S(2)}, u32[]{:S(2)}) collective-permute-start(f32[4,512]{1,0:T(4,128)S(1)} %add.286), channel_id=1, source_target_pairs={{0,8},{2,10},{4,12},{6,14},{8,0},{10,2},{12,4},{14,6},{16,24},{18,... | collective-permute-start | bytes 24584 | tf_op jit(solution)/shard_map/ppermute | solution.py:1022
  243.9 4.7 %collective-permute-start.63 = (f32[4,512]{1,0:T(4,128)S(1)}, f32[4,512]{1,0:T(4,128)S(1)}, u32[]{:S(2)}, u32[]{:S(2)}) collective-permute-start(f32[4,512]{1,0:T(4,128)S(1)} %add.287), channel_id=1, source_target_pairs={{0,16},{2,18},{4,20},{6,22},{8,24},{10,26},{12,28},{14,30},{16,0},... | collective-permute-start | bytes 24584 | tf_op jit(solution)/shard_map/ppermute | solution.py:1022
  246.3 16.0 %collective-permute-start.65 = (bf16[4,288,256]{2,1,0:T(8,128)(2,1)S(1)}, bf16[4,288,256]{2,1,0:T(8,128)(2,1)S(1)}, u32[]{:S(2)}, u32[]{:S(2)}) collective-permute-start(bf16[4,288,256]{2,1,0:T(8,128)(2,1)S(1)} %get-tuple-element.325), channel_id=1, source_target_pairs={{0,4},{2,6},{4,0},{6,2},{8,12},{10,14},{12,8},{14,10},{16,20},{18,... | collective-permute-start | bytes 1769480 | tf_op jit(solution)/shard_map/ppermute | solution.py:1022
  247.9 33.1 %collective-permute-start.73 = (bf16[1,672,256]{2,1,0:T(8,128)(2,1)S(1)}, bf16[1,672,256]{2,1,0:T(8,128)(2,1)S(1)}, u32[]{:S(2)}, u32[]{:S(2)}) collective-permute-start(bf16[1,672,256]{2,1,0:T(8,128)(2,1)S(1)} %pad_maximum_fusion.1), channel_id=1, source_target_pairs={{0,16},{2,18},{4,20},{6,22},{8,24},{10,26},{12,28},{14,30},{16,0},... | collective-permute-start | bytes 1032200 | tf_op jit(solution)/shard_map/ppermute | solution.py:1022
  250.4 3.7 %collective-permute-start.68 = (bf16[8,64,256]{2,1,0:T(8,128)(2,1)S(1)}, bf16[8,64,256]{2,1,0:T(8,128)(2,1)S(1)}, u32[]{:S(2)}, u32[]{:S(2)}) collective-permute-start(bf16[8,64,256]{2,1,0:T(8,128)(2,1)S(1)} %get-tuple-element.330), channel_id=1, source_target_pairs={{0,2},{2,0},{4,6},{6,4},{8,10},{10,8},{12,14},{14,12},{16,18},{18,... | collective-permute-start | bytes 786440 | tf_op jit(solution)/shard_map/ppermute | solution.py:1022
  250.4 18.4 %collective-permute-start.74 = (bf16[2,384,256]{2,1,0:T(8,128)(2,1)S(1)}, bf16[2,384,256]{2,1,0:T(8,128)(2,1)S(1)}, u32[]{:S(2)}, u32[]{:S(2)}) collective-permute-start(bf16[2,384,256]{2,1,0:T(8,128)(2,1)S(1)} %get-tuple-element.337), channel_id=1, source_target_pairs={{0,8},{2,10},{4,12},{6,14},{8,0},{10,2},{12,4},{14,6},{16,24},{18,... | collective-permute-start | bytes 1179656 | tf_op jit(solution)/shard_map/ppermute | solution.py:1022
  254.1 16.9 %collective-permute-start.69 = (bf16[4,64,256]{2,1,0:T(8,128)(2,1)S(1)}, bf16[4,64,256]{2,1,0:T(8,128)(2,1)S(1)}, u32[]{:S(2)}, u32[]{:S(2)}) collective-permute-start(bf16[4,64,256]{2,1,0:T(8,128)(2,1)S(1)} %get-tuple-element.387), channel_id=1, source_target_pairs={{0,4},{2,6},{4,0},{6,2},{8,12},{10,14},{12,8},{14,10},{16,20},{18,... | collective-permute-start | bytes 393224 | tf_op jit(solution)/shard_map/ppermute | solution.py:1022
  262.3 14.6 %collective-permute-start.66 = (bf16[2,288,256]{2,1,0:T(8,128)(2,1)S(1)}, bf16[2,288,256]{2,1,0:T(8,128)(2,1)S(1)}, u32[]{:S(2)}, u32[]{:S(2)}) collective-permute-start(bf16[2,288,256]{2,1,0:T(8,128)(2,1)S(1)} %get-tuple-element.328), channel_id=1, source_target_pairs={{0,8},{2,10},{4,12},{6,14},{8,0},{10,2},{12,4},{14,6},{16,24},{18,... | collective-permute-start | bytes 884744 | tf_op jit(solution)/shard_map/ppermute | solution.py:1022
  268.9 15.3 %collective-permute-start.75 = (bf16[1,384,256]{2,1,0:T(8,128)(2,1)S(1)}, bf16[1,384,256]{2,1,0:T(8,128)(2,1)S(1)}, u32[]{:S(2)}, u32[]{:S(2)}) collective-permute-start(bf16[1,384,256]{2,1,0:T(8,128)(2,1)S(1)} %get-tuple-element.380), channel_id=1, source_target_pairs={{0,16},{2,18},{4,20},{6,22},{8,24},{10,26},{12,28},{14,30},{16,0},... | collective-permute-start | bytes 589832 | tf_op jit(solution)/shard_map/ppermute | solution.py:1022
  271.0 9.5 %collective-permute-start.70 = (bf16[2,64,256]{2,1,0:T(8,128)(2,1)S(1)}, bf16[2,64,256]{2,1,0:T(8,128)(2,1)S(1)}, u32[]{:S(2)}, u32[]{:S(2)}) collective-permute-start(bf16[2,64,256]{2,1,0:T(8,128)(2,1)S(1)} %get-tuple-element.389), channel_id=1, source_target_pairs={{0,8},{2,10},{4,12},{6,14},{8,0},{10,2},{12,4},{14,6},{16,24},{18,... | collective-permute-start | bytes 196616 | tf_op jit(solution)/shard_map/ppermute | solution.py:1022
  277.0 11.0 %collective-permute-start.67 = (bf16[1,288,256]{2,1,0:T(8,128)(2,1)S(1)}, bf16[1,288,256]{2,1,0:T(8,128)(2,1)S(1)}, u32[]{:S(2)}, u32[]{:S(2)}) collective-permute-start(bf16[1,288,256]{2,1,0:T(8,128)(2,1)S(1)} %get-tuple-element.382), channel_id=1, source_target_pairs={{0,16},{2,18},{4,20},{6,22},{8,24},{10,26},{12,28},{14,30},{16,0},... | collective-permute-start | bytes 442376 | tf_op jit(solution)/shard_map/ppermute | solution.py:1022
  280.5 7.5 %collective-permute-start.71 = (bf16[1,64,256]{2,1,0:T(8,128)(2,1)S(1)}, bf16[1,64,256]{2,1,0:T(8,128)(2,1)S(1)}, u32[]{:S(2)}, u32[]{:S(2)}) collective-permute-start(bf16[1,64,256]{2,1,0:T(8,128)(2,1)S(1)} %get-tuple-element.390), channel_id=1, source_target_pairs={{0,16},{2,18},{4,20},{6,22},{8,24},{10,26},{12,28},{14,30},{16,0},... | collective-permute-start | bytes 98312 | tf_op jit(solution)/shard_map/ppermute | solution.py:1022
  (13 other events, 22.4 us)
